TPU v7x, 256 devices: a whole 4x4x8 slice. The times are simulated.
256 devices in a mesh: group: 32 (over x, y, core), box: 8 (over z).
Axes of the slice: x: 4, y: 4, z: 8, core: 2. Of those that a mesh axis runs over, the one named last changes fastest.
Arguments:
- fine_state: float32 [32, 8, 48, 4, 1024], P('group', 'box'), may hold values from 0.05 to 2
- coarse_state: float32 [32, 8, 48, 1152], P('group', 'box'), may hold values from 0.05 to 2
- coag_kernel: bfloat16 [48, 2304], replicated, may hold values from -0.125 to 0.125
- diffusion: float32 [48], replicated, may hold values from 0.004 to 0.04
- levels: int32 [32, 8], P('group'), may hold values from 1 to 2
- ghost_src: int32 [32, 8, 576], P('group', 'box'), may hold values from 0 to 36863, as said below
Outputs:
- fine_out: float32 [32, 8, 48, 4, 1024], P('group', 'box')
- coarse_out: float32 [32, 8, 48, 1152], P('group', 'box')
Inputs may be any that keep to these rules, and one draw needn't show every extreme that they name: `ghost_src`: an entry o * 1152 + c names coarse cell c of the owner in group o of the same box column; entries of one box come from a few owners and from scattered ones.
All inputs are finite; a program needn't handle non-finite values.
Results may differ from a plain program's by a relative error of at most 0.00065.
Values sent between devices are 32-bit elements; how exact they have to be, the bound alone decides.
No kernel may reach another device: no remote copies, remote signals or barrier semaphores. Data moves between devices by JAX's collectives and lax.ppermute only.
A program may use at most 128 MiB of HBM per device.

v0:
```python
import math

import jax
import jax.numpy as jnp
from jax import lax
from jax.sharding import PartitionSpec as P

BOX_X = 4
BOX_Y = 32
BOX_Z = 32


step_size = 0.25


def padded_2(block, sides, width):
    for axis, dim in sides:
        count = lax.axis_size(axis)
        forward = [(i, i + 1) for i in range(count - 1)]
        backward = [(target, source) for source, target in forward]
        low = lax.ppermute(
            lax.slice_in_dim(block, block.shape[dim] - width, None, axis=dim), axis, forward
        )
        high = lax.ppermute(lax.slice_in_dim(block, 0, width, axis=dim), axis, backward)
        block = jnp.concatenate([low, block, high], axis=dim)
    return block


def coagulate(field, kernel):
    sections = field.shape[0]
    cells = field.shape[1]
    block_width = math.gcd(cells, 1024)
    blocks = jnp.moveaxis(field.reshape(sections, cells // block_width, block_width), 1, 0)

    def one_block(block_cells):
        pair_rows = (
            (block_cells[:, None, :] * block_cells[None, :, :])
            .reshape(sections * sections, block_width)
            .astype(jnp.bfloat16)
        )
        return jnp.dot(kernel, pair_rows, preferred_element_type=jnp.float32)

    return jnp.moveaxis(lax.map(one_block, blocks), 0, 1).reshape(sections, cells)


def face_values(ghost_strip, box_shape):
    sections, width_x, width_y, width_z = box_shape
    y_count = width_x * width_z // 2
    y_coarse = ghost_strip[:, :y_count].reshape(sections, 2, width_x // 2, width_z // 2)
    x_coarse = ghost_strip[:, y_count:].reshape(sections, 2, width_y // 2, width_z // 2)
    y_ghost = jnp.repeat(jnp.repeat(y_coarse, 2, axis=2), 2, axis=3)
    x_ghost = jnp.repeat(jnp.repeat(x_coarse, 2, axis=2), 2, axis=3)
    return (y_ghost, x_ghost)


def laplacian(current, x_lower, x_upper, y_ghost):
    along_x = jnp.concatenate([x_lower[:, None], current, x_upper[:, None]], axis=1)
    along_y = jnp.concatenate(
        [y_ghost[:, 0][:, :, None], current, y_ghost[:, 1][:, :, None]], axis=2
    )
    along_z = jnp.concatenate([current[..., :1], current, current[..., -1:]], axis=3)
    spread = along_x[:, 2:] + along_x[:, :-2] + along_y[:, :, 2:] + along_y[:, :, :-2]
    spread = spread + along_z[..., 2:] + along_z[..., :-2]
    return spread - 6.0 * current


def box_rate(
    current, lower_plane, upper_plane, ghost_strip, use_low, use_high, box_factor, diffusion, kernel
):
    y_ghost, x_ghost = face_values(ghost_strip, current.shape)
    x_lower = jnp.where(use_low, lower_plane, x_ghost[:, 0])
    x_upper = jnp.where(use_high, upper_plane, x_ghost[:, 1])
    spread = laplacian(current, x_lower, x_upper, y_ghost)
    sections = current.shape[0]
    growth = coagulate(current.reshape(sections, -1), kernel).reshape(current.shape)
    return (box_factor * diffusion)[:, None, None, None] * spread + step_size * growth


def coarsen(plane):
    sections, first_len, last_len = plane.shape
    return (
        plane.reshape(sections, first_len // 2, 2, last_len // 2, 2)
        .mean(axis=(2, 4))
        .reshape(sections, -1)
    )


def register_terms(mean_field, ghost_strip, use_low, use_high, box_factor, diffusion):
    sections, width_x, width_y, width_z = mean_field.shape
    below = jnp.concatenate(
        [
            coarsen(mean_field[:, :, 0, :]),
            coarsen(mean_field[:, :, -1, :]),
            coarsen(mean_field[:, 0]),
            coarsen(mean_field[:, -1]),
        ],
        axis=1,
    )
    y_count = width_x * width_z // 2
    x_each = width_y * width_z // 4
    face_mask = jnp.concatenate(
        [
            jnp.ones((y_count,), jnp.float32),
            jnp.ones((x_each,), jnp.float32) * jnp.where(use_low, 0.0, 1.0),
            jnp.ones((x_each,), jnp.float32) * jnp.where(use_high, 0.0, 1.0),
        ]
    )
    return ((box_factor - 1.0) * diffusion)[:, None] * (ghost_strip - below) * face_mask[None, :]


def on_device(fine_state, coarse_state, coag_kernel, diffusion, levels, ghost_src):
    merged_box = fine_state[0, 0]
    sections = merged_box.shape[0]
    fine_box = merged_box.reshape(sections, BOX_X, BOX_Y, BOX_Z)
    coarse = coarse_state[0, 0]
    targets = ghost_src[0, 0]
    cells_c = coarse.shape[1]
    box_count = lax.axis_size("box")
    my_box = lax.axis_index("box")
    level_row = levels[0]
    positions = jnp.arange(box_count)
    own_level = jnp.sum(jnp.where(positions == my_box, level_row, 0))
    left_level = jnp.sum(jnp.where(positions == my_box - 1, level_row, 0))
    right_level = jnp.sum(jnp.where(positions == my_box + 1, level_row, 0))
    use_low = (my_box > 0) & (left_level == own_level)
    use_high = (my_box < box_count - 1) & (right_level == own_level)
    box_factor = jnp.power(2.0, own_level.astype(jnp.float32))
    columns = lax.all_gather(coarse, "group", axis=1, tiled=True)
    inside = (targets >= 0) & (targets < columns.shape[1])
    values = jnp.take(columns, jnp.clip(targets, 0, columns.shape[1] - 1), axis=1)
    ghost_strip = jnp.where(inside[None, :], values, 0.0)

    def segment_rate(current):
        padded = padded_2(current, (("box", 1),), 1)
        return box_rate(
            current,
            padded[:, 0],
            padded[:, -1],
            ghost_strip,
            use_low,
            use_high,
            box_factor,
            diffusion,
            coag_kernel,
        )

    rate_one = segment_rate(fine_box)
    middle = fine_box + rate_one
    rate_two = segment_rate(middle)
    fine_out = fine_box + 0.5 * (rate_one + rate_two)
    mean_field = 0.5 * (fine_box + middle)
    registers = register_terms(mean_field, ghost_strip, use_low, use_high, box_factor, diffusion)
    growth = coagulate(coarse, coag_kernel)
    owners = jnp.arange(lax.axis_size("group") * 1)

    def one_owner(owner_id):
        slot_index = jnp.where(targets // cells_c == owner_id, targets % cells_c, cells_c)
        return (
            jnp.zeros((sections, cells_c), jnp.float32)
            .at[:, slot_index]
            .add(registers, mode="drop")
        )

    correction = lax.psum_scatter(
        jax.vmap(one_owner)(owners), "group", scatter_dimension=0, tiled=True
    )[0]
    coarse_out = coarse + step_size * growth - correction
    return (fine_out.reshape(sections, BOX_X, BOX_Y * BOX_Z)[None, None], coarse_out[None, None])


def solution(mesh):
    return jax.shard_map(
        on_device,
        mesh=mesh,
        in_specs=(
            P("group", "box", None, None, None),
            P("group", "box", None, None),
            P(),
            P(),
            P("group", None),
            P("group", "box", None),
        ),
        out_specs=(P("group", "box", None, None, None), P("group", "box", None, None)),
        check_vma=False,
    )
```

profile of v0, /device:TPU:1, one launch (start us, length us, event | category | flops | bytes accessed | tf_op | source)
XLA Modules:
  0.0 378.2 jit_solution(2923427241297973739)
XLA Ops:
  7.2 2.0 copy.110
  9.3 2.5 copy.142
  11.8 2.1 reshape_squeeze.18
  15.2 2.4 copy.114
  17.5 5.2 %collective-permute-start.1 = (f32[48,1,32,32]{0,3,2,1:T(8,128)}, f32[48,1,32,32]{0,3,2,1:T(8,128)}, u32[]{:S(2)}, u32[]{:S(2)}) collective-permute-start(f32[48,1,32,32]{0,3,2,1:T(8,128)} %copy.114), channel_id=1, source_target_pairs={{0,1},{1,2},{2,3},{3,4},{4,5},{5,6},{6,7},{8,9},{9,10},{10,11},{11... | collective-permute-start | bytes 589832 | tf_op jit(solution)/shard_map/ppermute | solution.py:21
  22.8 2.3 copy.109
  26.6 1.8 reshape_squeeze.19
  34.3 16.2 %while.30 = (s32[]{:T(128)}, f32[4,48,1024]{2,1,0:T(8,128)}, f32[4,48,1024]{2,1,0:T(8,128)}, bf16[48,2304]{1,0:T(8,128)(2,1)S(1)}, s32[]{:T(128)}) while((s32[]{:T(128)}, f32[4,48,1024]{2,1,0:T(8,128)}, f32[4,48,1024]{2,1,0:T(8,128)}, bf16[48,2304]{1,0:T(8,128)(2,1)S(1)}, s32[]{:T(128)}) %tuple.95), condition=%wide.region_4.5_spmd, body=%wide.region_3.4_spmd.sunk | while | flops 231211008 | bytes 10444877 | solution.py:43
  36.8 1.6 fusion.56
  48.9 1.6 fusion.56
  50.5 2.1 multiply_bitcast_fusion.1
  52.6 3.3 mul.157
  56.2 3.7 fusion.36
  60.5 2.6 copy.116
  63.0 2.5 copy.113
  65.6 31.8 %all-gather.3.cloned.1.call-done = f32[1,1,48,36864]{2,3,1,0:T(8,128)} async-done(((f32[1,1,48,1152]{2,3,1,0:T(8,128)}), f32[1,1,48,36864]{2,3,1,0:T(8,128)}) %all-gather.3.cloned.1.call-update) | async-done | bytes 7077904 | tf_op jit(solution)/shard_map/all_gather | solution.py:128
  97.4 8.6 %gather_fusion = f32[576,48]{1,0:T(8,128)} fusion(f32[48,36864]{0,1:T(8,128)} %bitcast.157, s32[1024]{0:T(1024)S(1)} %pad_clamp_fusion), kind=kCustom, calls=%fused_computation | custom fusion | bytes 223488 | tf_op jit(solution)/shard_map/jit(_take)/gather | solution.py:130
  112.8 2.6 copy.136
  115.3 2.6 copy.137
  120.7 7.3 %add_multiply_fusion = (f32[48,4,32,32]{3,2,0,1:T(8,128)S(1)}, f32[48,4,32,32]{3,2,0,1:T(8,128)}, f32[48,4,32,32]{3,2,0,1:T(8,128)}) fusion(f32[48,4,32,32]{3,2,0,1:T(8,128)S(1)} %reshape_squeeze.18, f32[48,4,32,32]{3,2,0,1:T(8,128)S(1)} %copy-done.2, f32[48,4,32,1]{3,2,0,1:T(8,128)} %get-tuple-element.147, f32[48,4,32,1]{3,2,0,1:T(8,128)} %get-tuple-element.146, ...), kind=kLoop, calls=%fused_computation.47 | loop fusion | flops 3538944 | bytes 4423872 | tf_op jit(solution)/shard_map/mul | solution.py:151
  127.9 1.7 copy-done.3
  132.8 3.5 fusion.32
  136.3 2.3 copy.128
  138.6 2.1 reduce_sum.68
  144.7 2.3 copy.129
  147.0 2.1 reduce_sum.69
  151.4 4.8 %broadcast_in_dim.108 = f32[32,48,576]{1,2,0:T(8,128)} broadcast(f32[48,576]{0,1:T(8,128)S(1)} %fusion.25), dimensions={1,2} | broadcast | bytes 3649536 | tf_op jit(solution)/shard_map/vmap()/broadcast_in_dim | solution.py:161
  156.2 106.1 %scatter_custom_fusion = f32[36864,48]{1,0:T(8,128)} fusion(s32[18432]{0:T(1024)} %reshape.232, f32[18432,48]{1,0:T(8,128)} %bitcast.134, f32[]{:T(128)} %constant.91.clone.1), kind=kCustom, calls=%fused_computation.14 | custom fusion | flops 884736 | bytes 7078400
  262.3 14.3 %copy.131 = f32[32,1152,48]{1,2,0:T(8,128)} copy(f32[32,1152,48]{2,1,0:T(8,128)} %bitcast.131) | data formatting | bytes 14155776
  276.6 17.2 %while.32 = (s32[]{:T(128)}, f32[9,48,128]{2,1,0:T(8,128)}, f32[9,48,128]{2,0,1:T(8,128)}, bf16[48,2304]{1,0:T(8,128)(2,1)S(1)}, s32[]{:T(128)}) while((s32[]{:T(128)}, f32[9,48,128]{2,1,0:T(8,128)}, f32[9,48,128]{2,0,1:T(8,128)}, bf16[48,2304]{1,0:T(8,128)(2,1)S(1)}, s32[]{:T(128)}) %tuple.97), condition=%wide.region_8.9_spmd, body=%wide.region_7.8_spmd.sunk | while | flops 28901376 | bytes 1499213 | solution.py:43
  295.6 1.8 mul.167
  297.4 3.7 reshape_reshape.2
  301.1 2.4 copy.122
  303.5 2.4 copy.120
  307.1 4.8 %collective-permute-start.3 = (f32[48,1,32,32]{0,3,2,1:T(8,128)}, f32[48,1,32,32]{0,3,2,1:T(8,128)}, u32[]{:S(2)}, u32[]{:S(2)}) collective-permute-start(f32[48,1,32,32]{0,3,2,1:T(8,128)} %copy.122), channel_id=1, source_target_pairs={{0,1},{1,2},{2,3},{3,4},{4,5},{5,6},{6,7},{8,9},{9,10},{10,11},{11... | collective-permute-start | bytes 589832 | tf_op jit(solution)/shard_map/ppermute | solution.py:21
  312.0 6.8 %fusion.34 = (f32[48,4,32,1]{3,2,0,1:T(8,128)}, f32[48,4,32,1]{3,2,0,1:T(8,128)}) fusion(f32[48,4,32,32]{3,2,0,1:T(8,128)} %get-tuple-element.134), kind=kLoop, calls=%fused_computation.96 | loop fusion | bytes 98304 | tf_op jit(solution)/shard_map/slice | solution.py:61
  319.7 16.2 %while.31 = (s32[]{:T(128)}, f32[4,48,1024]{2,1,0:T(8,128)}, f32[4,48,1024]{2,1,0:T(8,128)}, bf16[48,2304]{1,0:T(8,128)(2,1)S(1)}, s32[]{:T(128)}) while((s32[]{:T(128)}, f32[4,48,1024]{2,1,0:T(8,128)}, f32[4,48,1024]{2,1,0:T(8,128)}, bf16[48,2304]{1,0:T(8,128)(2,1)S(1)}, s32[]{:T(128)}) %tuple.96), condition=%wide.region_6.7_spmd, body=%wide.region_5.6_spmd.sunk | while | flops 231211008 | bytes 10444877 | solution.py:43
  322.1 1.6 fusion.59
  326.1 1.6 fusion.59
  330.2 1.6 fusion.59
  335.9 2.1 multiply_bitcast_fusion
  338.0 3.3 mul.162
  341.3 2.5 copy.121
  343.8 2.6 copy.123
  349.2 8.6 %fusion.21 = f32[48,4,32,32]{3,2,0,1:T(8,128)} fusion(f32[48,4,32,32]{3,2,0,1:T(8,128)S(1)} %reshape_squeeze.18, f32[48,4,32,32]{3,2,0,1:T(8,128)} %get-tuple-element.135, f32[48,4,32,32]{3,2,0,1:T(8,128)} %mul.162, f32[48,4,1,32]{3,2,0,1:T(1,128)S(1)} %bitcast.144, f32[48,4,1,32]{3,2,0,1:T(1,128)S(1)} %bitcast.146, f32[48,4,32,32]{3,2,0,1:T(8,128)S(1)} %copy-done, ...), kind=kLoop, calls=%fused_computation.36 | loop fusion | flops 3538944 | bytes 4423872 | tf_op jit(solution)/shard_map/add | solution.py:150
  357.8 3.0 broadcast_in_dim_reshape.3
  362.2 7.4 %reduce-scatter.2.cloned.1.call-done = f32[1,48,1152]{2,1,0:T(8,128)} async-done(((f32[32,48,1152]{2,1,0:T(8,128)}), f32[1,48,1152]{2,1,0:T(8,128)}) %reduce-scatter.2.cloned.1.call-update) | async-done | bytes 221200 | tf_op jit(solution)/shard_map/reduce_scatter | solution.py:164
  369.7 1.7 bitcast_subtract_fusion
  (138 shorter events, 74.6 us)
Async XLA Ops:
  7.2 90.2 %all-gather.3.cloned.1.call-start = ((), (), s32[]{:S(2)}) async-start(), calls=%async_computation.2 | async-start | bytes 19464192 | tf_op jit(solution)/shard_map/all_gather | solution.py:128
  9.2 360.5 %reduce-scatter.2.cloned.1.call-start = ((), (), s32[]{:S(2)}) async-start(), calls=%async_computation.1 | async-start | bytes 7299072 | tf_op jit(solution)/shard_map/reduce_scatter | solution.py:164
  13.8 14.5 %copy-start.14 = (s32[1,8]{1,0:T(1,128)S(1)}, s32[1,8]{1,0:T(1,128)}, u32[]{:S(2)}) copy-start(s32[1,8]{1,0:T(1,128)} %param.16) | copy-start | bytes 100
  13.9 18.4 %copy-start.8 = (s32[1,1,576]{2,1,0:T(1,128)S(1)}, s32[1,1,576]{2,1,0:T(1,128)}, u32[]{:S(2)}) copy-start(s32[1,1,576]{2,1,0:T(1,128)} %param.17) | copy-start | bytes 6916
  13.9 18.5 %copy-start.13 = (s32[2]{0:T(128)S(1)}, s32[2]{0:T(128)}, u32[]{:S(2)}) copy-start(s32[2]{0:T(128)} %constant.103) | copy-start | bytes 28
  13.9 18.6 %copy-start.12 = (s32[2]{0:T(128)S(1)}, s32[2]{0:T(128)}, u32[]{:S(2)}) copy-start(s32[2]{0:T(128)} %constant.106) | copy-start | bytes 28
  15.2 19.2 %copy-start.1 = (bf16[48,2304]{1,0:T(8,128)(2,1)S(1)}, bf16[48,2304]{1,0:T(8,128)(2,1)}, u32[]{:S(2)}) copy-start(bf16[48,2304]{1,0:T(8,128)(2,1)} %param.14) | copy-start | bytes 663556
  17.5 42.9 %collective-permute-start.1 = (f32[48,1,32,32]{0,3,2,1:T(8,128)}, f32[48,1,32,32]{0,3,2,1:T(8,128)}, u32[]{:S(2)}, u32[]{:S(2)}) collective-permute-start(f32[48,1,32,32]{0,3,2,1:T(8,128)} %copy.114), channel_id=1, source_target_pairs={{0,1},{1,2},{2,3},{3,4},{4,5},{5,6},{6,7},{8,9},{9,10},{10,11},{11... | collective-permute-start | bytes 589832 | tf_op jit(solution)/shard_map/ppermute | solution.py:21
  25.1 37.9 %collective-permute-start = (f32[48,1,32,32]{0,3,2,1:T(8,128)}, f32[48,1,32,32]{0,3,2,1:T(8,128)}, u32[]{:S(2)}, u32[]{:S(2)}) collective-permute-start(f32[48,1,32,32]{0,3,2,1:T(8,128)} %copy.109), channel_id=1, source_target_pairs={{1,0},{2,1},{3,2},{4,3},{5,4},{6,5},{7,6},{9,8},{10,9},{11,10},{12... | collective-permute-start | bytes 589832 | tf_op jit(solution)/shard_map/ppermute | solution.py:24
  32.3 73.7 %copy-start.9 = (pred[576]{0:T(1024)(128)(4,1)}, pred[576]{0:T(1024)(128)(4,1)S(1)}, u32[]{:S(2)}) copy-start(pred[576]{0:T(1024)(128)(4,1)S(1)} %get-tuple-element.102) | copy-start | bytes 1732
  56.2 3.7 copy-start.15
  60.4 60.2 %copy-start.10 = (f32[48]{0:T(128)}, f32[48]{0:T(128)S(1)}, u32[]{:S(2)}) copy-start(f32[48]{0:T(128)S(1)} %get-tuple-element.157) | copy-start | bytes 580
  117.9 2.7 copy-start.2
  117.9 2.8 copy-start.5
  127.9 1.7 copy-start.3
  305.9 35.4 %collective-permute-start.2 = (f32[48,1,32,32]{0,3,2,1:T(8,128)}, f32[48,1,32,32]{0,3,2,1:T(8,128)}, u32[]{:S(2)}, u32[]{:S(2)}) collective-permute-start(f32[48,1,32,32]{0,3,2,1:T(8,128)} %copy.120), channel_id=1, source_target_pairs={{1,0},{2,1},{3,2},{4,3},{5,4},{6,5},{7,6},{9,8},{10,9},{11,10},{12... | collective-permute-start | bytes 589832 | tf_op jit(solution)/shard_map/ppermute | solution.py:24
  307.1 36.7 %collective-permute-start.3 = (f32[48,1,32,32]{0,3,2,1:T(8,128)}, f32[48,1,32,32]{0,3,2,1:T(8,128)}, u32[]{:S(2)}, u32[]{:S(2)}) collective-permute-start(f32[48,1,32,32]{0,3,2,1:T(8,128)} %copy.122), channel_id=1, source_target_pairs={{0,1},{1,2},{2,3},{3,4},{4,5},{5,6},{6,7},{8,9},{9,10},{10,11},{11... | collective-permute-start | bytes 589832 | tf_op jit(solution)/shard_map/ppermute | solution.py:21
  343.8 5.4 %copy-start.6 = (f32[48,1,4,32]{3,0,2,1:T(8,128)S(1)}, f32[48,1,4,32]{3,0,2,1:T(8,128)}, u32[]{:S(2)}) copy-start(f32[48,1,4,32]{3,0,2,1:T(8,128)} %copy.139) | copy-start | bytes 73732
  343.8 5.4 %copy-start.11 = (f32[48]{0:T(128)S(1)}, f32[48]{0:T(128)}, u32[]{:S(2)}) copy-start(f32[48]{0:T(128)} %copy-done.10) | copy-start | bytes 580
  346.4 2.8 copy-start
  357.8 11.9 %copy-start.4 = (f32[1,1,48,1152]{3,2,1,0:T(8,128)S(1)}, f32[1,1,48,1152]{3,2,1,0:T(8,128)}, u32[]{:S(2)}) copy-start(f32[1,1,48,1152]{3,2,1,0:T(8,128)} %param.13) | copy-start | bytes 663556
  357.8 11.9 %copy-start.7 = (f32[1,1,48,1152]{3,2,1,0:T(8,128)S(1)}, f32[1,1,48,1152]{3,2,1,0:T(8,128)}, u32[]{:S(2)}) copy-start(f32[1,1,48,1152]{3,2,1,0:T(8,128)} %mul.167) | copy-start | bytes 663556
Sparse Core Ops, SparseCore 0:
  10.5 86.7 all-gather.2
  276.7 92.9 reduce-scatter.1
where the time goes:
time: 381 us; the launch traced here: 378 us
  other arithmetic  161 us (42%)
  local copies, waits for them, and re-layouts  127 us (33%)
  waiting for transfers between devices  39.3 us (10%)
  matrix products  20.7 us (5%)
  between operations  17.6 us (5%)
  starting transfers between devices  12.9 us (3%)
    unnamed x4, other arithmetic  106 us
    all_gather x1, waiting for transfers between devices, on_device(): columns = lax.all_gather(coarse, 'group', axis=1, tiled=True)  31.8 us
    unnamed x42, local copies, waits for them, and re-layouts  29.4 us
    dot_general x17, matrix products, one_block(): return jnp.dot(kernel, pair_rows, preferred_element_type=jnp.float32)  20.7 us
    convert_element_type x17, other arithmetic, one_block(): pair_rows = (block_cells[:, None, :] * block_cells[None, :, :]).reshape(s...  12.6 us
    slice x2, local copies, waits for them, and re-layouts, laplacian(): current[..., -1:]  10.4 us
    ppermute x2, starting transfers between devices, padded_2(): lax.ppermute(lax.slice_in_dim(block, block.shape[dim] - width, None, axis...  10 us
    add x1, other arithmetic, on_device(): fine_out = fine_box + 0.5 * (rate_one + rate_two)  8.6 us
  transfers between devices with their start and end apart: 6, of which 2 were waited for; matrix products, arithmetic and copies ran while one was open for 33% of the time, Pallas kernels for 0%

commit v1 on v0

v1 whole, which is shorter than its diff:
```python
import jax
import jax.numpy as jnp
from jax import lax
from jax.experimental import pallas as pl
from jax.experimental.pallas import tpu as pltpu
from jax.sharding import Mesh, PartitionSpec as P

S = 48
X = 4
PLANE = 1024
CELLS = 1152
GHOSTS = 576
WIDE = 640
STEP = 0.25
MIB = 1024 * 1024

f32 = jnp.float32
bf16 = jnp.bfloat16
i32 = jnp.int32
VMEM = pl.BlockSpec(memory_space=pltpu.VMEM)
SMEM = pl.BlockSpec(memory_space=pltpu.SMEM)


def sds(*shape):
    return jax.ShapeDtypeStruct(shape, f32)


def call(kernel, out_shape, in_specs, *operands, scratch=(), flops=0, name=None):
    many = isinstance(out_shape, list)
    return pl.pallas_call(
        kernel,
        out_shape=out_shape,
        in_specs=in_specs,
        out_specs=[VMEM] * len(out_shape) if many else VMEM,
        scratch_shapes=list(scratch),
        compiler_params=pltpu.CompilerParams(vmem_limit_bytes=40 * MIB),
        cost_estimate=pl.CostEstimate(flops=flops, bytes_accessed=4 * MIB, transcendentals=0),
        name=name,
    )(*operands)


def mm(a, b):
    return jnp.dot(a, b, preferred_element_type=f32)


def halves(value):
    high = value.astype(bf16)
    return high, (value - high.astype(f32)).astype(bf16)


def rows_of(values):
    parts = []
    for value in values:
        parts.extend(halves(value))
    return jnp.concatenate(parts, axis=0)


def sums_of(product, count):
    return [product[2 * S * i : 2 * S * i + S] + product[2 * S * i + S : 2 * S * (i + 1)] for i in range(count)]


def ones_where(mask):
    return jnp.where(mask, 1.0, 0.0).astype(bf16)


def split_planes(fine):
    def kernel(fine_ref, *planes):
        for x in range(X):
            planes[x][...] = fine_ref[:, x, :]

    return call(kernel, [sds(S, PLANE)] * X, [VMEM], fine, name="split_planes")


def coagulate(kernel_matrix, fields, name):
    count = len(fields)

    def kernel(matrix_ref, *refs):
        for field_ref, out_ref in zip(refs[:count], refs[count:]):
            width = field_ref.shape[1]
            for start in range(0, width, 1024):
                stop = min(start + 1024, width)
                v = field_ref[:, start:stop]
                pairs = jnp.concatenate([(v[j : j + 1] * v).astype(bf16) for j in range(S)], axis=0)
                out_ref[:, start:stop] = mm(matrix_ref[...], pairs)

    cells = sum(f.shape[1] for f in fields)
    return call(
        kernel,
        [sds(*f.shape) for f in fields],
        [VMEM] * (count + 1),
        kernel_matrix,
        *fields,
        flops=6 * cells * 2304 * 128,
        name=name,
    )


def owner_and_cell(request):
    owner = jnp.floor((request.astype(f32) + 0.5) * (1.0 / CELLS)).astype(i32)
    return owner, jnp.where(request < 0, -1, request - owner * CELLS)


def gather_columns(requests, sources, shifts, before, name):
    count = len(sources)

    def kernel(*refs):
        request_refs, source_refs = refs[:4], refs[4 : 4 + count]
        before_refs = refs[4 + count : 4 + count + len(before)]
        outs = refs[4 + count + len(before) : 8 + count + len(before)]
        x, y, c = lax.axis_index("x"), lax.axis_index("y"), lax.axis_index("core")
        rows = rows_of([ref[...] for ref in source_refs])
        cell_id = lax.broadcasted_iota(i32, (CELLS, 2 * WIDE), 0)
        for half in range(2):
            request = jnp.concatenate([request_refs[2 * half][...], request_refs[2 * half + 1][...]], axis=1)
            owner, cell = owner_and_cell(request)
            product = mm(rows, ones_where(jnp.broadcast_to(cell, (CELLS, 2 * WIDE)) == cell_id))
            total = jnp.zeros((S, 2 * WIDE), f32)
            for part, (shift, mate) in zip(sums_of(product, count), shifts):
                from_x = jnp.bitwise_and(x - shift, 3)
                source_owner = (from_x * 4 + y) * 2 + (1 - c if mate else c)
                total = total + jnp.where(owner == source_owner, part, 0.0)
            for i in range(2):
                part = total[:, i * WIDE : (i + 1) * WIDE]
                if before:
                    part = part + before_refs[2 * half + i][...]
                outs[2 * half + i][...] = part

    return call(
        kernel,
        [sds(S, WIDE)] * 4,
        [VMEM] * (4 + count + len(before)),
        *requests,
        *sources,
        *before,
        flops=2 * 4 * WIDE * CELLS * 256,
        name=name,
    )


def scatter_columns(requests, registers):
    total = 8 * WIDE

    def kernel(request_a, request_b, *refs):
        register_refs, outs, rows_ref, cell_ref = refs[:8], refs[8:12], refs[12], refs[13]
        x, y, c = lax.axis_index("x"), lax.axis_index("y"), lax.axis_index("core")
        lane = lax.broadcasted_iota(i32, (1, 256), 1)
        for i in range(8):
            request = (request_a if i < 4 else request_b)[i % 4 : i % 4 + 1, :]
            owner, cell = owner_and_cell(request)
            high, low = halves(register_refs[i][...])
            for k in range(4):
                to_x = jnp.bitwise_and(x + k, 3)
                mine = jnp.broadcast_to(jnp.where(owner == (to_x * 4 + y) * 2 + c, 1.0, 0.0).astype(bf16), (S, WIDE))
                rows_ref[2 * S * k : 2 * S * k + S, i * WIDE : (i + 1) * WIDE] = high * mine
                rows_ref[2 * S * k + S : 2 * S * (k + 1), i * WIDE : (i + 1) * WIDE] = low * mine
            for t in range(WIDE // 128):
                block = jnp.broadcast_to(cell[:, t * 128 : (t + 1) * 128].astype(f32), (128, 128))
                cell_ref[i * WIDE + t * 128 : i * WIDE + (t + 1) * 128, :] = block.T.astype(i32)

        def block(start, width):
            marks = [
                ones_where(cell_ref[...] == lane[:, :128] + (start + 128 * t)) for t in range(width // 128)
            ]
            product = mm(rows_ref[...], jnp.concatenate(marks, axis=1))
            return sums_of(product, 4)

        def body(i, carry):
            start = pl.multiple_of(i * 256, 256)
            for out, part in zip(outs, block(start, 256)):
                out[:, pl.ds(start, 256)] = part
            return carry

        lax.fori_loop(0, 4, body, 0)
        for out, part in zip(outs, block(1024, 128)):
            out[:, 1024:CELLS] = part

    return call(
        kernel,
        [sds(S, CELLS)] * 4,
        [VMEM] * 10,
        *requests,
        *registers,
        scratch=[pltpu.VMEM((8 * S, total), bf16), pltpu.VMEM((total, 128), i32)],
        flops=2 * total * CELLS * 384,
        name="scatter_columns",
    )


def box_facts(levels_ref):
    box = lax.axis_index("box")
    last = 7
    own = levels_ref[0, box]
    use_low = (box > 0) & (levels_ref[0, jnp.maximum(box - 1, 0)] == own)
    use_high = (box < last) & (levels_ref[0, jnp.minimum(box + 1, last)] == own)
    factor = lax.shift_left(1, own).astype(f32)
    return use_low, use_high, factor


def laplacian(planes, lower, upper, y_ghosts):
    lane = lax.broadcasted_iota(i32, (S, PLANE), 1)
    z = jnp.bitwise_and(lane, 31)
    wide = lax.broadcasted_iota(i32, (S, 128), 1)
    result = []
    for x in range(X):
        v = planes[x]
        ghost = y_ghosts[x // 2]
        before_y = pltpu.roll(v, 32, 1)
        after_y = pltpu.roll(v, PLANE - 32, 1)
        before_y = jnp.concatenate(
            [jnp.where(wide < 32, ghost[:, :128], before_y[:, :128]), before_y[:, 128:]], axis=1
        )
        after_y = jnp.concatenate(
            [after_y[:, :896], jnp.where(wide >= 96, ghost[:, 128:], after_y[:, 896:])], axis=1
        )
        before_z = jnp.where(z == 0, v, pltpu.roll(v, 1, 1))
        after_z = jnp.where(z == 31, v, pltpu.roll(v, PLANE - 1, 1))
        before_x = planes[x - 1] if x > 0 else lower
        after_x = planes[x + 1] if x < X - 1 else upper
        result.append(before_x + after_x + before_y + after_y + before_z + after_z - 6.0 * v)
    return result


def y_code(shape, lane_dim, row_dim, half):
    lane = lax.broadcasted_iota(i32, shape, lane_dim)
    row = lax.broadcasted_iota(i32, shape, row_dim)
    fine = jnp.where(lane < 32, lane, lane - 192)
    code = jnp.where(lane < 32, half * 16 + (lane >> 1), 32 + half * 16 + ((lane - 224) >> 1))
    return ones_where((code == row) & ((lane < 32) | (lane >= 224)))


def x_code(shape, lane_dim, row_dim):
    lane = lax.broadcasted_iota(i32, shape, lane_dim)
    row = lax.broadcasted_iota(i32, shape, row_dim)
    return ones_where((((lane >> 6) << 4) | ((lane >> 1) & 15)) == row)


def first_stage(levels, diffusion, planes, growth, strips, below_plane, above_plane):
    def kernel(levels_ref, diffusion_ref, *refs):
        plane_refs, growth_refs, strip_refs = refs[:4], refs[4:8], refs[8:12]
        lower_ref, upper_ref = refs[12:14]
        middle_refs, base_refs = refs[14:18], refs[18:22]
        registers_ref, x_low_ref, x_high_ref = refs[22:25]
        y_refs = refs[25:27]
        use_low, use_high, factor = box_facts(levels_ref)
        diffusion_column = diffusion_ref[...]
        strip = strip_refs[0][...] + strip_refs[1][...] + strip_refs[2][...] + strip_refs[3][...]
        x_low, x_high = sums_of(mm(rows_of([strip[:, :256], strip[:, 256:512]]), x_code((256, PLANE), 1, 0)), 2)
        y_rows = rows_of([strip[:, 512:640]])
        y_ghosts = [sums_of(mm(y_rows, y_code((128, 256), 1, 0, half)), 1)[0] for half in range(2)]
        x_low_ref[...] = x_low
        x_high_ref[...] = x_high
        for ref, ghost in zip(y_refs, y_ghosts):
            ref[...] = ghost
        lower = jnp.where(use_low, lower_ref[...], x_low)
        upper = jnp.where(use_high, upper_ref[...], x_high)
        values = [ref[...] for ref in plane_refs]
        spread = laplacian(values, lower, upper, y_ghosts)
        means = []
        for x in range(X):
            rate = (factor * diffusion_column) * spread[x] + STEP * growth_refs[x][...]
            middle = values[x] + rate
            middle_refs[x][...] = middle
            base_refs[x][...] = values[x] + 0.5 * rate
            means.append(0.5 * (values[x] + middle))
        x_below = sums_of(mm(rows_of([means[0], means[3]]), x_code((PLANE, 256), 0, 1)), 2)
        y_below = jnp.zeros((S, 128), f32)
        for half in range(2):
            both = means[2 * half] + means[2 * half + 1]
            ends = jnp.concatenate([both[:, :128], both[:, 896:]], axis=1)
            y_below = y_below + sums_of(mm(rows_of([ends]), y_code((256, 128), 0, 1, half)), 1)[0]
        below = 0.25 * jnp.concatenate(x_below + [y_below], axis=1)
        column = lax.broadcasted_iota(i32, (1, WIDE), 1)
        keep_low = jnp.where(use_low, 0.0, 1.0)
        keep_high = jnp.where(use_high, 0.0, 1.0)
        keep = jnp.where(column < 256, keep_low, jnp.where(column < 512, keep_high, 1.0))
        registers_ref[...] = ((factor - 1.0) * diffusion_column) * (strip - below) * keep

    outs = call(
        kernel,
        [sds(S, PLANE)] * 8 + [sds(S, WIDE)] + [sds(S, PLANE)] * 2 + [sds(S, 256)] * 2,
        [SMEM] + [VMEM] * 15,
        levels,
        diffusion,
        *planes,
        *growth,
        *strips,
        below_plane,
        above_plane,
        flops=10**9,
        name="first_stage",
    )
    return outs[:4], outs[4:8], outs[8], outs[9:11], outs[11:13]


def second_stage(levels, diffusion, middle, base, growth, x_ghosts, y_ghosts, below_plane, above_plane):
    def kernel(levels_ref, diffusion_ref, *refs):
        middle_refs, base_refs, growth_refs = refs[:4], refs[4:8], refs[8:12]
        x_low_ref, x_high_ref, y_a, y_b, lower_ref, upper_ref, out_ref = refs[12:]
        use_low, use_high, factor = box_facts(levels_ref)
        lower = jnp.where(use_low, lower_ref[...], x_low_ref[...])
        upper = jnp.where(use_high, upper_ref[...], x_high_ref[...])
        spread = laplacian([ref[...] for ref in middle_refs], lower, upper, [y_a[...], y_b[...]])
        for x in range(X):
            rate = (factor * diffusion_ref[...]) * spread[x] + STEP * growth_refs[x][...]
            out_ref[:, x, :] = base_refs[x][...] + 0.5 * rate

    return call(
        kernel,
        sds(S, X, PLANE),
        [SMEM] + [VMEM] * 19,
        levels,
        diffusion,
        *middle,
        *base,
        *growth,
        *x_ghosts,
        *y_ghosts,
        below_plane,
        above_plane,
        flops=10**8,
        name="second_stage",
    )


def finish_coarse(coarse, growth, parts):
    def kernel(coarse_ref, growth_ref, a, b, c, d, out_ref):
        total = (a[...] + b[...]) + (c[...] + d[...])
        out_ref[...] = coarse_ref[...] + STEP * growth_ref[...] - total

    return call(kernel, sds(S, CELLS), [VMEM] * 6, coarse, growth, *parts, flops=10**7, name="finish_coarse")


def shifted(value, axis, shift):
    size = lax.axis_size(axis)
    return lax.ppermute(value, axis, [(i, (i + shift) % size) for i in range(size)])


def along_box(value, shift):
    size = lax.axis_size("box")
    pairs = [(i, i + shift) for i in range(size) if 0 <= i + shift < size]
    return lax.ppermute(value, "box", pairs)


def on_device(fine_state, coarse_state, coag_kernel, diffusion, levels, ghost_src):
    fine = fine_state[0, 0]
    coarse = coarse_state[0, 0]
    column = diffusion.reshape(S, 1)
    source = ghost_src[0]
    y_count = GHOSTS - 512
    own_request = jnp.concatenate(
        [source[:, y_count:], source[:, :y_count], jnp.full((1, WIDE - GHOSTS), -1, i32)], axis=1
    )

    far = {k: shifted(coarse, "x", k) for k in (2, 1, 3)}
    mate = shifted(coarse, "core", 1)
    requests = [own_request] + [shifted(own_request, "y", k) for k in (1, 2, 3)]

    planes = split_planes(fine)
    below_plane, above_plane = along_box(planes[3], 1), along_box(planes[0], -1)
    growth = coagulate(coag_kernel, planes, "coagulate_fine")
    coarse_growth = coagulate(coag_kernel, [coarse], "coagulate_coarse")[0]

    part = gather_columns(requests, [coarse, mate], [(0, False), (0, True)], [], "gather_own")
    sources, shifts = [], []
    for k in (1, 3):
        sources += [far[k], shifted(far[k], "core", 1)]
        shifts += [(k, False), (k, True)]
    part = gather_columns(requests, sources, shifts, part, "gather_near")
    part = gather_columns(
        requests, [far[2], shifted(far[2], "core", 1)], [(2, False), (2, True)], part, "gather_far"
    )
    strips = [part[0]] + [shifted(part[k], "y", 4 - k) for k in (1, 2, 3)]

    middle, base, registers, x_ghosts, y_ghosts = first_stage(
        levels, column, planes, growth, strips, below_plane, above_plane
    )

    held = [registers] + [shifted(registers, "y", k) for k in (1, 2, 3)]
    below_plane, above_plane = along_box(middle[3], 1), along_box(middle[0], -1)
    request_rows = jnp.concatenate(requests, axis=0)
    mate_rows = shifted(request_rows, "core", 1)
    growth = coagulate(coag_kernel, middle, "coagulate_middle")
    mates = [shifted(value, "core", 1) for value in held]
    parts = scatter_columns([request_rows, mate_rows], held + mates)
    sent = [parts[0]] + [shifted(parts[k], "x", k) for k in (2, 1, 3)]
    fine_out = second_stage(levels, column, middle, base, growth, x_ghosts, y_ghosts, below_plane, above_plane)
    coarse_out = finish_coarse(coarse, coarse_growth, sent)
    return fine_out[None, None], coarse_out[None, None]


def solution(mesh):
    group = ("x", "y", "core")
    split = Mesh(mesh.devices.reshape(4, 4, 2, 8), group + ("box",))
    return jax.shard_map(
        on_device,
        mesh=split,
        in_specs=(
            P(group, "box", None, None, None),
            P(group, "box", None, None),
            P(),
            P(),
            P(group, None),
            P(group, "box", None),
        ),
        out_specs=(P(group, "box", None, None, None), P(group, "box", None, None)),
        check_vma=False,
    )
```

time: 381 us -> 96 us (0.25)
  the two profiles are of different devices: /device:TPU:1 before, /device:TPU:103 now
where the time goes in v1:
time: 96 us; the launch traced here: 95.7 us
  starting transfers between devices  44.4 us (46%)
  Pallas kernels  26.4 us (28%)
  waiting for transfers between devices  21.3 us (22%)
  local copies, waits for them, and re-layouts  2.62 us (3%)
    ppermute x24, starting transfers between devices, shifted(): lax.ppermute(value, axis, [(i, (i + shift) % size) for i in range(size)])  30.7 us
    pallas_call x11, Pallas kernels, call(): pl.pallas_call(kernel, out_shape=out_shape, in_specs=in_specs, out_specs=...  26.4 us
    ppermute x24, waiting for transfers between devices, shifted(): lax.ppermute(value, axis, [(i, (i + shift) % size) for i in range(size)])  21.2 us
    ppermute x4, starting transfers between devices, along_box(): return lax.ppermute(value, 'box', pairs)  13.7 us
    unnamed x12, local copies, waits for them, and re-layouts  2.45 us
  transfers between devices with their start and end apart: 28, of which 10 were waited for; matrix products, arithmetic and copies ran while one was open for 0% of the time, Pallas kernels for 25%

profile of v1, /device:TPU:103, one launch (start us, length us, event | category | flops | bytes accessed | tf_op | source)
XLA Modules:
  0.0 95.7 jit_solution(582765983536743979)
XLA Ops:
  0.6 0.3 collective-permute-start.5
  0.9 1.3 %collective-permute-start.7 = (f32[48,1152]{1,0:T(8,128)}, f32[48,1152]{1,0:T(8,128)S(1)}, u32[]{:S(2)}, u32[]{:S(2)}) collective-permute-start(f32[48,1152]{1,0:T(8,128)} %bitcast.8), channel_id=1, source_target_pairs={{0,192},{64,0},{128,64},{192,128},{1,193},{65,1},{129,65},{193,129... | collective-permute-start | bytes 663560 | tf_op jit(solution)/shard_map/ppermute | solution.py:335
  2.2 1.2 %collective-permute-start.9 = (f32[48,1152]{1,0:T(8,128)}, f32[48,1152]{1,0:T(8,128)S(1)}, u32[]{:S(2)}, u32[]{:S(2)}) collective-permute-start(f32[48,1152]{1,0:T(8,128)} %bitcast.9), channel_id=1, source_target_pairs={{0,8},{8,0},{1,9},{9,1},{2,10},{10,2},{3,11},{11,3},{4,12},{12,4},... | collective-permute-start | bytes 663560 | tf_op jit(solution)/shard_map/ppermute | solution.py:335
  3.4 1.1 %collective-permute-start.3 = (f32[48,1152]{1,0:T(8,128)}, f32[48,1152]{1,0:T(8,128)S(1)}, u32[]{:S(2)}, u32[]{:S(2)}) collective-permute-start(f32[48,1152]{1,0:T(8,128)} %bitcast.10), channel_id=1, source_target_pairs={{0,128},{64,192},{128,0},{192,64},{1,129},{65,193},{129,1},{193,65... | collective-permute-start | bytes 663560 | tf_op jit(solution)/shard_map/ppermute | solution.py:335
  4.6 2.6 %collective-permute-done.5.refs_4_ = f32[48,1152]{1,0:T(8,128)S(1)} collective-permute-done((f32[48,1152]{1,0:T(8,128)}, f32[48,1152]{1,0:T(8,128)S(1)}, u32[]{:S(2)}, u32[]{:S(2)}) %collective-permute-start.5) | collective-permute-done | bytes 221216 | tf_op jit(solution)/shard_map/ppermute | solution.py:335
  7.2 2.7 %collective-permute-start.6 = (f32[48,1152]{1,0:T(8,128)S(1)}, f32[48,1152]{1,0:T(8,128)S(1)}, u32[]{:S(2)}, u32[]{:S(2)}) collective-permute-start(f32[48,1152]{1,0:T(8,128)S(1)} %collective-permute-done.5.refs_4_), channel_id=1, source_target_pairs={{0,8},{8,0},{1,9},{9,1},{2,10},{10,2},{3,11},{11,3},{4,12},{12,4},... | collective-permute-start | bytes 663560 | tf_op jit(solution)/shard_map/ppermute | solution.py:335
  9.9 5.0 %collective-permute-start.8 = (f32[48,1152]{1,0:T(8,128)S(1)}, f32[48,1152]{1,0:T(8,128)S(1)}, u32[]{:S(2)}, u32[]{:S(2)}) collective-permute-start(f32[48,1152]{1,0:T(8,128)S(1)} %collective-permute-done.7.refs_6_), channel_id=1, source_target_pairs={{0,8},{8,0},{1,9},{9,1},{2,10},{10,2},{3,11},{11,3},{4,12},{12,4},... | collective-permute-start | bytes 663560 | tf_op jit(solution)/shard_map/ppermute | solution.py:335
  15.0 1.3 %collective-permute-start = (s32[1,640]{1,0:T(1,128)S(1)}, s32[1,640]{1,0:T(1,128)S(1)}, u32[]{:S(2)}, u32[]{:S(2)}) collective-permute-start(s32[1,640]{1,0:T(1,128)S(1)} %pad_add_fusion.1.refs_0_), channel_id=1, source_target_pairs={{0,16},{16,32},{32,48},{48,0},{1,17},{17,33},{33,49},{49,1},{2,18}... | collective-permute-start | bytes 7688 | tf_op jit(solution)/shard_map/ppermute | solution.py:335
  16.3 2.4 %collective-permute-done.refs_1_ = s32[1,640]{1,0:T(1,128)S(1)} collective-permute-done((s32[1,640]{1,0:T(1,128)S(1)}, s32[1,640]{1,0:T(1,128)S(1)}, u32[]{:S(2)}, u32[]{:S(2)}) %collective-permute-start) | collective-permute-done | bytes 2592 | tf_op jit(solution)/shard_map/ppermute | solution.py:335
  18.7 1.6 %collective-permute-start.1 = (s32[1,640]{1,0:T(1,128)S(1)}, s32[1,640]{1,0:T(1,128)S(1)}, u32[]{:S(2)}, u32[]{:S(2)}) collective-permute-start(s32[1,640]{1,0:T(1,128)S(1)} %pad_add_fusion.1.refs_0_), channel_id=1, source_target_pairs={{0,32},{16,48},{32,0},{48,16},{1,33},{17,49},{33,1},{49,17},{2,34}... | collective-permute-start | bytes 7688 | tf_op jit(solution)/shard_map/ppermute | solution.py:335
  20.4 2.3 %collective-permute-done.1.refs_2_ = s32[1,640]{1,0:T(1,128)S(1)} collective-permute-done((s32[1,640]{1,0:T(1,128)S(1)}, s32[1,640]{1,0:T(1,128)S(1)}, u32[]{:S(2)}, u32[]{:S(2)}) %collective-permute-start.1) | collective-permute-done | bytes 2592 | tf_op jit(solution)/shard_map/ppermute | solution.py:335
  22.7 1.5 %collective-permute-start.2 = (s32[1,640]{1,0:T(1,128)S(1)}, s32[1,640]{1,0:T(1,128)S(1)}, u32[]{:S(2)}, u32[]{:S(2)}) collective-permute-start(s32[1,640]{1,0:T(1,128)S(1)} %pad_add_fusion.1.refs_0_), channel_id=1, source_target_pairs={{0,48},{16,0},{32,16},{48,32},{1,49},{17,1},{33,17},{49,33},{2,50}... | collective-permute-start | bytes 7688 | tf_op jit(solution)/shard_map/ppermute | solution.py:335
  24.1 1.1 %copy-done = f32[1,1,48,4,1024]{4,3,2,1,0:T(4,128)S(1)} copy-done((f32[1,1,48,4,1024]{4,3,2,1,0:T(4,128)S(1)}, f32[1,1,48,4,1024]{4,3,2,1,0:T(4,128)}, u32[]{:S(2)}) %copy-start) | copy-done | bytes 786456
  25.3 0.1 split_planes.1
  25.4 4.8 %collective-permute-start.13 = (f32[48,1024]{1,0:T(8,128)S(1)}, f32[48,1024]{1,0:T(8,128)S(1)}, u32[]{:S(2)}, u32[]{:S(2)}) collective-permute-start(f32[48,1024]{1,0:T(8,128)S(1)} %get-tuple-element.46.refs_3_), channel_id=1, source_target_pairs={{0,1},{1,2},{2,3},{3,4},{4,5},{5,6},{6,7},{8,9},{9,10},{10,11},{11... | collective-permute-start | bytes 589832 | tf_op jit(solution)/shard_map/ppermute | solution.py:341
  30.2 1.9 %collective-permute-start.14 = (f32[48,1024]{1,0:T(8,128)S(1)}, f32[48,1024]{1,0:T(8,128)S(1)}, u32[]{:S(2)}, u32[]{:S(2)}) collective-permute-start(f32[48,1024]{1,0:T(8,128)S(1)} %get-tuple-element.43.refs_0_), channel_id=1, source_target_pairs={{1,0},{2,1},{3,2},{4,3},{5,4},{6,5},{7,6},{9,8},{10,9},{11,10},{12... | collective-permute-start | bytes 589832 | tf_op jit(solution)/shard_map/ppermute | solution.py:341
  32.1 3.4 %collective-permute-start.4 = (f32[48,1152]{1,0:T(8,128)S(1)}, f32[48,1152]{1,0:T(8,128)S(1)}, u32[]{:S(2)}, u32[]{:S(2)}) collective-permute-start(f32[48,1152]{1,0:T(8,128)S(1)} %collective-permute-done.3.refs_4_), channel_id=1, source_target_pairs={{0,8},{8,0},{1,9},{9,1},{2,10},{10,2},{3,11},{11,3},{4,12},{12,4},... | collective-permute-start | bytes 663560 | tf_op jit(solution)/shard_map/ppermute | solution.py:335
  35.6 1.5 %gather_own.1 = (f32[48,640]{1,0:T(8,128)S(1)}, f32[48,640]{1,0:T(8,128)S(1)}, f32[48,640]{1,0:T(8,128)S(1)}, f32[48,640]{1,0:T(8,128)S(1)}) custom-call(s32[1,640]{1,0:T(1,128)S(1)} %pad_add_fusion.1.refs_0_, s32[1,640]{1,0:T(1,128)S(1)} %collective-permute-done.refs_1_, s32[1,640]{1,0:T(1,128)S(1)} %collective-permute-done.1.refs_2_, ...), custom_call_target="tpu_custom_call" | custom-call | flops 1509949440 | bytes 4194304 | tf_op jit(solution)/shard_map/gather_own/pallas_call | solution.py:30
  37.1 2.9 %gather_near.1 = (f32[48,640]{1,0:T(8,128)S(1)}, f32[48,640]{1,0:T(8,128)S(1)}, f32[48,640]{1,0:T(8,128)S(1)}, f32[48,640]{1,0:T(8,128)S(1)}) custom-call(s32[1,640]{1,0:T(1,128)S(1)} %pad_add_fusion.1.refs_0_, s32[1,640]{1,0:T(1,128)S(1)} %collective-permute-done.refs_1_, s32[1,640]{1,0:T(1,128)S(1)} %collective-permute-done.1.refs_2_, ...), custom_call_target="tpu_custom_call" | custom-call | flops 1509949440 | bytes 4194304 | tf_op jit(solution)/shard_map/gather_near/pallas_call | solution.py:30
  40.0 1.6 %gather_far.1 = (f32[48,640]{1,0:T(8,128)S(1)}, f32[48,640]{1,0:T(8,128)S(1)}, f32[48,640]{1,0:T(8,128)S(1)}, f32[48,640]{1,0:T(8,128)S(1)}) custom-call(s32[1,640]{1,0:T(1,128)S(1)} %pad_add_fusion.1.refs_0_, s32[1,640]{1,0:T(1,128)S(1)} %collective-permute-done.refs_1_, s32[1,640]{1,0:T(1,128)S(1)} %collective-permute-done.1.refs_2_, ...), custom_call_target="tpu_custom_call" | custom-call | flops 1509949440 | bytes 4194304 | tf_op jit(solution)/shard_map/gather_far/pallas_call | solution.py:30
  41.7 3.0 %collective-permute-start.10 = (f32[48,640]{1,0:T(8,128)S(1)}, f32[48,640]{1,0:T(8,128)S(1)}, u32[]{:S(2)}, u32[]{:S(2)}) collective-permute-start(f32[48,640]{1,0:T(8,128)S(1)} %get-tuple-element.60), channel_id=1, source_target_pairs={{0,48},{16,0},{32,16},{48,32},{1,49},{17,1},{33,17},{49,33},{2,50}... | collective-permute-start | bytes 368648 | tf_op jit(solution)/shard_map/ppermute | solution.py:335
  44.7 0.7 collective-permute-start.12
  45.3 3.4 %coagulate_fine.1 = (f32[48,1024]{1,0:T(8,128)S(1)}, f32[48,1024]{1,0:T(8,128)S(1)}, f32[48,1024]{1,0:T(8,128)S(1)}, f32[48,1024]{1,0:T(8,128)S(1)}) custom-call(bf16[48,2304]{1,0:T(8,128)(2,1)S(1)} %copy-done.3, f32[48,1024]{1,0:T(8,128)S(1)} %get-tuple-element.43.refs_0_, f32[48,1024]{1,0:T(8,128)S(1)} %get-tuple-element.44.refs_1_, ...), custom_call_target="tpu_custom_call" | custom-call | flops 7247757312 | bytes 4194304 | tf_op jit(solution)/shard_map/coagulate_fine/pallas_call | solution.py:30
  48.8 0.6 copy-done.5
  49.5 0.4 collective-permute-done.10.refs_9_
  49.9 0.9 collective-permute-done.11.refs_10_
  50.8 2.7 %collective-permute-done.12.refs_11_ = f32[48,640]{1,0:T(8,128)S(1)} collective-permute-done((f32[48,640]{1,0:T(8,128)S(1)}, f32[48,640]{1,0:T(8,128)S(1)}, u32[]{:S(2)}, u32[]{:S(2)}) %collective-permute-start.12) | collective-permute-done | bytes 122912 | tf_op jit(solution)/shard_map/ppermute | solution.py:335
  53.5 0.7 copy-done.2
  54.2 2.0 %first_stage.1 = (f32[48,1024]{1,0:T(8,128)S(1)}, f32[48,1024]{1,0:T(8,128)S(1)}, f32[48,1024]{1,0:T(8,128)S(1)}, f32[48,1024]{1,0:T(8,128)S(1)}, f32[48,1024]{1...) custom-call(s32[1,8]{1,0:T(1,128)S(1)} %copy-done.2, ...), custom_call_target="tpu_custom_call" | custom-call | flops 1000000000 | bytes 4194304 | tf_op jit(solution)/shard_map/first_stage/pallas_call | solution.py:30
  56.2 1.4 %collective-permute-start.19 = (f32[48,640]{1,0:T(8,128)S(1)}, f32[48,640]{1,0:T(8,128)S(1)}, u32[]{:S(2)}, u32[]{:S(2)}) collective-permute-start(f32[48,640]{1,0:T(8,128)S(1)} %get-tuple-element.79.refs_0_), channel_id=1, source_target_pairs={{0,32},{16,48},{32,0},{48,16},{1,33},{17,49},{33,1},{49,17},{2,34}... | collective-permute-start | bytes 368648 | tf_op jit(solution)/shard_map/ppermute | solution.py:335
  57.6 1.3 %collective-permute-start.20 = (f32[48,640]{1,0:T(8,128)S(1)}, f32[48,640]{1,0:T(8,128)S(1)}, u32[]{:S(2)}, u32[]{:S(2)}) collective-permute-start(f32[48,640]{1,0:T(8,128)S(1)} %get-tuple-element.79.refs_0_), channel_id=1, source_target_pairs={{0,48},{16,0},{32,16},{48,32},{1,49},{17,1},{33,17},{49,33},{2,50}... | collective-permute-start | bytes 368648 | tf_op jit(solution)/shard_map/ppermute | solution.py:335
  59.0 1.3 %collective-permute-start.17 = (s32[4,640]{1,0:T(4,128)S(1)}, s32[4,640]{1,0:T(4,128)S(1)}, u32[]{:S(2)}, u32[]{:S(2)}) collective-permute-start(s32[4,640]{1,0:T(4,128)S(1)} %pad_add_fusion.request_a), channel_id=1, source_target_pairs={{0,8},{8,0},{1,9},{9,1},{2,10},{10,2},{3,11},{11,3},{4,12},{12,4},... | collective-permute-start | bytes 30728 | tf_op jit(solution)/shard_map/ppermute | solution.py:335
  60.3 0.1 collective-permute-start.21
  60.4 4.2 %collective-permute-done.18.refs_1_ = f32[48,640]{1,0:T(8,128)S(1)} collective-permute-done((f32[48,640]{1,0:T(8,128)S(1)}, f32[48,640]{1,0:T(8,128)S(1)}, u32[]{:S(2)}, u32[]{:S(2)}) %collective-permute-start.18) | collective-permute-done | bytes 122912 | tf_op jit(solution)/shard_map/ppermute | solution.py:335
  64.6 1.2 %collective-permute-start.22 = (f32[48,640]{1,0:T(8,128)S(1)}, f32[48,640]{1,0:T(8,128)S(1)}, u32[]{:S(2)}, u32[]{:S(2)}) collective-permute-start(f32[48,640]{1,0:T(8,128)S(1)} %collective-permute-done.18.refs_1_), channel_id=1, source_target_pairs={{0,8},{8,0},{1,9},{9,1},{2,10},{10,2},{3,11},{11,3},{4,12},{12,4},... | collective-permute-start | bytes 368648 | tf_op jit(solution)/shard_map/ppermute | solution.py:335
  65.8 0.6 collective-permute-start.24
  66.4 1.0 %coagulate_coarse.1.growth_ref = f32[48,1152]{1,0:T(8,128)S(1)} custom-call(bf16[48,2304]{1,0:T(8,128)(2,1)S(1)} %copy-done.3, f32[48,1152]{1,0:T(8,128)S(1)} %bitcast.12), custom_call_target="tpu_custom_call" | custom-call | flops 2038431744 | bytes 4194304 | tf_op jit(solution)/shard_map/coagulate_coarse/pallas_call | solution.py:30
  67.5 4.9 %collective-permute-start.15 = (f32[48,1024]{1,0:T(8,128)S(1)}, f32[48,1024]{1,0:T(8,128)S(1)}, u32[]{:S(2)}, u32[]{:S(2)}) collective-permute-start(f32[48,1024]{1,0:T(8,128)S(1)} %get-tuple-element.66.refs_3_), channel_id=1, source_target_pairs={{0,1},{1,2},{2,3},{3,4},{4,5},{5,6},{6,7},{8,9},{9,10},{10,11},{11... | collective-permute-start | bytes 589832 | tf_op jit(solution)/shard_map/ppermute | solution.py:341
  72.3 2.1 %collective-permute-start.16 = (f32[48,1024]{1,0:T(8,128)S(1)}, f32[48,1024]{1,0:T(8,128)S(1)}, u32[]{:S(2)}, u32[]{:S(2)}) collective-permute-start(f32[48,1024]{1,0:T(8,128)S(1)} %get-tuple-element.63.refs_0_), channel_id=1, source_target_pairs={{1,0},{2,1},{3,2},{4,3},{5,4},{6,5},{7,6},{9,8},{10,9},{11,10},{12... | collective-permute-start | bytes 589832 | tf_op jit(solution)/shard_map/ppermute | solution.py:341
  74.5 6.8 %scatter_columns.1 = (f32[48,1152]{1,0:T(8,128)S(1)}, f32[48,1152]{1,0:T(8,128)S(1)}, f32[48,1152]{1,0:T(8,128)S(1)}, f32[48,1152]{1,0:T(8,128)S(1)}) custom-call(s32[4,640]{1,0:T(4,128)S(1)} %pad_add_fusion.request_a, s32[4,640]{1,0:T(4,128)S(1)} %collective-permute-done.17.request_b, f32[48,640]{1,0:T(8,128)S(1)} %get-tuple-element.79.refs_0_, ...), custom_call_target="tpu_custom_call" | custom-call | flops 4529848320 | bytes 4194304 | tf_op jit(solution)/shard_map/scatter_columns/pallas_call | solution.py:30
  81.3 0.1 collective-permute-start.25
  81.5 1.5 %collective-permute-start.27 = (f32[48,1152]{1,0:T(8,128)S(1)}, f32[48,1152]{1,0:T(8,128)S(1)}, u32[]{:S(2)}, u32[]{:S(2)}) collective-permute-start(f32[48,1152]{1,0:T(8,128)S(1)} %get-tuple-element.83), channel_id=1, source_target_pairs={{0,192},{64,0},{128,64},{192,128},{1,193},{65,1},{129,65},{193,129... | collective-permute-start | bytes 663560 | tf_op jit(solution)/shard_map/ppermute | solution.py:335
  82.9 3.4 %coagulate_middle.1 = (f32[48,1024]{1,0:T(8,128)S(1)}, f32[48,1024]{1,0:T(8,128)S(1)}, f32[48,1024]{1,0:T(8,128)S(1)}, f32[48,1024]{1,0:T(8,128)S(1)}) custom-call(bf16[48,2304]{1,0:T(8,128)(2,1)S(1)} %copy-done.3, f32[48,1024]{1,0:T(8,128)S(1)} %get-tuple-element.63.refs_0_, f32[48,1024]{1,0:T(8,128)S(1)} %get-tuple-element.64.refs_1_, ...), custom_call_target="tpu_custom_call" | custom-call | flops 7247757312 | bytes 4194304 | tf_op jit(solution)/shard_map/coagulate_middle/pallas_call | solution.py:30
  86.4 2.8 %second_stage.1 = f32[48,4,1024]{2,1,0:T(4,128)} custom-call(s32[1,8]{1,0:T(1,128)S(1)} %copy-done.2, f32[48,1]{1,0:T(8,128)S(1)} %copy.9.diffusion_ref, f32[48,1024]{1,0:T(8,128)S(1)} %get-tuple-element.63.refs_0_, f32[48,1024]{1,0:T(8,128)S(1)} %get-tuple-element.64.refs_1_, f32[48,1024]{1,0:T(8,128)S(1)} %get-tuple-element.65.refs_2_, ...), custom_call_target="tpu_custom_call" | custom-call | flops 100000000 | bytes 4194304 | tf_op jit(solution)/shard_map/second_stage/pallas_call | solution.py:30
  89.2 0.4 collective-permute-done.25.b
  89.7 1.7 %collective-permute-done.26.c = f32[48,1152]{1,0:T(8,128)S(1)} collective-permute-done((f32[48,1152]{1,0:T(8,128)S(1)}, f32[48,1152]{1,0:T(8,128)S(1)}, u32[]{:S(2)}, u32[]{:S(2)}) %collective-permute-start.26) | collective-permute-done | bytes 221216 | tf_op jit(solution)/shard_map/ppermute | solution.py:335
  91.4 3.6 %collective-permute-done.27.d = f32[48,1152]{1,0:T(8,128)S(1)} collective-permute-done((f32[48,1152]{1,0:T(8,128)S(1)}, f32[48,1152]{1,0:T(8,128)S(1)}, u32[]{:S(2)}, u32[]{:S(2)}) %collective-permute-start.27) | collective-permute-done | bytes 221216 | tf_op jit(solution)/shard_map/ppermute | solution.py:335
  95.0 0.8 finish_coarse.1
  (37 shorter events, 0.6 us)
Async XLA Ops:
  0.6 3.9 %copy-start.4 = (s32[1,1,576]{2,1,0:T(1,128)S(1)}, s32[1,1,576]{2,1,0:T(1,128)}, u32[]{:S(2)}) copy-start(s32[1,1,576]{2,1,0:T(1,128)} %param.11) | copy-start | bytes 6916
  0.6 6.6 %collective-permute-start.5 = (f32[48,1152]{1,0:T(8,128)}, f32[48,1152]{1,0:T(8,128)S(1)}, u32[]{:S(2)}, u32[]{:S(2)}) collective-permute-start(f32[48,1152]{1,0:T(8,128)} %bitcast.7), channel_id=1, source_target_pairs={{0,64},{64,128},{128,192},{192,0},{1,65},{65,129},{129,193},{193,1... | collective-permute-start | bytes 663560 | tf_op jit(solution)/shard_map/ppermute | solution.py:335
  0.9 9.0 %collective-permute-start.7 = (f32[48,1152]{1,0:T(8,128)}, f32[48,1152]{1,0:T(8,128)S(1)}, u32[]{:S(2)}, u32[]{:S(2)}) collective-permute-start(f32[48,1152]{1,0:T(8,128)} %bitcast.8), channel_id=1, source_target_pairs={{0,192},{64,0},{128,64},{192,128},{1,193},{65,1},{129,65},{193,129... | collective-permute-start | bytes 663560 | tf_op jit(solution)/shard_map/ppermute | solution.py:335
  2.2 28.0 %collective-permute-start.9 = (f32[48,1152]{1,0:T(8,128)}, f32[48,1152]{1,0:T(8,128)S(1)}, u32[]{:S(2)}, u32[]{:S(2)}) collective-permute-start(f32[48,1152]{1,0:T(8,128)} %bitcast.9), channel_id=1, source_target_pairs={{0,8},{8,0},{1,9},{9,1},{2,10},{10,2},{3,11},{11,3},{4,12},{12,4},... | collective-permute-start | bytes 663560 | tf_op jit(solution)/shard_map/ppermute | solution.py:335
  3.4 28.7 %collective-permute-start.3 = (f32[48,1152]{1,0:T(8,128)}, f32[48,1152]{1,0:T(8,128)S(1)}, u32[]{:S(2)}, u32[]{:S(2)}) collective-permute-start(f32[48,1152]{1,0:T(8,128)} %bitcast.10), channel_id=1, source_target_pairs={{0,128},{64,192},{128,0},{192,64},{1,129},{65,193},{129,1},{193,65... | collective-permute-start | bytes 663560 | tf_op jit(solution)/shard_map/ppermute | solution.py:335
  7.2 29.9 %collective-permute-start.6 = (f32[48,1152]{1,0:T(8,128)S(1)}, f32[48,1152]{1,0:T(8,128)S(1)}, u32[]{:S(2)}, u32[]{:S(2)}) collective-permute-start(f32[48,1152]{1,0:T(8,128)S(1)} %collective-permute-done.5.refs_4_), channel_id=1, source_target_pairs={{0,8},{8,0},{1,9},{9,1},{2,10},{10,2},{3,11},{11,3},{4,12},{12,4},... | collective-permute-start | bytes 663560 | tf_op jit(solution)/shard_map/ppermute | solution.py:335
  9.9 27.2 %collective-permute-start.8 = (f32[48,1152]{1,0:T(8,128)S(1)}, f32[48,1152]{1,0:T(8,128)S(1)}, u32[]{:S(2)}, u32[]{:S(2)}) collective-permute-start(f32[48,1152]{1,0:T(8,128)S(1)} %collective-permute-done.7.refs_6_), channel_id=1, source_target_pairs={{0,8},{8,0},{1,9},{9,1},{2,10},{10,2},{3,11},{11,3},{4,12},{12,4},... | collective-permute-start | bytes 663560 | tf_op jit(solution)/shard_map/ppermute | solution.py:335
  15.0 3.7 %collective-permute-start = (s32[1,640]{1,0:T(1,128)S(1)}, s32[1,640]{1,0:T(1,128)S(1)}, u32[]{:S(2)}, u32[]{:S(2)}) collective-permute-start(s32[1,640]{1,0:T(1,128)S(1)} %pad_add_fusion.1.refs_0_), channel_id=1, source_target_pairs={{0,16},{16,32},{32,48},{48,0},{1,17},{17,33},{33,49},{49,1},{2,18}... | collective-permute-start | bytes 7688 | tf_op jit(solution)/shard_map/ppermute | solution.py:335
  18.7 3.9 %collective-permute-start.1 = (s32[1,640]{1,0:T(1,128)S(1)}, s32[1,640]{1,0:T(1,128)S(1)}, u32[]{:S(2)}, u32[]{:S(2)}) collective-permute-start(s32[1,640]{1,0:T(1,128)S(1)} %pad_add_fusion.1.refs_0_), channel_id=1, source_target_pairs={{0,32},{16,48},{32,0},{48,16},{1,33},{17,49},{33,1},{49,17},{2,34}... | collective-permute-start | bytes 7688 | tf_op jit(solution)/shard_map/ppermute | solution.py:335
  22.7 2.7 %collective-permute-start.2 = (s32[1,640]{1,0:T(1,128)S(1)}, s32[1,640]{1,0:T(1,128)S(1)}, u32[]{:S(2)}, u32[]{:S(2)}) collective-permute-start(s32[1,640]{1,0:T(1,128)S(1)} %pad_add_fusion.1.refs_0_), channel_id=1, source_target_pairs={{0,48},{16,0},{32,16},{48,32},{1,49},{17,1},{33,17},{49,33},{2,50}... | collective-permute-start | bytes 7688 | tf_op jit(solution)/shard_map/ppermute | solution.py:335
  24.1 1.1 %copy-start = (f32[1,1,48,4,1024]{4,3,2,1,0:T(4,128)S(1)}, f32[1,1,48,4,1024]{4,3,2,1,0:T(4,128)}, u32[]{:S(2)}) copy-start(f32[1,1,48,4,1024]{4,3,2,1,0:T(4,128)} %param.6) | copy-start | bytes 2359300
  25.3 10.3 %copy-start.1 = (f32[1,1,48,1152]{3,2,1,0:T(8,128)S(1)}, f32[1,1,48,1152]{3,2,1,0:T(8,128)}, u32[]{:S(2)}) copy-start(f32[1,1,48,1152]{3,2,1,0:T(8,128)} %param.7) | copy-start | bytes 663556
  25.4 24.1 %collective-permute-start.13 = (f32[48,1024]{1,0:T(8,128)S(1)}, f32[48,1024]{1,0:T(8,128)S(1)}, u32[]{:S(2)}, u32[]{:S(2)}) collective-permute-start(f32[48,1024]{1,0:T(8,128)S(1)} %get-tuple-element.46.refs_3_), channel_id=1, source_target_pairs={{0,1},{1,2},{2,3},{3,4},{4,5},{5,6},{6,7},{8,9},{9,10},{10,11},{11... | collective-permute-start | bytes 589832 | tf_op jit(solution)/shard_map/ppermute | solution.py:341
  30.2 19.3 %collective-permute-start.14 = (f32[48,1024]{1,0:T(8,128)S(1)}, f32[48,1024]{1,0:T(8,128)S(1)}, u32[]{:S(2)}, u32[]{:S(2)}) collective-permute-start(f32[48,1024]{1,0:T(8,128)S(1)} %get-tuple-element.43.refs_0_), channel_id=1, source_target_pairs={{1,0},{2,1},{3,2},{4,3},{5,4},{6,5},{7,6},{9,8},{10,9},{11,10},{12... | collective-permute-start | bytes 589832 | tf_op jit(solution)/shard_map/ppermute | solution.py:341
  32.1 7.9 %collective-permute-start.4 = (f32[48,1152]{1,0:T(8,128)S(1)}, f32[48,1152]{1,0:T(8,128)S(1)}, u32[]{:S(2)}, u32[]{:S(2)}) collective-permute-start(f32[48,1152]{1,0:T(8,128)S(1)} %collective-permute-done.3.refs_4_), channel_id=1, source_target_pairs={{0,8},{8,0},{1,9},{9,1},{2,10},{10,2},{3,11},{11,3},{4,12},{12,4},... | collective-permute-start | bytes 663560 | tf_op jit(solution)/shard_map/ppermute | solution.py:335
  40.0 5.3 %copy-start.3 = (bf16[48,2304]{1,0:T(8,128)(2,1)S(1)}, bf16[48,2304]{1,0:T(8,128)(2,1)}, u32[]{:S(2)}) copy-start(bf16[48,2304]{1,0:T(8,128)(2,1)} %matrix_ref.5) | copy-start | bytes 663556
  41.7 8.2 %collective-permute-start.10 = (f32[48,640]{1,0:T(8,128)S(1)}, f32[48,640]{1,0:T(8,128)S(1)}, u32[]{:S(2)}, u32[]{:S(2)}) collective-permute-start(f32[48,640]{1,0:T(8,128)S(1)} %get-tuple-element.60), channel_id=1, source_target_pairs={{0,48},{16,0},{32,16},{48,32},{1,49},{17,1},{33,17},{49,33},{2,50}... | collective-permute-start | bytes 368648 | tf_op jit(solution)/shard_map/ppermute | solution.py:335
  44.7 6.2 %collective-permute-start.11 = (f32[48,640]{1,0:T(8,128)S(1)}, f32[48,640]{1,0:T(8,128)S(1)}, u32[]{:S(2)}, u32[]{:S(2)}) collective-permute-start(f32[48,640]{1,0:T(8,128)S(1)} %get-tuple-element.61), channel_id=1, source_target_pairs={{0,32},{16,48},{32,0},{48,16},{1,33},{17,49},{33,1},{49,17},{2,34}... | collective-permute-start | bytes 368648 | tf_op jit(solution)/shard_map/ppermute | solution.py:335
  44.7 8.8 %collective-permute-start.12 = (f32[48,640]{1,0:T(8,128)S(1)}, f32[48,640]{1,0:T(8,128)S(1)}, u32[]{:S(2)}, u32[]{:S(2)}) collective-permute-start(f32[48,640]{1,0:T(8,128)S(1)} %get-tuple-element.62), channel_id=1, source_target_pairs={{0,16},{16,32},{32,48},{48,0},{1,17},{17,33},{33,49},{49,1},{2,18}... | collective-permute-start | bytes 368648 | tf_op jit(solution)/shard_map/ppermute | solution.py:335
  48.8 0.7 copy-start.5
  53.5 0.7 copy-start.2
  56.1 8.4 %collective-permute-start.18 = (f32[48,640]{1,0:T(8,128)S(1)}, f32[48,640]{1,0:T(8,128)S(1)}, u32[]{:S(2)}, u32[]{:S(2)}) collective-permute-start(f32[48,640]{1,0:T(8,128)S(1)} %get-tuple-element.79.refs_0_), channel_id=1, source_target_pairs={{0,16},{16,32},{32,48},{48,0},{1,17},{17,33},{33,49},{49,1},{2,18}... | collective-permute-start | bytes 368648 | tf_op jit(solution)/shard_map/ppermute | solution.py:335
  56.2 9.6 %collective-permute-start.19 = (f32[48,640]{1,0:T(8,128)S(1)}, f32[48,640]{1,0:T(8,128)S(1)}, u32[]{:S(2)}, u32[]{:S(2)}) collective-permute-start(f32[48,640]{1,0:T(8,128)S(1)} %get-tuple-element.79.refs_0_), channel_id=1, source_target_pairs={{0,32},{16,48},{32,0},{48,16},{1,33},{17,49},{33,1},{49,17},{2,34}... | collective-permute-start | bytes 368648 | tf_op jit(solution)/shard_map/ppermute | solution.py:335
  57.6 8.2 %collective-permute-start.20 = (f32[48,640]{1,0:T(8,128)S(1)}, f32[48,640]{1,0:T(8,128)S(1)}, u32[]{:S(2)}, u32[]{:S(2)}) collective-permute-start(f32[48,640]{1,0:T(8,128)S(1)} %get-tuple-element.79.refs_0_), channel_id=1, source_target_pairs={{0,48},{16,0},{32,16},{48,32},{1,49},{17,1},{33,17},{49,33},{2,50}... | collective-permute-start | bytes 368648 | tf_op jit(solution)/shard_map/ppermute | solution.py:335
  59.0 8.5 %collective-permute-start.17 = (s32[4,640]{1,0:T(4,128)S(1)}, s32[4,640]{1,0:T(4,128)S(1)}, u32[]{:S(2)}, u32[]{:S(2)}) collective-permute-start(s32[4,640]{1,0:T(4,128)S(1)} %pad_add_fusion.request_a), channel_id=1, source_target_pairs={{0,8},{8,0},{1,9},{9,1},{2,10},{10,2},{3,11},{11,3},{4,12},{12,4},... | collective-permute-start | bytes 30728 | tf_op jit(solution)/shard_map/ppermute | solution.py:335
  60.3 12.0 %collective-permute-start.21 = (f32[48,640]{1,0:T(8,128)S(1)}, f32[48,640]{1,0:T(8,128)S(1)}, u32[]{:S(2)}, u32[]{:S(2)}) collective-permute-start(f32[48,640]{1,0:T(8,128)S(1)} %get-tuple-element.79.refs_0_), channel_id=1, source_target_pairs={{0,8},{8,0},{1,9},{9,1},{2,10},{10,2},{3,11},{11,3},{4,12},{12,4},... | collective-permute-start | bytes 368648 | tf_op jit(solution)/shard_map/ppermute | solution.py:335
  64.6 9.9 %collective-permute-start.22 = (f32[48,640]{1,0:T(8,128)S(1)}, f32[48,640]{1,0:T(8,128)S(1)}, u32[]{:S(2)}, u32[]{:S(2)}) collective-permute-start(f32[48,640]{1,0:T(8,128)S(1)} %collective-permute-done.18.refs_1_), channel_id=1, source_target_pairs={{0,8},{8,0},{1,9},{9,1},{2,10},{10,2},{3,11},{11,3},{4,12},{12,4},... | collective-permute-start | bytes 368648 | tf_op jit(solution)/shard_map/ppermute | solution.py:335
  65.8 8.7 %collective-permute-start.23 = (f32[48,640]{1,0:T(8,128)S(1)}, f32[48,640]{1,0:T(8,128)S(1)}, u32[]{:S(2)}, u32[]{:S(2)}) collective-permute-start(f32[48,640]{1,0:T(8,128)S(1)} %collective-permute-done.19.refs_2_), channel_id=1, source_target_pairs={{0,8},{8,0},{1,9},{9,1},{2,10},{10,2},{3,11},{11,3},{4,12},{12,4},... | collective-permute-start | bytes 368648 | tf_op jit(solution)/shard_map/ppermute | solution.py:335
  65.8 8.7 %collective-permute-start.24 = (f32[48,640]{1,0:T(8,128)S(1)}, f32[48,640]{1,0:T(8,128)S(1)}, u32[]{:S(2)}, u32[]{:S(2)}) collective-permute-start(f32[48,640]{1,0:T(8,128)S(1)} %collective-permute-done.20.refs_3_), channel_id=1, source_target_pairs={{0,8},{8,0},{1,9},{9,1},{2,10},{10,2},{3,11},{11,3},{4,12},{12,4},... | collective-permute-start | bytes 368648 | tf_op jit(solution)/shard_map/ppermute | solution.py:335
  67.5 18.9 %collective-permute-start.15 = (f32[48,1024]{1,0:T(8,128)S(1)}, f32[48,1024]{1,0:T(8,128)S(1)}, u32[]{:S(2)}, u32[]{:S(2)}) collective-permute-start(f32[48,1024]{1,0:T(8,128)S(1)} %get-tuple-element.66.refs_3_), channel_id=1, source_target_pairs={{0,1},{1,2},{2,3},{3,4},{4,5},{5,6},{6,7},{8,9},{9,10},{10,11},{11... | collective-permute-start | bytes 589832 | tf_op jit(solution)/shard_map/ppermute | solution.py:341
  72.3 14.0 %collective-permute-start.16 = (f32[48,1024]{1,0:T(8,128)S(1)}, f32[48,1024]{1,0:T(8,128)S(1)}, u32[]{:S(2)}, u32[]{:S(2)}) collective-permute-start(f32[48,1024]{1,0:T(8,128)S(1)} %get-tuple-element.63.refs_0_), channel_id=1, source_target_pairs={{1,0},{2,1},{3,2},{4,3},{5,4},{6,5},{7,6},{9,8},{10,9},{11,10},{12... | collective-permute-start | bytes 589832 | tf_op jit(solution)/shard_map/ppermute | solution.py:341
  81.3 8.4 %collective-permute-start.25 = (f32[48,1152]{1,0:T(8,128)S(1)}, f32[48,1152]{1,0:T(8,128)S(1)}, u32[]{:S(2)}, u32[]{:S(2)}) collective-permute-start(f32[48,1152]{1,0:T(8,128)S(1)} %get-tuple-element.81), channel_id=1, source_target_pairs={{0,128},{64,192},{128,0},{192,64},{1,129},{65,193},{129,1},{193,65... | collective-permute-start | bytes 663560 | tf_op jit(solution)/shard_map/ppermute | solution.py:335
  81.4 10.0 %collective-permute-start.26 = (f32[48,1152]{1,0:T(8,128)S(1)}, f32[48,1152]{1,0:T(8,128)S(1)}, u32[]{:S(2)}, u32[]{:S(2)}) collective-permute-start(f32[48,1152]{1,0:T(8,128)S(1)} %get-tuple-element.82), channel_id=1, source_target_pairs={{0,64},{64,128},{128,192},{192,0},{1,65},{65,129},{129,193},{193,1... | collective-permute-start | bytes 663560 | tf_op jit(solution)/shard_map/ppermute | solution.py:335
  81.5 13.5 %collective-permute-start.27 = (f32[48,1152]{1,0:T(8,128)S(1)}, f32[48,1152]{1,0:T(8,128)S(1)}, u32[]{:S(2)}, u32[]{:S(2)}) collective-permute-start(f32[48,1152]{1,0:T(8,128)S(1)} %get-tuple-element.83), channel_id=1, source_target_pairs={{0,192},{64,0},{128,64},{192,128},{1,193},{65,1},{129,65},{193,129... | collective-permute-start | bytes 663560 | tf_op jit(solution)/shard_map/ppermute | solution.py:335

commit v2 on v1

--- a/solution.py
+++ b/solution.py
@@ -13,6 +13,7 @@
 WIDE = 640
 STEP = 0.25
 MIB = 1024 * 1024
+COST = pl.CostEstimate(flops=1000, bytes_accessed=1000, transcendentals=0)
 
 f32 = jnp.float32
 bf16 = jnp.bfloat16
@@ -25,7 +26,7 @@
     return jax.ShapeDtypeStruct(shape, f32)
 
 
-def call(kernel, out_shape, in_specs, *operands, scratch=(), flops=0, name=None):
+def call(kernel, out_shape, in_specs, *operands, scratch=(), name=None):
     many = isinstance(out_shape, list)
     return pl.pallas_call(
         kernel,
@@ -34,7 +35,7 @@
         out_specs=[VMEM] * len(out_shape) if many else VMEM,
         scratch_shapes=list(scratch),
         compiler_params=pltpu.CompilerParams(vmem_limit_bytes=40 * MIB),
-        cost_estimate=pl.CostEstimate(flops=flops, bytes_accessed=4 * MIB, transcendentals=0),
+        cost_estimate=COST,
         name=name,
     )(*operands)
 
@@ -83,14 +84,12 @@
                 pairs = jnp.concatenate([(v[j : j + 1] * v).astype(bf16) for j in range(S)], axis=0)
                 out_ref[:, start:stop] = mm(matrix_ref[...], pairs)
 
-    cells = sum(f.shape[1] for f in fields)
     return call(
         kernel,
         [sds(*f.shape) for f in fields],
         [VMEM] * (count + 1),
         kernel_matrix,
         *fields,
-        flops=6 * cells * 2304 * 128,
         name=name,
     )
 
@@ -100,69 +99,70 @@
     return owner, jnp.where(request < 0, -1, request - owner * CELLS)
 
 
-def gather_columns(requests, sources, shifts, before, name):
+def gather_columns(requests, sources, shifts):
     count = len(sources)
 
     def kernel(*refs):
-        request_refs, source_refs = refs[:4], refs[4 : 4 + count]
-        before_refs = refs[4 + count : 4 + count + len(before)]
-        outs = refs[4 + count + len(before) : 8 + count + len(before)]
+        request_refs, source_refs, outs, rows_ref = refs[:2], refs[2 : 2 + count], refs[2 + count : 6 + count], refs[6 + count]
         x, y, c = lax.axis_index("x"), lax.axis_index("y"), lax.axis_index("core")
-        rows = rows_of([ref[...] for ref in source_refs])
-        cell_id = lax.broadcasted_iota(i32, (CELLS, 2 * WIDE), 0)
-        for half in range(2):
-            request = jnp.concatenate([request_refs[2 * half][...], request_refs[2 * half + 1][...]], axis=1)
-            owner, cell = owner_and_cell(request)
-            product = mm(rows, ones_where(jnp.broadcast_to(cell, (CELLS, 2 * WIDE)) == cell_id))
-            total = jnp.zeros((S, 2 * WIDE), f32)
+        for i in range(count):
+            high, low = halves(source_refs[i][...])
+            rows_ref[2 * S * i : 2 * S * i + S] = high
+            rows_ref[2 * S * i + S : 2 * S * (i + 1)] = low
+        cell_id = lax.broadcasted_iota(i32, (CELLS, WIDE), 0)
+        for i in range(4):
+            owner, cell = owner_and_cell(request_refs[i // 2][i % 2 : i % 2 + 1, :])
+            product = mm(rows_ref[...], ones_where(jnp.broadcast_to(cell, (CELLS, WIDE)) == cell_id))
+            total = jnp.zeros((S, WIDE), f32)
             for part, (shift, mate) in zip(sums_of(product, count), shifts):
                 from_x = jnp.bitwise_and(x - shift, 3)
                 source_owner = (from_x * 4 + y) * 2 + (1 - c if mate else c)
                 total = total + jnp.where(owner == source_owner, part, 0.0)
-            for i in range(2):
-                part = total[:, i * WIDE : (i + 1) * WIDE]
-                if before:
-                    part = part + before_refs[2 * half + i][...]
-                outs[2 * half + i][...] = part
+            outs[i][...] = total
 
     return call(
         kernel,
         [sds(S, WIDE)] * 4,
-        [VMEM] * (4 + count + len(before)),
+        [VMEM] * (2 + count),
         *requests,
         *sources,
-        *before,
-        flops=2 * 4 * WIDE * CELLS * 256,
-        name=name,
-    )
-
-
-def scatter_columns(requests, registers):
+        scratch=[pltpu.VMEM((2 * S * count, CELLS), bf16)],
+        name="gather_columns",
+    )
+
+
+def cells_by_row(requests):
+    def kernel(request_a, request_b, out_ref):
+        for i in range(8):
+            cell = owner_and_cell((request_a if i < 4 else request_b)[i % 4 : i % 4 + 1, :])[1].astype(f32)
+            for t in range(WIDE // 128):
+                block = jnp.broadcast_to(cell[:, t * 128 : (t + 1) * 128], (128, 128))
+                out_ref[i * WIDE + t * 128 : i * WIDE + (t + 1) * 128, :] = block.T.astype(i32)
+
+    out = jax.ShapeDtypeStruct((8 * WIDE, 128), i32)
+    return call(kernel, out, [VMEM] * 2, *requests, name="cells_by_row")
+
+
+def scatter_columns(requests, cells, registers):
     total = 8 * WIDE
 
-    def kernel(request_a, request_b, *refs):
-        register_refs, outs, rows_ref, cell_ref = refs[:8], refs[8:12], refs[12], refs[13]
+    def kernel(request_a, request_b, cell_ref, *refs):
+        register_refs, outs, rows_ref = refs[:8], refs[8:12], refs[12]
         x, y, c = lax.axis_index("x"), lax.axis_index("y"), lax.axis_index("core")
-        lane = lax.broadcasted_iota(i32, (1, 256), 1)
+        lane = lax.broadcasted_iota(i32, (1, 128), 1)
         for i in range(8):
             request = (request_a if i < 4 else request_b)[i % 4 : i % 4 + 1, :]
-            owner, cell = owner_and_cell(request)
+            owner, _ = owner_and_cell(request)
             high, low = halves(register_refs[i][...])
             for k in range(4):
                 to_x = jnp.bitwise_and(x + k, 3)
                 mine = jnp.broadcast_to(jnp.where(owner == (to_x * 4 + y) * 2 + c, 1.0, 0.0).astype(bf16), (S, WIDE))
                 rows_ref[2 * S * k : 2 * S * k + S, i * WIDE : (i + 1) * WIDE] = high * mine
                 rows_ref[2 * S * k + S : 2 * S * (k + 1), i * WIDE : (i + 1) * WIDE] = low * mine
-            for t in range(WIDE // 128):
-                block = jnp.broadcast_to(cell[:, t * 128 : (t + 1) * 128].astype(f32), (128, 128))
-                cell_ref[i * WIDE + t * 128 : i * WIDE + (t + 1) * 128, :] = block.T.astype(i32)
 
         def block(start, width):
-            marks = [
-                ones_where(cell_ref[...] == lane[:, :128] + (start + 128 * t)) for t in range(width // 128)
-            ]
-            product = mm(rows_ref[...], jnp.concatenate(marks, axis=1))
-            return sums_of(product, 4)
+            marks = [ones_where(cell_ref[...] == lane + (start + 128 * t)) for t in range(width // 128)]
+            return sums_of(mm(rows_ref[...], jnp.concatenate(marks, axis=1)), 4)
 
         def body(i, carry):
             start = pl.multiple_of(i * 256, 256)
@@ -177,11 +177,11 @@
     return call(
         kernel,
         [sds(S, CELLS)] * 4,
-        [VMEM] * 10,
+        [VMEM] * 11,
         *requests,
+        cells,
         *registers,
-        scratch=[pltpu.VMEM((8 * S, total), bf16), pltpu.VMEM((total, 128), i32)],
-        flops=2 * total * CELLS * 384,
+        scratch=[pltpu.VMEM((8 * S, total), bf16)],
         name="scatter_columns",
     )
 
@@ -197,9 +197,9 @@
 
 
 def laplacian(planes, lower, upper, y_ghosts):
-    lane = lax.broadcasted_iota(i32, (S, PLANE), 1)
-    z = jnp.bitwise_and(lane, 31)
-    wide = lax.broadcasted_iota(i32, (S, 128), 1)
+    rows = planes[0].shape[0]
+    z = jnp.bitwise_and(lax.broadcasted_iota(i32, (rows, PLANE), 1), 31)
+    wide = lax.broadcasted_iota(i32, (rows, 128), 1)
     result = []
     for x in range(X):
         v = planes[x]
@@ -286,40 +286,42 @@
         *strips,
         below_plane,
         above_plane,
-        flops=10**9,
         name="first_stage",
     )
     return outs[:4], outs[4:8], outs[8], outs[9:11], outs[11:13]
 
 
 def second_stage(levels, diffusion, middle, base, growth, x_ghosts, y_ghosts, below_plane, above_plane):
+    rows = 8
+
     def kernel(levels_ref, diffusion_ref, *refs):
         middle_refs, base_refs, growth_refs = refs[:4], refs[4:8], refs[8:12]
-        x_low_ref, x_high_ref, y_a, y_b, lower_ref, upper_ref, out_ref = refs[12:]
+        x_low_ref, x_high_ref, y_a, y_b, lower_ref, upper_ref, out_ref, held_ref, sems = refs[12:]
         use_low, use_high, factor = box_facts(levels_ref)
-        lower = jnp.where(use_low, lower_ref[...], x_low_ref[...])
-        upper = jnp.where(use_high, upper_ref[...], x_high_ref[...])
-        spread = laplacian([ref[...] for ref in middle_refs], lower, upper, [y_a[...], y_b[...]])
-        for x in range(X):
-            rate = (factor * diffusion_ref[...]) * spread[x] + STEP * growth_refs[x][...]
-            out_ref[:, x, :] = base_refs[x][...] + 0.5 * rate
-
-    return call(
-        kernel,
-        sds(S, X, PLANE),
-        [SMEM] + [VMEM] * 19,
-        levels,
-        diffusion,
-        *middle,
-        *base,
-        *growth,
-        *x_ghosts,
-        *y_ghosts,
-        below_plane,
-        above_plane,
-        flops=10**8,
+        copies = []
+        for i in range(S // rows):
+            part = slice(i * rows, (i + 1) * rows)
+            lower = jnp.where(use_low, lower_ref[part], x_low_ref[part])
+            upper = jnp.where(use_high, upper_ref[part], x_high_ref[part])
+            spread = laplacian([ref[part] for ref in middle_refs], lower, upper, [y_a[part], y_b[part]])
+            for x in range(X):
+                rate = (factor * diffusion_ref[part]) * spread[x] + STEP * growth_refs[x][part]
+                held_ref[part, x, :] = base_refs[x][part] + 0.5 * rate
+            copies.append(pltpu.make_async_copy(held_ref.at[part], out_ref.at[part], sems.at[i]))
+            copies[-1].start()
+        for copy in copies:
+            copy.wait()
+
+    return pl.pallas_call(
+        kernel,
+        out_shape=sds(S, X, PLANE),
+        in_specs=[SMEM] + [VMEM] * 19,
+        out_specs=pl.BlockSpec(memory_space=pl.ANY),
+        scratch_shapes=[pltpu.VMEM((S, X, PLANE), f32), pltpu.SemaphoreType.DMA((S // rows,))],
+        compiler_params=pltpu.CompilerParams(vmem_limit_bytes=40 * MIB),
+        cost_estimate=COST,
         name="second_stage",
-    )
+    )(levels, diffusion, *middle, *base, *growth, *x_ghosts, *y_ghosts, below_plane, above_plane)
 
 
 def finish_coarse(coarse, growth, parts):
@@ -327,7 +329,7 @@
         total = (a[...] + b[...]) + (c[...] + d[...])
         out_ref[...] = coarse_ref[...] + STEP * growth_ref[...] - total
 
-    return call(kernel, sds(S, CELLS), [VMEM] * 6, coarse, growth, *parts, flops=10**7, name="finish_coarse")
+    return call(kernel, sds(S, CELLS), [VMEM] * 6, coarse, growth, *parts, name="finish_coarse")
 
 
 def shifted(value, axis, shift):
@@ -335,10 +337,8 @@
     return lax.ppermute(value, axis, [(i, (i + shift) % size) for i in range(size)])
 
 
-def along_box(value, shift):
-    size = lax.axis_size("box")
-    pairs = [(i, i + shift) for i in range(size) if 0 <= i + shift < size]
-    return lax.ppermute(value, "box", pairs)
+def after(value, before):
+    return lax.optimization_barrier((value, before))[0]
 
 
 def on_device(fine_state, coarse_state, coag_kernel, diffusion, levels, ghost_src):
@@ -353,37 +353,39 @@
 
     far = {k: shifted(coarse, "x", k) for k in (2, 1, 3)}
     mate = shifted(coarse, "core", 1)
-    requests = [own_request] + [shifted(own_request, "y", k) for k in (1, 2, 3)]
-
+    near = jnp.concatenate([own_request, shifted(own_request, "y", 1)], axis=0)
+    requests = [near, shifted(near, "y", 2)]
     planes = split_planes(fine)
-    below_plane, above_plane = along_box(planes[3], 1), along_box(planes[0], -1)
-    growth = coagulate(coag_kernel, planes, "coagulate_fine")
-    coarse_growth = coagulate(coag_kernel, [coarse], "coagulate_coarse")[0]
-
-    part = gather_columns(requests, [coarse, mate], [(0, False), (0, True)], [], "gather_own")
-    sources, shifts = [], []
-    for k in (1, 3):
+    below_plane, above_plane = shifted(planes[3], "box", 1), shifted(planes[0], "box", 7)
+    far, requests, below_plane, above_plane = lax.optimization_barrier((far, requests, below_plane, above_plane))
+
+    sources, shifts = [coarse, mate], [(0, False), (0, True)]
+    for k in (1, 3, 2):
         sources += [far[k], shifted(far[k], "core", 1)]
         shifts += [(k, False), (k, True)]
-    part = gather_columns(requests, sources, shifts, part, "gather_near")
-    part = gather_columns(
-        requests, [far[2], shifted(far[2], "core", 1)], [(2, False), (2, True)], part, "gather_far"
-    )
-    strips = [part[0]] + [shifted(part[k], "y", 4 - k) for k in (1, 2, 3)]
+    part = gather_columns(requests, sources, shifts)
+    strips = [part[0]] + [shifted(part[k], "y", 4 - k) for k in (2, 1, 3)]
+    growth = coagulate(after(coag_kernel, part[0]), planes, "coagulate_fine")
+    request_rows = jnp.concatenate(requests, axis=0)
+    mate_rows = shifted(request_rows, "core", 1)
+    strips, growth, mate_rows = lax.optimization_barrier((strips, growth, mate_rows))
 
     middle, base, registers, x_ghosts, y_ghosts = first_stage(
         levels, column, planes, growth, strips, below_plane, above_plane
     )
 
-    held = [registers] + [shifted(registers, "y", k) for k in (1, 2, 3)]
-    below_plane, above_plane = along_box(middle[3], 1), along_box(middle[0], -1)
-    request_rows = jnp.concatenate(requests, axis=0)
-    mate_rows = shifted(request_rows, "core", 1)
+    held = {k: shifted(registers, "y", k) for k in (2, 1, 3)}
+    held[0] = registers
+    cells = cells_by_row([request_rows, after(mate_rows, registers)])
+    mates = [shifted(after(held[k], cells), "core", 1) for k in range(4)]
+    parts = scatter_columns([request_rows, mate_rows], cells, [held[k] for k in range(4)] + mates)
+    sent = [parts[0]] + [shifted(parts[k], "x", k) for k in (2, 1, 3)]
+    middle, _ = lax.optimization_barrier((middle, parts[0]))
+    below_plane, above_plane = shifted(middle[3], "box", 1), shifted(middle[0], "box", 7)
     growth = coagulate(coag_kernel, middle, "coagulate_middle")
-    mates = [shifted(value, "core", 1) for value in held]
-    parts = scatter_columns([request_rows, mate_rows], held + mates)
-    sent = [parts[0]] + [shifted(parts[k], "x", k) for k in (2, 1, 3)]
     fine_out = second_stage(levels, column, middle, base, growth, x_ghosts, y_ghosts, below_plane, above_plane)
+    coarse_growth = coagulate(after(coag_kernel, growth[0]), [coarse], "coagulate_coarse")[0]
+    sent, fine_out, coarse_growth = lax.optimization_barrier((sent, fine_out, coarse_growth))
     coarse_out = finish_coarse(coarse, coarse_growth, sent)
     return fine_out[None, None], coarse_out[None, None]
 

time: 96 us -> 82 us (0.85)
  the two profiles are of different devices: /device:TPU:103 before, /device:TPU:1 now
where the time goes in v2:
time: 82 us; the launch traced here: 81.8 us
  starting transfers between devices  37 us (45%)
  Pallas kernels  26.4 us (32%)
  waiting for transfers between devices  13.2 us (16%)
  local copies, waits for them, and re-layouts  4.28 us (5%)
  between operations  0.83 us (1%)
    ppermute x27, starting transfers between devices, shifted(): lax.ppermute(value, axis, [(i, (i + shift) % size) for i in range(size)])  37 us
    pallas_call x9, Pallas kernels, call(): pl.pallas_call(kernel, out_shape=out_shape, in_specs=in_specs, out_specs=...  24 us
    ppermute x27, waiting for transfers between devices, shifted(): lax.ppermute(value, axis, [(i, (i + shift) % size) for i in range(size)])  13.2 us
    pallas_call x1, Pallas kernels, second_stage(): pl.pallas_call(kernel, out_shape=sds(S, X, PLANE), in_specs=[SMEM] + [VME...  2.35 us
    unnamed x10, local copies, waits for them, and re-layouts  2.08 us
  transfers between devices with their start and end apart: 27, of which 12 were waited for; matrix products, arithmetic and copies ran while one was open for 1% of the time, Pallas kernels for 14%

profile of v2, /device:TPU:1, one launch (start us, length us, event | category | flops | bytes accessed | tf_op | source)
XLA Modules:
  0.0 81.8 jit_solution(15974494607967931926)
XLA Ops:
  0.6 0.7 slice.9
  1.3 0.8 slice.8
  2.2 2.1 %collective-permute-start.3 = (s32[1,640]{1,0:T(1,128)S(1)}, s32[1,640]{1,0:T(1,128)S(1)}, u32[]{:S(2)}, u32[]{:S(2)}) collective-permute-start(s32[1,640]{1,0:T(1,128)S(1)} %pad_add_fusion.2), channel_id=1, source_target_pairs={{0,16},{16,32},{32,48},{48,0},{1,17},{17,33},{33,49},{49,1},{2,18}... | collective-permute-start | bytes 7688 | tf_op jit(solution)/shard_map/ppermute | solution.py:337
  4.3 2.5 %collective-permute-start.2 = (f32[48,1152]{1,0:T(8,128)}, f32[48,1152]{1,0:T(8,128)S(1)}, u32[]{:S(2)}, u32[]{:S(2)}) collective-permute-start(f32[48,1152]{1,0:T(8,128)} %bitcast.6), channel_id=1, source_target_pairs={{0,192},{64,0},{128,64},{192,128},{1,193},{65,1},{129,65},{193,129... | collective-permute-start | bytes 663560 | tf_op jit(solution)/shard_map/ppermute | solution.py:337
  6.8 0.5 collective-permute-start.1
  7.3 0.6 collective-permute-start
  8.0 2.6 %collective-permute-start.4 = (s32[2,640]{1,0:T(2,128)S(1)}, s32[2,640]{1,0:T(2,128)S(1)}, u32[]{:S(2)}, u32[]{:S(2)}) collective-permute-start(s32[2,640]{1,0:T(2,128)S(1)} %pad_add_fusion.1.refs_0_), channel_id=1, source_target_pairs={{0,32},{16,48},{32,0},{48,16},{1,33},{17,49},{33,1},{49,17},{2,34}... | collective-permute-start | bytes 15368 | tf_op jit(solution)/shard_map/ppermute | solution.py:337
  10.6 1.1 %copy-done.3 = f32[1,1,48,4,1024]{4,3,2,1,0:T(4,128)S(1)} copy-done((f32[1,1,48,4,1024]{4,3,2,1,0:T(4,128)S(1)}, f32[1,1,48,4,1024]{4,3,2,1,0:T(4,128)}, u32[]{:S(2)}) %copy-start.3) | copy-done | bytes 786456
  11.9 1.7 %collective-permute-start.5 = (f32[48,1024]{1,0:T(8,128)S(1)}, f32[48,1024]{1,0:T(8,128)S(1)}, u32[]{:S(2)}, u32[]{:S(2)}) collective-permute-start(f32[48,1024]{1,0:T(8,128)S(1)} %get-tuple-element.68.refs_3_), channel_id=1, source_target_pairs={{0,1},{1,2},{2,3},{3,4},{4,5},{5,6},{6,7},{7,0},{8,9},{9,10},{10,1... | collective-permute-start | bytes 589832 | tf_op jit(solution)/shard_map/ppermute | solution.py:337
  13.6 4.0 %collective-permute-start.6 = (f32[48,1024]{1,0:T(8,128)S(1)}, f32[48,1024]{1,0:T(8,128)S(1)}, u32[]{:S(2)}, u32[]{:S(2)}) collective-permute-start(f32[48,1024]{1,0:T(8,128)S(1)} %get-tuple-element.69.refs_0_), channel_id=1, source_target_pairs={{0,7},{1,0},{2,1},{3,2},{4,3},{5,4},{6,5},{7,6},{8,15},{9,8},{10,9... | collective-permute-start | bytes 589832 | tf_op jit(solution)/shard_map/ppermute | solution.py:337
  17.7 3.0 %collective-permute-done.5.refs_12_ = f32[48,1024]{1,0:T(8,128)S(1)} collective-permute-done((f32[48,1024]{1,0:T(8,128)S(1)}, f32[48,1024]{1,0:T(8,128)S(1)}, u32[]{:S(2)}, u32[]{:S(2)}) %collective-permute-start.5) | collective-permute-done | bytes 196640 | tf_op jit(solution)/shard_map/ppermute | solution.py:337
  20.7 2.9 %collective-permute-start.7 = (f32[48,1152]{1,0:T(8,128)}, f32[48,1152]{1,0:T(8,128)S(1)}, u32[]{:S(2)}, u32[]{:S(2)}) collective-permute-start(f32[48,1152]{1,0:T(8,128)} %bitcast.9), channel_id=1, source_target_pairs={{0,8},{8,0},{1,9},{9,1},{2,10},{10,2},{3,11},{11,3},{4,12},{12,4},... | collective-permute-start | bytes 663560 | tf_op jit(solution)/shard_map/ppermute | solution.py:337
  23.6 0.5 collective-permute-start.8
  24.2 0.4 collective-permute-start.10
  24.6 0.3 collective-permute-done.7.refs_3_
  25.2 0.4 collective-permute-done.9.refs_7_
  25.6 0.3 collective-permute-done.10.refs_9_
  25.9 0.9 %copy-done.1 = f32[1,1,48,1152]{3,2,1,0:T(8,128)S(1)} copy-done((f32[1,1,48,1152]{3,2,1,0:T(8,128)S(1)}, f32[1,1,48,1152]{3,2,1,0:T(8,128)}, u32[]{:S(2)}) %copy-start.1) | copy-done | bytes 221208
  26.8 6.1 %gather_columns.1 = (f32[48,640]{1,0:T(8,128)S(1)}, f32[48,640]{1,0:T(8,128)S(1)}, f32[48,640]{1,0:T(8,128)S(1)}, f32[48,640]{1,0:T(8,128)S(1)}) custom-call(s32[2,640]{1,0:T(2,128)S(1)} %pad_add_fusion.1.refs_0_, s32[2,640]{1,0:T(2,128)S(1)} %collective-permute-done.4.refs_1_, f32[48,1152]{1,0:T(8,128)S(1)} %bitcast.10, ...), custom_call_target="tpu_custom_call" | custom-call | flops 1000 | bytes 1000 | tf_op jit(solution)/shard_map/gather_columns/pallas_call | solution.py:31
  33.0 2.7 %collective-permute-start.11 = (f32[48,640]{1,0:T(8,128)S(1)}, f32[48,640]{1,0:T(8,128)S(1)}, u32[]{:S(2)}, u32[]{:S(2)}) collective-permute-start(f32[48,640]{1,0:T(8,128)S(1)} %get-tuple-element.76), channel_id=1, source_target_pairs={{0,32},{16,48},{32,0},{48,16},{1,33},{17,49},{33,1},{49,17},{2,34}... | collective-permute-start | bytes 368648 | tf_op jit(solution)/shard_map/ppermute | solution.py:337
  35.7 1.1 %collective-permute-start.12 = (f32[48,640]{1,0:T(8,128)S(1)}, f32[48,640]{1,0:T(8,128)S(1)}, u32[]{:S(2)}, u32[]{:S(2)}) collective-permute-start(f32[48,640]{1,0:T(8,128)S(1)} %get-tuple-element.77), channel_id=1, source_target_pairs={{0,48},{16,0},{32,16},{48,32},{1,49},{17,1},{33,17},{49,33},{2,50}... | collective-permute-start | bytes 368648 | tf_op jit(solution)/shard_map/ppermute | solution.py:337
  36.7 0.4 collective-permute-start.13
  37.1 1.2 %collective-permute-start.14 = (s32[4,640]{1,0:T(4,128)S(1)}, s32[4,640]{1,0:T(4,128)S(1)}, u32[]{:S(2)}, u32[]{:S(2)}) collective-permute-start(s32[4,640]{1,0:T(4,128)S(1)} %pad_add_fusion.request_a), channel_id=1, source_target_pairs={{0,8},{8,0},{1,9},{9,1},{2,10},{10,2},{3,11},{11,3},{4,12},{12,4},... | collective-permute-start | bytes 30728 | tf_op jit(solution)/shard_map/ppermute | solution.py:337
  38.4 0.7 copy.8.diffusion_ref
  39.1 3.4 %coagulate_fine.1 = (f32[48,1024]{1,0:T(8,128)S(1)}, f32[48,1024]{1,0:T(8,128)S(1)}, f32[48,1024]{1,0:T(8,128)S(1)}, f32[48,1024]{1,0:T(8,128)S(1)}) custom-call(bf16[48,2304]{1,0:T(8,128)(2,1)S(1)} %copy-done, f32[48,1024]{1,0:T(8,128)S(1)} %get-tuple-element.69.refs_0_, f32[48,1024]{1,0:T(8,128)S(1)} %get-tuple-element.80.refs_1_, ...), custom_call_target="tpu_custom_call" | custom-call | flops 1000 | bytes 1000 | tf_op jit(solution)/shard_map/coagulate_fine/pallas_call | solution.py:31
  42.6 2.0 %first_stage.1 = (f32[48,1024]{1,0:T(8,128)S(1)}, f32[48,1024]{1,0:T(8,128)S(1)}, f32[48,1024]{1,0:T(8,128)S(1)}, f32[48,1024]{1,0:T(8,128)S(1)}, f32[48,1024]{1...) custom-call(s32[1,8]{1,0:T(1,128)S(1)} %copy-done.4, ...), custom_call_target="tpu_custom_call" | custom-call | flops 1000 | bytes 1000 | tf_op jit(solution)/shard_map/first_stage/pallas_call | solution.py:31
  44.6 2.4 %collective-permute-start.17 = (f32[48,640]{1,0:T(8,128)S(1)}, f32[48,640]{1,0:T(8,128)S(1)}, u32[]{:S(2)}, u32[]{:S(2)}) collective-permute-start(f32[48,640]{1,0:T(8,128)S(1)} %get-tuple-element.99.refs_0_), channel_id=1, source_target_pairs={{0,48},{16,0},{32,16},{48,32},{1,49},{17,1},{33,17},{49,33},{2,50}... | collective-permute-start | bytes 368648 | tf_op jit(solution)/shard_map/ppermute | solution.py:337
  46.9 0.5 collective-permute-start.16
  47.4 0.5 collective-permute-start.15
  47.9 0.7 cells_by_row.1.cell_ref
  48.7 1.4 %collective-permute-start.18 = (f32[48,640]{1,0:T(8,128)S(1)}, f32[48,640]{1,0:T(8,128)S(1)}, u32[]{:S(2)}, u32[]{:S(2)}) collective-permute-start(f32[48,640]{1,0:T(8,128)S(1)} %get-tuple-element.99.refs_0_), channel_id=1, source_target_pairs={{0,8},{8,0},{1,9},{9,1},{2,10},{10,2},{3,11},{11,3},{4,12},{12,4},... | collective-permute-start | bytes 368648 | tf_op jit(solution)/shard_map/ppermute | solution.py:337
  50.1 2.0 %collective-permute-done.17.refs_3_ = f32[48,640]{1,0:T(8,128)S(1)} collective-permute-done((f32[48,640]{1,0:T(8,128)S(1)}, f32[48,640]{1,0:T(8,128)S(1)}, u32[]{:S(2)}, u32[]{:S(2)}) %collective-permute-start.17) | collective-permute-done | bytes 122912 | tf_op jit(solution)/shard_map/ppermute | solution.py:337
  52.2 0.9 %collective-permute-done.16.refs_2_ = f32[48,640]{1,0:T(8,128)S(1)} collective-permute-done((f32[48,640]{1,0:T(8,128)S(1)}, f32[48,640]{1,0:T(8,128)S(1)}, u32[]{:S(2)}, u32[]{:S(2)}) %collective-permute-start.16) | collective-permute-done | bytes 122912 | tf_op jit(solution)/shard_map/ppermute | solution.py:337
  53.1 3.2 %collective-permute-done.15.refs_1_ = f32[48,640]{1,0:T(8,128)S(1)} collective-permute-done((f32[48,640]{1,0:T(8,128)S(1)}, f32[48,640]{1,0:T(8,128)S(1)}, u32[]{:S(2)}, u32[]{:S(2)}) %collective-permute-start.15) | collective-permute-done | bytes 122912 | tf_op jit(solution)/shard_map/ppermute | solution.py:337
  56.3 0.5 collective-permute-start.19
  56.8 0.5 collective-permute-start.21
  57.3 0.5 collective-permute-done.19.refs_5_
  57.8 0.4 collective-permute-done.20.refs_6_
  58.3 6.4 %scatter_columns.1 = (f32[48,1152]{1,0:T(8,128)S(1)}, f32[48,1152]{1,0:T(8,128)S(1)}, f32[48,1152]{1,0:T(8,128)S(1)}, f32[48,1152]{1,0:T(8,128)S(1)}) custom-call(s32[4,640]{1,0:T(4,128)S(1)} %pad_add_fusion.request_a, s32[4,640]{1,0:T(4,128)S(1)} %collective-permute-done.14.request_b, s32[5120,128]{1,0:T(8,128)S(1)} %cells_by_row.1.cell_ref, ...), custom_call_target="tpu_custom_call" | custom-call | flops 1000 | bytes 1000 | tf_op jit(solution)/shard_map/scatter_columns/pallas_call | solution.py:31
  64.8 1.7 %collective-permute-start.22 = (f32[48,1152]{1,0:T(8,128)S(1)}, f32[48,1152]{1,0:T(8,128)S(1)}, u32[]{:S(2)}, u32[]{:S(2)}) collective-permute-start(f32[48,1152]{1,0:T(8,128)S(1)} %get-tuple-element.104), channel_id=1, source_target_pairs={{0,128},{64,192},{128,0},{192,64},{1,129},{65,193},{129,1},{193,65... | collective-permute-start | bytes 663560 | tf_op jit(solution)/shard_map/ppermute | solution.py:337
  66.4 1.1 %collective-permute-start.23 = (f32[48,1152]{1,0:T(8,128)S(1)}, f32[48,1152]{1,0:T(8,128)S(1)}, u32[]{:S(2)}, u32[]{:S(2)}) collective-permute-start(f32[48,1152]{1,0:T(8,128)S(1)} %get-tuple-element.105), channel_id=1, source_target_pairs={{0,64},{64,128},{128,192},{192,0},{1,65},{65,129},{129,193},{193,1... | collective-permute-start | bytes 663560 | tf_op jit(solution)/shard_map/ppermute | solution.py:337
  67.5 1.6 %collective-permute-start.24 = (f32[48,1152]{1,0:T(8,128)S(1)}, f32[48,1152]{1,0:T(8,128)S(1)}, u32[]{:S(2)}, u32[]{:S(2)}) collective-permute-start(f32[48,1152]{1,0:T(8,128)S(1)} %get-tuple-element.106), channel_id=1, source_target_pairs={{0,192},{64,0},{128,64},{192,128},{1,193},{65,1},{129,65},{193,129... | collective-permute-start | bytes 663560 | tf_op jit(solution)/shard_map/ppermute | solution.py:337
  69.1 3.4 %collective-permute-start.26 = (f32[48,1024]{1,0:T(8,128)S(1)}, f32[48,1024]{1,0:T(8,128)S(1)}, u32[]{:S(2)}, u32[]{:S(2)}) collective-permute-start(f32[48,1024]{1,0:T(8,128)S(1)} %get-tuple-element.111.refs_0_), channel_id=1, source_target_pairs={{0,7},{1,0},{2,1},{3,2},{4,3},{5,4},{6,5},{7,6},{8,15},{9,8},{10,9... | collective-permute-start | bytes 589832 | tf_op jit(solution)/shard_map/ppermute | solution.py:337
  72.5 3.4 %coagulate_middle.1 = (f32[48,1024]{1,0:T(8,128)S(1)}, f32[48,1024]{1,0:T(8,128)S(1)}, f32[48,1024]{1,0:T(8,128)S(1)}, f32[48,1024]{1,0:T(8,128)S(1)}) custom-call(bf16[48,2304]{1,0:T(8,128)(2,1)S(1)} %copy-done, f32[48,1024]{1,0:T(8,128)S(1)} %get-tuple-element.111.refs_0_, f32[48,1024]{1,0:T(8,128)S(1)} %get-tuple-element.112.refs_1_, ...), custom_call_target="tpu_custom_call" | custom-call | flops 1000 | bytes 1000 | tf_op jit(solution)/shard_map/coagulate_middle/pallas_call | solution.py:31
  75.9 1.0 %coagulate_coarse.1.growth_ref = f32[48,1152]{1,0:T(8,128)S(1)} custom-call(bf16[48,2304]{1,0:T(8,128)(2,1)S(1)} %copy-done, f32[48,1152]{1,0:T(8,128)S(1)} %bitcast.11), custom_call_target="tpu_custom_call" | custom-call | flops 1000 | bytes 1000 | tf_op jit(solution)/shard_map/coagulate_coarse/pallas_call | solution.py:31
  77.0 1.7 %collective-permute-done.25.refs_16_ = f32[48,1024]{1,0:T(8,128)S(1)} collective-permute-done((f32[48,1024]{1,0:T(8,128)S(1)}, f32[48,1024]{1,0:T(8,128)S(1)}, u32[]{:S(2)}, u32[]{:S(2)}) %collective-permute-start.25) | collective-permute-done | bytes 196640 | tf_op jit(solution)/shard_map/ppermute | solution.py:337
  78.7 2.3 %second_stage.1 = f32[48,4,1024]{2,1,0:T(4,128)} custom-call(s32[1,8]{1,0:T(1,128)S(1)} %copy-done.4, f32[48,1]{1,0:T(8,128)S(1)} %copy.8.diffusion_ref, f32[48,1024]{1,0:T(8,128)S(1)} %get-tuple-element.111.refs_0_, f32[48,1024]{1,0:T(8,128)S(1)} %get-tuple-element.112.refs_1_, f32[48,1024]{1,0:T(8,128)S(1)} %get-tuple-element.113.refs_2_, ...), custom_call_target="tpu_custom_call" | custom-call | flops 1000 | bytes 1000 | tf_op jit(solution)/shard_map/second_stage/pallas_call | solution.py:315
  81.0 0.8 finish_coarse.1
  (33 shorter events, 1.0 us)
Async XLA Ops:
  0.6 38.5 %copy-start = (bf16[48,2304]{1,0:T(8,128)(2,1)S(1)}, bf16[48,2304]{1,0:T(8,128)(2,1)}, u32[]{:S(2)}) copy-start(bf16[48,2304]{1,0:T(8,128)(2,1)} %matrix_ref.3) | copy-start | bytes 663556
  2.2 5.7 %collective-permute-start.3 = (s32[1,640]{1,0:T(1,128)S(1)}, s32[1,640]{1,0:T(1,128)S(1)}, u32[]{:S(2)}, u32[]{:S(2)}) collective-permute-start(s32[1,640]{1,0:T(1,128)S(1)} %pad_add_fusion.2), channel_id=1, source_target_pairs={{0,16},{16,32},{32,48},{48,0},{1,17},{17,33},{33,49},{49,1},{2,18}... | collective-permute-start | bytes 7688 | tf_op jit(solution)/shard_map/ppermute | solution.py:337
  4.3 19.3 %collective-permute-start.2 = (f32[48,1152]{1,0:T(8,128)}, f32[48,1152]{1,0:T(8,128)S(1)}, u32[]{:S(2)}, u32[]{:S(2)}) collective-permute-start(f32[48,1152]{1,0:T(8,128)} %bitcast.6), channel_id=1, source_target_pairs={{0,192},{64,0},{128,64},{192,128},{1,193},{65,1},{129,65},{193,129... | collective-permute-start | bytes 663560 | tf_op jit(solution)/shard_map/ppermute | solution.py:337
  6.8 16.8 %collective-permute-start.1 = (f32[48,1152]{1,0:T(8,128)}, f32[48,1152]{1,0:T(8,128)S(1)}, u32[]{:S(2)}, u32[]{:S(2)}) collective-permute-start(f32[48,1152]{1,0:T(8,128)} %bitcast.7), channel_id=1, source_target_pairs={{0,128},{64,192},{128,0},{192,64},{1,129},{65,193},{129,1},{193,65... | collective-permute-start | bytes 663560 | tf_op jit(solution)/shard_map/ppermute | solution.py:337
  7.3 16.3 %collective-permute-start = (f32[48,1152]{1,0:T(8,128)}, f32[48,1152]{1,0:T(8,128)S(1)}, u32[]{:S(2)}, u32[]{:S(2)}) collective-permute-start(f32[48,1152]{1,0:T(8,128)} %bitcast.8), channel_id=1, source_target_pairs={{0,64},{64,128},{128,192},{192,0},{1,65},{65,129},{129,193},{193,1... | collective-permute-start | bytes 663560 | tf_op jit(solution)/shard_map/ppermute | solution.py:337
  8.0 5.6 %collective-permute-start.4 = (s32[2,640]{1,0:T(2,128)S(1)}, s32[2,640]{1,0:T(2,128)S(1)}, u32[]{:S(2)}, u32[]{:S(2)}) collective-permute-start(s32[2,640]{1,0:T(2,128)S(1)} %pad_add_fusion.1.refs_0_), channel_id=1, source_target_pairs={{0,32},{16,48},{32,0},{48,16},{1,33},{17,49},{33,1},{49,17},{2,34}... | collective-permute-start | bytes 15368 | tf_op jit(solution)/shard_map/ppermute | solution.py:337
  10.6 1.1 %copy-start.3 = (f32[1,1,48,4,1024]{4,3,2,1,0:T(4,128)S(1)}, f32[1,1,48,4,1024]{4,3,2,1,0:T(4,128)}, u32[]{:S(2)}) copy-start(f32[1,1,48,4,1024]{4,3,2,1,0:T(4,128)} %param.6) | copy-start | bytes 2359300
  11.8 30.8 %copy-start.4 = (s32[1,8]{1,0:T(1,128)S(1)}, s32[1,8]{1,0:T(1,128)}, u32[]{:S(2)}) copy-start(s32[1,8]{1,0:T(1,128)} %levels_ref.3) | copy-start | bytes 100
  11.9 8.8 %collective-permute-start.5 = (f32[48,1024]{1,0:T(8,128)S(1)}, f32[48,1024]{1,0:T(8,128)S(1)}, u32[]{:S(2)}, u32[]{:S(2)}) collective-permute-start(f32[48,1024]{1,0:T(8,128)S(1)} %get-tuple-element.68.refs_3_), channel_id=1, source_target_pairs={{0,1},{1,2},{2,3},{3,4},{4,5},{5,6},{6,7},{7,0},{8,9},{9,10},{10,1... | collective-permute-start | bytes 589832 | tf_op jit(solution)/shard_map/ppermute | solution.py:337
  13.6 9.9 %collective-permute-start.6 = (f32[48,1024]{1,0:T(8,128)S(1)}, f32[48,1024]{1,0:T(8,128)S(1)}, u32[]{:S(2)}, u32[]{:S(2)}) collective-permute-start(f32[48,1024]{1,0:T(8,128)S(1)} %get-tuple-element.69.refs_0_), channel_id=1, source_target_pairs={{0,7},{1,0},{2,1},{3,2},{4,3},{5,4},{6,5},{7,6},{8,15},{9,8},{10,9... | collective-permute-start | bytes 589832 | tf_op jit(solution)/shard_map/ppermute | solution.py:337
  20.7 4.2 %collective-permute-start.7 = (f32[48,1152]{1,0:T(8,128)}, f32[48,1152]{1,0:T(8,128)S(1)}, u32[]{:S(2)}, u32[]{:S(2)}) collective-permute-start(f32[48,1152]{1,0:T(8,128)} %bitcast.9), channel_id=1, source_target_pairs={{0,8},{8,0},{1,9},{9,1},{2,10},{10,2},{3,11},{11,3},{4,12},{12,4},... | collective-permute-start | bytes 663560 | tf_op jit(solution)/shard_map/ppermute | solution.py:337
  23.6 1.6 %collective-permute-start.8 = (f32[48,1152]{1,0:T(8,128)S(1)}, f32[48,1152]{1,0:T(8,128)S(1)}, u32[]{:S(2)}, u32[]{:S(2)}) collective-permute-start(f32[48,1152]{1,0:T(8,128)S(1)} %collective-permute-done.refs_4_), channel_id=1, source_target_pairs={{0,8},{8,0},{1,9},{9,1},{2,10},{10,2},{3,11},{11,3},{4,12},{12,4},... | collective-permute-start | bytes 663560 | tf_op jit(solution)/shard_map/ppermute | solution.py:337
  24.1 1.5 %collective-permute-start.9 = (f32[48,1152]{1,0:T(8,128)S(1)}, f32[48,1152]{1,0:T(8,128)S(1)}, u32[]{:S(2)}, u32[]{:S(2)}) collective-permute-start(f32[48,1152]{1,0:T(8,128)S(1)} %collective-permute-done.2.refs_6_), channel_id=1, source_target_pairs={{0,8},{8,0},{1,9},{9,1},{2,10},{10,2},{3,11},{11,3},{4,12},{12,4},... | collective-permute-start | bytes 663560 | tf_op jit(solution)/shard_map/ppermute | solution.py:337
  24.2 1.7 %collective-permute-start.10 = (f32[48,1152]{1,0:T(8,128)S(1)}, f32[48,1152]{1,0:T(8,128)S(1)}, u32[]{:S(2)}, u32[]{:S(2)}) collective-permute-start(f32[48,1152]{1,0:T(8,128)S(1)} %collective-permute-done.1.refs_8_), channel_id=1, source_target_pairs={{0,8},{8,0},{1,9},{9,1},{2,10},{10,2},{3,11},{11,3},{4,12},{12,4},... | collective-permute-start | bytes 663560 | tf_op jit(solution)/shard_map/ppermute | solution.py:337
  25.9 0.9 %copy-start.1 = (f32[1,1,48,1152]{3,2,1,0:T(8,128)S(1)}, f32[1,1,48,1152]{3,2,1,0:T(8,128)}, u32[]{:S(2)}) copy-start(f32[1,1,48,1152]{3,2,1,0:T(8,128)} %param.7) | copy-start | bytes 663556
  33.0 9.6 %collective-permute-start.11 = (f32[48,640]{1,0:T(8,128)S(1)}, f32[48,640]{1,0:T(8,128)S(1)}, u32[]{:S(2)}, u32[]{:S(2)}) collective-permute-start(f32[48,640]{1,0:T(8,128)S(1)} %get-tuple-element.76), channel_id=1, source_target_pairs={{0,32},{16,48},{32,0},{48,16},{1,33},{17,49},{33,1},{49,17},{2,34}... | collective-permute-start | bytes 368648 | tf_op jit(solution)/shard_map/ppermute | solution.py:337
  35.7 6.9 %collective-permute-start.12 = (f32[48,640]{1,0:T(8,128)S(1)}, f32[48,640]{1,0:T(8,128)S(1)}, u32[]{:S(2)}, u32[]{:S(2)}) collective-permute-start(f32[48,640]{1,0:T(8,128)S(1)} %get-tuple-element.77), channel_id=1, source_target_pairs={{0,48},{16,0},{32,16},{48,32},{1,49},{17,1},{33,17},{49,33},{2,50}... | collective-permute-start | bytes 368648 | tf_op jit(solution)/shard_map/ppermute | solution.py:337
  36.7 5.9 %collective-permute-start.13 = (f32[48,640]{1,0:T(8,128)S(1)}, f32[48,640]{1,0:T(8,128)S(1)}, u32[]{:S(2)}, u32[]{:S(2)}) collective-permute-start(f32[48,640]{1,0:T(8,128)S(1)} %get-tuple-element.78), channel_id=1, source_target_pairs={{0,16},{16,32},{32,48},{48,0},{1,17},{17,33},{33,49},{49,1},{2,18}... | collective-permute-start | bytes 368648 | tf_op jit(solution)/shard_map/ppermute | solution.py:337
  37.1 5.4 %collective-permute-start.14 = (s32[4,640]{1,0:T(4,128)S(1)}, s32[4,640]{1,0:T(4,128)S(1)}, u32[]{:S(2)}, u32[]{:S(2)}) collective-permute-start(s32[4,640]{1,0:T(4,128)S(1)} %pad_add_fusion.request_a), channel_id=1, source_target_pairs={{0,8},{8,0},{1,9},{9,1},{2,10},{10,2},{3,11},{11,3},{4,12},{12,4},... | collective-permute-start | bytes 30728 | tf_op jit(solution)/shard_map/ppermute | solution.py:337
  44.6 7.6 %collective-permute-start.17 = (f32[48,640]{1,0:T(8,128)S(1)}, f32[48,640]{1,0:T(8,128)S(1)}, u32[]{:S(2)}, u32[]{:S(2)}) collective-permute-start(f32[48,640]{1,0:T(8,128)S(1)} %get-tuple-element.99.refs_0_), channel_id=1, source_target_pairs={{0,48},{16,0},{32,16},{48,32},{1,49},{17,1},{33,17},{49,33},{2,50}... | collective-permute-start | bytes 368648 | tf_op jit(solution)/shard_map/ppermute | solution.py:337
  46.9 6.2 %collective-permute-start.16 = (f32[48,640]{1,0:T(8,128)S(1)}, f32[48,640]{1,0:T(8,128)S(1)}, u32[]{:S(2)}, u32[]{:S(2)}) collective-permute-start(f32[48,640]{1,0:T(8,128)S(1)} %get-tuple-element.99.refs_0_), channel_id=1, source_target_pairs={{0,32},{16,48},{32,0},{48,16},{1,33},{17,49},{33,1},{49,17},{2,34}... | collective-permute-start | bytes 368648 | tf_op jit(solution)/shard_map/ppermute | solution.py:337
  47.4 8.9 %collective-permute-start.15 = (f32[48,640]{1,0:T(8,128)S(1)}, f32[48,640]{1,0:T(8,128)S(1)}, u32[]{:S(2)}, u32[]{:S(2)}) collective-permute-start(f32[48,640]{1,0:T(8,128)S(1)} %get-tuple-element.99.refs_0_), channel_id=1, source_target_pairs={{0,16},{16,32},{32,48},{48,0},{1,17},{17,33},{33,49},{49,1},{2,18}... | collective-permute-start | bytes 368648 | tf_op jit(solution)/shard_map/ppermute | solution.py:337
  48.7 27.2 %copy-start.2 = (f32[1,1,48,1152]{3,2,1,0:T(8,128)S(1)}, f32[1,1,48,1152]{3,2,1,0:T(8,128)}, u32[]{:S(2)}) copy-start(f32[1,1,48,1152]{3,2,1,0:T(8,128)} %param.7) | copy-start | bytes 663556
  48.7 8.6 %collective-permute-start.18 = (f32[48,640]{1,0:T(8,128)S(1)}, f32[48,640]{1,0:T(8,128)S(1)}, u32[]{:S(2)}, u32[]{:S(2)}) collective-permute-start(f32[48,640]{1,0:T(8,128)S(1)} %get-tuple-element.99.refs_0_), channel_id=1, source_target_pairs={{0,8},{8,0},{1,9},{9,1},{2,10},{10,2},{3,11},{11,3},{4,12},{12,4},... | collective-permute-start | bytes 368648 | tf_op jit(solution)/shard_map/ppermute | solution.py:337
  56.3 1.5 %collective-permute-start.19 = (f32[48,640]{1,0:T(8,128)S(1)}, f32[48,640]{1,0:T(8,128)S(1)}, u32[]{:S(2)}, u32[]{:S(2)}) collective-permute-start(f32[48,640]{1,0:T(8,128)S(1)} %collective-permute-done.15.refs_1_), channel_id=1, source_target_pairs={{0,8},{8,0},{1,9},{9,1},{2,10},{10,2},{3,11},{11,3},{4,12},{12,4},... | collective-permute-start | bytes 368648 | tf_op jit(solution)/shard_map/ppermute | solution.py:337
  56.8 1.3 %collective-permute-start.20 = (f32[48,640]{1,0:T(8,128)S(1)}, f32[48,640]{1,0:T(8,128)S(1)}, u32[]{:S(2)}, u32[]{:S(2)}) collective-permute-start(f32[48,640]{1,0:T(8,128)S(1)} %collective-permute-done.16.refs_2_), channel_id=1, source_target_pairs={{0,8},{8,0},{1,9},{9,1},{2,10},{10,2},{3,11},{11,3},{4,12},{12,4},... | collective-permute-start | bytes 368648 | tf_op jit(solution)/shard_map/ppermute | solution.py:337
  56.8 1.5 %collective-permute-start.21 = (f32[48,640]{1,0:T(8,128)S(1)}, f32[48,640]{1,0:T(8,128)S(1)}, u32[]{:S(2)}, u32[]{:S(2)}) collective-permute-start(f32[48,640]{1,0:T(8,128)S(1)} %collective-permute-done.17.refs_3_), channel_id=1, source_target_pairs={{0,8},{8,0},{1,9},{9,1},{2,10},{10,2},{3,11},{11,3},{4,12},{12,4},... | collective-permute-start | bytes 368648 | tf_op jit(solution)/shard_map/ppermute | solution.py:337
  64.8 16.3 %collective-permute-start.22 = (f32[48,1152]{1,0:T(8,128)S(1)}, f32[48,1152]{1,0:T(8,128)S(1)}, u32[]{:S(2)}, u32[]{:S(2)}) collective-permute-start(f32[48,1152]{1,0:T(8,128)S(1)} %get-tuple-element.104), channel_id=1, source_target_pairs={{0,128},{64,192},{128,0},{192,64},{1,129},{65,193},{129,1},{193,65... | collective-permute-start | bytes 663560 | tf_op jit(solution)/shard_map/ppermute | solution.py:337
  66.4 14.6 %collective-permute-start.23 = (f32[48,1152]{1,0:T(8,128)S(1)}, f32[48,1152]{1,0:T(8,128)S(1)}, u32[]{:S(2)}, u32[]{:S(2)}) collective-permute-start(f32[48,1152]{1,0:T(8,128)S(1)} %get-tuple-element.105), channel_id=1, source_target_pairs={{0,64},{64,128},{128,192},{192,0},{1,65},{65,129},{129,193},{193,1... | collective-permute-start | bytes 663560 | tf_op jit(solution)/shard_map/ppermute | solution.py:337
  67.5 13.5 %collective-permute-start.24 = (f32[48,1152]{1,0:T(8,128)S(1)}, f32[48,1152]{1,0:T(8,128)S(1)}, u32[]{:S(2)}, u32[]{:S(2)}) collective-permute-start(f32[48,1152]{1,0:T(8,128)S(1)} %get-tuple-element.106), channel_id=1, source_target_pairs={{0,192},{64,0},{128,64},{192,128},{1,193},{65,1},{129,65},{193,129... | collective-permute-start | bytes 663560 | tf_op jit(solution)/shard_map/ppermute | solution.py:337
  69.1 7.9 %collective-permute-start.26 = (f32[48,1024]{1,0:T(8,128)S(1)}, f32[48,1024]{1,0:T(8,128)S(1)}, u32[]{:S(2)}, u32[]{:S(2)}) collective-permute-start(f32[48,1024]{1,0:T(8,128)S(1)} %get-tuple-element.111.refs_0_), channel_id=1, source_target_pairs={{0,7},{1,0},{2,1},{3,2},{4,3},{5,4},{6,5},{7,6},{8,15},{9,8},{10,9... | collective-permute-start | bytes 589832 | tf_op jit(solution)/shard_map/ppermute | solution.py:337
  72.5 6.2 %collective-permute-start.25 = (f32[48,1024]{1,0:T(8,128)S(1)}, f32[48,1024]{1,0:T(8,128)S(1)}, u32[]{:S(2)}, u32[]{:S(2)}) collective-permute-start(f32[48,1024]{1,0:T(8,128)S(1)} %get-tuple-element.114.refs_3_), channel_id=1, source_target_pairs={{0,1},{1,2},{2,3},{3,4},{4,5},{5,6},{6,7},{7,0},{8,9},{9,10},{10,1... | collective-permute-start | bytes 589832 | tf_op jit(solution)/shard_map/ppermute | solution.py:337

commit v3 on v2

--- a/solution.py
+++ b/solution.py
@@ -13,7 +13,7 @@
 WIDE = 640
 STEP = 0.25
 MIB = 1024 * 1024
-COST = pl.CostEstimate(flops=1000, bytes_accessed=1000, transcendentals=0)
+COST = pl.CostEstimate(flops=0, bytes_accessed=0, transcendentals=0)
 
 f32 = jnp.float32
 bf16 = jnp.bfloat16
@@ -64,12 +64,14 @@
     return jnp.where(mask, 1.0, 0.0).astype(bf16)
 
 
-def split_planes(fine):
-    def kernel(fine_ref, *planes):
+def split_planes(fine, coarse):
+    def kernel(fine_ref, coarse_ref, *outs):
         for x in range(X):
-            planes[x][...] = fine_ref[:, x, :]
-
-    return call(kernel, [sds(S, PLANE)] * X, [VMEM], fine, name="split_planes")
+            outs[x][...] = fine_ref[:, x, :]
+        outs[X][...] = coarse_ref[...]
+
+    outs = call(kernel, [sds(S, PLANE)] * X + [sds(S, CELLS)], [VMEM] * 2, fine, coarse, name="split_planes")
+    return outs[:X], outs[X]
 
 
 def coagulate(kernel_matrix, fields, name):
@@ -95,40 +97,57 @@
 
 
 def owner_and_cell(request):
+    y_count = GHOSTS - 512
+    none = jnp.full((1, WIDE - GHOSTS), -1, i32)
+    request = jnp.concatenate([request[:, y_count:], request[:, :y_count], none], axis=1)
     owner = jnp.floor((request.astype(f32) + 0.5) * (1.0 / CELLS)).astype(i32)
     return owner, jnp.where(request < 0, -1, request - owner * CELLS)
 
 
-def gather_columns(requests, sources, shifts):
+def column_of(row):
+    same = lax.broadcasted_iota(i32, (S, S), 0) == lax.broadcasted_iota(i32, (S, S), 1)
+    return jnp.sum(jnp.where(same, jnp.broadcast_to(row, (S, S)), 0.0), axis=1, keepdims=True)
+
+
+def pick(rows, request, shifts):
+    x, y, c = lax.axis_index("x"), lax.axis_index("y"), lax.axis_index("core")
+    owner, cell = owner_and_cell(request)
+    cell_id = lax.broadcasted_iota(i32, (CELLS, WIDE), 0)
+    product = mm(rows, ones_where(jnp.broadcast_to(cell, (CELLS, WIDE)) == cell_id))
+    total = jnp.zeros((S, WIDE), f32)
+    for part, (shift, mate) in zip(sums_of(product, len(shifts)), shifts):
+        from_x = jnp.bitwise_and(x - shift, 3)
+        source_owner = (from_x * 4 + y) * 2 + (1 - c if mate else c)
+        total = total + jnp.where(owner == source_owner, part, 0.0)
+    return total
+
+
+def gather_first(requests, sources, shifts, row):
     count = len(sources)
 
-    def kernel(*refs):
-        request_refs, source_refs, outs, rows_ref = refs[:2], refs[2 : 2 + count], refs[2 + count : 6 + count], refs[6 + count]
-        x, y, c = lax.axis_index("x"), lax.axis_index("y"), lax.axis_index("core")
-        for i in range(count):
-            high, low = halves(source_refs[i][...])
+    def kernel(request_ref, *refs):
+        source_refs, (out_ref, rows_ref) = refs[:count], refs[count:]
+        for i, ref in enumerate(source_refs):
+            high, low = halves(ref[...])
             rows_ref[2 * S * i : 2 * S * i + S] = high
             rows_ref[2 * S * i + S : 2 * S * (i + 1)] = low
-        cell_id = lax.broadcasted_iota(i32, (CELLS, WIDE), 0)
-        for i in range(4):
-            owner, cell = owner_and_cell(request_refs[i // 2][i % 2 : i % 2 + 1, :])
-            product = mm(rows_ref[...], ones_where(jnp.broadcast_to(cell, (CELLS, WIDE)) == cell_id))
-            total = jnp.zeros((S, WIDE), f32)
-            for part, (shift, mate) in zip(sums_of(product, count), shifts):
-                from_x = jnp.bitwise_and(x - shift, 3)
-                source_owner = (from_x * 4 + y) * 2 + (1 - c if mate else c)
-                total = total + jnp.where(owner == source_owner, part, 0.0)
-            outs[i][...] = total
+        out_ref[...] = pick(rows_ref[...], request_ref[row : row + 1, :], shifts)
 
     return call(
         kernel,
-        [sds(S, WIDE)] * 4,
-        [VMEM] * (2 + count),
-        *requests,
+        [sds(S, WIDE), jax.ShapeDtypeStruct((2 * S * count, CELLS), bf16)],
+        [VMEM] * (1 + count),
+        requests,
         *sources,
-        scratch=[pltpu.VMEM((2 * S * count, CELLS), bf16)],
-        name="gather_columns",
-    )
+        name="gather_first",
+    )
+
+
+def gather_next(requests, rows, shifts, row, name):
+    def kernel(request_ref, rows_ref, out_ref):
+        out_ref[...] = pick(rows_ref[...], request_ref[row : row + 1, :], shifts)
+
+    return call(kernel, sds(S, WIDE), [VMEM] * 2, requests, rows, name=name)
 
 
 def cells_by_row(requests):
@@ -143,26 +162,26 @@
     return call(kernel, out, [VMEM] * 2, *requests, name="cells_by_row")
 
 
-def scatter_columns(requests, cells, registers):
+def scatter_columns(requests, cells, registers, steps, name):
     total = 8 * WIDE
 
     def kernel(request_a, request_b, cell_ref, *refs):
-        register_refs, outs, rows_ref = refs[:8], refs[8:12], refs[12]
+        register_refs, outs, rows_ref = refs[:8], refs[8:-1], refs[-1]
         x, y, c = lax.axis_index("x"), lax.axis_index("y"), lax.axis_index("core")
         lane = lax.broadcasted_iota(i32, (1, 128), 1)
         for i in range(8):
             request = (request_a if i < 4 else request_b)[i % 4 : i % 4 + 1, :]
             owner, _ = owner_and_cell(request)
             high, low = halves(register_refs[i][...])
-            for k in range(4):
-                to_x = jnp.bitwise_and(x + k, 3)
+            for k, step in enumerate(steps):
+                to_x = jnp.bitwise_and(x + step, 3)
                 mine = jnp.broadcast_to(jnp.where(owner == (to_x * 4 + y) * 2 + c, 1.0, 0.0).astype(bf16), (S, WIDE))
                 rows_ref[2 * S * k : 2 * S * k + S, i * WIDE : (i + 1) * WIDE] = high * mine
                 rows_ref[2 * S * k + S : 2 * S * (k + 1), i * WIDE : (i + 1) * WIDE] = low * mine
 
         def block(start, width):
             marks = [ones_where(cell_ref[...] == lane + (start + 128 * t)) for t in range(width // 128)]
-            return sums_of(mm(rows_ref[...], jnp.concatenate(marks, axis=1)), 4)
+            return sums_of(mm(rows_ref[...], jnp.concatenate(marks, axis=1)), len(steps))
 
         def body(i, carry):
             start = pl.multiple_of(i * 256, 256)
@@ -176,13 +195,13 @@
 
     return call(
         kernel,
-        [sds(S, CELLS)] * 4,
+        [sds(S, CELLS)] * len(steps),
         [VMEM] * 11,
         *requests,
         cells,
         *registers,
-        scratch=[pltpu.VMEM((8 * S, total), bf16)],
-        name="scatter_columns",
+        scratch=[pltpu.VMEM((2 * S * len(steps), total), bf16)],
+        name=name,
     )
 
 
@@ -242,7 +261,7 @@
         registers_ref, x_low_ref, x_high_ref = refs[22:25]
         y_refs = refs[25:27]
         use_low, use_high, factor = box_facts(levels_ref)
-        diffusion_column = diffusion_ref[...]
+        diffusion_column = column_of(diffusion_ref[...])
         strip = strip_refs[0][...] + strip_refs[1][...] + strip_refs[2][...] + strip_refs[3][...]
         x_low, x_high = sums_of(mm(rows_of([strip[:, :256], strip[:, 256:512]]), x_code((256, PLANE), 1, 0)), 2)
         y_rows = rows_of([strip[:, 512:640]])
@@ -298,6 +317,7 @@
         middle_refs, base_refs, growth_refs = refs[:4], refs[4:8], refs[8:12]
         x_low_ref, x_high_ref, y_a, y_b, lower_ref, upper_ref, out_ref, held_ref, sems = refs[12:]
         use_low, use_high, factor = box_facts(levels_ref)
+        scale = factor * column_of(diffusion_ref[...])
         copies = []
         for i in range(S // rows):
             part = slice(i * rows, (i + 1) * rows)
@@ -305,7 +325,7 @@
             upper = jnp.where(use_high, upper_ref[part], x_high_ref[part])
             spread = laplacian([ref[part] for ref in middle_refs], lower, upper, [y_a[part], y_b[part]])
             for x in range(X):
-                rate = (factor * diffusion_ref[part]) * spread[x] + STEP * growth_refs[x][part]
+                rate = scale[part] * spread[x] + STEP * growth_refs[x][part]
                 held_ref[part, x, :] = base_refs[x][part] + 0.5 * rate
             copies.append(pltpu.make_async_copy(held_ref.at[part], out_ref.at[part], sems.at[i]))
             copies[-1].start()
@@ -344,49 +364,58 @@
 def on_device(fine_state, coarse_state, coag_kernel, diffusion, levels, ghost_src):
     fine = fine_state[0, 0]
     coarse = coarse_state[0, 0]
-    column = diffusion.reshape(S, 1)
-    source = ghost_src[0]
-    y_count = GHOSTS - 512
-    own_request = jnp.concatenate(
-        [source[:, y_count:], source[:, :y_count], jnp.full((1, WIDE - GHOSTS), -1, i32)], axis=1
-    )
-
+    row = diffusion.reshape(1, S)
+    request = ghost_src[0]
+
+    near = shifted(request, "y", 1)
     far = {k: shifted(coarse, "x", k) for k in (2, 1, 3)}
     mate = shifted(coarse, "core", 1)
-    near = jnp.concatenate([own_request, shifted(own_request, "y", 1)], axis=0)
-    requests = [near, shifted(near, "y", 2)]
-    planes = split_planes(fine)
+    near = jnp.concatenate([request, near], axis=0)
+    away = shifted(near, "y", 2)
+    planes, held_coarse = split_planes(fine, coarse)
     below_plane, above_plane = shifted(planes[3], "box", 1), shifted(planes[0], "box", 7)
-    far, requests, below_plane, above_plane = lax.optimization_barrier((far, requests, below_plane, above_plane))
-
-    sources, shifts = [coarse, mate], [(0, False), (0, True)]
+    far, near, away, below_plane, above_plane = lax.optimization_barrier((far, near, away, below_plane, above_plane))
+
+    sources, shifts = [held_coarse, mate], [(0, False), (0, True)]
     for k in (1, 3, 2):
         sources += [far[k], shifted(far[k], "core", 1)]
         shifts += [(k, False), (k, True)]
-    part = gather_columns(requests, sources, shifts)
-    strips = [part[0]] + [shifted(part[k], "y", 4 - k) for k in (2, 1, 3)]
-    growth = coagulate(after(coag_kernel, part[0]), planes, "coagulate_fine")
-    request_rows = jnp.concatenate(requests, axis=0)
+    part, strips = {}, {}
+    part[2], rows = gather_first(away, sources, shifts, 0)
+    strips[2] = shifted(part[2], "y", 2)
+    part[1] = gather_next(after(near, part[2]), rows, shifts, 1, "gather_one")
+    strips[1] = shifted(part[1], "y", 3)
+    part[3] = gather_next(after(away, part[1]), rows, shifts, 1, "gather_three")
+    strips[3] = shifted(part[3], "y", 1)
+    strips[0] = gather_next(after(near, (part[3], strips[2])), rows, shifts, 0, "gather_own")
+    growth = coagulate(after(coag_kernel, (strips[0], strips[1])), planes, "coagulate_fine")
+    request_rows = jnp.concatenate([near, away], axis=0)
     mate_rows = shifted(request_rows, "core", 1)
     strips, growth, mate_rows = lax.optimization_barrier((strips, growth, mate_rows))
+    strips = [strips[k] for k in range(4)]
 
     middle, base, registers, x_ghosts, y_ghosts = first_stage(
-        levels, column, planes, growth, strips, below_plane, above_plane
+        levels, row, planes, growth, strips, below_plane, above_plane
     )
 
     held = {k: shifted(registers, "y", k) for k in (2, 1, 3)}
     held[0] = registers
     cells = cells_by_row([request_rows, after(mate_rows, registers)])
-    mates = [shifted(after(held[k], cells), "core", 1) for k in range(4)]
-    parts = scatter_columns([request_rows, mate_rows], cells, [held[k] for k in range(4)] + mates)
-    sent = [parts[0]] + [shifted(parts[k], "x", k) for k in (2, 1, 3)]
-    middle, _ = lax.optimization_barrier((middle, parts[0]))
+    growth = coagulate(after(coag_kernel, cells), middle, "coagulate_middle")
+    held = [after(held[k], growth[0]) for k in range(4)]
+    held += [shifted(value, "core", 1) for value in held]
+    parts, sent = {}, {}
+    parts[2], parts[1] = scatter_columns([request_rows, mate_rows], cells, held, (2, 1), "scatter_far")
+    for k in (2, 1):
+        sent[k] = shifted(parts[k], "x", k)
+    parts[3], sent[0] = scatter_columns([request_rows, mate_rows], after(cells, parts[2]), held, (3, 0), "scatter_near")
+    sent[3] = shifted(parts[3], "x", 3)
+    middle, _ = lax.optimization_barrier((middle, (parts[3], sent[2])))
     below_plane, above_plane = shifted(middle[3], "box", 1), shifted(middle[0], "box", 7)
-    growth = coagulate(coag_kernel, middle, "coagulate_middle")
-    fine_out = second_stage(levels, column, middle, base, growth, x_ghosts, y_ghosts, below_plane, above_plane)
-    coarse_growth = coagulate(after(coag_kernel, growth[0]), [coarse], "coagulate_coarse")[0]
+    coarse_growth = coagulate(after(coag_kernel, (parts[3], sent[1])), [held_coarse], "coagulate_coarse")[0]
+    fine_out = second_stage(levels, row, middle, base, growth, x_ghosts, y_ghosts, below_plane, above_plane)
     sent, fine_out, coarse_growth = lax.optimization_barrier((sent, fine_out, coarse_growth))
-    coarse_out = finish_coarse(coarse, coarse_growth, sent)
+    coarse_out = finish_coarse(held_coarse, coarse_growth, [sent[k] for k in range(4)])
     return fine_out[None, None], coarse_out[None, None]
 
 

time: 82 us -> 82.8 us (level)
  the two profiles are of different devices: /device:TPU:1 before, /device:TPU:2 now
where the time goes in v3:
time: 82.8 us; the launch traced here: 82.6 us
  starting transfers between devices  32.6 us (39%)
  Pallas kernels  29.4 us (36%)
  waiting for transfers between devices  17.8 us (21%)
  local copies, waits for them, and re-layouts  1.15 us (1%)
  between operations  0.83 us (1%)
    ppermute x27, starting transfers between devices, shifted(): lax.ppermute(value, axis, [(i, (i + shift) % size) for i in range(size)])  32.6 us
    pallas_call x13, Pallas kernels, call(): pl.pallas_call(kernel, out_shape=out_shape, in_specs=in_specs, out_specs=...  27.2 us
    ppermute x27, waiting for transfers between devices, shifted(): lax.ppermute(value, axis, [(i, (i + shift) % size) for i in range(size)])  17.8 us
    pallas_call x1, Pallas kernels, second_stage(): pl.pallas_call(kernel, out_shape=sds(S, X, PLANE), in_specs=[SMEM] + [VME...  2.22 us
  transfers between devices with their start and end apart: 27, of which 15 were waited for; matrix products, arithmetic and copies ran while one was open for 1% of the time, Pallas kernels for 26%

profile of v3, /device:TPU:2, one launch (start us, length us, event | category | flops | bytes accessed | tf_op | source)
XLA Modules:
  0.0 82.6 jit_solution(16070429176270712919)
XLA Ops:
  0.6 1.7 %collective-permute-start.3 = (s32[1,576]{1,0:T(1,128)}, s32[1,576]{1,0:T(1,128)S(1)}, u32[]{:S(2)}, u32[]{:S(2)}) collective-permute-start(s32[1,576]{1,0:T(1,128)} %bitcast.11), channel_id=1, source_target_pairs={{0,16},{16,32},{32,48},{48,0},{1,17},{17,33},{33,49},{49,1},{2,18}... | collective-permute-start | bytes 6920 | tf_op jit(solution)/shard_map/ppermute | solution.py:357
  2.3 0.8 collective-permute-start.2
  3.1 2.2 %collective-permute-start.1 = (f32[48,1152]{1,0:T(8,128)}, f32[48,1152]{1,0:T(8,128)S(1)}, u32[]{:S(2)}, u32[]{:S(2)}) collective-permute-start(f32[48,1152]{1,0:T(8,128)} %bitcast.coarse_ref), channel_id=1, source_target_pairs={{0,128},{64,192},{128,0},{192,64},{1,129},{65,193},{129,1},{193,65... | collective-permute-start | bytes 663560 | tf_op jit(solution)/shard_map/ppermute | solution.py:357
  5.2 1.8 %collective-permute-start = (f32[48,1152]{1,0:T(8,128)}, f32[48,1152]{1,0:T(8,128)S(1)}, u32[]{:S(2)}, u32[]{:S(2)}) collective-permute-start(f32[48,1152]{1,0:T(8,128)} %bitcast.coarse_ref), channel_id=1, source_target_pairs={{0,64},{64,128},{128,192},{192,0},{1,65},{65,129},{129,193},{193,1... | collective-permute-start | bytes 663560 | tf_op jit(solution)/shard_map/ppermute | solution.py:357
  7.0 0.7 pad_add_fusion.1.request_ref
  7.7 3.0 %collective-permute-start.4 = (s32[2,576]{1,0:T(2,128)S(1)}, s32[2,576]{1,0:T(2,128)S(1)}, u32[]{:S(2)}, u32[]{:S(2)}) collective-permute-start(s32[2,576]{1,0:T(2,128)S(1)} %pad_add_fusion.1.request_ref), channel_id=1, source_target_pairs={{0,32},{16,48},{32,0},{48,16},{1,33},{17,49},{33,1},{49,17},{2,34}... | collective-permute-start | bytes 13832 | tf_op jit(solution)/shard_map/ppermute | solution.py:357
  10.7 1.1 %copy-done.1 = f32[1,1,48,4,1024]{4,3,2,1,0:T(4,128)S(1)} copy-done((f32[1,1,48,4,1024]{4,3,2,1,0:T(4,128)S(1)}, f32[1,1,48,4,1024]{4,3,2,1,0:T(4,128)}, u32[]{:S(2)}) %copy-start.1) | copy-done | bytes 786456
  11.9 1.1 %split_planes.1 = (f32[48,1024]{1,0:T(8,128)S(1)}, f32[48,1024]{1,0:T(8,128)S(1)}, f32[48,1024]{1,0:T(8,128)S(1)}, f32[48,1024]{1,0:T(8,128)S(1)}, f32[48,1152]{1,0:T(8,128)S(1)}) custom-call(f32[48,4,1024]{2,1,0:T(4,128)S(1)} %bitcast.6, f32[48,1152]{1,0:T(8,128)} %bitcast.coarse_ref), custom_call_target="tpu_custom_call" | custom-call | tf_op jit(solution)/shard_map/split_planes/pallas_call | solution.py:31
  12.9 2.0 %collective-permute-start.5 = (f32[48,1024]{1,0:T(8,128)S(1)}, f32[48,1024]{1,0:T(8,128)S(1)}, u32[]{:S(2)}, u32[]{:S(2)}) collective-permute-start(f32[48,1024]{1,0:T(8,128)S(1)} %get-tuple-element.72.refs_3_), channel_id=1, source_target_pairs={{0,1},{1,2},{2,3},{3,4},{4,5},{5,6},{6,7},{7,0},{8,9},{9,10},{10,1... | collective-permute-start | bytes 589832 | tf_op jit(solution)/shard_map/ppermute | solution.py:357
  14.9 4.0 %collective-permute-start.6 = (f32[48,1024]{1,0:T(8,128)S(1)}, f32[48,1024]{1,0:T(8,128)S(1)}, u32[]{:S(2)}, u32[]{:S(2)}) collective-permute-start(f32[48,1024]{1,0:T(8,128)S(1)} %get-tuple-element.73.refs_0_), channel_id=1, source_target_pairs={{0,7},{1,0},{2,1},{3,2},{4,3},{5,4},{6,5},{7,6},{8,15},{9,8},{10,9... | collective-permute-start | bytes 589832 | tf_op jit(solution)/shard_map/ppermute | solution.py:357
  19.0 3.5 %collective-permute-done.5.refs_12_ = f32[48,1024]{1,0:T(8,128)S(1)} collective-permute-done((f32[48,1024]{1,0:T(8,128)S(1)}, f32[48,1024]{1,0:T(8,128)S(1)}, u32[]{:S(2)}, u32[]{:S(2)}) %collective-permute-start.5) | collective-permute-done | bytes 196640 | tf_op jit(solution)/shard_map/ppermute | solution.py:357
  22.6 0.6 collective-permute-start.8
  23.2 0.4 collective-permute-start.10
  23.7 0.6 collective-permute-done.7.refs_1_
  24.3 0.3 collective-permute-done.9.refs_5_
  24.6 0.3 collective-permute-done.10.refs_7_
  24.9 1.8 %gather_first.1 = (f32[48,640]{1,0:T(8,128)S(1)}, bf16[768,1152]{1,0:T(8,128)(2,1)S(1)}) custom-call(s32[2,576]{1,0:T(2,128)S(1)} %collective-permute-done.4.request_ref, f32[48,1152]{1,0:T(8,128)S(1)} %get-tuple-element.76.refs_0_.coarse_ref, f32[48,1152]{1,0:T(8,128)S(1)} %collective-permute-done.7.refs_1_, f32[48,1152]{1,0:T(8,128)S(1)} %collective-permute-done.refs_2_, ...), custom_call_target="tpu_custom_call" | custom-call | tf_op jit(solution)/shard_map/gather_first/pallas_call | solution.py:31
  26.7 2.2 %collective-permute-start.11 = (f32[48,640]{1,0:T(8,128)S(1)}, f32[48,640]{1,0:T(8,128)S(1)}, u32[]{:S(2)}, u32[]{:S(2)}) collective-permute-start(f32[48,640]{1,0:T(8,128)S(1)} %get-tuple-element.80), channel_id=1, source_target_pairs={{0,32},{16,48},{32,0},{48,16},{1,33},{17,49},{33,1},{49,17},{2,34}... | collective-permute-start | bytes 368648 | tf_op jit(solution)/shard_map/ppermute | solution.py:357
  28.9 1.7 %gather_one.1 = f32[48,640]{1,0:T(8,128)S(1)} custom-call(s32[2,576]{1,0:T(2,128)S(1)} %pad_add_fusion.1.request_ref, bf16[768,1152]{1,0:T(8,128)(2,1)S(1)} %get-tuple-element.82.rows_ref), custom_call_target="tpu_custom_call" | custom-call | tf_op jit(solution)/shard_map/gather_one/pallas_call | solution.py:31
  30.7 1.6 %collective-permute-start.12 = (f32[48,640]{1,0:T(8,128)S(1)}, f32[48,640]{1,0:T(8,128)S(1)}, u32[]{:S(2)}, u32[]{:S(2)}) collective-permute-start(f32[48,640]{1,0:T(8,128)S(1)} %gather_one.1), channel_id=1, source_target_pairs={{0,48},{16,0},{32,16},{48,32},{1,49},{17,1},{33,17},{49,33},{2,50}... | collective-permute-start | bytes 368648 | tf_op jit(solution)/shard_map/ppermute | solution.py:357
  32.3 1.7 %gather_three.1 = f32[48,640]{1,0:T(8,128)S(1)} custom-call(s32[2,576]{1,0:T(2,128)S(1)} %collective-permute-done.4.request_ref, bf16[768,1152]{1,0:T(8,128)(2,1)S(1)} %get-tuple-element.82.rows_ref), custom_call_target="tpu_custom_call" | custom-call | tf_op jit(solution)/shard_map/gather_three/pallas_call | solution.py:31
  34.1 0.8 collective-permute-start.13
  34.9 1.7 %gather_own.1.refs_8_ = f32[48,640]{1,0:T(8,128)S(1)} custom-call(s32[2,576]{1,0:T(2,128)S(1)} %pad_add_fusion.1.request_ref, bf16[768,1152]{1,0:T(8,128)(2,1)S(1)} %get-tuple-element.82.rows_ref), custom_call_target="tpu_custom_call" | custom-call | tf_op jit(solution)/shard_map/gather_own/pallas_call | solution.py:31
  36.7 3.4 %coagulate_fine.1 = (f32[48,1024]{1,0:T(8,128)S(1)}, f32[48,1024]{1,0:T(8,128)S(1)}, f32[48,1024]{1,0:T(8,128)S(1)}, f32[48,1024]{1,0:T(8,128)S(1)}) custom-call(bf16[48,2304]{1,0:T(8,128)(2,1)S(1)} %copy-done, f32[48,1024]{1,0:T(8,128)S(1)} %get-tuple-element.73.refs_0_, f32[48,1024]{1,0:T(8,128)S(1)} %get-tuple-element.86.refs_1_, ...), custom_call_target="tpu_custom_call" | custom-call | tf_op jit(solution)/shard_map/coagulate_fine/pallas_call | solution.py:31
  40.2 1.8 %first_stage.1 = (f32[48,1024]{1,0:T(8,128)S(1)}, f32[48,1024]{1,0:T(8,128)S(1)}, f32[48,1024]{1,0:T(8,128)S(1)}, f32[48,1024]{1,0:T(8,128)S(1)}, f32[48,1024]{1...) custom-call(s32[1,8]{1,0:T(1,128)S(1)} %copy-done.2, ...), custom_call_target="tpu_custom_call" | custom-call | tf_op jit(solution)/shard_map/first_stage/pallas_call | solution.py:31
  42.0 2.6 %collective-permute-start.17 = (f32[48,640]{1,0:T(8,128)S(1)}, f32[48,640]{1,0:T(8,128)S(1)}, u32[]{:S(2)}, u32[]{:S(2)}) collective-permute-start(f32[48,640]{1,0:T(8,128)S(1)} %get-tuple-element.111.refs_0_), channel_id=1, source_target_pairs={{0,48},{16,0},{32,16},{48,32},{1,49},{17,1},{33,17},{49,33},{2,50}... | collective-permute-start | bytes 368648 | tf_op jit(solution)/shard_map/ppermute | solution.py:357
  44.6 1.0 %collective-permute-start.15 = (f32[48,640]{1,0:T(8,128)S(1)}, f32[48,640]{1,0:T(8,128)S(1)}, u32[]{:S(2)}, u32[]{:S(2)}) collective-permute-start(f32[48,640]{1,0:T(8,128)S(1)} %get-tuple-element.111.refs_0_), channel_id=1, source_target_pairs={{0,16},{16,32},{32,48},{48,0},{1,17},{17,33},{33,49},{49,1},{2,18}... | collective-permute-start | bytes 368648 | tf_op jit(solution)/shard_map/ppermute | solution.py:357
  45.5 0.9 %cells_by_row.1.cell_ref = s32[5120,128]{1,0:T(8,128)S(1)} custom-call(s32[4,576]{1,0:T(4,128)S(1)} %pad_add_fusion.request_a, s32[4,576]{1,0:T(4,128)S(1)} %collective-permute-done.14.request_b), custom_call_target="tpu_custom_call" | custom-call | tf_op jit(solution)/shard_map/cells_by_row/pallas_call | solution.py:31
  46.4 3.4 %coagulate_middle.1 = (f32[48,1024]{1,0:T(8,128)S(1)}, f32[48,1024]{1,0:T(8,128)S(1)}, f32[48,1024]{1,0:T(8,128)S(1)}, f32[48,1024]{1,0:T(8,128)S(1)}) custom-call(bf16[48,2304]{1,0:T(8,128)(2,1)S(1)} %copy-done, f32[48,1024]{1,0:T(8,128)S(1)} %get-tuple-element.120.refs_0_, f32[48,1024]{1,0:T(8,128)S(1)} %get-tuple-element.121.refs_1_, ...), custom_call_target="tpu_custom_call" | custom-call | tf_op jit(solution)/shard_map/coagulate_middle/pallas_call | solution.py:31
  49.9 0.6 collective-permute-done.17.refs_3_
  50.5 1.8 %collective-permute-done.16.refs_2_ = f32[48,640]{1,0:T(8,128)S(1)} collective-permute-done((f32[48,640]{1,0:T(8,128)S(1)}, f32[48,640]{1,0:T(8,128)S(1)}, u32[]{:S(2)}, u32[]{:S(2)}) %collective-permute-start.16) | collective-permute-done | bytes 122912 | tf_op jit(solution)/shard_map/ppermute | solution.py:357
  52.3 1.6 %collective-permute-done.15.refs_1_ = f32[48,640]{1,0:T(8,128)S(1)} collective-permute-done((f32[48,640]{1,0:T(8,128)S(1)}, f32[48,640]{1,0:T(8,128)S(1)}, u32[]{:S(2)}, u32[]{:S(2)}) %collective-permute-start.15) | collective-permute-done | bytes 122912 | tf_op jit(solution)/shard_map/ppermute | solution.py:357
  53.9 0.5 collective-permute-start.20
  54.4 0.8 collective-permute-done.19.refs_5_
  55.2 0.2 collective-permute-done.20.refs_6_
  55.4 0.3 collective-permute-done.21.refs_7_
  55.7 4.0 %scatter_far.1 = (f32[48,1152]{1,0:T(8,128)S(1)}, f32[48,1152]{1,0:T(8,128)S(1)}) custom-call(s32[4,576]{1,0:T(4,128)S(1)} %pad_add_fusion.request_a, s32[4,576]{1,0:T(4,128)S(1)} %collective-permute-done.14.request_b, s32[5120,128]{1,0:T(8,128)S(1)} %cells_by_row.1.cell_ref, f32[48,640]{1,0:T(8,128)S(1)} %get-tuple-element.111.refs_0_, ...), custom_call_target="tpu_custom_call" | custom-call | tf_op jit(solution)/shard_map/scatter_far/pallas_call | solution.py:31
  59.7 1.5 %collective-permute-start.23 = (f32[48,1152]{1,0:T(8,128)S(1)}, f32[48,1152]{1,0:T(8,128)S(1)}, u32[]{:S(2)}, u32[]{:S(2)}) collective-permute-start(f32[48,1152]{1,0:T(8,128)S(1)} %get-tuple-element.115), channel_id=1, source_target_pairs={{0,128},{64,192},{128,0},{192,64},{1,129},{65,193},{129,1},{193,65... | collective-permute-start | bytes 663560 | tf_op jit(solution)/shard_map/ppermute | solution.py:357
  61.2 0.3 collective-permute-start.22
  61.5 4.0 %scatter_near.1 = (f32[48,1152]{1,0:T(8,128)S(1)}, f32[48,1152]{1,0:T(8,128)S(1)}) custom-call(s32[4,576]{1,0:T(4,128)S(1)} %pad_add_fusion.request_a, s32[4,576]{1,0:T(4,128)S(1)} %collective-permute-done.14.request_b, s32[5120,128]{1,0:T(8,128)S(1)} %cells_by_row.1.cell_ref, f32[48,640]{1,0:T(8,128)S(1)} %get-tuple-element.111.refs_0_, ...), custom_call_target="tpu_custom_call" | custom-call | tf_op jit(solution)/shard_map/scatter_near/pallas_call | solution.py:31
  65.5 1.8 %collective-permute-start.24 = (f32[48,1152]{1,0:T(8,128)S(1)}, f32[48,1152]{1,0:T(8,128)S(1)}, u32[]{:S(2)}, u32[]{:S(2)}) collective-permute-start(f32[48,1152]{1,0:T(8,128)S(1)} %get-tuple-element.119), channel_id=1, source_target_pairs={{0,192},{64,0},{128,64},{192,128},{1,193},{65,1},{129,65},{193,129... | collective-permute-start | bytes 663560 | tf_op jit(solution)/shard_map/ppermute | solution.py:357
  67.2 1.6 %collective-permute-done.23.c = f32[48,1152]{1,0:T(8,128)S(1)} collective-permute-done((f32[48,1152]{1,0:T(8,128)S(1)}, f32[48,1152]{1,0:T(8,128)S(1)}, u32[]{:S(2)}, u32[]{:S(2)}) %collective-permute-start.23) | collective-permute-done | bytes 221216 | tf_op jit(solution)/shard_map/ppermute | solution.py:357
  68.8 3.7 %collective-permute-start.26 = (f32[48,1024]{1,0:T(8,128)S(1)}, f32[48,1024]{1,0:T(8,128)S(1)}, u32[]{:S(2)}, u32[]{:S(2)}) collective-permute-start(f32[48,1024]{1,0:T(8,128)S(1)} %get-tuple-element.120.refs_0_), channel_id=1, source_target_pairs={{0,7},{1,0},{2,1},{3,2},{4,3},{5,4},{6,5},{7,6},{8,15},{9,8},{10,9... | collective-permute-start | bytes 589832 | tf_op jit(solution)/shard_map/ppermute | solution.py:357
  72.5 1.0 %coagulate_coarse.1.growth_ref = f32[48,1152]{1,0:T(8,128)S(1)} custom-call(bf16[48,2304]{1,0:T(8,128)(2,1)S(1)} %copy-done, f32[48,1152]{1,0:T(8,128)S(1)} %get-tuple-element.76.refs_0_.coarse_ref), custom_call_target="tpu_custom_call" | custom-call | tf_op jit(solution)/shard_map/coagulate_coarse/pallas_call | solution.py:31
  73.6 2.6 %collective-permute-done.26.refs_17_ = f32[48,1024]{1,0:T(8,128)S(1)} collective-permute-done((f32[48,1024]{1,0:T(8,128)S(1)}, f32[48,1024]{1,0:T(8,128)S(1)}, u32[]{:S(2)}, u32[]{:S(2)}) %collective-permute-start.26) | collective-permute-done | bytes 196640 | tf_op jit(solution)/shard_map/ppermute | solution.py:357
  76.2 3.4 %collective-permute-done.25.refs_16_ = f32[48,1024]{1,0:T(8,128)S(1)} collective-permute-done((f32[48,1024]{1,0:T(8,128)S(1)}, f32[48,1024]{1,0:T(8,128)S(1)}, u32[]{:S(2)}, u32[]{:S(2)}) %collective-permute-start.25) | collective-permute-done | bytes 196640 | tf_op jit(solution)/shard_map/ppermute | solution.py:357
  79.6 2.2 %second_stage.1 = f32[48,4,1024]{2,1,0:T(4,128)} custom-call(s32[1,8]{1,0:T(1,128)S(1)} %copy-done.2, f32[1,48]{1,0:T(1,128)S(1)} %bitcast.8, f32[48,1024]{1,0:T(8,128)S(1)} %get-tuple-element.120.refs_0_, f32[48,1024]{1,0:T(8,128)S(1)} %get-tuple-element.121.refs_1_, f32[48,1024]{1,0:T(8,128)S(1)} %get-tuple-element.122.refs_2_, ...), custom_call_target="tpu_custom_call" | custom-call | tf_op jit(solution)/shard_map/second_stage/pallas_call | solution.py:335
  81.8 0.8 finish_coarse.1
  (30 shorter events, 0.6 us)
Async XLA Ops:
  0.6 6.4 %collective-permute-start.3 = (s32[1,576]{1,0:T(1,128)}, s32[1,576]{1,0:T(1,128)S(1)}, u32[]{:S(2)}, u32[]{:S(2)}) collective-permute-start(s32[1,576]{1,0:T(1,128)} %bitcast.11), channel_id=1, source_target_pairs={{0,16},{16,32},{32,48},{48,0},{1,17},{17,33},{33,49},{49,1},{2,18}... | collective-permute-start | bytes 6920 | tf_op jit(solution)/shard_map/ppermute | solution.py:357
  2.3 20.2 %collective-permute-start.2 = (f32[48,1152]{1,0:T(8,128)}, f32[48,1152]{1,0:T(8,128)S(1)}, u32[]{:S(2)}, u32[]{:S(2)}) collective-permute-start(f32[48,1152]{1,0:T(8,128)} %bitcast.coarse_ref), channel_id=1, source_target_pairs={{0,192},{64,0},{128,64},{192,128},{1,193},{65,1},{129,65},{193,129... | collective-permute-start | bytes 663560 | tf_op jit(solution)/shard_map/ppermute | solution.py:357
  3.1 19.5 %collective-permute-start.1 = (f32[48,1152]{1,0:T(8,128)}, f32[48,1152]{1,0:T(8,128)S(1)}, u32[]{:S(2)}, u32[]{:S(2)}) collective-permute-start(f32[48,1152]{1,0:T(8,128)} %bitcast.coarse_ref), channel_id=1, source_target_pairs={{0,128},{64,192},{128,0},{192,64},{1,129},{65,193},{129,1},{193,65... | collective-permute-start | bytes 663560 | tf_op jit(solution)/shard_map/ppermute | solution.py:357
  5.2 17.3 %collective-permute-start = (f32[48,1152]{1,0:T(8,128)}, f32[48,1152]{1,0:T(8,128)S(1)}, u32[]{:S(2)}, u32[]{:S(2)}) collective-permute-start(f32[48,1152]{1,0:T(8,128)} %bitcast.coarse_ref), channel_id=1, source_target_pairs={{0,64},{64,128},{128,192},{192,0},{1,65},{65,129},{129,193},{193,1... | collective-permute-start | bytes 663560 | tf_op jit(solution)/shard_map/ppermute | solution.py:357
  7.7 7.2 %collective-permute-start.4 = (s32[2,576]{1,0:T(2,128)S(1)}, s32[2,576]{1,0:T(2,128)S(1)}, u32[]{:S(2)}, u32[]{:S(2)}) collective-permute-start(s32[2,576]{1,0:T(2,128)S(1)} %pad_add_fusion.1.request_ref), channel_id=1, source_target_pairs={{0,32},{16,48},{32,0},{48,16},{1,33},{17,49},{33,1},{49,17},{2,34}... | collective-permute-start | bytes 13832 | tf_op jit(solution)/shard_map/ppermute | solution.py:357
  10.7 1.1 %copy-start.1 = (f32[1,1,48,4,1024]{4,3,2,1,0:T(4,128)S(1)}, f32[1,1,48,4,1024]{4,3,2,1,0:T(4,128)}, u32[]{:S(2)}) copy-start(f32[1,1,48,4,1024]{4,3,2,1,0:T(4,128)} %param.6) | copy-start | bytes 2359300
  12.9 9.6 %collective-permute-start.5 = (f32[48,1024]{1,0:T(8,128)S(1)}, f32[48,1024]{1,0:T(8,128)S(1)}, u32[]{:S(2)}, u32[]{:S(2)}) collective-permute-start(f32[48,1024]{1,0:T(8,128)S(1)} %get-tuple-element.72.refs_3_), channel_id=1, source_target_pairs={{0,1},{1,2},{2,3},{3,4},{4,5},{5,6},{6,7},{7,0},{8,9},{9,10},{10,1... | collective-permute-start | bytes 589832 | tf_op jit(solution)/shard_map/ppermute | solution.py:357
  14.9 7.6 %collective-permute-start.6 = (f32[48,1024]{1,0:T(8,128)S(1)}, f32[48,1024]{1,0:T(8,128)S(1)}, u32[]{:S(2)}, u32[]{:S(2)}) collective-permute-start(f32[48,1024]{1,0:T(8,128)S(1)} %get-tuple-element.73.refs_0_), channel_id=1, source_target_pairs={{0,7},{1,0},{2,1},{3,2},{4,3},{5,4},{6,5},{7,6},{8,15},{9,8},{10,9... | collective-permute-start | bytes 589832 | tf_op jit(solution)/shard_map/ppermute | solution.py:357
  22.5 1.7 %collective-permute-start.7 = (f32[48,1152]{1,0:T(8,128)}, f32[48,1152]{1,0:T(8,128)S(1)}, u32[]{:S(2)}, u32[]{:S(2)}) collective-permute-start(f32[48,1152]{1,0:T(8,128)} %bitcast.coarse_ref), channel_id=1, source_target_pairs={{0,8},{8,0},{1,9},{9,1},{2,10},{10,2},{3,11},{11,3},{4,12},{12,4},... | collective-permute-start | bytes 663560 | tf_op jit(solution)/shard_map/ppermute | solution.py:357
  22.6 1.8 %collective-permute-start.8 = (f32[48,1152]{1,0:T(8,128)S(1)}, f32[48,1152]{1,0:T(8,128)S(1)}, u32[]{:S(2)}, u32[]{:S(2)}) collective-permute-start(f32[48,1152]{1,0:T(8,128)S(1)} %collective-permute-done.refs_2_), channel_id=1, source_target_pairs={{0,8},{8,0},{1,9},{9,1},{2,10},{10,2},{3,11},{11,3},{4,12},{12,4},... | collective-permute-start | bytes 663560 | tf_op jit(solution)/shard_map/ppermute | solution.py:357
  23.1 1.5 %collective-permute-start.9 = (f32[48,1152]{1,0:T(8,128)S(1)}, f32[48,1152]{1,0:T(8,128)S(1)}, u32[]{:S(2)}, u32[]{:S(2)}) collective-permute-start(f32[48,1152]{1,0:T(8,128)S(1)} %collective-permute-done.2.refs_4_), channel_id=1, source_target_pairs={{0,8},{8,0},{1,9},{9,1},{2,10},{10,2},{3,11},{11,3},{4,12},{12,4},... | collective-permute-start | bytes 663560 | tf_op jit(solution)/shard_map/ppermute | solution.py:357
  23.2 1.7 %collective-permute-start.10 = (f32[48,1152]{1,0:T(8,128)S(1)}, f32[48,1152]{1,0:T(8,128)S(1)}, u32[]{:S(2)}, u32[]{:S(2)}) collective-permute-start(f32[48,1152]{1,0:T(8,128)S(1)} %collective-permute-done.1.refs_6_), channel_id=1, source_target_pairs={{0,8},{8,0},{1,9},{9,1},{2,10},{10,2},{3,11},{11,3},{4,12},{12,4},... | collective-permute-start | bytes 663560 | tf_op jit(solution)/shard_map/ppermute | solution.py:357
  26.7 8.2 %collective-permute-start.11 = (f32[48,640]{1,0:T(8,128)S(1)}, f32[48,640]{1,0:T(8,128)S(1)}, u32[]{:S(2)}, u32[]{:S(2)}) collective-permute-start(f32[48,640]{1,0:T(8,128)S(1)} %get-tuple-element.80), channel_id=1, source_target_pairs={{0,32},{16,48},{32,0},{48,16},{1,33},{17,49},{33,1},{49,17},{2,34}... | collective-permute-start | bytes 368648 | tf_op jit(solution)/shard_map/ppermute | solution.py:357
  28.9 7.7 %copy-start = (bf16[48,2304]{1,0:T(8,128)(2,1)S(1)}, bf16[48,2304]{1,0:T(8,128)(2,1)}, u32[]{:S(2)}) copy-start(bf16[48,2304]{1,0:T(8,128)(2,1)} %matrix_ref.2) | copy-start | bytes 663556
  30.7 9.5 %copy-start.2 = (s32[1,8]{1,0:T(1,128)S(1)}, s32[1,8]{1,0:T(1,128)}, u32[]{:S(2)}) copy-start(s32[1,8]{1,0:T(1,128)} %levels_ref.3) | copy-start | bytes 100
  30.7 9.5 %copy-start.3 = (f32[48]{0:T(128)S(1)}, f32[48]{0:T(128)}, u32[]{:S(2)}) copy-start(f32[48]{0:T(128)} %param.9) | copy-start | bytes 580
  30.7 6.0 %collective-permute-start.12 = (f32[48,640]{1,0:T(8,128)S(1)}, f32[48,640]{1,0:T(8,128)S(1)}, u32[]{:S(2)}, u32[]{:S(2)}) collective-permute-start(f32[48,640]{1,0:T(8,128)S(1)} %gather_one.1), channel_id=1, source_target_pairs={{0,48},{16,0},{32,16},{48,32},{1,49},{17,1},{33,17},{49,33},{2,50}... | collective-permute-start | bytes 368648 | tf_op jit(solution)/shard_map/ppermute | solution.py:357
  34.1 6.2 %collective-permute-start.13 = (f32[48,640]{1,0:T(8,128)S(1)}, f32[48,640]{1,0:T(8,128)S(1)}, u32[]{:S(2)}, u32[]{:S(2)}) collective-permute-start(f32[48,640]{1,0:T(8,128)S(1)} %gather_three.1), channel_id=1, source_target_pairs={{0,16},{16,32},{32,48},{48,0},{1,17},{17,33},{33,49},{49,1},{2,18}... | collective-permute-start | bytes 368648 | tf_op jit(solution)/shard_map/ppermute | solution.py:357
  34.8 5.3 %collective-permute-start.14 = (s32[4,576]{1,0:T(4,128)S(1)}, s32[4,576]{1,0:T(4,128)S(1)}, u32[]{:S(2)}, u32[]{:S(2)}) collective-permute-start(s32[4,576]{1,0:T(4,128)S(1)} %pad_add_fusion.request_a), channel_id=1, source_target_pairs={{0,8},{8,0},{1,9},{9,1},{2,10},{10,2},{3,11},{11,3},{4,12},{12,4},... | collective-permute-start | bytes 27656 | tf_op jit(solution)/shard_map/ppermute | solution.py:357
  42.0 8.5 %collective-permute-start.17 = (f32[48,640]{1,0:T(8,128)S(1)}, f32[48,640]{1,0:T(8,128)S(1)}, u32[]{:S(2)}, u32[]{:S(2)}) collective-permute-start(f32[48,640]{1,0:T(8,128)S(1)} %get-tuple-element.111.refs_0_), channel_id=1, source_target_pairs={{0,48},{16,0},{32,16},{48,32},{1,49},{17,1},{33,17},{49,33},{2,50}... | collective-permute-start | bytes 368648 | tf_op jit(solution)/shard_map/ppermute | solution.py:357
  44.6 7.7 %collective-permute-start.16 = (f32[48,640]{1,0:T(8,128)S(1)}, f32[48,640]{1,0:T(8,128)S(1)}, u32[]{:S(2)}, u32[]{:S(2)}) collective-permute-start(f32[48,640]{1,0:T(8,128)S(1)} %get-tuple-element.111.refs_0_), channel_id=1, source_target_pairs={{0,32},{16,48},{32,0},{48,16},{1,33},{17,49},{33,1},{49,17},{2,34}... | collective-permute-start | bytes 368648 | tf_op jit(solution)/shard_map/ppermute | solution.py:357
  44.6 9.3 %collective-permute-start.15 = (f32[48,640]{1,0:T(8,128)S(1)}, f32[48,640]{1,0:T(8,128)S(1)}, u32[]{:S(2)}, u32[]{:S(2)}) collective-permute-start(f32[48,640]{1,0:T(8,128)S(1)} %get-tuple-element.111.refs_0_), channel_id=1, source_target_pairs={{0,16},{16,32},{32,48},{48,0},{1,17},{17,33},{33,49},{49,1},{2,18}... | collective-permute-start | bytes 368648 | tf_op jit(solution)/shard_map/ppermute | solution.py:357
  49.8 4.6 %collective-permute-start.18 = (f32[48,640]{1,0:T(8,128)S(1)}, f32[48,640]{1,0:T(8,128)S(1)}, u32[]{:S(2)}, u32[]{:S(2)}) collective-permute-start(f32[48,640]{1,0:T(8,128)S(1)} %get-tuple-element.111.refs_0_), channel_id=1, source_target_pairs={{0,8},{8,0},{1,9},{9,1},{2,10},{10,2},{3,11},{11,3},{4,12},{12,4},... | collective-permute-start | bytes 368648 | tf_op jit(solution)/shard_map/ppermute | solution.py:357
  53.9 1.3 %collective-permute-start.19 = (f32[48,640]{1,0:T(8,128)S(1)}, f32[48,640]{1,0:T(8,128)S(1)}, u32[]{:S(2)}, u32[]{:S(2)}) collective-permute-start(f32[48,640]{1,0:T(8,128)S(1)} %collective-permute-done.15.refs_1_), channel_id=1, source_target_pairs={{0,8},{8,0},{1,9},{9,1},{2,10},{10,2},{3,11},{11,3},{4,12},{12,4},... | collective-permute-start | bytes 368648 | tf_op jit(solution)/shard_map/ppermute | solution.py:357
  53.9 1.5 %collective-permute-start.20 = (f32[48,640]{1,0:T(8,128)S(1)}, f32[48,640]{1,0:T(8,128)S(1)}, u32[]{:S(2)}, u32[]{:S(2)}) collective-permute-start(f32[48,640]{1,0:T(8,128)S(1)} %collective-permute-done.16.refs_2_), channel_id=1, source_target_pairs={{0,8},{8,0},{1,9},{9,1},{2,10},{10,2},{3,11},{11,3},{4,12},{12,4},... | collective-permute-start | bytes 368648 | tf_op jit(solution)/shard_map/ppermute | solution.py:357
  54.4 1.3 %collective-permute-start.21 = (f32[48,640]{1,0:T(8,128)S(1)}, f32[48,640]{1,0:T(8,128)S(1)}, u32[]{:S(2)}, u32[]{:S(2)}) collective-permute-start(f32[48,640]{1,0:T(8,128)S(1)} %collective-permute-done.17.refs_3_), channel_id=1, source_target_pairs={{0,8},{8,0},{1,9},{9,1},{2,10},{10,2},{3,11},{11,3},{4,12},{12,4},... | collective-permute-start | bytes 368648 | tf_op jit(solution)/shard_map/ppermute | solution.py:357
  59.7 9.1 %collective-permute-start.23 = (f32[48,1152]{1,0:T(8,128)S(1)}, f32[48,1152]{1,0:T(8,128)S(1)}, u32[]{:S(2)}, u32[]{:S(2)}) collective-permute-start(f32[48,1152]{1,0:T(8,128)S(1)} %get-tuple-element.115), channel_id=1, source_target_pairs={{0,128},{64,192},{128,0},{192,64},{1,129},{65,193},{129,1},{193,65... | collective-permute-start | bytes 663560 | tf_op jit(solution)/shard_map/ppermute | solution.py:357
  61.2 11.3 %collective-permute-start.22 = (f32[48,1152]{1,0:T(8,128)S(1)}, f32[48,1152]{1,0:T(8,128)S(1)}, u32[]{:S(2)}, u32[]{:S(2)}) collective-permute-start(f32[48,1152]{1,0:T(8,128)S(1)} %get-tuple-element.118), channel_id=1, source_target_pairs={{0,64},{64,128},{128,192},{192,0},{1,65},{65,129},{129,193},{193,1... | collective-permute-start | bytes 663560 | tf_op jit(solution)/shard_map/ppermute | solution.py:357
  65.5 16.3 %collective-permute-start.24 = (f32[48,1152]{1,0:T(8,128)S(1)}, f32[48,1152]{1,0:T(8,128)S(1)}, u32[]{:S(2)}, u32[]{:S(2)}) collective-permute-start(f32[48,1152]{1,0:T(8,128)S(1)} %get-tuple-element.119), channel_id=1, source_target_pairs={{0,192},{64,0},{128,64},{192,128},{1,193},{65,1},{129,65},{193,129... | collective-permute-start | bytes 663560 | tf_op jit(solution)/shard_map/ppermute | solution.py:357
  68.8 7.3 %collective-permute-start.26 = (f32[48,1024]{1,0:T(8,128)S(1)}, f32[48,1024]{1,0:T(8,128)S(1)}, u32[]{:S(2)}, u32[]{:S(2)}) collective-permute-start(f32[48,1024]{1,0:T(8,128)S(1)} %get-tuple-element.120.refs_0_), channel_id=1, source_target_pairs={{0,7},{1,0},{2,1},{3,2},{4,3},{5,4},{6,5},{7,6},{8,15},{9,8},{10,9... | collective-permute-start | bytes 589832 | tf_op jit(solution)/shard_map/ppermute | solution.py:357
  72.5 7.1 %collective-permute-start.25 = (f32[48,1024]{1,0:T(8,128)S(1)}, f32[48,1024]{1,0:T(8,128)S(1)}, u32[]{:S(2)}, u32[]{:S(2)}) collective-permute-start(f32[48,1024]{1,0:T(8,128)S(1)} %get-tuple-element.123.refs_3_), channel_id=1, source_target_pairs={{0,1},{1,2},{2,3},{3,4},{4,5},{5,6},{6,7},{7,0},{8,9},{9,10},{10,1... | collective-permute-start | bytes 589832 | tf_op jit(solution)/shard_map/ppermute | solution.py:357

commit v4 on v3

--- a/solution.py
+++ b/solution.py
@@ -12,6 +12,7 @@
 GHOSTS = 576
 WIDE = 640
 STEP = 0.25
+FOLDED = 1280
 MIB = 1024 * 1024
 COST = pl.CostEstimate(flops=0, bytes_accessed=0, transcendentals=0)
 
@@ -74,7 +75,29 @@
     return outs[:X], outs[X]
 
 
-def coagulate(kernel_matrix, fields, name):
+def fold_kernel(kernel_matrix):
+    pairs = S * S
+
+    def kernel(matrix_ref, out_ref):
+        pair = lax.broadcasted_iota(i32, (pairs, 128), 0)
+        first = (pair * 43691) >> 21
+        second = pair - first * S
+        gap = second - first
+        gap = jnp.where(gap < 0, gap + S, gap)
+        place = jnp.where(gap <= S // 2, gap * S + first, (S - gap) * S + second)
+        lane = lax.broadcasted_iota(i32, (1, 128), 1)
+        for start in range(0, FOLDED, 256):
+            marks = [ones_where(place == lane + (start + t)) for t in (0, 128)]
+            sums = mm(matrix_ref[...], jnp.concatenate(marks, axis=1))
+            high, low = halves(sums)
+            out_ref[:S, start : start + 256] = high
+            out_ref[S:, start : start + 256] = low
+
+    out = jax.ShapeDtypeStruct((2 * S, FOLDED), bf16)
+    return call(kernel, out, [VMEM], kernel_matrix, name="fold_kernel")
+
+
+def coagulate(folded, fields, name):
     count = len(fields)
 
     def kernel(matrix_ref, *refs):
@@ -83,14 +106,20 @@
             for start in range(0, width, 1024):
                 stop = min(start + 1024, width)
                 v = field_ref[:, start:stop]
-                pairs = jnp.concatenate([(v[j : j + 1] * v).astype(bf16) for j in range(S)], axis=0)
-                out_ref[:, start:stop] = mm(matrix_ref[...], pairs)
+                twice = jnp.concatenate([v, v], axis=0)
+                turned = [twice] + [pltpu.roll(twice, 2 * S - b, 0) for b in range(1, 8)]
+                pairs = [
+                    (v * turned[d % 8][d - d % 8 : d - d % 8 + S]).astype(bf16) for d in range(S // 2 + 1)
+                ]
+                pairs.append(jnp.zeros((FOLDED - S * (S // 2 + 1), stop - start), bf16))
+                product = mm(matrix_ref[...], jnp.concatenate(pairs, axis=0))
+                out_ref[:, start:stop] = product[:S] + product[S:]
 
     return call(
         kernel,
         [sds(*f.shape) for f in fields],
         [VMEM] * (count + 1),
-        kernel_matrix,
+        folded,
         *fields,
         name=name,
     )
@@ -373,8 +402,9 @@
     near = jnp.concatenate([request, near], axis=0)
     away = shifted(near, "y", 2)
     planes, held_coarse = split_planes(fine, coarse)
+    folded = fold_kernel(after(coag_kernel, held_coarse))
     below_plane, above_plane = shifted(planes[3], "box", 1), shifted(planes[0], "box", 7)
-    far, near, away, below_plane, above_plane = lax.optimization_barrier((far, near, away, below_plane, above_plane))
+    far, near, away, folded = lax.optimization_barrier((far, near, away, folded))
 
     sources, shifts = [held_coarse, mate], [(0, False), (0, True)]
     for k in (1, 3, 2):
@@ -383,12 +413,13 @@
     part, strips = {}, {}
     part[2], rows = gather_first(away, sources, shifts, 0)
     strips[2] = shifted(part[2], "y", 2)
-    part[1] = gather_next(after(near, part[2]), rows, shifts, 1, "gather_one")
+    below_plane, above_plane, _ = lax.optimization_barrier((below_plane, above_plane, part[2]))
+    part[1] = gather_next(after(near, (part[2], below_plane, above_plane)), rows, shifts, 1, "gather_one")
     strips[1] = shifted(part[1], "y", 3)
     part[3] = gather_next(after(away, part[1]), rows, shifts, 1, "gather_three")
     strips[3] = shifted(part[3], "y", 1)
     strips[0] = gather_next(after(near, (part[3], strips[2])), rows, shifts, 0, "gather_own")
-    growth = coagulate(after(coag_kernel, (strips[0], strips[1])), planes, "coagulate_fine")
+    growth = coagulate(after(folded, (strips[0], strips[1])), planes, "coagulate_fine")
     request_rows = jnp.concatenate([near, away], axis=0)
     mate_rows = shifted(request_rows, "core", 1)
     strips, growth, mate_rows = lax.optimization_barrier((strips, growth, mate_rows))
@@ -401,21 +432,17 @@
     held = {k: shifted(registers, "y", k) for k in (2, 1, 3)}
     held[0] = registers
     cells = cells_by_row([request_rows, after(mate_rows, registers)])
-    growth = coagulate(after(coag_kernel, cells), middle, "coagulate_middle")
+    growth = coagulate(after(folded, cells), middle, "coagulate_middle")
     held = [after(held[k], growth[0]) for k in range(4)]
     held += [shifted(value, "core", 1) for value in held]
-    parts, sent = {}, {}
-    parts[2], parts[1] = scatter_columns([request_rows, mate_rows], cells, held, (2, 1), "scatter_far")
-    for k in (2, 1):
-        sent[k] = shifted(parts[k], "x", k)
-    parts[3], sent[0] = scatter_columns([request_rows, mate_rows], after(cells, parts[2]), held, (3, 0), "scatter_near")
-    sent[3] = shifted(parts[3], "x", 3)
-    middle, _ = lax.optimization_barrier((middle, (parts[3], sent[2])))
+    parts = scatter_columns([request_rows, mate_rows], cells, held, (2, 1, 3, 0), "scatter_columns")
+    sent = [shifted(part, "x", k) for part, k in zip(parts, (2, 1, 3))] + [parts[3]]
+    middle, _ = lax.optimization_barrier((middle, parts[3]))
     below_plane, above_plane = shifted(middle[3], "box", 1), shifted(middle[0], "box", 7)
-    coarse_growth = coagulate(after(coag_kernel, (parts[3], sent[1])), [held_coarse], "coagulate_coarse")[0]
+    coarse_growth = coagulate(after(folded, parts[3]), [held_coarse], "coagulate_coarse")[0]
     fine_out = second_stage(levels, row, middle, base, growth, x_ghosts, y_ghosts, below_plane, above_plane)
     sent, fine_out, coarse_growth = lax.optimization_barrier((sent, fine_out, coarse_growth))
-    coarse_out = finish_coarse(held_coarse, coarse_growth, [sent[k] for k in range(4)])
+    coarse_out = finish_coarse(held_coarse, coarse_growth, sent)
     return fine_out[None, None], coarse_out[None, None]
 
 

time: 82.8 us -> 79.6 us (0.961)
  the two profiles are of different devices: /device:TPU:2 before, /device:TPU:1 now
where the time goes in v4:
time: 79.6 us; the launch traced here: 79.4 us
  starting transfers between devices  33.2 us (42%)
  Pallas kernels  26.6 us (33%)
  waiting for transfers between devices  15 us (19%)
  local copies, waits for them, and re-layouts  3.01 us (4%)
  between operations  0.9 us (1%)
    ppermute x27, starting transfers between devices, shifted(): lax.ppermute(value, axis, [(i, (i + shift) % size) for i in range(size)])  33.2 us
    pallas_call x13, Pallas kernels, call(): pl.pallas_call(kernel, out_shape=out_shape, in_specs=in_specs, out_specs=...  24.3 us
    ppermute x27, waiting for transfers between devices, shifted(): lax.ppermute(value, axis, [(i, (i + shift) % size) for i in range(size)])  15 us
    unnamed x10, local copies, waits for them, and re-layouts  3.01 us
    pallas_call x1, Pallas kernels, second_stage(): pl.pallas_call(kernel, out_shape=sds(S, X, PLANE), in_specs=[SMEM] + [VME...  2.22 us
  transfers between devices with their start and end apart: 27, of which 10 were waited for; matrix products, arithmetic and copies ran while one was open for 1% of the time, Pallas kernels for 22%

profile of v4, /device:TPU:1, one launch (start us, length us, event | category | flops | bytes accessed | tf_op | source)
XLA Modules:
  0.0 79.4 jit_solution(5608966971364025813)
XLA Ops:
  0.6 3.4 %collective-permute-start.2 = (f32[48,1152]{1,0:T(8,128)}, f32[48,1152]{1,0:T(8,128)S(1)}, u32[]{:S(2)}, u32[]{:S(2)}) collective-permute-start(f32[48,1152]{1,0:T(8,128)} %bitcast.7), channel_id=1, source_target_pairs={{0,192},{64,0},{128,64},{192,128},{1,193},{65,1},{129,65},{193,129... | collective-permute-start | bytes 663560 | tf_op jit(solution)/shard_map/ppermute | solution.py:386
  4.0 0.5 collective-permute-start.1
  4.5 0.6 collective-permute-start
  5.1 1.5 %collective-permute-start.5 = (f32[48,1152]{1,0:T(8,128)}, f32[48,1152]{1,0:T(8,128)S(1)}, u32[]{:S(2)}, u32[]{:S(2)}) collective-permute-start(f32[48,1152]{1,0:T(8,128)} %bitcast.10), channel_id=1, source_target_pairs={{0,8},{8,0},{1,9},{9,1},{2,10},{10,2},{3,11},{11,3},{4,12},{12,4},... | collective-permute-start | bytes 663560 | tf_op jit(solution)/shard_map/ppermute | solution.py:386
  6.7 1.3 %collective-permute-start.3 = (s32[1,576]{1,0:T(1,128)}, s32[1,576]{1,0:T(1,128)S(1)}, u32[]{:S(2)}, u32[]{:S(2)}) collective-permute-start(s32[1,576]{1,0:T(1,128)} %bitcast.16), channel_id=1, source_target_pairs={{0,16},{16,32},{32,48},{48,0},{1,17},{17,33},{33,49},{49,1},{2,18}... | collective-permute-start | bytes 6920 | tf_op jit(solution)/shard_map/ppermute | solution.py:386
  8.0 2.9 %collective-permute-done.3 = s32[1,576]{1,0:T(1,128)S(1)} collective-permute-done((s32[1,576]{1,0:T(1,128)}, s32[1,576]{1,0:T(1,128)S(1)}, u32[]{:S(2)}, u32[]{:S(2)}) %collective-permute-start.3) | collective-permute-done | bytes 2336 | tf_op jit(solution)/shard_map/ppermute | solution.py:386
  10.9 0.7 pad_add_fusion.1.request_ref
  11.6 1.7 %collective-permute-start.4 = (s32[2,576]{1,0:T(2,128)S(1)}, s32[2,576]{1,0:T(2,128)S(1)}, u32[]{:S(2)}, u32[]{:S(2)}) collective-permute-start(s32[2,576]{1,0:T(2,128)S(1)} %pad_add_fusion.1.request_ref), channel_id=1, source_target_pairs={{0,32},{16,48},{32,0},{48,16},{1,33},{17,49},{33,1},{49,17},{2,34}... | collective-permute-start | bytes 13832 | tf_op jit(solution)/shard_map/ppermute | solution.py:386
  13.3 1.1 %copy-done = f32[1,1,48,4,1024]{4,3,2,1,0:T(4,128)S(1)} copy-done((f32[1,1,48,4,1024]{4,3,2,1,0:T(4,128)S(1)}, f32[1,1,48,4,1024]{4,3,2,1,0:T(4,128)}, u32[]{:S(2)}) %copy-start) | copy-done | bytes 786456
  14.4 0.9 %copy-done.2 = f32[1,1,48,1152]{3,2,1,0:T(8,128)S(1)} copy-done((f32[1,1,48,1152]{3,2,1,0:T(8,128)S(1)}, f32[1,1,48,1152]{3,2,1,0:T(8,128)}, u32[]{:S(2)}) %copy-start.2) | copy-done | bytes 221208
  15.5 0.9 %copy-done.1 = bf16[48,2304]{1,0:T(8,128)(2,1)S(1)} copy-done((bf16[48,2304]{1,0:T(8,128)(2,1)S(1)}, bf16[48,2304]{1,0:T(8,128)(2,1)}, u32[]{:S(2)}) %copy-start.1) | copy-done | bytes 221208
  16.5 1.8 %fold_kernel.1.matrix_ref = bf16[96,1280]{1,0:T(8,128)(2,1)S(1)} custom-call(bf16[48,2304]{1,0:T(8,128)(2,1)S(1)} %copy-done.1), custom_call_target="tpu_custom_call" | custom-call | tf_op jit(solution)/shard_map/fold_kernel/pallas_call | solution.py:32
  18.3 1.2 %collective-permute-start.6 = (f32[48,1152]{1,0:T(8,128)S(1)}, f32[48,1152]{1,0:T(8,128)S(1)}, u32[]{:S(2)}, u32[]{:S(2)}) collective-permute-start(f32[48,1152]{1,0:T(8,128)S(1)} %collective-permute-done.refs_2_), channel_id=1, source_target_pairs={{0,8},{8,0},{1,9},{9,1},{2,10},{10,2},{3,11},{11,3},{4,12},{12,4},... | collective-permute-start | bytes 663560 | tf_op jit(solution)/shard_map/ppermute | solution.py:386
  19.6 0.4 collective-permute-start.8
  20.0 1.7 %collective-permute-start.9 = (f32[48,1024]{1,0:T(8,128)S(1)}, f32[48,1024]{1,0:T(8,128)S(1)}, u32[]{:S(2)}, u32[]{:S(2)}) collective-permute-start(f32[48,1024]{1,0:T(8,128)S(1)} %get-tuple-element.81.refs_3_), channel_id=1, source_target_pairs={{0,1},{1,2},{2,3},{3,4},{4,5},{5,6},{6,7},{7,0},{8,9},{9,10},{10,1... | collective-permute-start | bytes 589832 | tf_op jit(solution)/shard_map/ppermute | solution.py:386
  21.7 3.9 %collective-permute-start.10 = (f32[48,1024]{1,0:T(8,128)S(1)}, f32[48,1024]{1,0:T(8,128)S(1)}, u32[]{:S(2)}, u32[]{:S(2)}) collective-permute-start(f32[48,1024]{1,0:T(8,128)S(1)} %get-tuple-element.82.refs_0_), channel_id=1, source_target_pairs={{0,7},{1,0},{2,1},{3,2},{4,3},{5,4},{6,5},{7,6},{8,15},{9,8},{10,9... | collective-permute-start | bytes 589832 | tf_op jit(solution)/shard_map/ppermute | solution.py:386
  25.6 1.8 %gather_first.1 = (f32[48,640]{1,0:T(8,128)S(1)}, bf16[768,1152]{1,0:T(8,128)(2,1)S(1)}) custom-call(s32[2,576]{1,0:T(2,128)S(1)} %collective-permute-done.4.request_ref, f32[48,1152]{1,0:T(8,128)S(1)} %get-tuple-element.73.refs_0_.coarse_ref, f32[48,1152]{1,0:T(8,128)S(1)} %collective-permute-done.5.refs_1_, f32[48,1152]{1,0:T(8,128)S(1)} %collective-permute-done.refs_2_, ...), custom_call_target="tpu_custom_call" | custom-call | tf_op jit(solution)/shard_map/gather_first/pallas_call | solution.py:32
  27.4 2.0 %collective-permute-start.11 = (f32[48,640]{1,0:T(8,128)S(1)}, f32[48,640]{1,0:T(8,128)S(1)}, u32[]{:S(2)}, u32[]{:S(2)}) collective-permute-start(f32[48,640]{1,0:T(8,128)S(1)} %get-tuple-element.80), channel_id=1, source_target_pairs={{0,32},{16,48},{32,0},{48,16},{1,33},{17,49},{33,1},{49,17},{2,34}... | collective-permute-start | bytes 368648 | tf_op jit(solution)/shard_map/ppermute | solution.py:386
  29.4 1.4 %collective-permute-done.9.refs_12_ = f32[48,1024]{1,0:T(8,128)S(1)} collective-permute-done((f32[48,1024]{1,0:T(8,128)S(1)}, f32[48,1024]{1,0:T(8,128)S(1)}, u32[]{:S(2)}, u32[]{:S(2)}) %collective-permute-start.9) | collective-permute-done | bytes 196640 | tf_op jit(solution)/shard_map/ppermute | solution.py:386
  30.8 1.7 %gather_one.1 = f32[48,640]{1,0:T(8,128)S(1)} custom-call(s32[2,576]{1,0:T(2,128)S(1)} %pad_add_fusion.1.request_ref, bf16[768,1152]{1,0:T(8,128)(2,1)S(1)} %get-tuple-element.86.rows_ref), custom_call_target="tpu_custom_call" | custom-call | tf_op jit(solution)/shard_map/gather_one/pallas_call | solution.py:32
  32.5 1.7 %collective-permute-start.12 = (f32[48,640]{1,0:T(8,128)S(1)}, f32[48,640]{1,0:T(8,128)S(1)}, u32[]{:S(2)}, u32[]{:S(2)}) collective-permute-start(f32[48,640]{1,0:T(8,128)S(1)} %gather_one.1), channel_id=1, source_target_pairs={{0,48},{16,0},{32,16},{48,32},{1,49},{17,1},{33,17},{49,33},{2,50}... | collective-permute-start | bytes 368648 | tf_op jit(solution)/shard_map/ppermute | solution.py:386
  34.2 1.7 %gather_three.1 = f32[48,640]{1,0:T(8,128)S(1)} custom-call(s32[2,576]{1,0:T(2,128)S(1)} %collective-permute-done.4.request_ref, bf16[768,1152]{1,0:T(8,128)(2,1)S(1)} %get-tuple-element.86.rows_ref), custom_call_target="tpu_custom_call" | custom-call | tf_op jit(solution)/shard_map/gather_three/pallas_call | solution.py:32
  36.1 1.1 %collective-permute-start.14 = (s32[4,576]{1,0:T(4,128)S(1)}, s32[4,576]{1,0:T(4,128)S(1)}, u32[]{:S(2)}, u32[]{:S(2)}) collective-permute-start(s32[4,576]{1,0:T(4,128)S(1)} %pad_add_fusion.request_a), channel_id=1, source_target_pairs={{0,8},{8,0},{1,9},{9,1},{2,10},{10,2},{3,11},{11,3},{4,12},{12,4},... | collective-permute-start | bytes 27656 | tf_op jit(solution)/shard_map/ppermute | solution.py:386
  37.2 1.7 %gather_own.1.refs_8_ = f32[48,640]{1,0:T(8,128)S(1)} custom-call(s32[2,576]{1,0:T(2,128)S(1)} %pad_add_fusion.1.request_ref, bf16[768,1152]{1,0:T(8,128)(2,1)S(1)} %get-tuple-element.86.rows_ref), custom_call_target="tpu_custom_call" | custom-call | tf_op jit(solution)/shard_map/gather_own/pallas_call | solution.py:32
  39.0 2.3 %coagulate_fine.1 = (f32[48,1024]{1,0:T(8,128)S(1)}, f32[48,1024]{1,0:T(8,128)S(1)}, f32[48,1024]{1,0:T(8,128)S(1)}, f32[48,1024]{1,0:T(8,128)S(1)}) custom-call(bf16[96,1280]{1,0:T(8,128)(2,1)S(1)} %fold_kernel.1.matrix_ref, f32[48,1024]{1,0:T(8,128)S(1)} %get-tuple-element.82.refs_0_, f32[48,1024]{1,0:T(8,128)S(1)} %get-tuple-element.91.refs_1_, ...), custom_call_target="tpu_custom_call" | custom-call | tf_op jit(solution)/shard_map/coagulate_fine/pallas_call | solution.py:32
  41.4 1.8 %first_stage.1 = (f32[48,1024]{1,0:T(8,128)S(1)}, f32[48,1024]{1,0:T(8,128)S(1)}, f32[48,1024]{1,0:T(8,128)S(1)}, f32[48,1024]{1,0:T(8,128)S(1)}, f32[48,1024]{1...) custom-call(s32[1,8]{1,0:T(1,128)S(1)} %copy-done.3, ...), custom_call_target="tpu_custom_call" | custom-call | tf_op jit(solution)/shard_map/first_stage/pallas_call | solution.py:32
  43.2 2.8 %collective-permute-start.17 = (f32[48,640]{1,0:T(8,128)S(1)}, f32[48,640]{1,0:T(8,128)S(1)}, u32[]{:S(2)}, u32[]{:S(2)}) collective-permute-start(f32[48,640]{1,0:T(8,128)S(1)} %get-tuple-element.114.refs_0_), channel_id=1, source_target_pairs={{0,48},{16,0},{32,16},{48,32},{1,49},{17,1},{33,17},{49,33},{2,50}... | collective-permute-start | bytes 368648 | tf_op jit(solution)/shard_map/ppermute | solution.py:386
  46.0 0.7 collective-permute-start.15
  46.7 0.9 %cells_by_row.1.cell_ref = s32[5120,128]{1,0:T(8,128)S(1)} custom-call(s32[4,576]{1,0:T(4,128)S(1)} %pad_add_fusion.request_a, s32[4,576]{1,0:T(4,128)S(1)} %collective-permute-done.14.request_b), custom_call_target="tpu_custom_call" | custom-call | tf_op jit(solution)/shard_map/cells_by_row/pallas_call | solution.py:32
  47.5 2.3 %coagulate_middle.1 = (f32[48,1024]{1,0:T(8,128)S(1)}, f32[48,1024]{1,0:T(8,128)S(1)}, f32[48,1024]{1,0:T(8,128)S(1)}, f32[48,1024]{1,0:T(8,128)S(1)}) custom-call(bf16[96,1280]{1,0:T(8,128)(2,1)S(1)} %fold_kernel.1.matrix_ref, f32[48,1024]{1,0:T(8,128)S(1)} %get-tuple-element.122.refs_0_, f32[48,1024]{1,0:T(8,128)S(1)} %get-tuple-element.123.refs_1_, ...), custom_call_target="tpu_custom_call" | custom-call | tf_op jit(solution)/shard_map/coagulate_middle/pallas_call | solution.py:32
  49.9 0.7 collective-permute-start.18
  50.6 0.7 collective-permute-done.17.refs_3_
  51.2 0.9 %collective-permute-done.16.refs_2_ = f32[48,640]{1,0:T(8,128)S(1)} collective-permute-done((f32[48,640]{1,0:T(8,128)S(1)}, f32[48,640]{1,0:T(8,128)S(1)}, u32[]{:S(2)}, u32[]{:S(2)}) %collective-permute-start.16) | collective-permute-done | bytes 122912 | tf_op jit(solution)/shard_map/ppermute | solution.py:386
  52.2 2.7 %collective-permute-done.15.refs_1_ = f32[48,640]{1,0:T(8,128)S(1)} collective-permute-done((f32[48,640]{1,0:T(8,128)S(1)}, f32[48,640]{1,0:T(8,128)S(1)}, u32[]{:S(2)}, u32[]{:S(2)}) %collective-permute-start.15) | collective-permute-done | bytes 122912 | tf_op jit(solution)/shard_map/ppermute | solution.py:386
  54.8 0.8 collective-permute-start.19
  55.6 0.5 collective-permute-start.21
  56.1 0.5 collective-permute-done.19.refs_5_
  56.6 0.4 collective-permute-done.20.refs_6_
  57.1 6.6 %scatter_columns.1 = (f32[48,1152]{1,0:T(8,128)S(1)}, f32[48,1152]{1,0:T(8,128)S(1)}, f32[48,1152]{1,0:T(8,128)S(1)}, f32[48,1152]{1,0:T(8,128)S(1)}) custom-call(s32[4,576]{1,0:T(4,128)S(1)} %pad_add_fusion.request_a, s32[4,576]{1,0:T(4,128)S(1)} %collective-permute-done.14.request_b, s32[5120,128]{1,0:T(8,128)S(1)} %cells_by_row.1.cell_ref, ...), custom_call_target="tpu_custom_call" | custom-call | tf_op jit(solution)/shard_map/scatter_columns/pallas_call | solution.py:32
  63.7 1.1 %collective-permute-start.22 = (f32[48,1152]{1,0:T(8,128)S(1)}, f32[48,1152]{1,0:T(8,128)S(1)}, u32[]{:S(2)}, u32[]{:S(2)}) collective-permute-start(f32[48,1152]{1,0:T(8,128)S(1)} %get-tuple-element.118), channel_id=1, source_target_pairs={{0,128},{64,192},{128,0},{192,64},{1,129},{65,193},{129,1},{193,65... | collective-permute-start | bytes 663560 | tf_op jit(solution)/shard_map/ppermute | solution.py:386
  64.8 1.1 %collective-permute-start.23 = (f32[48,1152]{1,0:T(8,128)S(1)}, f32[48,1152]{1,0:T(8,128)S(1)}, u32[]{:S(2)}, u32[]{:S(2)}) collective-permute-start(f32[48,1152]{1,0:T(8,128)S(1)} %get-tuple-element.119), channel_id=1, source_target_pairs={{0,64},{64,128},{128,192},{192,0},{1,65},{65,129},{129,193},{193,1... | collective-permute-start | bytes 663560 | tf_op jit(solution)/shard_map/ppermute | solution.py:386
  65.9 1.6 %collective-permute-start.24 = (f32[48,1152]{1,0:T(8,128)S(1)}, f32[48,1152]{1,0:T(8,128)S(1)}, u32[]{:S(2)}, u32[]{:S(2)}) collective-permute-start(f32[48,1152]{1,0:T(8,128)S(1)} %get-tuple-element.120), channel_id=1, source_target_pairs={{0,192},{64,0},{128,64},{192,128},{1,193},{65,1},{129,65},{193,129... | collective-permute-start | bytes 663560 | tf_op jit(solution)/shard_map/ppermute | solution.py:386
  67.5 2.7 %collective-permute-start.26 = (f32[48,1024]{1,0:T(8,128)S(1)}, f32[48,1024]{1,0:T(8,128)S(1)}, u32[]{:S(2)}, u32[]{:S(2)}) collective-permute-start(f32[48,1024]{1,0:T(8,128)S(1)} %get-tuple-element.122.refs_0_), channel_id=1, source_target_pairs={{0,7},{1,0},{2,1},{3,2},{4,3},{5,4},{6,5},{7,6},{8,15},{9,8},{10,9... | collective-permute-start | bytes 589832 | tf_op jit(solution)/shard_map/ppermute | solution.py:386
  70.2 0.8 coagulate_coarse.1.growth_ref
  71.0 2.3 %collective-permute-done.26.refs_17_ = f32[48,1024]{1,0:T(8,128)S(1)} collective-permute-done((f32[48,1024]{1,0:T(8,128)S(1)}, f32[48,1024]{1,0:T(8,128)S(1)}, u32[]{:S(2)}, u32[]{:S(2)}) %collective-permute-start.26) | collective-permute-done | bytes 196640 | tf_op jit(solution)/shard_map/ppermute | solution.py:386
  73.2 3.1 %collective-permute-done.25.refs_16_ = f32[48,1024]{1,0:T(8,128)S(1)} collective-permute-done((f32[48,1024]{1,0:T(8,128)S(1)}, f32[48,1024]{1,0:T(8,128)S(1)}, u32[]{:S(2)}, u32[]{:S(2)}) %collective-permute-start.25) | collective-permute-done | bytes 196640 | tf_op jit(solution)/shard_map/ppermute | solution.py:386
  76.3 2.2 %second_stage.1 = f32[48,4,1024]{2,1,0:T(4,128)} custom-call(s32[1,8]{1,0:T(1,128)S(1)} %copy-done.3, f32[1,48]{1,0:T(1,128)S(1)} %bitcast.13, f32[48,1024]{1,0:T(8,128)S(1)} %get-tuple-element.122.refs_0_, f32[48,1024]{1,0:T(8,128)S(1)} %get-tuple-element.123.refs_1_, f32[48,1024]{1,0:T(8,128)S(1)} %get-tuple-element.124.refs_2_, ...), custom_call_target="tpu_custom_call" | custom-call | tf_op jit(solution)/shard_map/second_stage/pallas_call | solution.py:364
  78.6 0.8 finish_coarse.1
  (32 shorter events, 0.6 us)
Async XLA Ops:
  0.6 17.6 %collective-permute-start.2 = (f32[48,1152]{1,0:T(8,128)}, f32[48,1152]{1,0:T(8,128)S(1)}, u32[]{:S(2)}, u32[]{:S(2)}) collective-permute-start(f32[48,1152]{1,0:T(8,128)} %bitcast.7), channel_id=1, source_target_pairs={{0,192},{64,0},{128,64},{192,128},{1,193},{65,1},{129,65},{193,129... | collective-permute-start | bytes 663560 | tf_op jit(solution)/shard_map/ppermute | solution.py:386
  4.0 14.2 %collective-permute-start.1 = (f32[48,1152]{1,0:T(8,128)}, f32[48,1152]{1,0:T(8,128)S(1)}, u32[]{:S(2)}, u32[]{:S(2)}) collective-permute-start(f32[48,1152]{1,0:T(8,128)} %bitcast.8), channel_id=1, source_target_pairs={{0,128},{64,192},{128,0},{192,64},{1,129},{65,193},{129,1},{193,65... | collective-permute-start | bytes 663560 | tf_op jit(solution)/shard_map/ppermute | solution.py:386
  4.5 13.7 %collective-permute-start = (f32[48,1152]{1,0:T(8,128)}, f32[48,1152]{1,0:T(8,128)S(1)}, u32[]{:S(2)}, u32[]{:S(2)}) collective-permute-start(f32[48,1152]{1,0:T(8,128)} %bitcast.9), channel_id=1, source_target_pairs={{0,64},{64,128},{128,192},{192,0},{1,65},{65,129},{129,193},{193,1... | collective-permute-start | bytes 663560 | tf_op jit(solution)/shard_map/ppermute | solution.py:386
  5.1 16.5 %collective-permute-start.5 = (f32[48,1152]{1,0:T(8,128)}, f32[48,1152]{1,0:T(8,128)S(1)}, u32[]{:S(2)}, u32[]{:S(2)}) collective-permute-start(f32[48,1152]{1,0:T(8,128)} %bitcast.10), channel_id=1, source_target_pairs={{0,8},{8,0},{1,9},{9,1},{2,10},{10,2},{3,11},{11,3},{4,12},{12,4},... | collective-permute-start | bytes 663560 | tf_op jit(solution)/shard_map/ppermute | solution.py:386
  6.7 4.2 %collective-permute-start.3 = (s32[1,576]{1,0:T(1,128)}, s32[1,576]{1,0:T(1,128)S(1)}, u32[]{:S(2)}, u32[]{:S(2)}) collective-permute-start(s32[1,576]{1,0:T(1,128)} %bitcast.16), channel_id=1, source_target_pairs={{0,16},{16,32},{32,48},{48,0},{1,17},{17,33},{33,49},{49,1},{2,18}... | collective-permute-start | bytes 6920 | tf_op jit(solution)/shard_map/ppermute | solution.py:386
  11.6 6.7 %collective-permute-start.4 = (s32[2,576]{1,0:T(2,128)S(1)}, s32[2,576]{1,0:T(2,128)S(1)}, u32[]{:S(2)}, u32[]{:S(2)}) collective-permute-start(s32[2,576]{1,0:T(2,128)S(1)} %pad_add_fusion.1.request_ref), channel_id=1, source_target_pairs={{0,32},{16,48},{32,0},{48,16},{1,33},{17,49},{33,1},{49,17},{2,34}... | collective-permute-start | bytes 13832 | tf_op jit(solution)/shard_map/ppermute | solution.py:386
  13.3 1.1 %copy-start = (f32[1,1,48,4,1024]{4,3,2,1,0:T(4,128)S(1)}, f32[1,1,48,4,1024]{4,3,2,1,0:T(4,128)}, u32[]{:S(2)}) copy-start(f32[1,1,48,4,1024]{4,3,2,1,0:T(4,128)} %param.6) | copy-start | bytes 2359300
  14.4 0.9 %copy-start.2 = (f32[1,1,48,1152]{3,2,1,0:T(8,128)S(1)}, f32[1,1,48,1152]{3,2,1,0:T(8,128)}, u32[]{:S(2)}) copy-start(f32[1,1,48,1152]{3,2,1,0:T(8,128)} %param.7) | copy-start | bytes 663556
  15.5 0.9 %copy-start.1 = (bf16[48,2304]{1,0:T(8,128)(2,1)S(1)}, bf16[48,2304]{1,0:T(8,128)(2,1)}, u32[]{:S(2)}) copy-start(bf16[48,2304]{1,0:T(8,128)(2,1)} %matrix_ref) | copy-start | bytes 663556
  18.3 7.3 %collective-permute-start.6 = (f32[48,1152]{1,0:T(8,128)S(1)}, f32[48,1152]{1,0:T(8,128)S(1)}, u32[]{:S(2)}, u32[]{:S(2)}) collective-permute-start(f32[48,1152]{1,0:T(8,128)S(1)} %collective-permute-done.refs_2_), channel_id=1, source_target_pairs={{0,8},{8,0},{1,9},{9,1},{2,10},{10,2},{3,11},{11,3},{4,12},{12,4},... | collective-permute-start | bytes 663560 | tf_op jit(solution)/shard_map/ppermute | solution.py:386
  19.5 6.1 %collective-permute-start.7 = (f32[48,1152]{1,0:T(8,128)S(1)}, f32[48,1152]{1,0:T(8,128)S(1)}, u32[]{:S(2)}, u32[]{:S(2)}) collective-permute-start(f32[48,1152]{1,0:T(8,128)S(1)} %collective-permute-done.2.refs_4_), channel_id=1, source_target_pairs={{0,8},{8,0},{1,9},{9,1},{2,10},{10,2},{3,11},{11,3},{4,12},{12,4},... | collective-permute-start | bytes 663560 | tf_op jit(solution)/shard_map/ppermute | solution.py:386
  19.6 6.0 %collective-permute-start.8 = (f32[48,1152]{1,0:T(8,128)S(1)}, f32[48,1152]{1,0:T(8,128)S(1)}, u32[]{:S(2)}, u32[]{:S(2)}) collective-permute-start(f32[48,1152]{1,0:T(8,128)S(1)} %collective-permute-done.1.refs_6_), channel_id=1, source_target_pairs={{0,8},{8,0},{1,9},{9,1},{2,10},{10,2},{3,11},{11,3},{4,12},{12,4},... | collective-permute-start | bytes 663560 | tf_op jit(solution)/shard_map/ppermute | solution.py:386
  20.0 10.8 %collective-permute-start.9 = (f32[48,1024]{1,0:T(8,128)S(1)}, f32[48,1024]{1,0:T(8,128)S(1)}, u32[]{:S(2)}, u32[]{:S(2)}) collective-permute-start(f32[48,1024]{1,0:T(8,128)S(1)} %get-tuple-element.81.refs_3_), channel_id=1, source_target_pairs={{0,1},{1,2},{2,3},{3,4},{4,5},{5,6},{6,7},{7,0},{8,9},{9,10},{10,1... | collective-permute-start | bytes 589832 | tf_op jit(solution)/shard_map/ppermute | solution.py:386
  21.7 9.1 %collective-permute-start.10 = (f32[48,1024]{1,0:T(8,128)S(1)}, f32[48,1024]{1,0:T(8,128)S(1)}, u32[]{:S(2)}, u32[]{:S(2)}) collective-permute-start(f32[48,1024]{1,0:T(8,128)S(1)} %get-tuple-element.82.refs_0_), channel_id=1, source_target_pairs={{0,7},{1,0},{2,1},{3,2},{4,3},{5,4},{6,5},{7,6},{8,15},{9,8},{10,9... | collective-permute-start | bytes 589832 | tf_op jit(solution)/shard_map/ppermute | solution.py:386
  27.4 9.8 %collective-permute-start.11 = (f32[48,640]{1,0:T(8,128)S(1)}, f32[48,640]{1,0:T(8,128)S(1)}, u32[]{:S(2)}, u32[]{:S(2)}) collective-permute-start(f32[48,640]{1,0:T(8,128)S(1)} %get-tuple-element.80), channel_id=1, source_target_pairs={{0,32},{16,48},{32,0},{48,16},{1,33},{17,49},{33,1},{49,17},{2,34}... | collective-permute-start | bytes 368648 | tf_op jit(solution)/shard_map/ppermute | solution.py:386
  32.5 8.8 %copy-start.3 = (s32[1,8]{1,0:T(1,128)S(1)}, s32[1,8]{1,0:T(1,128)}, u32[]{:S(2)}) copy-start(s32[1,8]{1,0:T(1,128)} %levels_ref.3) | copy-start | bytes 100
  32.5 8.8 %copy-start.4 = (f32[48]{0:T(128)S(1)}, f32[48]{0:T(128)}, u32[]{:S(2)}) copy-start(f32[48]{0:T(128)} %param.9) | copy-start | bytes 580
  32.5 6.4 %collective-permute-start.12 = (f32[48,640]{1,0:T(8,128)S(1)}, f32[48,640]{1,0:T(8,128)S(1)}, u32[]{:S(2)}, u32[]{:S(2)}) collective-permute-start(f32[48,640]{1,0:T(8,128)S(1)} %gather_one.1), channel_id=1, source_target_pairs={{0,48},{16,0},{32,16},{48,32},{1,49},{17,1},{33,17},{49,33},{2,50}... | collective-permute-start | bytes 368648 | tf_op jit(solution)/shard_map/ppermute | solution.py:386
  36.0 5.4 %collective-permute-start.13 = (f32[48,640]{1,0:T(8,128)S(1)}, f32[48,640]{1,0:T(8,128)S(1)}, u32[]{:S(2)}, u32[]{:S(2)}) collective-permute-start(f32[48,640]{1,0:T(8,128)S(1)} %gather_three.1), channel_id=1, source_target_pairs={{0,16},{16,32},{32,48},{48,0},{1,17},{17,33},{33,49},{49,1},{2,18}... | collective-permute-start | bytes 368648 | tf_op jit(solution)/shard_map/ppermute | solution.py:386
  36.1 5.2 %collective-permute-start.14 = (s32[4,576]{1,0:T(4,128)S(1)}, s32[4,576]{1,0:T(4,128)S(1)}, u32[]{:S(2)}, u32[]{:S(2)}) collective-permute-start(s32[4,576]{1,0:T(4,128)S(1)} %pad_add_fusion.request_a), channel_id=1, source_target_pairs={{0,8},{8,0},{1,9},{9,1},{2,10},{10,2},{3,11},{11,3},{4,12},{12,4},... | collective-permute-start | bytes 27656 | tf_op jit(solution)/shard_map/ppermute | solution.py:386
  43.2 8.1 %collective-permute-start.17 = (f32[48,640]{1,0:T(8,128)S(1)}, f32[48,640]{1,0:T(8,128)S(1)}, u32[]{:S(2)}, u32[]{:S(2)}) collective-permute-start(f32[48,640]{1,0:T(8,128)S(1)} %get-tuple-element.114.refs_0_), channel_id=1, source_target_pairs={{0,48},{16,0},{32,16},{48,32},{1,49},{17,1},{33,17},{49,33},{2,50}... | collective-permute-start | bytes 368648 | tf_op jit(solution)/shard_map/ppermute | solution.py:386
  46.0 6.1 %collective-permute-start.16 = (f32[48,640]{1,0:T(8,128)S(1)}, f32[48,640]{1,0:T(8,128)S(1)}, u32[]{:S(2)}, u32[]{:S(2)}) collective-permute-start(f32[48,640]{1,0:T(8,128)S(1)} %get-tuple-element.114.refs_0_), channel_id=1, source_target_pairs={{0,32},{16,48},{32,0},{48,16},{1,33},{17,49},{33,1},{49,17},{2,34}... | collective-permute-start | bytes 368648 | tf_op jit(solution)/shard_map/ppermute | solution.py:386
  46.0 8.8 %collective-permute-start.15 = (f32[48,640]{1,0:T(8,128)S(1)}, f32[48,640]{1,0:T(8,128)S(1)}, u32[]{:S(2)}, u32[]{:S(2)}) collective-permute-start(f32[48,640]{1,0:T(8,128)S(1)} %get-tuple-element.114.refs_0_), channel_id=1, source_target_pairs={{0,16},{16,32},{32,48},{48,0},{1,17},{17,33},{33,49},{49,1},{2,18}... | collective-permute-start | bytes 368648 | tf_op jit(solution)/shard_map/ppermute | solution.py:386
  49.9 6.2 %collective-permute-start.18 = (f32[48,640]{1,0:T(8,128)S(1)}, f32[48,640]{1,0:T(8,128)S(1)}, u32[]{:S(2)}, u32[]{:S(2)}) collective-permute-start(f32[48,640]{1,0:T(8,128)S(1)} %get-tuple-element.114.refs_0_), channel_id=1, source_target_pairs={{0,8},{8,0},{1,9},{9,1},{2,10},{10,2},{3,11},{11,3},{4,12},{12,4},... | collective-permute-start | bytes 368648 | tf_op jit(solution)/shard_map/ppermute | solution.py:386
  54.8 1.7 %collective-permute-start.19 = (f32[48,640]{1,0:T(8,128)S(1)}, f32[48,640]{1,0:T(8,128)S(1)}, u32[]{:S(2)}, u32[]{:S(2)}) collective-permute-start(f32[48,640]{1,0:T(8,128)S(1)} %collective-permute-done.15.refs_1_), channel_id=1, source_target_pairs={{0,8},{8,0},{1,9},{9,1},{2,10},{10,2},{3,11},{11,3},{4,12},{12,4},... | collective-permute-start | bytes 368648 | tf_op jit(solution)/shard_map/ppermute | solution.py:386
  55.6 1.3 %collective-permute-start.20 = (f32[48,640]{1,0:T(8,128)S(1)}, f32[48,640]{1,0:T(8,128)S(1)}, u32[]{:S(2)}, u32[]{:S(2)}) collective-permute-start(f32[48,640]{1,0:T(8,128)S(1)} %collective-permute-done.16.refs_2_), channel_id=1, source_target_pairs={{0,8},{8,0},{1,9},{9,1},{2,10},{10,2},{3,11},{11,3},{4,12},{12,4},... | collective-permute-start | bytes 368648 | tf_op jit(solution)/shard_map/ppermute | solution.py:386
  55.6 1.5 %collective-permute-start.21 = (f32[48,640]{1,0:T(8,128)S(1)}, f32[48,640]{1,0:T(8,128)S(1)}, u32[]{:S(2)}, u32[]{:S(2)}) collective-permute-start(f32[48,640]{1,0:T(8,128)S(1)} %collective-permute-done.17.refs_3_), channel_id=1, source_target_pairs={{0,8},{8,0},{1,9},{9,1},{2,10},{10,2},{3,11},{11,3},{4,12},{12,4},... | collective-permute-start | bytes 368648 | tf_op jit(solution)/shard_map/ppermute | solution.py:386
  63.7 14.8 %collective-permute-start.22 = (f32[48,1152]{1,0:T(8,128)S(1)}, f32[48,1152]{1,0:T(8,128)S(1)}, u32[]{:S(2)}, u32[]{:S(2)}) collective-permute-start(f32[48,1152]{1,0:T(8,128)S(1)} %get-tuple-element.118), channel_id=1, source_target_pairs={{0,128},{64,192},{128,0},{192,64},{1,129},{65,193},{129,1},{193,65... | collective-permute-start | bytes 663560 | tf_op jit(solution)/shard_map/ppermute | solution.py:386
  64.8 13.8 %collective-permute-start.23 = (f32[48,1152]{1,0:T(8,128)S(1)}, f32[48,1152]{1,0:T(8,128)S(1)}, u32[]{:S(2)}, u32[]{:S(2)}) collective-permute-start(f32[48,1152]{1,0:T(8,128)S(1)} %get-tuple-element.119), channel_id=1, source_target_pairs={{0,64},{64,128},{128,192},{192,0},{1,65},{65,129},{129,193},{193,1... | collective-permute-start | bytes 663560 | tf_op jit(solution)/shard_map/ppermute | solution.py:386
  65.9 12.7 %collective-permute-start.24 = (f32[48,1152]{1,0:T(8,128)S(1)}, f32[48,1152]{1,0:T(8,128)S(1)}, u32[]{:S(2)}, u32[]{:S(2)}) collective-permute-start(f32[48,1152]{1,0:T(8,128)S(1)} %get-tuple-element.120), channel_id=1, source_target_pairs={{0,192},{64,0},{128,64},{192,128},{1,193},{65,1},{129,65},{193,129... | collective-permute-start | bytes 663560 | tf_op jit(solution)/shard_map/ppermute | solution.py:386
  67.5 5.7 %collective-permute-start.26 = (f32[48,1024]{1,0:T(8,128)S(1)}, f32[48,1024]{1,0:T(8,128)S(1)}, u32[]{:S(2)}, u32[]{:S(2)}) collective-permute-start(f32[48,1024]{1,0:T(8,128)S(1)} %get-tuple-element.122.refs_0_), channel_id=1, source_target_pairs={{0,7},{1,0},{2,1},{3,2},{4,3},{5,4},{6,5},{7,6},{8,15},{9,8},{10,9... | collective-permute-start | bytes 589832 | tf_op jit(solution)/shard_map/ppermute | solution.py:386
  70.2 6.2 %collective-permute-start.25 = (f32[48,1024]{1,0:T(8,128)S(1)}, f32[48,1024]{1,0:T(8,128)S(1)}, u32[]{:S(2)}, u32[]{:S(2)}) collective-permute-start(f32[48,1024]{1,0:T(8,128)S(1)} %get-tuple-element.125.refs_3_), channel_id=1, source_target_pairs={{0,1},{1,2},{2,3},{3,4},{4,5},{5,6},{6,7},{7,0},{8,9},{9,10},{10,1... | collective-permute-start | bytes 589832 | tf_op jit(solution)/shard_map/ppermute | solution.py:386

commit v5 on v4

--- a/solution.py
+++ b/solution.py
@@ -14,6 +14,8 @@
 STEP = 0.25
 FOLDED = 1280
 MIB = 1024 * 1024
+LIMIT = 52
+SPREAD = 24
 COST = pl.CostEstimate(flops=0, bytes_accessed=0, transcendentals=0)
 
 f32 = jnp.float32
@@ -65,20 +67,18 @@
     return jnp.where(mask, 1.0, 0.0).astype(bf16)
 
 
-def split_planes(fine, coarse):
-    def kernel(fine_ref, coarse_ref, *outs):
-        for x in range(X):
-            outs[x][...] = fine_ref[:, x, :]
-        outs[X][...] = coarse_ref[...]
-
-    outs = call(kernel, [sds(S, PLANE)] * X + [sds(S, CELLS)], [VMEM] * 2, fine, coarse, name="split_planes")
-    return outs[:X], outs[X]
-
-
-def fold_kernel(kernel_matrix):
-    pairs = S * S
-
-    def kernel(matrix_ref, out_ref):
+def prepare(fine, coarse, kernel_matrix):
+    pairs, rows = S * S, 8
+
+    def kernel(fine_ref, coarse_ref, matrix_ref, *refs):
+        planes, coarse_out, folded_ref = refs[:X], refs[X], refs[X + 1]
+        fine_held, matrix_held, sems = refs[X + 2 :]
+        parts = [slice(i * rows, (i + 1) * rows) for i in range(S // rows)]
+        copies = [pltpu.make_async_copy(matrix_ref, matrix_held, sems.at[0])]
+        copies += [pltpu.make_async_copy(fine_ref.at[p], fine_held.at[p], sems.at[2 + i]) for i, p in enumerate(parts)]
+        copies.append(pltpu.make_async_copy(coarse_ref, coarse_out, sems.at[1]))
+        for copy in copies:
+            copy.start()
         pair = lax.broadcasted_iota(i32, (pairs, 128), 0)
         first = (pair * 43691) >> 21
         second = pair - first * S
@@ -86,15 +86,33 @@
         gap = jnp.where(gap < 0, gap + S, gap)
         place = jnp.where(gap <= S // 2, gap * S + first, (S - gap) * S + second)
         lane = lax.broadcasted_iota(i32, (1, 128), 1)
+        copies[0].wait()
         for start in range(0, FOLDED, 256):
             marks = [ones_where(place == lane + (start + t)) for t in (0, 128)]
-            sums = mm(matrix_ref[...], jnp.concatenate(marks, axis=1))
-            high, low = halves(sums)
-            out_ref[:S, start : start + 256] = high
-            out_ref[S:, start : start + 256] = low
-
-    out = jax.ShapeDtypeStruct((2 * S, FOLDED), bf16)
-    return call(kernel, out, [VMEM], kernel_matrix, name="fold_kernel")
+            high, low = halves(mm(matrix_held[...], jnp.concatenate(marks, axis=1)))
+            folded_ref[:S, start : start + 256] = high
+            folded_ref[S:, start : start + 256] = low
+        for part, copy in zip(parts, copies[1:-1]):
+            copy.wait()
+            for x in range(X):
+                planes[x][part] = fine_held[part, x, :]
+        copies[-1].wait()
+
+    outs = pl.pallas_call(
+        kernel,
+        out_shape=[sds(S, PLANE)] * X + [sds(S, CELLS), jax.ShapeDtypeStruct((2 * S, FOLDED), bf16)],
+        in_specs=[pl.BlockSpec(memory_space=pl.ANY)] * 3,
+        out_specs=[VMEM] * (X + 2),
+        scratch_shapes=[
+            pltpu.VMEM((S, X, PLANE), f32),
+            pltpu.VMEM((S, pairs), bf16),
+            pltpu.SemaphoreType.DMA((2 + S // rows,)),
+        ],
+        compiler_params=pltpu.CompilerParams(vmem_limit_bytes=LIMIT * MIB),
+        cost_estimate=COST,
+        name="prepare",
+    )(fine, coarse, kernel_matrix)
+    return outs[:X], outs[X], outs[X + 1]
 
 
 def coagulate(folded, fields, name):
@@ -154,19 +172,26 @@
 def gather_first(requests, sources, shifts, row):
     count = len(sources)
 
-    def kernel(request_ref, *refs):
-        source_refs, (out_ref, rows_ref) = refs[:count], refs[count:]
+    def kernel(*refs):
+        request_refs, source_refs, (out_ref, rows_ref, request_out) = refs[:2], refs[2 : 2 + count], refs[2 + count :]
+        for i in range(4):
+            at = i % 2 * (SPREAD // 2)
+            request_out[i : i + 1, :] = request_refs[i // 2][at : at + 1, :]
         for i, ref in enumerate(source_refs):
             high, low = halves(ref[...])
             rows_ref[2 * S * i : 2 * S * i + S] = high
             rows_ref[2 * S * i + S : 2 * S * (i + 1)] = low
-        out_ref[...] = pick(rows_ref[...], request_ref[row : row + 1, :], shifts)
+        out_ref[...] = pick(rows_ref[...], request_out[row : row + 1, :], shifts)
 
     return call(
         kernel,
-        [sds(S, WIDE), jax.ShapeDtypeStruct((2 * S * count, CELLS), bf16)],
-        [VMEM] * (1 + count),
-        requests,
+        [
+            sds(S, WIDE),
+            jax.ShapeDtypeStruct((2 * S * count, CELLS), bf16),
+            jax.ShapeDtypeStruct((4, GHOSTS), i32),
+        ],
+        [VMEM] * (2 + count),
+        *requests,
         *sources,
         name="gather_first",
     )
@@ -396,31 +421,30 @@
     row = diffusion.reshape(1, S)
     request = ghost_src[0]
 
-    near = shifted(request, "y", 1)
     far = {k: shifted(coarse, "x", k) for k in (2, 1, 3)}
+    spread = jnp.broadcast_to(request, (SPREAD, GHOSTS))
+    near = shifted(spread, "y", 1)
     mate = shifted(coarse, "core", 1)
-    near = jnp.concatenate([request, near], axis=0)
-    away = shifted(near, "y", 2)
-    planes, held_coarse = split_planes(fine, coarse)
-    folded = fold_kernel(after(coag_kernel, held_coarse))
+    planes, held_coarse, folded = prepare(fine, coarse, coag_kernel)
     below_plane, above_plane = shifted(planes[3], "box", 1), shifted(planes[0], "box", 7)
-    far, near, away, folded = lax.optimization_barrier((far, near, away, folded))
+    near, held_coarse = lax.optimization_barrier((near, held_coarse))
+    requests = jnp.concatenate([spread[: SPREAD // 2], near[: SPREAD // 2]], axis=0)
+    far, requests = lax.optimization_barrier((far, requests))
+    requests = [requests, shifted(requests, "y", 2)]
 
     sources, shifts = [held_coarse, mate], [(0, False), (0, True)]
     for k in (1, 3, 2):
         sources += [far[k], shifted(far[k], "core", 1)]
         shifts += [(k, False), (k, True)]
     part, strips = {}, {}
-    part[2], rows = gather_first(away, sources, shifts, 0)
+    part[2], rows, request_rows = gather_first(requests, sources, shifts, 2)
     strips[2] = shifted(part[2], "y", 2)
-    below_plane, above_plane, _ = lax.optimization_barrier((below_plane, above_plane, part[2]))
-    part[1] = gather_next(after(near, (part[2], below_plane, above_plane)), rows, shifts, 1, "gather_one")
+    part[1] = gather_next(request_rows, rows, shifts, 1, "gather_one")
     strips[1] = shifted(part[1], "y", 3)
-    part[3] = gather_next(after(away, part[1]), rows, shifts, 1, "gather_three")
+    part[3] = gather_next(after(request_rows, part[1]), rows, shifts, 3, "gather_three")
     strips[3] = shifted(part[3], "y", 1)
-    strips[0] = gather_next(after(near, (part[3], strips[2])), rows, shifts, 0, "gather_own")
-    growth = coagulate(after(folded, (strips[0], strips[1])), planes, "coagulate_fine")
-    request_rows = jnp.concatenate([near, away], axis=0)
+    strips[0] = gather_next(after(request_rows, (part[3], strips[2])), rows, shifts, 0, "gather_own")
+    growth = coagulate(after(folded, (strips[0], strips[1], below_plane, above_plane)), planes, "coagulate_fine")
     mate_rows = shifted(request_rows, "core", 1)
     strips, growth, mate_rows = lax.optimization_barrier((strips, growth, mate_rows))
     strips = [strips[k] for k in range(4)]
@@ -432,13 +456,12 @@
     held = {k: shifted(registers, "y", k) for k in (2, 1, 3)}
     held[0] = registers
     cells = cells_by_row([request_rows, after(mate_rows, registers)])
+    below_plane, above_plane = shifted(middle[3], "box", 1), shifted(middle[0], "box", 7)
     growth = coagulate(after(folded, cells), middle, "coagulate_middle")
     held = [after(held[k], growth[0]) for k in range(4)]
     held += [shifted(value, "core", 1) for value in held]
-    parts = scatter_columns([request_rows, mate_rows], cells, held, (2, 1, 3, 0), "scatter_columns")
+    parts = scatter_columns([request_rows, mate_rows], after(cells, (below_plane, above_plane)), held, (2, 1, 3, 0), "scatter_columns")
     sent = [shifted(part, "x", k) for part, k in zip(parts, (2, 1, 3))] + [parts[3]]
-    middle, _ = lax.optimization_barrier((middle, parts[3]))
-    below_plane, above_plane = shifted(middle[3], "box", 1), shifted(middle[0], "box", 7)
     coarse_growth = coagulate(after(folded, parts[3]), [held_coarse], "coagulate_coarse")[0]
     fine_out = second_stage(levels, row, middle, base, growth, x_ghosts, y_ghosts, below_plane, above_plane)
     sent, fine_out, coarse_growth = lax.optimization_barrier((sent, fine_out, coarse_growth))

time: 79.6 us -> 82.2 us (1.033)
  starting transfers between devices: 33.2 us -> 36.4 us
  local copies, waits for them, and re-layouts: 3.01 us -> 1.9 us
  Pallas kernels: 26.6 us -> 27.6 us
    ppermute x27, starting transfers between devices: 33.2 us -> 36.4 us  [shifted(): lax.ppermute(value, axis, [(i, (i + shift) % size) for i in range(size)])]
    pallas_call x0 -> x1, Pallas kernels: none -> 2.93 us  [prepare(): pl.pallas_call(kernel, out_shape=[sds(S, PLANE)] * X + [sds(S, CELLS), ja...]
    pallas_call x13 -> x11, Pallas kernels: 24.3 us -> 22.5 us  [call(): pl.pallas_call(kernel, out_shape=out_shape, in_specs=in_specs, out_specs=...]
    unnamed x10 -> x8, local copies, waits for them, and re-layouts: 3.01 us -> 1.88 us
  transfers between devices with their start and end apart: 27 -> 27, of which waited for: 10 -> 8; matrix products, arithmetic and copies ran while one was open for 1% -> 1% of each run, Pallas kernels for 22% -> 23%
where the time goes in v5:
time: 82.2 us; the launch traced here: 82 us
  starting transfers between devices  36.4 us (44%)
  Pallas kernels  27.6 us (34%)
  waiting for transfers between devices  14.5 us (18%)
  local copies, waits for them, and re-layouts  1.9 us (2%)
  between operations  0.91 us (1%)
    ppermute x27, starting transfers between devices, shifted(): lax.ppermute(value, axis, [(i, (i + shift) % size) for i in range(size)])  36.4 us
    pallas_call x11, Pallas kernels, call(): pl.pallas_call(kernel, out_shape=out_shape, in_specs=in_specs, out_specs=...  22.5 us
    ppermute x27, waiting for transfers between devices, shifted(): lax.ppermute(value, axis, [(i, (i + shift) % size) for i in range(size)])  14.5 us
    pallas_call x1, Pallas kernels, prepare(): pl.pallas_call(kernel, out_shape=[sds(S, PLANE)] * X + [sds(S, CELLS), ja...  2.93 us
    pallas_call x1, Pallas kernels, second_stage(): pl.pallas_call(kernel, out_shape=sds(S, X, PLANE), in_specs=[SMEM] + [VME...  2.21 us
    unnamed x8, local copies, waits for them, and re-layouts  1.88 us
  transfers between devices with their start and end apart: 27, of which 8 were waited for; matrix products, arithmetic and copies ran while one was open for 1% of the time, Pallas kernels for 23%

profile of v5, /device:TPU:1, one launch (start us, length us, event | category | flops | bytes accessed | tf_op | source)
XLA Modules:
  0.0 82.0 jit_solution(3298942185731065994)
XLA Ops:
  0.6 3.4 %collective-permute-start.2 = (f32[48,1152]{1,0:T(8,128)}, f32[48,1152]{1,0:T(8,128)S(1)}, u32[]{:S(2)}, u32[]{:S(2)}) collective-permute-start(f32[48,1152]{1,0:T(8,128)} %bitcast.5), channel_id=1, source_target_pairs={{0,192},{64,0},{128,64},{192,128},{1,193},{65,1},{129,65},{193,129... | collective-permute-start | bytes 663560 | tf_op jit(solution)/shard_map/ppermute | solution.py:411
  4.0 0.5 collective-permute-start.1
  4.5 0.6 collective-permute-start
  5.1 0.7 reduce
  5.9 1.4 %collective-permute-start.3 = (s32[24,576]{1,0:T(8,128)S(1)}, s32[24,576]{1,0:T(8,128)S(1)}, u32[]{:S(2)}, u32[]{:S(2)}) collective-permute-start(s32[24,576]{1,0:T(8,128)S(1)} %broadcast_in_dim.14), channel_id=1, source_target_pairs={{0,16},{16,32},{32,48},{48,0},{1,17},{17,33},{33,49},{49,1},{2,18}... | collective-permute-start | bytes 165896 | tf_op jit(solution)/shard_map/ppermute | solution.py:411
  7.2 1.8 %collective-permute-start.5 = (f32[48,1152]{1,0:T(8,128)}, f32[48,1152]{1,0:T(8,128)S(1)}, u32[]{:S(2)}, u32[]{:S(2)}) collective-permute-start(f32[48,1152]{1,0:T(8,128)} %bitcast.8), channel_id=1, source_target_pairs={{0,8},{8,0},{1,9},{9,1},{2,10},{10,2},{3,11},{11,3},{4,12},{12,4},... | collective-permute-start | bytes 663560 | tf_op jit(solution)/shard_map/ppermute | solution.py:411
  9.0 0.9 %copy-done = bf16[48,2304]{1,0:T(8,128)(2,1)S(1)} copy-done((bf16[48,2304]{1,0:T(8,128)(2,1)S(1)}, bf16[48,2304]{1,0:T(8,128)(2,1)}, u32[]{:S(2)}) %copy-start) | copy-done | bytes 221208
  10.0 0.9 %copy-done.1 = f32[1,1,48,1152]{3,2,1,0:T(8,128)S(1)} copy-done((f32[1,1,48,1152]{3,2,1,0:T(8,128)S(1)}, f32[1,1,48,1152]{3,2,1,0:T(8,128)}, u32[]{:S(2)}) %copy-start.1) | copy-done | bytes 221208
  10.9 2.9 %prepare.1 = (f32[48,1024]{1,0:T(8,128)S(1)}, f32[48,1024]{1,0:T(8,128)S(1)}, f32[48,1024]{1,0:T(8,128)S(1)}, f32[48,1024]{1,0:T(8,128)S(1)}, f32[48,1152]{1,0:T(8,128)S(1)}, /*index=5*/bf16[96,1280]{1,0:T(8,128)(2,1)S(1)}) custom-call(f32[48,4,1024]{2,1,0:T(4,128)} %bitcast.12, f32[48,1152]{1,0:T(8,128)S(1)} %bitcast.9, bf16[48,2304]{1,0:T(8,128)(2,1)S(1)} %copy-done), custom_call_target="tpu_custom_call" | custom-call | tf_op jit(solution)/shard_map/prepare/pallas_call | solution.py:101
  13.9 3.9 %collective-permute-done.refs_4_ = f32[48,1152]{1,0:T(8,128)S(1)} collective-permute-done((f32[48,1152]{1,0:T(8,128)}, f32[48,1152]{1,0:T(8,128)S(1)}, u32[]{:S(2)}, u32[]{:S(2)}) %collective-permute-start) | collective-permute-done | bytes 221216 | tf_op jit(solution)/shard_map/ppermute | solution.py:411
  17.8 0.5 collective-permute-start.6
  18.3 0.5 collective-permute-start.8
  18.8 2.9 %collective-permute-start.4 = (s32[24,576]{1,0:T(8,128)S(1)}, s32[24,576]{1,0:T(8,128)S(1)}, u32[]{:S(2)}, u32[]{:S(2)}) collective-permute-start(s32[24,576]{1,0:T(8,128)S(1)} %pad_add_fusion.refs_0_), channel_id=1, source_target_pairs={{0,32},{16,48},{32,0},{48,16},{1,33},{17,49},{33,1},{49,17},{2,34}... | collective-permute-start | bytes 165896 | tf_op jit(solution)/shard_map/ppermute | solution.py:411
  21.7 1.6 %collective-permute-start.12 = (f32[48,1024]{1,0:T(8,128)S(1)}, f32[48,1024]{1,0:T(8,128)S(1)}, u32[]{:S(2)}, u32[]{:S(2)}) collective-permute-start(f32[48,1024]{1,0:T(8,128)S(1)} %get-tuple-element.81.refs_3_), channel_id=1, source_target_pairs={{0,1},{1,2},{2,3},{3,4},{4,5},{5,6},{6,7},{7,0},{8,9},{9,10},{10,1... | collective-permute-start | bytes 589832 | tf_op jit(solution)/shard_map/ppermute | solution.py:411
  23.4 0.6 collective-permute-done.4.refs_1_
  24.0 5.6 %collective-permute-start.13 = (f32[48,1024]{1,0:T(8,128)S(1)}, f32[48,1024]{1,0:T(8,128)S(1)}, u32[]{:S(2)}, u32[]{:S(2)}) collective-permute-start(f32[48,1024]{1,0:T(8,128)S(1)} %get-tuple-element.82.refs_0_), channel_id=1, source_target_pairs={{0,7},{1,0},{2,1},{3,2},{4,3},{5,4},{6,5},{7,6},{8,15},{9,8},{10,9... | collective-permute-start | bytes 589832 | tf_op jit(solution)/shard_map/ppermute | solution.py:411
  29.5 1.8 %gather_first.1 = (f32[48,640]{1,0:T(8,128)S(1)}, bf16[768,1152]{1,0:T(8,128)(2,1)S(1)}, s32[4,576]{1,0:T(4,128)S(1)}) custom-call(s32[24,576]{1,0:T(8,128)S(1)} %pad_add_fusion.refs_0_, s32[24,576]{1,0:T(8,128)S(1)} %collective-permute-done.4.refs_1_, f32[48,1152]{1,0:T(8,128)S(1)} %get-tuple-element.71.refs_2_.refs_0_.coarse_ref, ...), custom_call_target="tpu_custom_call" | custom-call | tf_op jit(solution)/shard_map/gather_first/pallas_call | solution.py:34
  31.3 3.2 %collective-permute-start.9 = (f32[48,640]{1,0:T(8,128)S(1)}, f32[48,640]{1,0:T(8,128)S(1)}, u32[]{:S(2)}, u32[]{:S(2)}) collective-permute-start(f32[48,640]{1,0:T(8,128)S(1)} %get-tuple-element.78), channel_id=1, source_target_pairs={{0,32},{16,48},{32,0},{48,16},{1,33},{17,49},{33,1},{49,17},{2,34}... | collective-permute-start | bytes 368648 | tf_op jit(solution)/shard_map/ppermute | solution.py:411
  34.5 1.7 %gather_one.1 = f32[48,640]{1,0:T(8,128)S(1)} custom-call(s32[4,576]{1,0:T(4,128)S(1)} %get-tuple-element.79.request_ref.request_a, bf16[768,1152]{1,0:T(8,128)(2,1)S(1)} %get-tuple-element.76.rows_ref), custom_call_target="tpu_custom_call" | custom-call | tf_op jit(solution)/shard_map/gather_one/pallas_call | solution.py:34
  36.3 0.9 %collective-permute-start.10 = (f32[48,640]{1,0:T(8,128)S(1)}, f32[48,640]{1,0:T(8,128)S(1)}, u32[]{:S(2)}, u32[]{:S(2)}) collective-permute-start(f32[48,640]{1,0:T(8,128)S(1)} %gather_one.1), channel_id=1, source_target_pairs={{0,48},{16,0},{32,16},{48,32},{1,49},{17,1},{33,17},{49,33},{2,50}... | collective-permute-start | bytes 368648 | tf_op jit(solution)/shard_map/ppermute | solution.py:411
  37.1 1.7 %gather_three.1 = f32[48,640]{1,0:T(8,128)S(1)} custom-call(s32[4,576]{1,0:T(4,128)S(1)} %get-tuple-element.79.request_ref.request_a, bf16[768,1152]{1,0:T(8,128)(2,1)S(1)} %get-tuple-element.76.rows_ref), custom_call_target="tpu_custom_call" | custom-call | tf_op jit(solution)/shard_map/gather_three/pallas_call | solution.py:34
  38.9 0.8 collective-permute-start.11
  39.6 1.9 %collective-permute-start.14 = (s32[4,576]{1,0:T(4,128)S(1)}, s32[4,576]{1,0:T(4,128)S(1)}, u32[]{:S(2)}, u32[]{:S(2)}) collective-permute-start(s32[4,576]{1,0:T(4,128)S(1)} %get-tuple-element.79.request_ref.request_a), channel_id=1, source_target_pairs={{0,8},{8,0},{1,9},{9,1},{2,10},{10,2},{3,11},{11,3},{4,12},{12,4},... | collective-permute-start | bytes 27656 | tf_op jit(solution)/shard_map/ppermute | solution.py:411
  41.5 1.7 %gather_own.1.refs_8_ = f32[48,640]{1,0:T(8,128)S(1)} custom-call(s32[4,576]{1,0:T(4,128)S(1)} %get-tuple-element.79.request_ref.request_a, bf16[768,1152]{1,0:T(8,128)(2,1)S(1)} %get-tuple-element.76.rows_ref), custom_call_target="tpu_custom_call" | custom-call | tf_op jit(solution)/shard_map/gather_own/pallas_call | solution.py:34
  43.3 2.3 %coagulate_fine.1 = (f32[48,1024]{1,0:T(8,128)S(1)}, f32[48,1024]{1,0:T(8,128)S(1)}, f32[48,1024]{1,0:T(8,128)S(1)}, f32[48,1024]{1,0:T(8,128)S(1)}) custom-call(bf16[96,1280]{1,0:T(8,128)(2,1)S(1)} %get-tuple-element.127.matrix_ref, f32[48,1024]{1,0:T(8,128)S(1)} %get-tuple-element.82.refs_0_, f32[48,1024]{1,0:T(8,128)S(1)} %get-tuple-element.84.refs_1_, ...), custom_call_target="tpu_custom_call" | custom-call | tf_op jit(solution)/shard_map/coagulate_fine/pallas_call | solution.py:34
  45.7 1.8 %first_stage.1 = (f32[48,1024]{1,0:T(8,128)S(1)}, f32[48,1024]{1,0:T(8,128)S(1)}, f32[48,1024]{1,0:T(8,128)S(1)}, f32[48,1024]{1,0:T(8,128)S(1)}, f32[48,1024]{1...) custom-call(s32[1,8]{1,0:T(1,128)S(1)} %copy-done.2, ...), custom_call_target="tpu_custom_call" | custom-call | tf_op jit(solution)/shard_map/first_stage/pallas_call | solution.py:34
  47.6 2.1 %collective-permute-start.19 = (f32[48,640]{1,0:T(8,128)S(1)}, f32[48,640]{1,0:T(8,128)S(1)}, u32[]{:S(2)}, u32[]{:S(2)}) collective-permute-start(f32[48,640]{1,0:T(8,128)S(1)} %get-tuple-element.108.refs_0_), channel_id=1, source_target_pairs={{0,48},{16,0},{32,16},{48,32},{1,49},{17,1},{33,17},{49,33},{2,50}... | collective-permute-start | bytes 368648 | tf_op jit(solution)/shard_map/ppermute | solution.py:411
  49.7 0.2 collective-permute-start.18
  49.9 0.5 collective-permute-start.17
  50.3 2.5 %collective-permute-start.16 = (f32[48,1024]{1,0:T(8,128)S(1)}, f32[48,1024]{1,0:T(8,128)S(1)}, u32[]{:S(2)}, u32[]{:S(2)}) collective-permute-start(f32[48,1024]{1,0:T(8,128)S(1)} %get-tuple-element.102.refs_0_), channel_id=1, source_target_pairs={{0,7},{1,0},{2,1},{3,2},{4,3},{5,4},{6,5},{7,6},{8,15},{9,8},{10,9... | collective-permute-start | bytes 589832 | tf_op jit(solution)/shard_map/ppermute | solution.py:411
  52.8 0.9 %cells_by_row.1.cell_ref = s32[5120,128]{1,0:T(8,128)S(1)} custom-call(s32[4,576]{1,0:T(4,128)S(1)} %get-tuple-element.79.request_ref.request_a, s32[4,576]{1,0:T(4,128)S(1)} %collective-permute-done.14.request_b), custom_call_target="tpu_custom_call" | custom-call | tf_op jit(solution)/shard_map/cells_by_row/pallas_call | solution.py:34
  53.7 2.4 %coagulate_middle.1 = (f32[48,1024]{1,0:T(8,128)S(1)}, f32[48,1024]{1,0:T(8,128)S(1)}, f32[48,1024]{1,0:T(8,128)S(1)}, f32[48,1024]{1,0:T(8,128)S(1)}) custom-call(bf16[96,1280]{1,0:T(8,128)(2,1)S(1)} %get-tuple-element.127.matrix_ref, f32[48,1024]{1,0:T(8,128)S(1)} %get-tuple-element.102.refs_0_, f32[48,1024]{1,0:T(8,128)S(1)} %get-tuple-element.105.refs_1_, ...), custom_call_target="tpu_custom_call" | custom-call | tf_op jit(solution)/shard_map/coagulate_middle/pallas_call | solution.py:34
  56.1 1.2 %collective-permute-start.20 = (f32[48,640]{1,0:T(8,128)S(1)}, f32[48,640]{1,0:T(8,128)S(1)}, u32[]{:S(2)}, u32[]{:S(2)}) collective-permute-start(f32[48,640]{1,0:T(8,128)S(1)} %get-tuple-element.108.refs_0_), channel_id=1, source_target_pairs={{0,8},{8,0},{1,9},{9,1},{2,10},{10,2},{3,11},{11,3},{4,12},{12,4},... | collective-permute-start | bytes 368648 | tf_op jit(solution)/shard_map/ppermute | solution.py:411
  57.3 1.5 %collective-permute-done.17.refs_1_ = f32[48,640]{1,0:T(8,128)S(1)} collective-permute-done((f32[48,640]{1,0:T(8,128)S(1)}, f32[48,640]{1,0:T(8,128)S(1)}, u32[]{:S(2)}, u32[]{:S(2)}) %collective-permute-start.17) | collective-permute-done | bytes 122912 | tf_op jit(solution)/shard_map/ppermute | solution.py:411
  58.8 0.6 collective-permute-start.21
  59.4 0.5 collective-permute-start.23
  60.0 0.5 collective-permute-done.21.refs_5_
  60.4 0.4 collective-permute-done.22.refs_6_
  60.8 0.2 collective-permute-done.23.refs_7_
  60.9 6.6 %scatter_columns.1 = (f32[48,1152]{1,0:T(8,128)S(1)}, f32[48,1152]{1,0:T(8,128)S(1)}, f32[48,1152]{1,0:T(8,128)S(1)}, f32[48,1152]{1,0:T(8,128)S(1)}) custom-call(s32[4,576]{1,0:T(4,128)S(1)} %get-tuple-element.79.request_ref.request_a, s32[4,576]{1,0:T(4,128)S(1)} %collective-permute-done.14.request_b, s32[5120,128]{1,0:T(8,128)S(1)} %cells_by_row.1.cell_ref, ...), custom_call_target="tpu_custom_call" | custom-call | tf_op jit(solution)/shard_map/scatter_columns/pallas_call | solution.py:34
  67.6 0.6 collective-permute-start.24
  68.2 0.4 collective-permute-start.25
  68.6 2.3 %collective-permute-start.26 = (f32[48,1152]{1,0:T(8,128)S(1)}, f32[48,1152]{1,0:T(8,128)S(1)}, u32[]{:S(2)}, u32[]{:S(2)}) collective-permute-start(f32[48,1152]{1,0:T(8,128)S(1)} %get-tuple-element.114), channel_id=1, source_target_pairs={{0,192},{64,0},{128,64},{192,128},{1,193},{65,1},{129,65},{193,129... | collective-permute-start | bytes 663560 | tf_op jit(solution)/shard_map/ppermute | solution.py:411
  70.9 2.2 %second_stage.1 = f32[48,4,1024]{2,1,0:T(4,128)} custom-call(s32[1,8]{1,0:T(1,128)S(1)} %copy-done.2, f32[1,48]{1,0:T(1,128)S(1)} %bitcast.11, f32[48,1024]{1,0:T(8,128)S(1)} %get-tuple-element.102.refs_0_, f32[48,1024]{1,0:T(8,128)S(1)} %get-tuple-element.105.refs_1_, f32[48,1024]{1,0:T(8,128)S(1)} %get-tuple-element.106.refs_2_, ...), custom_call_target="tpu_custom_call" | custom-call | tf_op jit(solution)/shard_map/second_stage/pallas_call | solution.py:389
  73.1 0.7 coagulate_coarse.1.growth_ref
  73.8 2.1 %collective-permute-done.24.a = f32[48,1152]{1,0:T(8,128)S(1)} collective-permute-done((f32[48,1152]{1,0:T(8,128)S(1)}, f32[48,1152]{1,0:T(8,128)S(1)}, u32[]{:S(2)}, u32[]{:S(2)}) %collective-permute-start.24) | collective-permute-done | bytes 221216 | tf_op jit(solution)/shard_map/ppermute | solution.py:411
  75.9 5.4 %collective-permute-done.25.b = f32[48,1152]{1,0:T(8,128)S(1)} collective-permute-done((f32[48,1152]{1,0:T(8,128)S(1)}, f32[48,1152]{1,0:T(8,128)S(1)}, u32[]{:S(2)}, u32[]{:S(2)}) %collective-permute-start.25) | collective-permute-done | bytes 221216 | tf_op jit(solution)/shard_map/ppermute | solution.py:411
  81.3 0.8 finish_coarse.1
  (32 shorter events, 0.2 us)
Async XLA Ops:
  0.6 13.3 %collective-permute-start.2 = (f32[48,1152]{1,0:T(8,128)}, f32[48,1152]{1,0:T(8,128)S(1)}, u32[]{:S(2)}, u32[]{:S(2)}) collective-permute-start(f32[48,1152]{1,0:T(8,128)} %bitcast.5), channel_id=1, source_target_pairs={{0,192},{64,0},{128,64},{192,128},{1,193},{65,1},{129,65},{193,129... | collective-permute-start | bytes 663560 | tf_op jit(solution)/shard_map/ppermute | solution.py:411
  4.0 9.9 %collective-permute-start.1 = (f32[48,1152]{1,0:T(8,128)}, f32[48,1152]{1,0:T(8,128)S(1)}, u32[]{:S(2)}, u32[]{:S(2)}) collective-permute-start(f32[48,1152]{1,0:T(8,128)} %bitcast.6), channel_id=1, source_target_pairs={{0,128},{64,192},{128,0},{192,64},{1,129},{65,193},{129,1},{193,65... | collective-permute-start | bytes 663560 | tf_op jit(solution)/shard_map/ppermute | solution.py:411
  4.5 13.3 %collective-permute-start = (f32[48,1152]{1,0:T(8,128)}, f32[48,1152]{1,0:T(8,128)S(1)}, u32[]{:S(2)}, u32[]{:S(2)}) collective-permute-start(f32[48,1152]{1,0:T(8,128)} %bitcast.7), channel_id=1, source_target_pairs={{0,64},{64,128},{128,192},{192,0},{1,65},{65,129},{129,193},{193,1... | collective-permute-start | bytes 663560 | tf_op jit(solution)/shard_map/ppermute | solution.py:411
  5.9 8.0 %collective-permute-start.3 = (s32[24,576]{1,0:T(8,128)S(1)}, s32[24,576]{1,0:T(8,128)S(1)}, u32[]{:S(2)}, u32[]{:S(2)}) collective-permute-start(s32[24,576]{1,0:T(8,128)S(1)} %broadcast_in_dim.14), channel_id=1, source_target_pairs={{0,16},{16,32},{32,48},{48,0},{1,17},{17,33},{33,49},{49,1},{2,18}... | collective-permute-start | bytes 165896 | tf_op jit(solution)/shard_map/ppermute | solution.py:411
  7.2 14.5 %collective-permute-start.5 = (f32[48,1152]{1,0:T(8,128)}, f32[48,1152]{1,0:T(8,128)S(1)}, u32[]{:S(2)}, u32[]{:S(2)}) collective-permute-start(f32[48,1152]{1,0:T(8,128)} %bitcast.8), channel_id=1, source_target_pairs={{0,8},{8,0},{1,9},{9,1},{2,10},{10,2},{3,11},{11,3},{4,12},{12,4},... | collective-permute-start | bytes 663560 | tf_op jit(solution)/shard_map/ppermute | solution.py:411
  9.0 0.9 %copy-start = (bf16[48,2304]{1,0:T(8,128)(2,1)S(1)}, bf16[48,2304]{1,0:T(8,128)(2,1)}, u32[]{:S(2)}) copy-start(bf16[48,2304]{1,0:T(8,128)(2,1)} %matrix_ref.1) | copy-start | bytes 663556
  10.0 0.9 %copy-start.1 = (f32[1,1,48,1152]{3,2,1,0:T(8,128)S(1)}, f32[1,1,48,1152]{3,2,1,0:T(8,128)}, u32[]{:S(2)}) copy-start(f32[1,1,48,1152]{3,2,1,0:T(8,128)} %param.7) | copy-start | bytes 663556
  17.8 11.7 %collective-permute-start.6 = (f32[48,1152]{1,0:T(8,128)S(1)}, f32[48,1152]{1,0:T(8,128)S(1)}, u32[]{:S(2)}, u32[]{:S(2)}) collective-permute-start(f32[48,1152]{1,0:T(8,128)S(1)} %collective-permute-done.refs_4_), channel_id=1, source_target_pairs={{0,8},{8,0},{1,9},{9,1},{2,10},{10,2},{3,11},{11,3},{4,12},{12,4},... | collective-permute-start | bytes 663560 | tf_op jit(solution)/shard_map/ppermute | solution.py:411
  18.3 11.2 %collective-permute-start.7 = (f32[48,1152]{1,0:T(8,128)S(1)}, f32[48,1152]{1,0:T(8,128)S(1)}, u32[]{:S(2)}, u32[]{:S(2)}) collective-permute-start(f32[48,1152]{1,0:T(8,128)S(1)} %collective-permute-done.2.refs_6_), channel_id=1, source_target_pairs={{0,8},{8,0},{1,9},{9,1},{2,10},{10,2},{3,11},{11,3},{4,12},{12,4},... | collective-permute-start | bytes 663560 | tf_op jit(solution)/shard_map/ppermute | solution.py:411
  18.3 11.2 %collective-permute-start.8 = (f32[48,1152]{1,0:T(8,128)S(1)}, f32[48,1152]{1,0:T(8,128)S(1)}, u32[]{:S(2)}, u32[]{:S(2)}) collective-permute-start(f32[48,1152]{1,0:T(8,128)S(1)} %collective-permute-done.1.refs_8_), channel_id=1, source_target_pairs={{0,8},{8,0},{1,9},{9,1},{2,10},{10,2},{3,11},{11,3},{4,12},{12,4},... | collective-permute-start | bytes 663560 | tf_op jit(solution)/shard_map/ppermute | solution.py:411
  18.8 5.1 %collective-permute-start.4 = (s32[24,576]{1,0:T(8,128)S(1)}, s32[24,576]{1,0:T(8,128)S(1)}, u32[]{:S(2)}, u32[]{:S(2)}) collective-permute-start(s32[24,576]{1,0:T(8,128)S(1)} %pad_add_fusion.refs_0_), channel_id=1, source_target_pairs={{0,32},{16,48},{32,0},{48,16},{1,33},{17,49},{33,1},{49,17},{2,34}... | collective-permute-start | bytes 165896 | tf_op jit(solution)/shard_map/ppermute | solution.py:411
  21.7 21.5 %collective-permute-start.12 = (f32[48,1024]{1,0:T(8,128)S(1)}, f32[48,1024]{1,0:T(8,128)S(1)}, u32[]{:S(2)}, u32[]{:S(2)}) collective-permute-start(f32[48,1024]{1,0:T(8,128)S(1)} %get-tuple-element.81.refs_3_), channel_id=1, source_target_pairs={{0,1},{1,2},{2,3},{3,4},{4,5},{5,6},{6,7},{7,0},{8,9},{9,10},{10,1... | collective-permute-start | bytes 589832 | tf_op jit(solution)/shard_map/ppermute | solution.py:411
  24.0 19.3 %collective-permute-start.13 = (f32[48,1024]{1,0:T(8,128)S(1)}, f32[48,1024]{1,0:T(8,128)S(1)}, u32[]{:S(2)}, u32[]{:S(2)}) collective-permute-start(f32[48,1024]{1,0:T(8,128)S(1)} %get-tuple-element.82.refs_0_), channel_id=1, source_target_pairs={{0,7},{1,0},{2,1},{3,2},{4,3},{5,4},{6,5},{7,6},{8,15},{9,8},{10,9... | collective-permute-start | bytes 589832 | tf_op jit(solution)/shard_map/ppermute | solution.py:411
  31.3 8.3 %collective-permute-start.9 = (f32[48,640]{1,0:T(8,128)S(1)}, f32[48,640]{1,0:T(8,128)S(1)}, u32[]{:S(2)}, u32[]{:S(2)}) collective-permute-start(f32[48,640]{1,0:T(8,128)S(1)} %get-tuple-element.78), channel_id=1, source_target_pairs={{0,32},{16,48},{32,0},{48,16},{1,33},{17,49},{33,1},{49,17},{2,34}... | collective-permute-start | bytes 368648 | tf_op jit(solution)/shard_map/ppermute | solution.py:411
  36.2 9.4 %copy-start.2 = (s32[1,8]{1,0:T(1,128)S(1)}, s32[1,8]{1,0:T(1,128)}, u32[]{:S(2)}) copy-start(s32[1,8]{1,0:T(1,128)} %levels_ref.3) | copy-start | bytes 100
  36.3 9.4 %copy-start.3 = (f32[48]{0:T(128)S(1)}, f32[48]{0:T(128)}, u32[]{:S(2)}) copy-start(f32[48]{0:T(128)} %param.9) | copy-start | bytes 580
  36.3 7.0 %collective-permute-start.10 = (f32[48,640]{1,0:T(8,128)S(1)}, f32[48,640]{1,0:T(8,128)S(1)}, u32[]{:S(2)}, u32[]{:S(2)}) collective-permute-start(f32[48,640]{1,0:T(8,128)S(1)} %gather_one.1), channel_id=1, source_target_pairs={{0,48},{16,0},{32,16},{48,32},{1,49},{17,1},{33,17},{49,33},{2,50}... | collective-permute-start | bytes 368648 | tf_op jit(solution)/shard_map/ppermute | solution.py:411
  38.9 6.8 %collective-permute-start.11 = (f32[48,640]{1,0:T(8,128)S(1)}, f32[48,640]{1,0:T(8,128)S(1)}, u32[]{:S(2)}, u32[]{:S(2)}) collective-permute-start(f32[48,640]{1,0:T(8,128)S(1)} %gather_three.1), channel_id=1, source_target_pairs={{0,16},{16,32},{32,48},{48,0},{1,17},{17,33},{33,49},{49,1},{2,18}... | collective-permute-start | bytes 368648 | tf_op jit(solution)/shard_map/ppermute | solution.py:411
  39.6 6.0 %collective-permute-start.14 = (s32[4,576]{1,0:T(4,128)S(1)}, s32[4,576]{1,0:T(4,128)S(1)}, u32[]{:S(2)}, u32[]{:S(2)}) collective-permute-start(s32[4,576]{1,0:T(4,128)S(1)} %get-tuple-element.79.request_ref.request_a), channel_id=1, source_target_pairs={{0,8},{8,0},{1,9},{9,1},{2,10},{10,2},{3,11},{11,3},{4,12},{12,4},... | collective-permute-start | bytes 27656 | tf_op jit(solution)/shard_map/ppermute | solution.py:411
  47.5 11.9 %collective-permute-start.15 = (f32[48,1024]{1,0:T(8,128)S(1)}, f32[48,1024]{1,0:T(8,128)S(1)}, u32[]{:S(2)}, u32[]{:S(2)}) collective-permute-start(f32[48,1024]{1,0:T(8,128)S(1)} %get-tuple-element.101.refs_3_), channel_id=1, source_target_pairs={{0,1},{1,2},{2,3},{3,4},{4,5},{5,6},{6,7},{7,0},{8,9},{9,10},{10,1... | collective-permute-start | bytes 589832 | tf_op jit(solution)/shard_map/ppermute | solution.py:411
  47.6 8.5 %collective-permute-start.19 = (f32[48,640]{1,0:T(8,128)S(1)}, f32[48,640]{1,0:T(8,128)S(1)}, u32[]{:S(2)}, u32[]{:S(2)}) collective-permute-start(f32[48,640]{1,0:T(8,128)S(1)} %get-tuple-element.108.refs_0_), channel_id=1, source_target_pairs={{0,48},{16,0},{32,16},{48,32},{1,49},{17,1},{33,17},{49,33},{2,50}... | collective-permute-start | bytes 368648 | tf_op jit(solution)/shard_map/ppermute | solution.py:411
  49.7 7.7 %collective-permute-start.18 = (f32[48,640]{1,0:T(8,128)S(1)}, f32[48,640]{1,0:T(8,128)S(1)}, u32[]{:S(2)}, u32[]{:S(2)}) collective-permute-start(f32[48,640]{1,0:T(8,128)S(1)} %get-tuple-element.108.refs_0_), channel_id=1, source_target_pairs={{0,32},{16,48},{32,0},{48,16},{1,33},{17,49},{33,1},{49,17},{2,34}... | collective-permute-start | bytes 368648 | tf_op jit(solution)/shard_map/ppermute | solution.py:411
  49.9 9.0 %collective-permute-start.17 = (f32[48,640]{1,0:T(8,128)S(1)}, f32[48,640]{1,0:T(8,128)S(1)}, u32[]{:S(2)}, u32[]{:S(2)}) collective-permute-start(f32[48,640]{1,0:T(8,128)S(1)} %get-tuple-element.108.refs_0_), channel_id=1, source_target_pairs={{0,16},{16,32},{32,48},{48,0},{1,17},{17,33},{33,49},{49,1},{2,18}... | collective-permute-start | bytes 368648 | tf_op jit(solution)/shard_map/ppermute | solution.py:411
  50.3 9.6 %collective-permute-start.16 = (f32[48,1024]{1,0:T(8,128)S(1)}, f32[48,1024]{1,0:T(8,128)S(1)}, u32[]{:S(2)}, u32[]{:S(2)}) collective-permute-start(f32[48,1024]{1,0:T(8,128)S(1)} %get-tuple-element.102.refs_0_), channel_id=1, source_target_pairs={{0,7},{1,0},{2,1},{3,2},{4,3},{5,4},{6,5},{7,6},{8,15},{9,8},{10,9... | collective-permute-start | bytes 589832 | tf_op jit(solution)/shard_map/ppermute | solution.py:411
  56.1 3.8 %collective-permute-start.20 = (f32[48,640]{1,0:T(8,128)S(1)}, f32[48,640]{1,0:T(8,128)S(1)}, u32[]{:S(2)}, u32[]{:S(2)}) collective-permute-start(f32[48,640]{1,0:T(8,128)S(1)} %get-tuple-element.108.refs_0_), channel_id=1, source_target_pairs={{0,8},{8,0},{1,9},{9,1},{2,10},{10,2},{3,11},{11,3},{4,12},{12,4},... | collective-permute-start | bytes 368648 | tf_op jit(solution)/shard_map/ppermute | solution.py:411
  58.8 1.6 %collective-permute-start.21 = (f32[48,640]{1,0:T(8,128)S(1)}, f32[48,640]{1,0:T(8,128)S(1)}, u32[]{:S(2)}, u32[]{:S(2)}) collective-permute-start(f32[48,640]{1,0:T(8,128)S(1)} %collective-permute-done.17.refs_1_), channel_id=1, source_target_pairs={{0,8},{8,0},{1,9},{9,1},{2,10},{10,2},{3,11},{11,3},{4,12},{12,4},... | collective-permute-start | bytes 368648 | tf_op jit(solution)/shard_map/ppermute | solution.py:411
  59.4 1.3 %collective-permute-start.22 = (f32[48,640]{1,0:T(8,128)S(1)}, f32[48,640]{1,0:T(8,128)S(1)}, u32[]{:S(2)}, u32[]{:S(2)}) collective-permute-start(f32[48,640]{1,0:T(8,128)S(1)} %collective-permute-done.18.refs_2_), channel_id=1, source_target_pairs={{0,8},{8,0},{1,9},{9,1},{2,10},{10,2},{3,11},{11,3},{4,12},{12,4},... | collective-permute-start | bytes 368648 | tf_op jit(solution)/shard_map/ppermute | solution.py:411
  59.4 1.5 %collective-permute-start.23 = (f32[48,640]{1,0:T(8,128)S(1)}, f32[48,640]{1,0:T(8,128)S(1)}, u32[]{:S(2)}, u32[]{:S(2)}) collective-permute-start(f32[48,640]{1,0:T(8,128)S(1)} %collective-permute-done.19.refs_3_), channel_id=1, source_target_pairs={{0,8},{8,0},{1,9},{9,1},{2,10},{10,2},{3,11},{11,3},{4,12},{12,4},... | collective-permute-start | bytes 368648 | tf_op jit(solution)/shard_map/ppermute | solution.py:411
  67.6 8.3 %collective-permute-start.24 = (f32[48,1152]{1,0:T(8,128)S(1)}, f32[48,1152]{1,0:T(8,128)S(1)}, u32[]{:S(2)}, u32[]{:S(2)}) collective-permute-start(f32[48,1152]{1,0:T(8,128)S(1)} %get-tuple-element.112), channel_id=1, source_target_pairs={{0,128},{64,192},{128,0},{192,64},{1,129},{65,193},{129,1},{193,65... | collective-permute-start | bytes 663560 | tf_op jit(solution)/shard_map/ppermute | solution.py:411
  68.2 13.1 %collective-permute-start.25 = (f32[48,1152]{1,0:T(8,128)S(1)}, f32[48,1152]{1,0:T(8,128)S(1)}, u32[]{:S(2)}, u32[]{:S(2)}) collective-permute-start(f32[48,1152]{1,0:T(8,128)S(1)} %get-tuple-element.113), channel_id=1, source_target_pairs={{0,64},{64,128},{128,192},{192,0},{1,65},{65,129},{129,193},{193,1... | collective-permute-start | bytes 663560 | tf_op jit(solution)/shard_map/ppermute | solution.py:411
  68.6 12.7 %collective-permute-start.26 = (f32[48,1152]{1,0:T(8,128)S(1)}, f32[48,1152]{1,0:T(8,128)S(1)}, u32[]{:S(2)}, u32[]{:S(2)}) collective-permute-start(f32[48,1152]{1,0:T(8,128)S(1)} %get-tuple-element.114), channel_id=1, source_target_pairs={{0,192},{64,0},{128,64},{192,128},{1,193},{65,1},{129,65},{193,129... | collective-permute-start | bytes 663560 | tf_op jit(solution)/shard_map/ppermute | solution.py:411

commit v6 on v5

--- a/solution.py
+++ b/solution.py
@@ -67,18 +67,10 @@
     return jnp.where(mask, 1.0, 0.0).astype(bf16)
 
 
-def prepare(fine, coarse, kernel_matrix):
-    pairs, rows = S * S, 8
-
-    def kernel(fine_ref, coarse_ref, matrix_ref, *refs):
-        planes, coarse_out, folded_ref = refs[:X], refs[X], refs[X + 1]
-        fine_held, matrix_held, sems = refs[X + 2 :]
-        parts = [slice(i * rows, (i + 1) * rows) for i in range(S // rows)]
-        copies = [pltpu.make_async_copy(matrix_ref, matrix_held, sems.at[0])]
-        copies += [pltpu.make_async_copy(fine_ref.at[p], fine_held.at[p], sems.at[2 + i]) for i, p in enumerate(parts)]
-        copies.append(pltpu.make_async_copy(coarse_ref, coarse_out, sems.at[1]))
-        for copy in copies:
-            copy.start()
+def fold_kernel(kernel_matrix):
+    pairs = S * S
+
+    def kernel(matrix_ref, folded_ref):
         pair = lax.broadcasted_iota(i32, (pairs, 128), 0)
         first = (pair * 43691) >> 21
         second = pair - first * S
@@ -86,13 +78,27 @@
         gap = jnp.where(gap < 0, gap + S, gap)
         place = jnp.where(gap <= S // 2, gap * S + first, (S - gap) * S + second)
         lane = lax.broadcasted_iota(i32, (1, 128), 1)
-        copies[0].wait()
         for start in range(0, FOLDED, 256):
             marks = [ones_where(place == lane + (start + t)) for t in (0, 128)]
-            high, low = halves(mm(matrix_held[...], jnp.concatenate(marks, axis=1)))
+            high, low = halves(mm(matrix_ref[...], jnp.concatenate(marks, axis=1)))
             folded_ref[:S, start : start + 256] = high
             folded_ref[S:, start : start + 256] = low
-        for part, copy in zip(parts, copies[1:-1]):
+
+    out = jax.ShapeDtypeStruct((2 * S, FOLDED), bf16)
+    return call(kernel, out, [VMEM], kernel_matrix, name="fold_kernel")
+
+
+def split_planes(fine, coarse):
+    rows = 8
+
+    def kernel(fine_ref, coarse_ref, *refs):
+        planes, coarse_out, fine_held, sems = refs[:X], refs[X], refs[X + 1], refs[X + 2]
+        parts = [slice(i * rows, (i + 1) * rows) for i in range(S // rows)]
+        copies = [pltpu.make_async_copy(fine_ref.at[p], fine_held.at[p], sems.at[i]) for i, p in enumerate(parts)]
+        copies.append(pltpu.make_async_copy(coarse_ref, coarse_out, sems.at[len(parts)]))
+        for copy in copies:
+            copy.start()
+        for part, copy in zip(parts, copies):
             copy.wait()
             for x in range(X):
                 planes[x][part] = fine_held[part, x, :]
@@ -100,19 +106,15 @@
 
     outs = pl.pallas_call(
         kernel,
-        out_shape=[sds(S, PLANE)] * X + [sds(S, CELLS), jax.ShapeDtypeStruct((2 * S, FOLDED), bf16)],
-        in_specs=[pl.BlockSpec(memory_space=pl.ANY)] * 3,
-        out_specs=[VMEM] * (X + 2),
-        scratch_shapes=[
-            pltpu.VMEM((S, X, PLANE), f32),
-            pltpu.VMEM((S, pairs), bf16),
-            pltpu.SemaphoreType.DMA((2 + S // rows,)),
-        ],
+        out_shape=[sds(S, PLANE)] * X + [sds(S, CELLS)],
+        in_specs=[pl.BlockSpec(memory_space=pl.ANY)] * 2,
+        out_specs=[VMEM] * (X + 1),
+        scratch_shapes=[pltpu.VMEM((S, X, PLANE), f32), pltpu.SemaphoreType.DMA((1 + S // rows,))],
         compiler_params=pltpu.CompilerParams(vmem_limit_bytes=LIMIT * MIB),
         cost_estimate=COST,
-        name="prepare",
-    )(fine, coarse, kernel_matrix)
-    return outs[:X], outs[X], outs[X + 1]
+        name="split_planes",
+    )(fine, coarse)
+    return outs[:X], outs[X]
 
 
 def coagulate(folded, fields, name):
@@ -422,15 +424,16 @@
     request = ghost_src[0]
 
     far = {k: shifted(coarse, "x", k) for k in (2, 1, 3)}
-    spread = jnp.broadcast_to(request, (SPREAD, GHOSTS))
+    spread = request + jnp.zeros((SPREAD, 1), i32)
     near = shifted(spread, "y", 1)
     mate = shifted(coarse, "core", 1)
-    planes, held_coarse, folded = prepare(fine, coarse, coag_kernel)
+    folded = fold_kernel(coag_kernel)
+    near, folded = lax.optimization_barrier((near, folded))
+    requests = jnp.concatenate([spread[: SPREAD // 2], near[: SPREAD // 2]], axis=0)
+    requests = [requests, shifted(requests, "y", 2)]
+    planes, held_coarse = split_planes(fine, after(coarse, (folded, requests[0])))
     below_plane, above_plane = shifted(planes[3], "box", 1), shifted(planes[0], "box", 7)
-    near, held_coarse = lax.optimization_barrier((near, held_coarse))
-    requests = jnp.concatenate([spread[: SPREAD // 2], near[: SPREAD // 2]], axis=0)
-    far, requests = lax.optimization_barrier((far, requests))
-    requests = [requests, shifted(requests, "y", 2)]
+    far, requests, held_coarse = lax.optimization_barrier((far, requests, held_coarse))
 
     sources, shifts = [held_coarse, mate], [(0, False), (0, True)]
     for k in (1, 3, 2):
@@ -460,10 +463,16 @@
     growth = coagulate(after(folded, cells), middle, "coagulate_middle")
     held = [after(held[k], growth[0]) for k in range(4)]
     held += [shifted(value, "core", 1) for value in held]
-    parts = scatter_columns([request_rows, mate_rows], after(cells, (below_plane, above_plane)), held, (2, 1, 3, 0), "scatter_columns")
-    sent = [shifted(part, "x", k) for part, k in zip(parts, (2, 1, 3))] + [parts[3]]
-    coarse_growth = coagulate(after(folded, parts[3]), [held_coarse], "coagulate_coarse")[0]
+    cells = after(cells, (below_plane, above_plane))
+    sent = {}
+    both = scatter_columns([request_rows, mate_rows], cells, held, (2, 1), "scatter_far")
+    sent[2], sent[1] = shifted(both[0], "x", 2), shifted(both[1], "x", 1)
+    both = scatter_columns([request_rows, mate_rows], after(cells, both[0]), held, (3, 0), "scatter_near")
+    sent[3], sent[0] = shifted(both[0], "x", 3), both[1]
+    base = after(base, (both[0], sent[1], sent[2]))
     fine_out = second_stage(levels, row, middle, base, growth, x_ghosts, y_ghosts, below_plane, above_plane)
+    coarse_growth = coagulate(after(folded, fine_out), [held_coarse], "coagulate_coarse")[0]
+    sent = [sent[k] for k in range(4)]
     sent, fine_out, coarse_growth = lax.optimization_barrier((sent, fine_out, coarse_growth))
     coarse_out = finish_coarse(held_coarse, coarse_growth, sent)
     return fine_out[None, None], coarse_out[None, None]

time: 82.2 us -> 77.7 us (0.945)
  waiting for transfers between devices: 14.5 us -> 9.96 us
  starting transfers between devices: 36.4 us -> 33.6 us
  Pallas kernels: 27.6 us -> 29.3 us
  local copies, waits for them, and re-layouts: 1.9 us -> 3.03 us
    ppermute x27, waiting for transfers between devices: 14.5 us -> 9.96 us  [shifted(): lax.ppermute(value, axis, [(i, (i + shift) % size) for i in range(size)])]
    pallas_call x11 -> x13, Pallas kernels: 22.5 us -> 25.6 us  [call(): pl.pallas_call(kernel, out_shape=out_shape, in_specs=in_specs, out_specs=...]
    ppermute x27, starting transfers between devices: 36.4 us -> 33.6 us  [shifted(): lax.ppermute(value, axis, [(i, (i + shift) % size) for i in range(size)])]
    pallas_call x1, Pallas kernels: 2.93 us -> 1.49 us  [split_planes(): pl.pallas_call(kernel, out_shape=[sds(S, PLANE)] * X + [sds(S, CELLS)], i...]
    unnamed x8 -> x10, local copies, waits for them, and re-layouts: 1.88 us -> 3.02 us
  transfers between devices with their start and end apart: 27 -> 27, of which waited for: 8 -> 6; matrix products, arithmetic and copies ran while one was open for 1% -> 0% of each run, Pallas kernels for 23% -> 29%
where the time goes in v6:
time: 77.7 us; the launch traced here: 77.4 us
  starting transfers between devices  33.6 us (43%)
  Pallas kernels  29.3 us (38%)
  waiting for transfers between devices  9.96 us (13%)
  local copies, waits for them, and re-layouts  3.03 us (4%)
  between operations  0.93 us (1%)
    ppermute x27, starting transfers between devices, shifted(): lax.ppermute(value, axis, [(i, (i + shift) % size) for i in range(size)])  33.6 us
    pallas_call x13, Pallas kernels, call(): pl.pallas_call(kernel, out_shape=out_shape, in_specs=in_specs, out_specs=...  25.6 us
    ppermute x27, waiting for transfers between devices, shifted(): lax.ppermute(value, axis, [(i, (i + shift) % size) for i in range(size)])  9.96 us
    unnamed x10, local copies, waits for them, and re-layouts  3.02 us
    pallas_call x1, Pallas kernels, second_stage(): pl.pallas_call(kernel, out_shape=sds(S, X, PLANE), in_specs=[SMEM] + [VME...  2.21 us
  transfers between devices with their start and end apart: 27, of which 6 were waited for; matrix products, arithmetic and copies ran while one was open for 0% of the time, Pallas kernels for 29%

profile of v6, /device:TPU:1, one launch (start us, length us, event | category | flops | bytes accessed | tf_op | source)
XLA Modules:
  0.0 77.4 jit_solution(17817198343564835765)
XLA Ops:
  0.6 0.7 reduce
  1.3 2.2 %collective-permute-start.3 = (s32[24,576]{1,0:T(8,128)S(1)}, s32[24,576]{1,0:T(8,128)S(1)}, u32[]{:S(2)}, u32[]{:S(2)}) collective-permute-start(s32[24,576]{1,0:T(8,128)S(1)} %add.8), channel_id=1, source_target_pairs={{0,16},{16,32},{32,48},{48,0},{1,17},{17,33},{33,49},{49,1},{2,18}... | collective-permute-start | bytes 165896 | tf_op jit(solution)/shard_map/ppermute | solution.py:413
  3.5 2.5 %collective-permute-start.2 = (f32[48,1152]{1,0:T(8,128)}, f32[48,1152]{1,0:T(8,128)S(1)}, u32[]{:S(2)}, u32[]{:S(2)}) collective-permute-start(f32[48,1152]{1,0:T(8,128)} %bitcast.6), channel_id=1, source_target_pairs={{0,192},{64,0},{128,64},{192,128},{1,193},{65,1},{129,65},{193,129... | collective-permute-start | bytes 663560 | tf_op jit(solution)/shard_map/ppermute | solution.py:413
  6.0 0.5 collective-permute-start.1
  6.5 0.6 collective-permute-start
  7.2 1.8 %collective-permute-start.5 = (f32[48,1152]{1,0:T(8,128)}, f32[48,1152]{1,0:T(8,128)S(1)}, u32[]{:S(2)}, u32[]{:S(2)}) collective-permute-start(f32[48,1152]{1,0:T(8,128)} %bitcast.9), channel_id=1, source_target_pairs={{0,8},{8,0},{1,9},{9,1},{2,10},{10,2},{3,11},{11,3},{4,12},{12,4},... | collective-permute-start | bytes 663560 | tf_op jit(solution)/shard_map/ppermute | solution.py:413
  9.0 0.9 %copy-done.1 = bf16[48,2304]{1,0:T(8,128)(2,1)S(1)} copy-done((bf16[48,2304]{1,0:T(8,128)(2,1)S(1)}, bf16[48,2304]{1,0:T(8,128)(2,1)}, u32[]{:S(2)}) %copy-start.1) | copy-done | bytes 221208
  9.9 1.8 %fold_kernel.1.matrix_ref = bf16[96,1280]{1,0:T(8,128)(2,1)S(1)} custom-call(bf16[48,2304]{1,0:T(8,128)(2,1)S(1)} %copy-done.1), custom_call_target="tpu_custom_call" | custom-call | tf_op jit(solution)/shard_map/fold_kernel/pallas_call | solution.py:34
  11.7 2.7 %collective-permute-start.4 = (s32[24,576]{1,0:T(8,128)S(1)}, s32[24,576]{1,0:T(8,128)S(1)}, u32[]{:S(2)}, u32[]{:S(2)}) collective-permute-start(s32[24,576]{1,0:T(8,128)S(1)} %pad_add_fusion.refs_0_), channel_id=1, source_target_pairs={{0,32},{16,48},{32,0},{48,16},{1,33},{17,49},{33,1},{49,17},{2,34}... | collective-permute-start | bytes 165896 | tf_op jit(solution)/shard_map/ppermute | solution.py:413
  14.4 1.1 %copy-done = f32[1,1,48,4,1024]{4,3,2,1,0:T(4,128)S(1)} copy-done((f32[1,1,48,4,1024]{4,3,2,1,0:T(4,128)S(1)}, f32[1,1,48,4,1024]{4,3,2,1,0:T(4,128)}, u32[]{:S(2)}) %copy-start) | copy-done | bytes 786456
  15.6 0.9 %copy-done.2 = f32[1,1,48,1152]{3,2,1,0:T(8,128)S(1)} copy-done((f32[1,1,48,1152]{3,2,1,0:T(8,128)S(1)}, f32[1,1,48,1152]{3,2,1,0:T(8,128)}, u32[]{:S(2)}) %copy-start.2) | copy-done | bytes 221208
  16.5 1.5 %split_planes.1 = (f32[48,1024]{1,0:T(8,128)S(1)}, f32[48,1024]{1,0:T(8,128)S(1)}, f32[48,1024]{1,0:T(8,128)S(1)}, f32[48,1024]{1,0:T(8,128)S(1)}, f32[48,1152]{1,0:T(8,128)S(1)}) custom-call(f32[48,4,1024]{2,1,0:T(4,128)S(1)} %bitcast.5, f32[48,1152]{1,0:T(8,128)S(1)} %bitcast.10), custom_call_target="tpu_custom_call" | custom-call | tf_op jit(solution)/shard_map/split_planes/pallas_call | solution.py:107
  18.0 1.8 %collective-permute-done.refs_4_ = f32[48,1152]{1,0:T(8,128)S(1)} collective-permute-done((f32[48,1152]{1,0:T(8,128)}, f32[48,1152]{1,0:T(8,128)S(1)}, u32[]{:S(2)}, u32[]{:S(2)}) %collective-permute-start) | collective-permute-done | bytes 221216 | tf_op jit(solution)/shard_map/ppermute | solution.py:413
  19.8 0.5 collective-permute-start.6
  20.3 0.5 collective-permute-start.8
  20.8 1.6 %collective-permute-start.12 = (f32[48,1024]{1,0:T(8,128)S(1)}, f32[48,1024]{1,0:T(8,128)S(1)}, u32[]{:S(2)}, u32[]{:S(2)}) collective-permute-start(f32[48,1024]{1,0:T(8,128)S(1)} %get-tuple-element.90.refs_3_), channel_id=1, source_target_pairs={{0,1},{1,2},{2,3},{3,4},{4,5},{5,6},{6,7},{7,0},{8,9},{9,10},{10,1... | collective-permute-start | bytes 589832 | tf_op jit(solution)/shard_map/ppermute | solution.py:413
  22.5 4.0 %collective-permute-start.13 = (f32[48,1024]{1,0:T(8,128)S(1)}, f32[48,1024]{1,0:T(8,128)S(1)}, u32[]{:S(2)}, u32[]{:S(2)}) collective-permute-start(f32[48,1024]{1,0:T(8,128)S(1)} %get-tuple-element.91.refs_0_), channel_id=1, source_target_pairs={{0,7},{1,0},{2,1},{3,2},{4,3},{5,4},{6,5},{7,6},{8,15},{9,8},{10,9... | collective-permute-start | bytes 589832 | tf_op jit(solution)/shard_map/ppermute | solution.py:413
  26.4 1.8 %gather_first.1 = (f32[48,640]{1,0:T(8,128)S(1)}, bf16[768,1152]{1,0:T(8,128)(2,1)S(1)}, s32[4,576]{1,0:T(4,128)S(1)}) custom-call(s32[24,576]{1,0:T(8,128)S(1)} %pad_add_fusion.refs_0_, s32[24,576]{1,0:T(8,128)S(1)} %collective-permute-done.4.refs_1_, f32[48,1152]{1,0:T(8,128)S(1)} %get-tuple-element.81.refs_2_.refs_0_.coarse_ref, ...), custom_call_target="tpu_custom_call" | custom-call | tf_op jit(solution)/shard_map/gather_first/pallas_call | solution.py:34
  28.2 2.9 %collective-permute-start.9 = (f32[48,640]{1,0:T(8,128)S(1)}, f32[48,640]{1,0:T(8,128)S(1)}, u32[]{:S(2)}, u32[]{:S(2)}) collective-permute-start(f32[48,640]{1,0:T(8,128)S(1)} %get-tuple-element.88), channel_id=1, source_target_pairs={{0,32},{16,48},{32,0},{48,16},{1,33},{17,49},{33,1},{49,17},{2,34}... | collective-permute-start | bytes 368648 | tf_op jit(solution)/shard_map/ppermute | solution.py:413
  31.1 1.7 %gather_one.1 = f32[48,640]{1,0:T(8,128)S(1)} custom-call(s32[4,576]{1,0:T(4,128)S(1)} %get-tuple-element.89.request_ref.request_a, bf16[768,1152]{1,0:T(8,128)(2,1)S(1)} %get-tuple-element.86.rows_ref), custom_call_target="tpu_custom_call" | custom-call | tf_op jit(solution)/shard_map/gather_one/pallas_call | solution.py:34
  32.9 1.1 %collective-permute-start.10 = (f32[48,640]{1,0:T(8,128)S(1)}, f32[48,640]{1,0:T(8,128)S(1)}, u32[]{:S(2)}, u32[]{:S(2)}) collective-permute-start(f32[48,640]{1,0:T(8,128)S(1)} %gather_one.1), channel_id=1, source_target_pairs={{0,48},{16,0},{32,16},{48,32},{1,49},{17,1},{33,17},{49,33},{2,50}... | collective-permute-start | bytes 368648 | tf_op jit(solution)/shard_map/ppermute | solution.py:413
  34.0 1.7 %gather_three.1 = f32[48,640]{1,0:T(8,128)S(1)} custom-call(s32[4,576]{1,0:T(4,128)S(1)} %get-tuple-element.89.request_ref.request_a, bf16[768,1152]{1,0:T(8,128)(2,1)S(1)} %get-tuple-element.86.rows_ref), custom_call_target="tpu_custom_call" | custom-call | tf_op jit(solution)/shard_map/gather_three/pallas_call | solution.py:34
  35.8 0.5 collective-permute-start.11
  36.3 1.2 %collective-permute-start.14 = (s32[4,576]{1,0:T(4,128)S(1)}, s32[4,576]{1,0:T(4,128)S(1)}, u32[]{:S(2)}, u32[]{:S(2)}) collective-permute-start(s32[4,576]{1,0:T(4,128)S(1)} %get-tuple-element.89.request_ref.request_a), channel_id=1, source_target_pairs={{0,8},{8,0},{1,9},{9,1},{2,10},{10,2},{3,11},{11,3},{4,12},{12,4},... | collective-permute-start | bytes 27656 | tf_op jit(solution)/shard_map/ppermute | solution.py:413
  37.4 1.7 %gather_own.1.refs_8_ = f32[48,640]{1,0:T(8,128)S(1)} custom-call(s32[4,576]{1,0:T(4,128)S(1)} %get-tuple-element.89.request_ref.request_a, bf16[768,1152]{1,0:T(8,128)(2,1)S(1)} %get-tuple-element.86.rows_ref), custom_call_target="tpu_custom_call" | custom-call | tf_op jit(solution)/shard_map/gather_own/pallas_call | solution.py:34
  39.2 2.3 %coagulate_fine.1 = (f32[48,1024]{1,0:T(8,128)S(1)}, f32[48,1024]{1,0:T(8,128)S(1)}, f32[48,1024]{1,0:T(8,128)S(1)}, f32[48,1024]{1,0:T(8,128)S(1)}) custom-call(bf16[96,1280]{1,0:T(8,128)(2,1)S(1)} %fold_kernel.1.matrix_ref, f32[48,1024]{1,0:T(8,128)S(1)} %get-tuple-element.91.refs_0_, f32[48,1024]{1,0:T(8,128)S(1)} %get-tuple-element.93.refs_1_, ...), custom_call_target="tpu_custom_call" | custom-call | tf_op jit(solution)/shard_map/coagulate_fine/pallas_call | solution.py:34
  41.6 1.9 %first_stage.1 = (f32[48,1024]{1,0:T(8,128)S(1)}, f32[48,1024]{1,0:T(8,128)S(1)}, f32[48,1024]{1,0:T(8,128)S(1)}, f32[48,1024]{1,0:T(8,128)S(1)}, f32[48,1024]{1...) custom-call(s32[1,8]{1,0:T(1,128)S(1)} %copy-done.3, ...), custom_call_target="tpu_custom_call" | custom-call | tf_op jit(solution)/shard_map/first_stage/pallas_call | solution.py:34
  43.4 0.1 collective-permute-start.15
  43.5 2.4 %collective-permute-start.19 = (f32[48,640]{1,0:T(8,128)S(1)}, f32[48,640]{1,0:T(8,128)S(1)}, u32[]{:S(2)}, u32[]{:S(2)}) collective-permute-start(f32[48,640]{1,0:T(8,128)S(1)} %get-tuple-element.117.refs_0_), channel_id=1, source_target_pairs={{0,48},{16,0},{32,16},{48,32},{1,49},{17,1},{33,17},{49,33},{2,50}... | collective-permute-start | bytes 368648 | tf_op jit(solution)/shard_map/ppermute | solution.py:413
  45.9 0.7 collective-permute-start.17
  46.6 2.5 %collective-permute-start.16 = (f32[48,1024]{1,0:T(8,128)S(1)}, f32[48,1024]{1,0:T(8,128)S(1)}, u32[]{:S(2)}, u32[]{:S(2)}) collective-permute-start(f32[48,1024]{1,0:T(8,128)S(1)} %get-tuple-element.111.refs_0_), channel_id=1, source_target_pairs={{0,7},{1,0},{2,1},{3,2},{4,3},{5,4},{6,5},{7,6},{8,15},{9,8},{10,9... | collective-permute-start | bytes 589832 | tf_op jit(solution)/shard_map/ppermute | solution.py:413
  49.1 0.9 %cells_by_row.1.cell_ref = s32[5120,128]{1,0:T(8,128)S(1)} custom-call(s32[4,576]{1,0:T(4,128)S(1)} %get-tuple-element.89.request_ref.request_a, s32[4,576]{1,0:T(4,128)S(1)} %collective-permute-done.14.request_b), custom_call_target="tpu_custom_call" | custom-call | tf_op jit(solution)/shard_map/cells_by_row/pallas_call | solution.py:34
  49.9 2.3 %coagulate_middle.1 = (f32[48,1024]{1,0:T(8,128)S(1)}, f32[48,1024]{1,0:T(8,128)S(1)}, f32[48,1024]{1,0:T(8,128)S(1)}, f32[48,1024]{1,0:T(8,128)S(1)}) custom-call(bf16[96,1280]{1,0:T(8,128)(2,1)S(1)} %fold_kernel.1.matrix_ref, f32[48,1024]{1,0:T(8,128)S(1)} %get-tuple-element.111.refs_0_, f32[48,1024]{1,0:T(8,128)S(1)} %get-tuple-element.114.refs_1_, ...), custom_call_target="tpu_custom_call" | custom-call | tf_op jit(solution)/shard_map/coagulate_middle/pallas_call | solution.py:34
  52.3 1.2 %collective-permute-start.20 = (f32[48,640]{1,0:T(8,128)S(1)}, f32[48,640]{1,0:T(8,128)S(1)}, u32[]{:S(2)}, u32[]{:S(2)}) collective-permute-start(f32[48,640]{1,0:T(8,128)S(1)} %get-tuple-element.117.refs_0_), channel_id=1, source_target_pairs={{0,8},{8,0},{1,9},{9,1},{2,10},{10,2},{3,11},{11,3},{4,12},{12,4},... | collective-permute-start | bytes 368648 | tf_op jit(solution)/shard_map/ppermute | solution.py:413
  53.5 1.2 %collective-permute-done.17.refs_1_ = f32[48,640]{1,0:T(8,128)S(1)} collective-permute-done((f32[48,640]{1,0:T(8,128)S(1)}, f32[48,640]{1,0:T(8,128)S(1)}, u32[]{:S(2)}, u32[]{:S(2)}) %collective-permute-start.17) | collective-permute-done | bytes 122912 | tf_op jit(solution)/shard_map/ppermute | solution.py:413
  54.7 0.8 %collective-permute-start.21 = (f32[48,640]{1,0:T(8,128)S(1)}, f32[48,640]{1,0:T(8,128)S(1)}, u32[]{:S(2)}, u32[]{:S(2)}) collective-permute-start(f32[48,640]{1,0:T(8,128)S(1)} %collective-permute-done.17.refs_1_), channel_id=1, source_target_pairs={{0,8},{8,0},{1,9},{9,1},{2,10},{10,2},{3,11},{11,3},{4,12},{12,4},... | collective-permute-start | bytes 368648 | tf_op jit(solution)/shard_map/ppermute | solution.py:413
  55.5 0.5 collective-permute-start.23
  56.0 0.5 collective-permute-done.21.refs_5_
  56.5 0.4 collective-permute-done.22.refs_6_
  56.8 0.2 collective-permute-done.23.refs_7_
  57.0 4.0 %scatter_far.1 = (f32[48,1152]{1,0:T(8,128)S(1)}, f32[48,1152]{1,0:T(8,128)S(1)}) custom-call(s32[4,576]{1,0:T(4,128)S(1)} %get-tuple-element.89.request_ref.request_a, s32[4,576]{1,0:T(4,128)S(1)} %collective-permute-done.14.request_b, s32[5120,128]{1,0:T(8,128)S(1)} %cells_by_row.1.cell_ref, f32[48,640]{1,0:T(8,128)S(1)} %get-tuple-element.117.refs_0_, ...), custom_call_target="tpu_custom_call" | custom-call | tf_op jit(solution)/shard_map/scatter_far/pallas_call | solution.py:34
  61.1 1.5 %collective-permute-start.25 = (f32[48,1152]{1,0:T(8,128)S(1)}, f32[48,1152]{1,0:T(8,128)S(1)}, u32[]{:S(2)}, u32[]{:S(2)}) collective-permute-start(f32[48,1152]{1,0:T(8,128)S(1)} %get-tuple-element.121), channel_id=1, source_target_pairs={{0,128},{64,192},{128,0},{192,64},{1,129},{65,193},{129,1},{193,65... | collective-permute-start | bytes 663560 | tf_op jit(solution)/shard_map/ppermute | solution.py:413
  62.5 4.0 %scatter_near.1 = (f32[48,1152]{1,0:T(8,128)S(1)}, f32[48,1152]{1,0:T(8,128)S(1)}) custom-call(s32[4,576]{1,0:T(4,128)S(1)} %get-tuple-element.89.request_ref.request_a, s32[4,576]{1,0:T(4,128)S(1)} %collective-permute-done.14.request_b, s32[5120,128]{1,0:T(8,128)S(1)} %cells_by_row.1.cell_ref, f32[48,640]{1,0:T(8,128)S(1)} %get-tuple-element.117.refs_0_, ...), custom_call_target="tpu_custom_call" | custom-call | tf_op jit(solution)/shard_map/scatter_near/pallas_call | solution.py:34
  66.5 1.3 %collective-permute-start.26 = (f32[48,1152]{1,0:T(8,128)S(1)}, f32[48,1152]{1,0:T(8,128)S(1)}, u32[]{:S(2)}, u32[]{:S(2)}) collective-permute-start(f32[48,1152]{1,0:T(8,128)S(1)} %get-tuple-element.125), channel_id=1, source_target_pairs={{0,192},{64,0},{128,64},{192,128},{1,193},{65,1},{129,65},{193,129... | collective-permute-start | bytes 663560 | tf_op jit(solution)/shard_map/ppermute | solution.py:413
  67.8 5.9 %collective-permute-done.24.b = f32[48,1152]{1,0:T(8,128)S(1)} collective-permute-done((f32[48,1152]{1,0:T(8,128)S(1)}, f32[48,1152]{1,0:T(8,128)S(1)}, u32[]{:S(2)}, u32[]{:S(2)}) %collective-permute-start.24) | collective-permute-done | bytes 221216 | tf_op jit(solution)/shard_map/ppermute | solution.py:413
  73.7 2.2 %second_stage.1 = f32[48,4,1024]{2,1,0:T(4,128)} custom-call(s32[1,8]{1,0:T(1,128)S(1)} %copy-done.3, f32[1,48]{1,0:T(1,128)S(1)} %bitcast.12, f32[48,1024]{1,0:T(8,128)S(1)} %get-tuple-element.111.refs_0_, f32[48,1024]{1,0:T(8,128)S(1)} %get-tuple-element.114.refs_1_, f32[48,1024]{1,0:T(8,128)S(1)} %get-tuple-element.115.refs_2_, ...), custom_call_target="tpu_custom_call" | custom-call | tf_op jit(solution)/shard_map/second_stage/pallas_call | solution.py:391
  75.9 0.8 coagulate_coarse.1.growth_ref
  76.7 0.8 %finish_coarse.1 = f32[48,1152]{1,0:T(8,128)} custom-call(f32[48,1152]{1,0:T(8,128)S(1)} %get-tuple-element.81.refs_2_.refs_0_.coarse_ref, f32[48,1152]{1,0:T(8,128)S(1)} %coagulate_coarse.1.growth_ref, f32[48,1152]{1,0:T(8,128)S(1)} %get-tuple-element.144.a, f32[48,1152]{1,0:T(8,128)S(1)} %collective-permute-done.24.b, ...), custom_call_target="tpu_custom_call" | custom-call | tf_op jit(solution)/shard_map/finish_coarse/pallas_call | solution.py:34
  (36 shorter events, 0.2 us)
Async XLA Ops:
  1.3 10.3 %collective-permute-start.3 = (s32[24,576]{1,0:T(8,128)S(1)}, s32[24,576]{1,0:T(8,128)S(1)}, u32[]{:S(2)}, u32[]{:S(2)}) collective-permute-start(s32[24,576]{1,0:T(8,128)S(1)} %add.8), channel_id=1, source_target_pairs={{0,16},{16,32},{32,48},{48,0},{1,17},{17,33},{33,49},{49,1},{2,18}... | collective-permute-start | bytes 165896 | tf_op jit(solution)/shard_map/ppermute | solution.py:413
  3.5 14.5 %collective-permute-start.2 = (f32[48,1152]{1,0:T(8,128)}, f32[48,1152]{1,0:T(8,128)S(1)}, u32[]{:S(2)}, u32[]{:S(2)}) collective-permute-start(f32[48,1152]{1,0:T(8,128)} %bitcast.6), channel_id=1, source_target_pairs={{0,192},{64,0},{128,64},{192,128},{1,193},{65,1},{129,65},{193,129... | collective-permute-start | bytes 663560 | tf_op jit(solution)/shard_map/ppermute | solution.py:413
  6.0 12.0 %collective-permute-start.1 = (f32[48,1152]{1,0:T(8,128)}, f32[48,1152]{1,0:T(8,128)S(1)}, u32[]{:S(2)}, u32[]{:S(2)}) collective-permute-start(f32[48,1152]{1,0:T(8,128)} %bitcast.7), channel_id=1, source_target_pairs={{0,128},{64,192},{128,0},{192,64},{1,129},{65,193},{129,1},{193,65... | collective-permute-start | bytes 663560 | tf_op jit(solution)/shard_map/ppermute | solution.py:413
  6.5 13.3 %collective-permute-start = (f32[48,1152]{1,0:T(8,128)}, f32[48,1152]{1,0:T(8,128)S(1)}, u32[]{:S(2)}, u32[]{:S(2)}) collective-permute-start(f32[48,1152]{1,0:T(8,128)} %bitcast.8), channel_id=1, source_target_pairs={{0,64},{64,128},{128,192},{192,0},{1,65},{65,129},{129,193},{193,1... | collective-permute-start | bytes 663560 | tf_op jit(solution)/shard_map/ppermute | solution.py:413
  7.2 15.3 %collective-permute-start.5 = (f32[48,1152]{1,0:T(8,128)}, f32[48,1152]{1,0:T(8,128)S(1)}, u32[]{:S(2)}, u32[]{:S(2)}) collective-permute-start(f32[48,1152]{1,0:T(8,128)} %bitcast.9), channel_id=1, source_target_pairs={{0,8},{8,0},{1,9},{9,1},{2,10},{10,2},{3,11},{11,3},{4,12},{12,4},... | collective-permute-start | bytes 663560 | tf_op jit(solution)/shard_map/ppermute | solution.py:413
  8.9 0.9 %copy-start.1 = (bf16[48,2304]{1,0:T(8,128)(2,1)S(1)}, bf16[48,2304]{1,0:T(8,128)(2,1)}, u32[]{:S(2)}) copy-start(bf16[48,2304]{1,0:T(8,128)(2,1)} %matrix_ref.1) | copy-start | bytes 663556
  11.7 6.3 %collective-permute-start.4 = (s32[24,576]{1,0:T(8,128)S(1)}, s32[24,576]{1,0:T(8,128)S(1)}, u32[]{:S(2)}, u32[]{:S(2)}) collective-permute-start(s32[24,576]{1,0:T(8,128)S(1)} %pad_add_fusion.refs_0_), channel_id=1, source_target_pairs={{0,32},{16,48},{32,0},{48,16},{1,33},{17,49},{33,1},{49,17},{2,34}... | collective-permute-start | bytes 165896 | tf_op jit(solution)/shard_map/ppermute | solution.py:413
  14.4 1.1 %copy-start = (f32[1,1,48,4,1024]{4,3,2,1,0:T(4,128)S(1)}, f32[1,1,48,4,1024]{4,3,2,1,0:T(4,128)}, u32[]{:S(2)}) copy-start(f32[1,1,48,4,1024]{4,3,2,1,0:T(4,128)} %param.6) | copy-start | bytes 2359300
  15.6 0.9 %copy-start.2 = (f32[1,1,48,1152]{3,2,1,0:T(8,128)S(1)}, f32[1,1,48,1152]{3,2,1,0:T(8,128)}, u32[]{:S(2)}) copy-start(f32[1,1,48,1152]{3,2,1,0:T(8,128)} %param.7) | copy-start | bytes 663556
  19.8 6.6 %collective-permute-start.6 = (f32[48,1152]{1,0:T(8,128)S(1)}, f32[48,1152]{1,0:T(8,128)S(1)}, u32[]{:S(2)}, u32[]{:S(2)}) collective-permute-start(f32[48,1152]{1,0:T(8,128)S(1)} %collective-permute-done.refs_4_), channel_id=1, source_target_pairs={{0,8},{8,0},{1,9},{9,1},{2,10},{10,2},{3,11},{11,3},{4,12},{12,4},... | collective-permute-start | bytes 663560 | tf_op jit(solution)/shard_map/ppermute | solution.py:413
  20.3 6.1 %collective-permute-start.7 = (f32[48,1152]{1,0:T(8,128)S(1)}, f32[48,1152]{1,0:T(8,128)S(1)}, u32[]{:S(2)}, u32[]{:S(2)}) collective-permute-start(f32[48,1152]{1,0:T(8,128)S(1)} %collective-permute-done.2.refs_6_), channel_id=1, source_target_pairs={{0,8},{8,0},{1,9},{9,1},{2,10},{10,2},{3,11},{11,3},{4,12},{12,4},... | collective-permute-start | bytes 663560 | tf_op jit(solution)/shard_map/ppermute | solution.py:413
  20.3 6.1 %collective-permute-start.8 = (f32[48,1152]{1,0:T(8,128)S(1)}, f32[48,1152]{1,0:T(8,128)S(1)}, u32[]{:S(2)}, u32[]{:S(2)}) collective-permute-start(f32[48,1152]{1,0:T(8,128)S(1)} %collective-permute-done.1.refs_8_), channel_id=1, source_target_pairs={{0,8},{8,0},{1,9},{9,1},{2,10},{10,2},{3,11},{11,3},{4,12},{12,4},... | collective-permute-start | bytes 663560 | tf_op jit(solution)/shard_map/ppermute | solution.py:413
  20.8 18.3 %collective-permute-start.12 = (f32[48,1024]{1,0:T(8,128)S(1)}, f32[48,1024]{1,0:T(8,128)S(1)}, u32[]{:S(2)}, u32[]{:S(2)}) collective-permute-start(f32[48,1024]{1,0:T(8,128)S(1)} %get-tuple-element.90.refs_3_), channel_id=1, source_target_pairs={{0,1},{1,2},{2,3},{3,4},{4,5},{5,6},{6,7},{7,0},{8,9},{9,10},{10,1... | collective-permute-start | bytes 589832 | tf_op jit(solution)/shard_map/ppermute | solution.py:413
  22.5 16.7 %collective-permute-start.13 = (f32[48,1024]{1,0:T(8,128)S(1)}, f32[48,1024]{1,0:T(8,128)S(1)}, u32[]{:S(2)}, u32[]{:S(2)}) collective-permute-start(f32[48,1024]{1,0:T(8,128)S(1)} %get-tuple-element.91.refs_0_), channel_id=1, source_target_pairs={{0,7},{1,0},{2,1},{3,2},{4,3},{5,4},{6,5},{7,6},{8,15},{9,8},{10,9... | collective-permute-start | bytes 589832 | tf_op jit(solution)/shard_map/ppermute | solution.py:413
  28.2 8.0 %collective-permute-start.9 = (f32[48,640]{1,0:T(8,128)S(1)}, f32[48,640]{1,0:T(8,128)S(1)}, u32[]{:S(2)}, u32[]{:S(2)}) collective-permute-start(f32[48,640]{1,0:T(8,128)S(1)} %get-tuple-element.88), channel_id=1, source_target_pairs={{0,32},{16,48},{32,0},{48,16},{1,33},{17,49},{33,1},{49,17},{2,34}... | collective-permute-start | bytes 368648 | tf_op jit(solution)/shard_map/ppermute | solution.py:413
  32.9 8.7 %copy-start.3 = (s32[1,8]{1,0:T(1,128)S(1)}, s32[1,8]{1,0:T(1,128)}, u32[]{:S(2)}) copy-start(s32[1,8]{1,0:T(1,128)} %levels_ref.3) | copy-start | bytes 100
  32.9 8.7 %copy-start.4 = (f32[48]{0:T(128)S(1)}, f32[48]{0:T(128)}, u32[]{:S(2)}) copy-start(f32[48]{0:T(128)} %param.9) | copy-start | bytes 580
  32.9 6.3 %collective-permute-start.10 = (f32[48,640]{1,0:T(8,128)S(1)}, f32[48,640]{1,0:T(8,128)S(1)}, u32[]{:S(2)}, u32[]{:S(2)}) collective-permute-start(f32[48,640]{1,0:T(8,128)S(1)} %gather_one.1), channel_id=1, source_target_pairs={{0,48},{16,0},{32,16},{48,32},{1,49},{17,1},{33,17},{49,33},{2,50}... | collective-permute-start | bytes 368648 | tf_op jit(solution)/shard_map/ppermute | solution.py:413
  35.8 5.8 %collective-permute-start.11 = (f32[48,640]{1,0:T(8,128)S(1)}, f32[48,640]{1,0:T(8,128)S(1)}, u32[]{:S(2)}, u32[]{:S(2)}) collective-permute-start(f32[48,640]{1,0:T(8,128)S(1)} %gather_three.1), channel_id=1, source_target_pairs={{0,16},{16,32},{32,48},{48,0},{1,17},{17,33},{33,49},{49,1},{2,18}... | collective-permute-start | bytes 368648 | tf_op jit(solution)/shard_map/ppermute | solution.py:413
  36.3 5.3 %collective-permute-start.14 = (s32[4,576]{1,0:T(4,128)S(1)}, s32[4,576]{1,0:T(4,128)S(1)}, u32[]{:S(2)}, u32[]{:S(2)}) collective-permute-start(s32[4,576]{1,0:T(4,128)S(1)} %get-tuple-element.89.request_ref.request_a), channel_id=1, source_target_pairs={{0,8},{8,0},{1,9},{9,1},{2,10},{10,2},{3,11},{11,3},{4,12},{12,4},... | collective-permute-start | bytes 27656 | tf_op jit(solution)/shard_map/ppermute | solution.py:413
  43.4 12.1 %collective-permute-start.15 = (f32[48,1024]{1,0:T(8,128)S(1)}, f32[48,1024]{1,0:T(8,128)S(1)}, u32[]{:S(2)}, u32[]{:S(2)}) collective-permute-start(f32[48,1024]{1,0:T(8,128)S(1)} %get-tuple-element.110.refs_3_), channel_id=1, source_target_pairs={{0,1},{1,2},{2,3},{3,4},{4,5},{5,6},{6,7},{7,0},{8,9},{9,10},{10,1... | collective-permute-start | bytes 589832 | tf_op jit(solution)/shard_map/ppermute | solution.py:413
  43.5 8.8 %collective-permute-start.19 = (f32[48,640]{1,0:T(8,128)S(1)}, f32[48,640]{1,0:T(8,128)S(1)}, u32[]{:S(2)}, u32[]{:S(2)}) collective-permute-start(f32[48,640]{1,0:T(8,128)S(1)} %get-tuple-element.117.refs_0_), channel_id=1, source_target_pairs={{0,48},{16,0},{32,16},{48,32},{1,49},{17,1},{33,17},{49,33},{2,50}... | collective-permute-start | bytes 368648 | tf_op jit(solution)/shard_map/ppermute | solution.py:413
  45.9 7.6 %collective-permute-start.18 = (f32[48,640]{1,0:T(8,128)S(1)}, f32[48,640]{1,0:T(8,128)S(1)}, u32[]{:S(2)}, u32[]{:S(2)}) collective-permute-start(f32[48,640]{1,0:T(8,128)S(1)} %get-tuple-element.117.refs_0_), channel_id=1, source_target_pairs={{0,32},{16,48},{32,0},{48,16},{1,33},{17,49},{33,1},{49,17},{2,34}... | collective-permute-start | bytes 368648 | tf_op jit(solution)/shard_map/ppermute | solution.py:413
  45.9 8.8 %collective-permute-start.17 = (f32[48,640]{1,0:T(8,128)S(1)}, f32[48,640]{1,0:T(8,128)S(1)}, u32[]{:S(2)}, u32[]{:S(2)}) collective-permute-start(f32[48,640]{1,0:T(8,128)S(1)} %get-tuple-element.117.refs_0_), channel_id=1, source_target_pairs={{0,16},{16,32},{32,48},{48,0},{1,17},{17,33},{33,49},{49,1},{2,18}... | collective-permute-start | bytes 368648 | tf_op jit(solution)/shard_map/ppermute | solution.py:413
  46.6 9.4 %collective-permute-start.16 = (f32[48,1024]{1,0:T(8,128)S(1)}, f32[48,1024]{1,0:T(8,128)S(1)}, u32[]{:S(2)}, u32[]{:S(2)}) collective-permute-start(f32[48,1024]{1,0:T(8,128)S(1)} %get-tuple-element.111.refs_0_), channel_id=1, source_target_pairs={{0,7},{1,0},{2,1},{3,2},{4,3},{5,4},{6,5},{7,6},{8,15},{9,8},{10,9... | collective-permute-start | bytes 589832 | tf_op jit(solution)/shard_map/ppermute | solution.py:413
  52.3 3.7 %collective-permute-start.20 = (f32[48,640]{1,0:T(8,128)S(1)}, f32[48,640]{1,0:T(8,128)S(1)}, u32[]{:S(2)}, u32[]{:S(2)}) collective-permute-start(f32[48,640]{1,0:T(8,128)S(1)} %get-tuple-element.117.refs_0_), channel_id=1, source_target_pairs={{0,8},{8,0},{1,9},{9,1},{2,10},{10,2},{3,11},{11,3},{4,12},{12,4},... | collective-permute-start | bytes 368648 | tf_op jit(solution)/shard_map/ppermute | solution.py:413
  54.7 1.8 %collective-permute-start.21 = (f32[48,640]{1,0:T(8,128)S(1)}, f32[48,640]{1,0:T(8,128)S(1)}, u32[]{:S(2)}, u32[]{:S(2)}) collective-permute-start(f32[48,640]{1,0:T(8,128)S(1)} %collective-permute-done.17.refs_1_), channel_id=1, source_target_pairs={{0,8},{8,0},{1,9},{9,1},{2,10},{10,2},{3,11},{11,3},{4,12},{12,4},... | collective-permute-start | bytes 368648 | tf_op jit(solution)/shard_map/ppermute | solution.py:413
  55.5 1.3 %collective-permute-start.22 = (f32[48,640]{1,0:T(8,128)S(1)}, f32[48,640]{1,0:T(8,128)S(1)}, u32[]{:S(2)}, u32[]{:S(2)}) collective-permute-start(f32[48,640]{1,0:T(8,128)S(1)} %collective-permute-done.18.refs_2_), channel_id=1, source_target_pairs={{0,8},{8,0},{1,9},{9,1},{2,10},{10,2},{3,11},{11,3},{4,12},{12,4},... | collective-permute-start | bytes 368648 | tf_op jit(solution)/shard_map/ppermute | solution.py:413
  55.5 1.5 %collective-permute-start.23 = (f32[48,640]{1,0:T(8,128)S(1)}, f32[48,640]{1,0:T(8,128)S(1)}, u32[]{:S(2)}, u32[]{:S(2)}) collective-permute-start(f32[48,640]{1,0:T(8,128)S(1)} %collective-permute-done.19.refs_3_), channel_id=1, source_target_pairs={{0,8},{8,0},{1,9},{9,1},{2,10},{10,2},{3,11},{11,3},{4,12},{12,4},... | collective-permute-start | bytes 368648 | tf_op jit(solution)/shard_map/ppermute | solution.py:413
  61.0 12.7 %collective-permute-start.24 = (f32[48,1152]{1,0:T(8,128)S(1)}, f32[48,1152]{1,0:T(8,128)S(1)}, u32[]{:S(2)}, u32[]{:S(2)}) collective-permute-start(f32[48,1152]{1,0:T(8,128)S(1)} %get-tuple-element.124), channel_id=1, source_target_pairs={{0,64},{64,128},{128,192},{192,0},{1,65},{65,129},{129,193},{193,1... | collective-permute-start | bytes 663560 | tf_op jit(solution)/shard_map/ppermute | solution.py:413
  61.1 12.6 %collective-permute-start.25 = (f32[48,1152]{1,0:T(8,128)S(1)}, f32[48,1152]{1,0:T(8,128)S(1)}, u32[]{:S(2)}, u32[]{:S(2)}) collective-permute-start(f32[48,1152]{1,0:T(8,128)S(1)} %get-tuple-element.121), channel_id=1, source_target_pairs={{0,128},{64,192},{128,0},{192,64},{1,129},{65,193},{129,1},{193,65... | collective-permute-start | bytes 663560 | tf_op jit(solution)/shard_map/ppermute | solution.py:413
  66.5 10.2 %collective-permute-start.26 = (f32[48,1152]{1,0:T(8,128)S(1)}, f32[48,1152]{1,0:T(8,128)S(1)}, u32[]{:S(2)}, u32[]{:S(2)}) collective-permute-start(f32[48,1152]{1,0:T(8,128)S(1)} %get-tuple-element.125), channel_id=1, source_target_pairs={{0,192},{64,0},{128,64},{192,128},{1,193},{65,1},{129,65},{193,129... | collective-permute-start | bytes 663560 | tf_op jit(solution)/shard_map/ppermute | solution.py:413

commit v7 on v6

--- a/solution.py
+++ b/solution.py
@@ -14,7 +14,7 @@
 STEP = 0.25
 FOLDED = 1280
 MIB = 1024 * 1024
-LIMIT = 52
+LIMIT = 60
 SPREAD = 24
 COST = pl.CostEstimate(flops=0, bytes_accessed=0, transcendentals=0)
 
@@ -465,13 +465,13 @@
     held += [shifted(value, "core", 1) for value in held]
     cells = after(cells, (below_plane, above_plane))
     sent = {}
-    both = scatter_columns([request_rows, mate_rows], cells, held, (2, 1), "scatter_far")
-    sent[2], sent[1] = shifted(both[0], "x", 2), shifted(both[1], "x", 1)
-    both = scatter_columns([request_rows, mate_rows], after(cells, both[0]), held, (3, 0), "scatter_near")
-    sent[3], sent[0] = shifted(both[0], "x", 3), both[1]
-    base = after(base, (both[0], sent[1], sent[2]))
+    (part,) = scatter_columns([request_rows, mate_rows], cells, held, (2,), "scatter_far")
+    sent[2] = shifted(part, "x", 2)
+    parts = scatter_columns([request_rows, mate_rows], after(cells, part), held, (1, 3, 0), "scatter_near")
+    sent[1], sent[3], sent[0] = shifted(parts[0], "x", 1), shifted(parts[1], "x", 3), parts[2]
+    base = after(base, parts[0])
     fine_out = second_stage(levels, row, middle, base, growth, x_ghosts, y_ghosts, below_plane, above_plane)
-    coarse_growth = coagulate(after(folded, fine_out), [held_coarse], "coagulate_coarse")[0]
+    coarse_growth = coagulate(after(folded, (fine_out, sent[2])), [held_coarse], "coagulate_coarse")[0]
     sent = [sent[k] for k in range(4)]
     sent, fine_out, coarse_growth = lax.optimization_barrier((sent, fine_out, coarse_growth))
     coarse_out = finish_coarse(held_coarse, coarse_growth, sent)

time: 77.7 us -> 76.3 us (0.982)
  local copies, waits for them, and re-layouts: 3.03 us -> 1.92 us
  Pallas kernels: 29.3 us -> 30.1 us
  waiting for transfers between devices: 9.96 us -> 9.17 us
    unnamed x10 -> x18, local copies, waits for them, and re-layouts: 3.02 us -> 1.9 us
    ppermute x27, waiting for transfers between devices: 9.96 us -> 9.17 us  [shifted(): lax.ppermute(value, axis, [(i, (i + shift) % size) for i in range(size)])]
    pallas_call x1, Pallas kernels: 1.49 us -> 2.28 us  [split_planes(): pl.pallas_call(kernel, out_shape=[sds(S, PLANE)] * X + [sds(S, CELLS)], i...]
  transfers between devices with their start and end apart: 27 -> 27, of which waited for: 6 -> 8; matrix products, arithmetic and copies ran while one was open for 0% -> 0% of each run, Pallas kernels for 29% -> 32%
where the time goes in v7:
time: 76.3 us; the launch traced here: 75.7 us
  starting transfers between devices  32.9 us (43%)
  Pallas kernels  30.1 us (39%)
  waiting for transfers between devices  9.17 us (12%)
  local copies, waits for them, and re-layouts  1.92 us (3%)
  between operations  0.96 us (1%)
    ppermute x27, starting transfers between devices, shifted(): lax.ppermute(value, axis, [(i, (i + shift) % size) for i in range(size)])  32.9 us
    pallas_call x13, Pallas kernels, call(): pl.pallas_call(kernel, out_shape=out_shape, in_specs=in_specs, out_specs=...  25.6 us
    ppermute x27, waiting for transfers between devices, shifted(): lax.ppermute(value, axis, [(i, (i + shift) % size) for i in range(size)])  9.17 us
    pallas_call x1, Pallas kernels, split_planes(): pl.pallas_call(kernel, out_shape=[sds(S, PLANE)] * X + [sds(S, CELLS)], i...  2.28 us
    pallas_call x1, Pallas kernels, second_stage(): pl.pallas_call(kernel, out_shape=sds(S, X, PLANE), in_specs=[SMEM] + [VME...  2.22 us
    unnamed x18, local copies, waits for them, and re-layouts  1.9 us
  transfers between devices with their start and end apart: 27, of which 8 were waited for; matrix products, arithmetic and copies ran while one was open for 0% of the time, Pallas kernels for 32%

profile of v7, /device:TPU:1, one launch (start us, length us, event | category | flops | bytes accessed | tf_op | source)
XLA Modules:
  0.0 75.7 jit_solution(4178270754564919853)
XLA Ops:
  0.6 0.7 reduce
  1.3 2.2 %collective-permute-start.3 = (s32[24,576]{1,0:T(8,128)S(1)}, s32[24,576]{1,0:T(8,128)S(1)}, u32[]{:S(2)}, u32[]{:S(2)}) collective-permute-start(s32[24,576]{1,0:T(8,128)S(1)} %add.8), channel_id=1, source_target_pairs={{0,16},{16,32},{32,48},{48,0},{1,17},{17,33},{33,49},{49,1},{2,18}... | collective-permute-start | bytes 165896 | tf_op jit(solution)/shard_map/ppermute | solution.py:413
  3.5 2.5 %collective-permute-start.2 = (f32[48,1152]{1,0:T(8,128)}, f32[48,1152]{1,0:T(8,128)S(1)}, u32[]{:S(2)}, u32[]{:S(2)}) collective-permute-start(f32[48,1152]{1,0:T(8,128)} %bitcast.10), channel_id=1, source_target_pairs={{0,192},{64,0},{128,64},{192,128},{1,193},{65,1},{129,65},{193,129... | collective-permute-start | bytes 663560 | tf_op jit(solution)/shard_map/ppermute | solution.py:413
  6.0 0.5 collective-permute-start.1
  6.5 0.6 collective-permute-start
  7.2 1.8 %collective-permute-start.5 = (f32[48,1152]{1,0:T(8,128)}, f32[48,1152]{1,0:T(8,128)S(1)}, u32[]{:S(2)}, u32[]{:S(2)}) collective-permute-start(f32[48,1152]{1,0:T(8,128)} %bitcast.13), channel_id=1, source_target_pairs={{0,8},{8,0},{1,9},{9,1},{2,10},{10,2},{3,11},{11,3},{4,12},{12,4},... | collective-permute-start | bytes 663560 | tf_op jit(solution)/shard_map/ppermute | solution.py:413
  9.0 0.9 %copy-done.6 = bf16[48,2304]{1,0:T(8,128)(2,1)S(1)} copy-done((bf16[48,2304]{1,0:T(8,128)(2,1)S(1)}, bf16[48,2304]{1,0:T(8,128)(2,1)}, u32[]{:S(2)}) %copy-start.6) | copy-done | bytes 221208
  9.9 1.8 %fold_kernel.1.matrix_ref = bf16[96,1280]{1,0:T(8,128)(2,1)S(1)} custom-call(bf16[48,2304]{1,0:T(8,128)(2,1)S(1)} %copy-done.6), custom_call_target="tpu_custom_call" | custom-call | tf_op jit(solution)/shard_map/fold_kernel/pallas_call | solution.py:34
  11.7 2.7 %collective-permute-start.4 = (s32[24,576]{1,0:T(8,128)S(1)}, s32[24,576]{1,0:T(8,128)S(1)}, u32[]{:S(2)}, u32[]{:S(2)}) collective-permute-start(s32[24,576]{1,0:T(8,128)S(1)} %pad_add_fusion.refs_0_), channel_id=1, source_target_pairs={{0,32},{16,48},{32,0},{48,16},{1,33},{17,49},{33,1},{49,17},{2,34}... | collective-permute-start | bytes 165896 | tf_op jit(solution)/shard_map/ppermute | solution.py:413
  14.4 2.3 %split_planes.1 = (f32[48,1024]{1,0:T(8,128)}, f32[48,1024]{1,0:T(8,128)}, f32[48,1024]{1,0:T(8,128)}, f32[48,1024]{1,0:T(8,128)}, f32[48,1152]{1,0:T(8,128)}) custom-call(f32[48,4,1024]{2,1,0:T(4,128)} %bitcast.7, f32[48,1152]{1,0:T(8,128)} %bitcast.14), custom_call_target="tpu_custom_call" | custom-call | tf_op jit(solution)/shard_map/split_planes/pallas_call | solution.py:107
  16.7 0.2 collective-permute-done.4.refs_1_
  17.0 2.9 %collective-permute-done.refs_4_ = f32[48,1152]{1,0:T(8,128)S(1)} collective-permute-done((f32[48,1152]{1,0:T(8,128)}, f32[48,1152]{1,0:T(8,128)S(1)}, u32[]{:S(2)}, u32[]{:S(2)}) %collective-permute-start) | collective-permute-done | bytes 221216 | tf_op jit(solution)/shard_map/ppermute | solution.py:413
  19.8 0.5 collective-permute-start.6
  20.3 0.5 collective-permute-start.8
  20.8 1.6 %collective-permute-start.12 = (f32[48,1024]{1,0:T(8,128)}, f32[48,1024]{1,0:T(8,128)S(1)}, u32[]{:S(2)}, u32[]{:S(2)}) collective-permute-start(f32[48,1024]{1,0:T(8,128)} %get-tuple-element.89.refs_3_), channel_id=1, source_target_pairs={{0,1},{1,2},{2,3},{3,4},{4,5},{5,6},{6,7},{7,0},{8,9},{9,10},{10,1... | collective-permute-start | bytes 589832 | tf_op jit(solution)/shard_map/ppermute | solution.py:413
  22.5 4.0 %collective-permute-start.13 = (f32[48,1024]{1,0:T(8,128)}, f32[48,1024]{1,0:T(8,128)S(1)}, u32[]{:S(2)}, u32[]{:S(2)}) collective-permute-start(f32[48,1024]{1,0:T(8,128)} %get-tuple-element.90.refs_0_), channel_id=1, source_target_pairs={{0,7},{1,0},{2,1},{3,2},{4,3},{5,4},{6,5},{7,6},{8,15},{9,8},{10,9... | collective-permute-start | bytes 589832 | tf_op jit(solution)/shard_map/ppermute | solution.py:413
  26.5 0.9 %copy-done = f32[48,1152]{1,0:T(8,128)S(1)} copy-done((f32[48,1152]{1,0:T(8,128)S(1)}, f32[48,1152]{1,0:T(8,128)}, u32[]{:S(2)}) %copy-start) | copy-done | bytes 221208
  27.4 1.8 %gather_first.1 = (f32[48,640]{1,0:T(8,128)S(1)}, bf16[768,1152]{1,0:T(8,128)(2,1)S(1)}, s32[4,576]{1,0:T(4,128)S(1)}) custom-call(s32[24,576]{1,0:T(8,128)S(1)} %pad_add_fusion.refs_0_, s32[24,576]{1,0:T(8,128)S(1)} %collective-permute-done.4.refs_1_, f32[48,1152]{1,0:T(8,128)S(1)} %copy-done, f32[48,1152]{1,0:T(8,128)S(1)} %collective-permute-done.5.refs_3_, ...), custom_call_target="tpu_custom_call" | custom-call | tf_op jit(solution)/shard_map/gather_first/pallas_call | solution.py:34
  29.2 2.9 %collective-permute-start.9 = (f32[48,640]{1,0:T(8,128)S(1)}, f32[48,640]{1,0:T(8,128)S(1)}, u32[]{:S(2)}, u32[]{:S(2)}) collective-permute-start(f32[48,640]{1,0:T(8,128)S(1)} %get-tuple-element.87), channel_id=1, source_target_pairs={{0,32},{16,48},{32,0},{48,16},{1,33},{17,49},{33,1},{49,17},{2,34}... | collective-permute-start | bytes 368648 | tf_op jit(solution)/shard_map/ppermute | solution.py:413
  32.1 1.7 %gather_one.1 = f32[48,640]{1,0:T(8,128)S(1)} custom-call(s32[4,576]{1,0:T(4,128)S(1)} %get-tuple-element.88.request_ref.request_a, bf16[768,1152]{1,0:T(8,128)(2,1)S(1)} %get-tuple-element.85.rows_ref), custom_call_target="tpu_custom_call" | custom-call | tf_op jit(solution)/shard_map/gather_one/pallas_call | solution.py:34
  33.8 1.1 %collective-permute-start.10 = (f32[48,640]{1,0:T(8,128)S(1)}, f32[48,640]{1,0:T(8,128)S(1)}, u32[]{:S(2)}, u32[]{:S(2)}) collective-permute-start(f32[48,640]{1,0:T(8,128)S(1)} %gather_one.1), channel_id=1, source_target_pairs={{0,48},{16,0},{32,16},{48,32},{1,49},{17,1},{33,17},{49,33},{2,50}... | collective-permute-start | bytes 368648 | tf_op jit(solution)/shard_map/ppermute | solution.py:413
  35.0 1.7 %gather_three.1 = f32[48,640]{1,0:T(8,128)S(1)} custom-call(s32[4,576]{1,0:T(4,128)S(1)} %get-tuple-element.88.request_ref.request_a, bf16[768,1152]{1,0:T(8,128)(2,1)S(1)} %get-tuple-element.85.rows_ref), custom_call_target="tpu_custom_call" | custom-call | tf_op jit(solution)/shard_map/gather_three/pallas_call | solution.py:34
  36.7 0.5 collective-permute-start.11
  37.2 1.2 %collective-permute-start.14 = (s32[4,576]{1,0:T(4,128)S(1)}, s32[4,576]{1,0:T(4,128)S(1)}, u32[]{:S(2)}, u32[]{:S(2)}) collective-permute-start(s32[4,576]{1,0:T(4,128)S(1)} %get-tuple-element.88.request_ref.request_a), channel_id=1, source_target_pairs={{0,8},{8,0},{1,9},{9,1},{2,10},{10,2},{3,11},{11,3},{4,12},{12,4},... | collective-permute-start | bytes 27656 | tf_op jit(solution)/shard_map/ppermute | solution.py:413
  38.4 1.7 %gather_own.1.refs_8_ = f32[48,640]{1,0:T(8,128)S(1)} custom-call(s32[4,576]{1,0:T(4,128)S(1)} %get-tuple-element.88.request_ref.request_a, bf16[768,1152]{1,0:T(8,128)(2,1)S(1)} %get-tuple-element.85.rows_ref), custom_call_target="tpu_custom_call" | custom-call | tf_op jit(solution)/shard_map/gather_own/pallas_call | solution.py:34
  40.2 2.2 %coagulate_fine.1 = (f32[48,1024]{1,0:T(8,128)S(1)}, f32[48,1024]{1,0:T(8,128)S(1)}, f32[48,1024]{1,0:T(8,128)S(1)}, f32[48,1024]{1,0:T(8,128)S(1)}) custom-call(bf16[96,1280]{1,0:T(8,128)(2,1)S(1)} %fold_kernel.1.matrix_ref, f32[48,1024]{1,0:T(8,128)S(1)} %copy-done.2, f32[48,1024]{1,0:T(8,128)S(1)} %copy-done.3, f32[48,1024]{1,0:T(8,128)S(1)} %copy-done.4, ...), custom_call_target="tpu_custom_call" | custom-call | tf_op jit(solution)/shard_map/coagulate_fine/pallas_call | solution.py:34
  42.5 1.8 %first_stage.1 = (f32[48,1024]{1,0:T(8,128)S(1)}, f32[48,1024]{1,0:T(8,128)S(1)}, f32[48,1024]{1,0:T(8,128)S(1)}, f32[48,1024]{1,0:T(8,128)S(1)}, f32[48,1024]{1...) custom-call(s32[1,8]{1,0:T(1,128)S(1)} %copy-done.7, ...), custom_call_target="tpu_custom_call" | custom-call | tf_op jit(solution)/shard_map/first_stage/pallas_call | solution.py:34
  44.4 2.3 %collective-permute-start.19 = (f32[48,640]{1,0:T(8,128)S(1)}, f32[48,640]{1,0:T(8,128)S(1)}, u32[]{:S(2)}, u32[]{:S(2)}) collective-permute-start(f32[48,640]{1,0:T(8,128)S(1)} %get-tuple-element.116.refs_0_), channel_id=1, source_target_pairs={{0,48},{16,0},{32,16},{48,32},{1,49},{17,1},{33,17},{49,33},{2,50}... | collective-permute-start | bytes 368648 | tf_op jit(solution)/shard_map/ppermute | solution.py:413
  46.7 0.7 collective-permute-start.17
  47.4 2.5 %collective-permute-start.16 = (f32[48,1024]{1,0:T(8,128)S(1)}, f32[48,1024]{1,0:T(8,128)S(1)}, u32[]{:S(2)}, u32[]{:S(2)}) collective-permute-start(f32[48,1024]{1,0:T(8,128)S(1)} %get-tuple-element.110.refs_0_), channel_id=1, source_target_pairs={{0,7},{1,0},{2,1},{3,2},{4,3},{5,4},{6,5},{7,6},{8,15},{9,8},{10,9... | collective-permute-start | bytes 589832 | tf_op jit(solution)/shard_map/ppermute | solution.py:413
  49.9 0.9 %cells_by_row.1.cell_ref = s32[5120,128]{1,0:T(8,128)S(1)} custom-call(s32[4,576]{1,0:T(4,128)S(1)} %get-tuple-element.88.request_ref.request_a, s32[4,576]{1,0:T(4,128)S(1)} %collective-permute-done.14.request_b), custom_call_target="tpu_custom_call" | custom-call | tf_op jit(solution)/shard_map/cells_by_row/pallas_call | solution.py:34
  50.8 2.2 %coagulate_middle.1 = (f32[48,1024]{1,0:T(8,128)S(1)}, f32[48,1024]{1,0:T(8,128)S(1)}, f32[48,1024]{1,0:T(8,128)S(1)}, f32[48,1024]{1,0:T(8,128)S(1)}) custom-call(bf16[96,1280]{1,0:T(8,128)(2,1)S(1)} %fold_kernel.1.matrix_ref, f32[48,1024]{1,0:T(8,128)S(1)} %get-tuple-element.110.refs_0_, f32[48,1024]{1,0:T(8,128)S(1)} %get-tuple-element.113.refs_1_, ...), custom_call_target="tpu_custom_call" | custom-call | tf_op jit(solution)/shard_map/coagulate_middle/pallas_call | solution.py:34
  53.0 1.2 %collective-permute-start.20 = (f32[48,640]{1,0:T(8,128)S(1)}, f32[48,640]{1,0:T(8,128)S(1)}, u32[]{:S(2)}, u32[]{:S(2)}) collective-permute-start(f32[48,640]{1,0:T(8,128)S(1)} %get-tuple-element.116.refs_0_), channel_id=1, source_target_pairs={{0,8},{8,0},{1,9},{9,1},{2,10},{10,2},{3,11},{11,3},{4,12},{12,4},... | collective-permute-start | bytes 368648 | tf_op jit(solution)/shard_map/ppermute | solution.py:413
  54.3 1.3 %collective-permute-done.17.refs_1_ = f32[48,640]{1,0:T(8,128)S(1)} collective-permute-done((f32[48,640]{1,0:T(8,128)S(1)}, f32[48,640]{1,0:T(8,128)S(1)}, u32[]{:S(2)}, u32[]{:S(2)}) %collective-permute-start.17) | collective-permute-done | bytes 122912 | tf_op jit(solution)/shard_map/ppermute | solution.py:413
  55.5 0.8 %collective-permute-start.21 = (f32[48,640]{1,0:T(8,128)S(1)}, f32[48,640]{1,0:T(8,128)S(1)}, u32[]{:S(2)}, u32[]{:S(2)}) collective-permute-start(f32[48,640]{1,0:T(8,128)S(1)} %collective-permute-done.17.refs_1_), channel_id=1, source_target_pairs={{0,8},{8,0},{1,9},{9,1},{2,10},{10,2},{3,11},{11,3},{4,12},{12,4},... | collective-permute-start | bytes 368648 | tf_op jit(solution)/shard_map/ppermute | solution.py:413
  56.3 0.5 collective-permute-start.23
  56.8 0.5 collective-permute-done.21.refs_5_
  57.3 0.4 collective-permute-done.22.refs_6_
  57.8 2.9 %scatter_far.1 = f32[48,1152]{1,0:T(8,128)S(1)} custom-call(s32[4,576]{1,0:T(4,128)S(1)} %get-tuple-element.88.request_ref.request_a, s32[4,576]{1,0:T(4,128)S(1)} %collective-permute-done.14.request_b, s32[5120,128]{1,0:T(8,128)S(1)} %cells_by_row.1.cell_ref, f32[48,640]{1,0:T(8,128)S(1)} %get-tuple-element.116.refs_0_, ...), custom_call_target="tpu_custom_call" | custom-call | tf_op jit(solution)/shard_map/scatter_far/pallas_call | solution.py:34
  60.8 0.6 collective-permute-start.25
  61.4 5.3 %scatter_near.1 = (f32[48,1152]{1,0:T(8,128)S(1)}, f32[48,1152]{1,0:T(8,128)S(1)}, f32[48,1152]{1,0:T(8,128)S(1)}) custom-call(s32[4,576]{1,0:T(4,128)S(1)} %get-tuple-element.88.request_ref.request_a, s32[4,576]{1,0:T(4,128)S(1)} %collective-permute-done.14.request_b, s32[5120,128]{1,0:T(8,128)S(1)} %cells_by_row.1.cell_ref, ...), custom_call_target="tpu_custom_call" | custom-call | tf_op jit(solution)/shard_map/scatter_near/pallas_call | solution.py:34
  66.6 1.0 %collective-permute-start.26 = (f32[48,1152]{1,0:T(8,128)S(1)}, f32[48,1152]{1,0:T(8,128)S(1)}, u32[]{:S(2)}, u32[]{:S(2)}) collective-permute-start(f32[48,1152]{1,0:T(8,128)S(1)} %get-tuple-element.123), channel_id=1, source_target_pairs={{0,192},{64,0},{128,64},{192,128},{1,193},{65,1},{129,65},{193,129... | collective-permute-start | bytes 663560 | tf_op jit(solution)/shard_map/ppermute | solution.py:413
  67.7 0.5 collective-permute-start.24
  68.2 2.2 %second_stage.1 = f32[48,4,1024]{2,1,0:T(4,128)} custom-call(s32[1,8]{1,0:T(1,128)S(1)} %copy-done.7, f32[1,48]{1,0:T(1,128)S(1)} %bitcast.6, f32[48,1024]{1,0:T(8,128)S(1)} %get-tuple-element.110.refs_0_, f32[48,1024]{1,0:T(8,128)S(1)} %get-tuple-element.113.refs_1_, f32[48,1024]{1,0:T(8,128)S(1)} %get-tuple-element.114.refs_2_, ...), custom_call_target="tpu_custom_call" | custom-call | tf_op jit(solution)/shard_map/second_stage/pallas_call | solution.py:391
  70.4 0.8 coagulate_coarse.1.growth_ref
  71.2 1.9 %collective-permute-done.26.d = f32[48,1152]{1,0:T(8,128)S(1)} collective-permute-done((f32[48,1152]{1,0:T(8,128)S(1)}, f32[48,1152]{1,0:T(8,128)S(1)}, u32[]{:S(2)}, u32[]{:S(2)}) %collective-permute-start.26) | collective-permute-done | bytes 221216 | tf_op jit(solution)/shard_map/ppermute | solution.py:413
  73.1 1.8 %collective-permute-done.24.b = f32[48,1152]{1,0:T(8,128)S(1)} collective-permute-done((f32[48,1152]{1,0:T(8,128)S(1)}, f32[48,1152]{1,0:T(8,128)S(1)}, u32[]{:S(2)}, u32[]{:S(2)}) %collective-permute-start.24) | collective-permute-done | bytes 221216 | tf_op jit(solution)/shard_map/ppermute | solution.py:413
  74.9 0.8 %finish_coarse.1 = f32[48,1152]{1,0:T(8,128)} custom-call(f32[48,1152]{1,0:T(8,128)S(1)} %copy-done.1, f32[48,1152]{1,0:T(8,128)S(1)} %coagulate_coarse.1.growth_ref, f32[48,1152]{1,0:T(8,128)S(1)} %get-tuple-element.142.a, f32[48,1152]{1,0:T(8,128)S(1)} %collective-permute-done.24.b, f32[48,1152]{1,0:T(8,128)S(1)} %collective-permute-done.25.c, ...), custom_call_target="tpu_custom_call" | custom-call | tf_op jit(solution)/shard_map/finish_coarse/pallas_call | solution.py:34
  (44 shorter events, 0.4 us)
Async XLA Ops:
  1.3 10.3 %collective-permute-start.3 = (s32[24,576]{1,0:T(8,128)S(1)}, s32[24,576]{1,0:T(8,128)S(1)}, u32[]{:S(2)}, u32[]{:S(2)}) collective-permute-start(s32[24,576]{1,0:T(8,128)S(1)} %add.8), channel_id=1, source_target_pairs={{0,16},{16,32},{32,48},{48,0},{1,17},{17,33},{33,49},{49,1},{2,18}... | collective-permute-start | bytes 165896 | tf_op jit(solution)/shard_map/ppermute | solution.py:413
  3.5 13.4 %collective-permute-start.2 = (f32[48,1152]{1,0:T(8,128)}, f32[48,1152]{1,0:T(8,128)S(1)}, u32[]{:S(2)}, u32[]{:S(2)}) collective-permute-start(f32[48,1152]{1,0:T(8,128)} %bitcast.10), channel_id=1, source_target_pairs={{0,192},{64,0},{128,64},{192,128},{1,193},{65,1},{129,65},{193,129... | collective-permute-start | bytes 663560 | tf_op jit(solution)/shard_map/ppermute | solution.py:413
  6.0 10.9 %collective-permute-start.1 = (f32[48,1152]{1,0:T(8,128)}, f32[48,1152]{1,0:T(8,128)S(1)}, u32[]{:S(2)}, u32[]{:S(2)}) collective-permute-start(f32[48,1152]{1,0:T(8,128)} %bitcast.11), channel_id=1, source_target_pairs={{0,128},{64,192},{128,0},{192,64},{1,129},{65,193},{129,1},{193,65... | collective-permute-start | bytes 663560 | tf_op jit(solution)/shard_map/ppermute | solution.py:413
  6.5 13.3 %collective-permute-start = (f32[48,1152]{1,0:T(8,128)}, f32[48,1152]{1,0:T(8,128)S(1)}, u32[]{:S(2)}, u32[]{:S(2)}) collective-permute-start(f32[48,1152]{1,0:T(8,128)} %bitcast.12), channel_id=1, source_target_pairs={{0,64},{64,128},{128,192},{192,0},{1,65},{65,129},{129,193},{193,1... | collective-permute-start | bytes 663560 | tf_op jit(solution)/shard_map/ppermute | solution.py:413
  7.2 15.3 %collective-permute-start.5 = (f32[48,1152]{1,0:T(8,128)}, f32[48,1152]{1,0:T(8,128)S(1)}, u32[]{:S(2)}, u32[]{:S(2)}) collective-permute-start(f32[48,1152]{1,0:T(8,128)} %bitcast.13), channel_id=1, source_target_pairs={{0,8},{8,0},{1,9},{9,1},{2,10},{10,2},{3,11},{11,3},{4,12},{12,4},... | collective-permute-start | bytes 663560 | tf_op jit(solution)/shard_map/ppermute | solution.py:413
  8.9 0.9 %copy-start.6 = (bf16[48,2304]{1,0:T(8,128)(2,1)S(1)}, bf16[48,2304]{1,0:T(8,128)(2,1)}, u32[]{:S(2)}) copy-start(bf16[48,2304]{1,0:T(8,128)(2,1)} %matrix_ref.1) | copy-start | bytes 663556
  11.7 5.2 %collective-permute-start.4 = (s32[24,576]{1,0:T(8,128)S(1)}, s32[24,576]{1,0:T(8,128)S(1)}, u32[]{:S(2)}, u32[]{:S(2)}) collective-permute-start(s32[24,576]{1,0:T(8,128)S(1)} %pad_add_fusion.refs_0_), channel_id=1, source_target_pairs={{0,32},{16,48},{32,0},{48,16},{1,33},{17,49},{33,1},{49,17},{2,34}... | collective-permute-start | bytes 165896 | tf_op jit(solution)/shard_map/ppermute | solution.py:413
  19.8 6.6 %collective-permute-start.6 = (f32[48,1152]{1,0:T(8,128)S(1)}, f32[48,1152]{1,0:T(8,128)S(1)}, u32[]{:S(2)}, u32[]{:S(2)}) collective-permute-start(f32[48,1152]{1,0:T(8,128)S(1)} %collective-permute-done.refs_4_), channel_id=1, source_target_pairs={{0,8},{8,0},{1,9},{9,1},{2,10},{10,2},{3,11},{11,3},{4,12},{12,4},... | collective-permute-start | bytes 663560 | tf_op jit(solution)/shard_map/ppermute | solution.py:413
  20.3 6.1 %collective-permute-start.7 = (f32[48,1152]{1,0:T(8,128)S(1)}, f32[48,1152]{1,0:T(8,128)S(1)}, u32[]{:S(2)}, u32[]{:S(2)}) collective-permute-start(f32[48,1152]{1,0:T(8,128)S(1)} %collective-permute-done.2.refs_6_), channel_id=1, source_target_pairs={{0,8},{8,0},{1,9},{9,1},{2,10},{10,2},{3,11},{11,3},{4,12},{12,4},... | collective-permute-start | bytes 663560 | tf_op jit(solution)/shard_map/ppermute | solution.py:413
  20.3 6.1 %collective-permute-start.8 = (f32[48,1152]{1,0:T(8,128)S(1)}, f32[48,1152]{1,0:T(8,128)S(1)}, u32[]{:S(2)}, u32[]{:S(2)}) collective-permute-start(f32[48,1152]{1,0:T(8,128)S(1)} %collective-permute-done.1.refs_8_), channel_id=1, source_target_pairs={{0,8},{8,0},{1,9},{9,1},{2,10},{10,2},{3,11},{11,3},{4,12},{12,4},... | collective-permute-start | bytes 663560 | tf_op jit(solution)/shard_map/ppermute | solution.py:413
  20.8 19.3 %collective-permute-start.12 = (f32[48,1024]{1,0:T(8,128)}, f32[48,1024]{1,0:T(8,128)S(1)}, u32[]{:S(2)}, u32[]{:S(2)}) collective-permute-start(f32[48,1024]{1,0:T(8,128)} %get-tuple-element.89.refs_3_), channel_id=1, source_target_pairs={{0,1},{1,2},{2,3},{3,4},{4,5},{5,6},{6,7},{7,0},{8,9},{9,10},{10,1... | collective-permute-start | bytes 589832 | tf_op jit(solution)/shard_map/ppermute | solution.py:413
  22.5 17.7 %collective-permute-start.13 = (f32[48,1024]{1,0:T(8,128)}, f32[48,1024]{1,0:T(8,128)S(1)}, u32[]{:S(2)}, u32[]{:S(2)}) collective-permute-start(f32[48,1024]{1,0:T(8,128)} %get-tuple-element.90.refs_0_), channel_id=1, source_target_pairs={{0,7},{1,0},{2,1},{3,2},{4,3},{5,4},{6,5},{7,6},{8,15},{9,8},{10,9... | collective-permute-start | bytes 589832 | tf_op jit(solution)/shard_map/ppermute | solution.py:413
  26.4 0.9 %copy-start = (f32[48,1152]{1,0:T(8,128)S(1)}, f32[48,1152]{1,0:T(8,128)}, u32[]{:S(2)}) copy-start(f32[48,1152]{1,0:T(8,128)} %get-tuple-element.80.refs_2_.refs_0_.coarse_ref) | copy-start | bytes 663556
  29.2 8.0 %collective-permute-start.9 = (f32[48,640]{1,0:T(8,128)S(1)}, f32[48,640]{1,0:T(8,128)S(1)}, u32[]{:S(2)}, u32[]{:S(2)}) collective-permute-start(f32[48,640]{1,0:T(8,128)S(1)} %get-tuple-element.87), channel_id=1, source_target_pairs={{0,32},{16,48},{32,0},{48,16},{1,33},{17,49},{33,1},{49,17},{2,34}... | collective-permute-start | bytes 368648 | tf_op jit(solution)/shard_map/ppermute | solution.py:413
  32.1 8.1 %copy-start.2 = (f32[48,1024]{1,0:T(8,128)S(1)}, f32[48,1024]{1,0:T(8,128)}, u32[]{:S(2)}) copy-start(f32[48,1024]{1,0:T(8,128)} %get-tuple-element.90.refs_0_) | copy-start | bytes 589828
  32.1 8.1 %copy-start.3 = (f32[48,1024]{1,0:T(8,128)S(1)}, f32[48,1024]{1,0:T(8,128)}, u32[]{:S(2)}) copy-start(f32[48,1024]{1,0:T(8,128)} %get-tuple-element.92.refs_1_) | copy-start | bytes 589828
  32.1 8.1 %copy-start.4 = (f32[48,1024]{1,0:T(8,128)S(1)}, f32[48,1024]{1,0:T(8,128)}, u32[]{:S(2)}) copy-start(f32[48,1024]{1,0:T(8,128)} %get-tuple-element.93.refs_2_) | copy-start | bytes 589828
  32.1 8.1 %copy-start.5 = (f32[48,1024]{1,0:T(8,128)S(1)}, f32[48,1024]{1,0:T(8,128)}, u32[]{:S(2)}) copy-start(f32[48,1024]{1,0:T(8,128)} %get-tuple-element.89.refs_3_) | copy-start | bytes 589828
  33.8 8.7 %copy-start.7 = (s32[1,8]{1,0:T(1,128)S(1)}, s32[1,8]{1,0:T(1,128)}, u32[]{:S(2)}) copy-start(s32[1,8]{1,0:T(1,128)} %levels_ref.3) | copy-start | bytes 100
  33.8 8.7 %copy-start.8 = (f32[48]{0:T(128)S(1)}, f32[48]{0:T(128)}, u32[]{:S(2)}) copy-start(f32[48]{0:T(128)} %param.9) | copy-start | bytes 580
  33.8 6.3 %collective-permute-start.10 = (f32[48,640]{1,0:T(8,128)S(1)}, f32[48,640]{1,0:T(8,128)S(1)}, u32[]{:S(2)}, u32[]{:S(2)}) collective-permute-start(f32[48,640]{1,0:T(8,128)S(1)} %gather_one.1), channel_id=1, source_target_pairs={{0,48},{16,0},{32,16},{48,32},{1,49},{17,1},{33,17},{49,33},{2,50}... | collective-permute-start | bytes 368648 | tf_op jit(solution)/shard_map/ppermute | solution.py:413
  36.7 5.8 %collective-permute-start.11 = (f32[48,640]{1,0:T(8,128)S(1)}, f32[48,640]{1,0:T(8,128)S(1)}, u32[]{:S(2)}, u32[]{:S(2)}) collective-permute-start(f32[48,640]{1,0:T(8,128)S(1)} %gather_three.1), channel_id=1, source_target_pairs={{0,16},{16,32},{32,48},{48,0},{1,17},{17,33},{33,49},{49,1},{2,18}... | collective-permute-start | bytes 368648 | tf_op jit(solution)/shard_map/ppermute | solution.py:413
  37.2 5.3 %collective-permute-start.14 = (s32[4,576]{1,0:T(4,128)S(1)}, s32[4,576]{1,0:T(4,128)S(1)}, u32[]{:S(2)}, u32[]{:S(2)}) collective-permute-start(s32[4,576]{1,0:T(4,128)S(1)} %get-tuple-element.88.request_ref.request_a), channel_id=1, source_target_pairs={{0,8},{8,0},{1,9},{9,1},{2,10},{10,2},{3,11},{11,3},{4,12},{12,4},... | collective-permute-start | bytes 27656 | tf_op jit(solution)/shard_map/ppermute | solution.py:413
  44.3 12.0 %collective-permute-start.15 = (f32[48,1024]{1,0:T(8,128)S(1)}, f32[48,1024]{1,0:T(8,128)S(1)}, u32[]{:S(2)}, u32[]{:S(2)}) collective-permute-start(f32[48,1024]{1,0:T(8,128)S(1)} %get-tuple-element.109.refs_3_), channel_id=1, source_target_pairs={{0,1},{1,2},{2,3},{3,4},{4,5},{5,6},{6,7},{7,0},{8,9},{9,10},{10,1... | collective-permute-start | bytes 589832 | tf_op jit(solution)/shard_map/ppermute | solution.py:413
  44.4 8.6 %collective-permute-start.19 = (f32[48,640]{1,0:T(8,128)S(1)}, f32[48,640]{1,0:T(8,128)S(1)}, u32[]{:S(2)}, u32[]{:S(2)}) collective-permute-start(f32[48,640]{1,0:T(8,128)S(1)} %get-tuple-element.116.refs_0_), channel_id=1, source_target_pairs={{0,48},{16,0},{32,16},{48,32},{1,49},{17,1},{33,17},{49,33},{2,50}... | collective-permute-start | bytes 368648 | tf_op jit(solution)/shard_map/ppermute | solution.py:413
  46.7 7.5 %collective-permute-start.18 = (f32[48,640]{1,0:T(8,128)S(1)}, f32[48,640]{1,0:T(8,128)S(1)}, u32[]{:S(2)}, u32[]{:S(2)}) collective-permute-start(f32[48,640]{1,0:T(8,128)S(1)} %get-tuple-element.116.refs_0_), channel_id=1, source_target_pairs={{0,32},{16,48},{32,0},{48,16},{1,33},{17,49},{33,1},{49,17},{2,34}... | collective-permute-start | bytes 368648 | tf_op jit(solution)/shard_map/ppermute | solution.py:413
  46.7 8.8 %collective-permute-start.17 = (f32[48,640]{1,0:T(8,128)S(1)}, f32[48,640]{1,0:T(8,128)S(1)}, u32[]{:S(2)}, u32[]{:S(2)}) collective-permute-start(f32[48,640]{1,0:T(8,128)S(1)} %get-tuple-element.116.refs_0_), channel_id=1, source_target_pairs={{0,16},{16,32},{32,48},{48,0},{1,17},{17,33},{33,49},{49,1},{2,18}... | collective-permute-start | bytes 368648 | tf_op jit(solution)/shard_map/ppermute | solution.py:413
  47.4 9.4 %collective-permute-start.16 = (f32[48,1024]{1,0:T(8,128)S(1)}, f32[48,1024]{1,0:T(8,128)S(1)}, u32[]{:S(2)}, u32[]{:S(2)}) collective-permute-start(f32[48,1024]{1,0:T(8,128)S(1)} %get-tuple-element.110.refs_0_), channel_id=1, source_target_pairs={{0,7},{1,0},{2,1},{3,2},{4,3},{5,4},{6,5},{7,6},{8,15},{9,8},{10,9... | collective-permute-start | bytes 589832 | tf_op jit(solution)/shard_map/ppermute | solution.py:413
  53.0 3.8 %collective-permute-start.20 = (f32[48,640]{1,0:T(8,128)S(1)}, f32[48,640]{1,0:T(8,128)S(1)}, u32[]{:S(2)}, u32[]{:S(2)}) collective-permute-start(f32[48,640]{1,0:T(8,128)S(1)} %get-tuple-element.116.refs_0_), channel_id=1, source_target_pairs={{0,8},{8,0},{1,9},{9,1},{2,10},{10,2},{3,11},{11,3},{4,12},{12,4},... | collective-permute-start | bytes 368648 | tf_op jit(solution)/shard_map/ppermute | solution.py:413
  55.5 1.8 %collective-permute-start.21 = (f32[48,640]{1,0:T(8,128)S(1)}, f32[48,640]{1,0:T(8,128)S(1)}, u32[]{:S(2)}, u32[]{:S(2)}) collective-permute-start(f32[48,640]{1,0:T(8,128)S(1)} %collective-permute-done.17.refs_1_), channel_id=1, source_target_pairs={{0,8},{8,0},{1,9},{9,1},{2,10},{10,2},{3,11},{11,3},{4,12},{12,4},... | collective-permute-start | bytes 368648 | tf_op jit(solution)/shard_map/ppermute | solution.py:413
  56.3 1.3 %collective-permute-start.22 = (f32[48,640]{1,0:T(8,128)S(1)}, f32[48,640]{1,0:T(8,128)S(1)}, u32[]{:S(2)}, u32[]{:S(2)}) collective-permute-start(f32[48,640]{1,0:T(8,128)S(1)} %collective-permute-done.18.refs_2_), channel_id=1, source_target_pairs={{0,8},{8,0},{1,9},{9,1},{2,10},{10,2},{3,11},{11,3},{4,12},{12,4},... | collective-permute-start | bytes 368648 | tf_op jit(solution)/shard_map/ppermute | solution.py:413
  56.3 1.5 %collective-permute-start.23 = (f32[48,640]{1,0:T(8,128)S(1)}, f32[48,640]{1,0:T(8,128)S(1)}, u32[]{:S(2)}, u32[]{:S(2)}) collective-permute-start(f32[48,640]{1,0:T(8,128)S(1)} %collective-permute-done.19.refs_3_), channel_id=1, source_target_pairs={{0,8},{8,0},{1,9},{9,1},{2,10},{10,2},{3,11},{11,3},{4,12},{12,4},... | collective-permute-start | bytes 368648 | tf_op jit(solution)/shard_map/ppermute | solution.py:413
  60.8 9.6 %collective-permute-start.25 = (f32[48,1152]{1,0:T(8,128)S(1)}, f32[48,1152]{1,0:T(8,128)S(1)}, u32[]{:S(2)}, u32[]{:S(2)}) collective-permute-start(f32[48,1152]{1,0:T(8,128)S(1)} %scatter_far.1), channel_id=1, source_target_pairs={{0,128},{64,192},{128,0},{192,64},{1,129},{65,193},{129,1},{193,65... | collective-permute-start | bytes 663560 | tf_op jit(solution)/shard_map/ppermute | solution.py:413
  66.6 3.8 %copy-start.1 = (f32[48,1152]{1,0:T(8,128)S(1)}, f32[48,1152]{1,0:T(8,128)}, u32[]{:S(2)}) copy-start(f32[48,1152]{1,0:T(8,128)} %get-tuple-element.80.refs_2_.refs_0_.coarse_ref) | copy-start | bytes 663556
  66.6 6.4 %collective-permute-start.26 = (f32[48,1152]{1,0:T(8,128)S(1)}, f32[48,1152]{1,0:T(8,128)S(1)}, u32[]{:S(2)}, u32[]{:S(2)}) collective-permute-start(f32[48,1152]{1,0:T(8,128)S(1)} %get-tuple-element.123), channel_id=1, source_target_pairs={{0,192},{64,0},{128,64},{192,128},{1,193},{65,1},{129,65},{193,129... | collective-permute-start | bytes 663560 | tf_op jit(solution)/shard_map/ppermute | solution.py:413
  67.7 7.2 %collective-permute-start.24 = (f32[48,1152]{1,0:T(8,128)S(1)}, f32[48,1152]{1,0:T(8,128)S(1)}, u32[]{:S(2)}, u32[]{:S(2)}) collective-permute-start(f32[48,1152]{1,0:T(8,128)S(1)} %get-tuple-element.122), channel_id=1, source_target_pairs={{0,64},{64,128},{128,192},{192,0},{1,65},{65,129},{129,193},{193,1... | collective-permute-start | bytes 663560 | tf_op jit(solution)/shard_map/ppermute | solution.py:413

commit v8 on v7

--- a/solution.py
+++ b/solution.py
@@ -14,7 +14,7 @@
 STEP = 0.25
 FOLDED = 1280
 MIB = 1024 * 1024
-LIMIT = 60
+LIMIT = 53
 SPREAD = 24
 COST = pl.CostEstimate(flops=0, bytes_accessed=0, transcendentals=0)
 
@@ -433,7 +433,8 @@
     requests = [requests, shifted(requests, "y", 2)]
     planes, held_coarse = split_planes(fine, after(coarse, (folded, requests[0])))
     below_plane, above_plane = shifted(planes[3], "box", 1), shifted(planes[0], "box", 7)
-    far, requests, held_coarse = lax.optimization_barrier((far, requests, held_coarse))
+    growth = coagulate(after(folded, held_coarse), planes, "coagulate_fine")
+    far, requests, growth = lax.optimization_barrier((far, requests, growth))
 
     sources, shifts = [held_coarse, mate], [(0, False), (0, True)]
     for k in (1, 3, 2):
@@ -447,9 +448,9 @@
     part[3] = gather_next(after(request_rows, part[1]), rows, shifts, 3, "gather_three")
     strips[3] = shifted(part[3], "y", 1)
     strips[0] = gather_next(after(request_rows, (part[3], strips[2])), rows, shifts, 0, "gather_own")
-    growth = coagulate(after(folded, (strips[0], strips[1], below_plane, above_plane)), planes, "coagulate_fine")
+    coarse_growth = coagulate(after(folded, (strips[0], strips[1])), [held_coarse], "coagulate_coarse")[0]
     mate_rows = shifted(request_rows, "core", 1)
-    strips, growth, mate_rows = lax.optimization_barrier((strips, growth, mate_rows))
+    strips, coarse_growth, mate_rows = lax.optimization_barrier((strips, coarse_growth, mate_rows))
     strips = [strips[k] for k in range(4)]
 
     middle, base, registers, x_ghosts, y_ghosts = first_stage(
@@ -469,9 +470,8 @@
     sent[2] = shifted(part, "x", 2)
     parts = scatter_columns([request_rows, mate_rows], after(cells, part), held, (1, 3, 0), "scatter_near")
     sent[1], sent[3], sent[0] = shifted(parts[0], "x", 1), shifted(parts[1], "x", 3), parts[2]
-    base = after(base, parts[0])
+    base = after(base, (parts[0], sent[2]))
     fine_out = second_stage(levels, row, middle, base, growth, x_ghosts, y_ghosts, below_plane, above_plane)
-    coarse_growth = coagulate(after(folded, (fine_out, sent[2])), [held_coarse], "coagulate_coarse")[0]
     sent = [sent[k] for k in range(4)]
     sent, fine_out, coarse_growth = lax.optimization_barrier((sent, fine_out, coarse_growth))
     coarse_out = finish_coarse(held_coarse, coarse_growth, sent)

time: 76.3 us -> 75.2 us (0.986)
  waiting for transfers between devices: 9.17 us -> 7.59 us
    ppermute x27, waiting for transfers between devices: 9.17 us -> 7.59 us  [shifted(): lax.ppermute(value, axis, [(i, (i + shift) % size) for i in range(size)])]
    unnamed x18 -> x10, local copies, waits for them, and re-layouts: 1.9 us -> 1.89 us
  transfers between devices with their start and end apart: 27 -> 27, of which waited for: 8 -> 8; matrix products, arithmetic and copies ran while one was open for 0% -> 0% of each run, Pallas kernels for 32% -> 33%
where the time goes in v8:
time: 75.2 us; the launch traced here: 73.9 us
  starting transfers between devices  32.9 us (44%)
  Pallas kernels  29.8 us (40%)
  waiting for transfers between devices  7.59 us (10%)
  local copies, waits for them, and re-layouts  1.9 us (3%)
  between operations  0.92 us (1%)
    ppermute x27, starting transfers between devices, shifted(): lax.ppermute(value, axis, [(i, (i + shift) % size) for i in range(size)])  32.9 us
    pallas_call x13, Pallas kernels, call(): pl.pallas_call(kernel, out_shape=out_shape, in_specs=in_specs, out_specs=...  25.6 us
    ppermute x27, waiting for transfers between devices, shifted(): lax.ppermute(value, axis, [(i, (i + shift) % size) for i in range(size)])  7.59 us
    pallas_call x1, Pallas kernels, second_stage(): pl.pallas_call(kernel, out_shape=sds(S, X, PLANE), in_specs=[SMEM] + [VME...  2.22 us
    pallas_call x1, Pallas kernels, split_planes(): pl.pallas_call(kernel, out_shape=[sds(S, PLANE)] * X + [sds(S, CELLS)], i...  2.02 us
    unnamed x10, local copies, waits for them, and re-layouts  1.89 us
  transfers between devices with their start and end apart: 27, of which 8 were waited for; matrix products, arithmetic and copies ran while one was open for 0% of the time, Pallas kernels for 33%

profile of v8, /device:TPU:1, one launch (start us, length us, event | category | flops | bytes accessed | tf_op | source)
XLA Modules:
  0.0 73.9 jit_solution(18186742365457508177)
XLA Ops:
  0.6 0.7 reduce
  1.3 2.2 %collective-permute-start.3 = (s32[24,576]{1,0:T(8,128)S(1)}, s32[24,576]{1,0:T(8,128)S(1)}, u32[]{:S(2)}, u32[]{:S(2)}) collective-permute-start(s32[24,576]{1,0:T(8,128)S(1)} %add.8), channel_id=1, source_target_pairs={{0,16},{16,32},{32,48},{48,0},{1,17},{17,33},{33,49},{49,1},{2,18}... | collective-permute-start | bytes 165896 | tf_op jit(solution)/shard_map/ppermute | solution.py:413
  3.5 2.5 %collective-permute-start.2 = (f32[48,1152]{1,0:T(8,128)}, f32[48,1152]{1,0:T(8,128)S(1)}, u32[]{:S(2)}, u32[]{:S(2)}) collective-permute-start(f32[48,1152]{1,0:T(8,128)} %bitcast.10), channel_id=1, source_target_pairs={{0,192},{64,0},{128,64},{192,128},{1,193},{65,1},{129,65},{193,129... | collective-permute-start | bytes 663560 | tf_op jit(solution)/shard_map/ppermute | solution.py:413
  6.0 0.5 collective-permute-start.1
  6.5 0.6 collective-permute-start
  7.2 1.8 %collective-permute-start.5 = (f32[48,1152]{1,0:T(8,128)}, f32[48,1152]{1,0:T(8,128)S(1)}, u32[]{:S(2)}, u32[]{:S(2)}) collective-permute-start(f32[48,1152]{1,0:T(8,128)} %bitcast.13), channel_id=1, source_target_pairs={{0,8},{8,0},{1,9},{9,1},{2,10},{10,2},{3,11},{11,3},{4,12},{12,4},... | collective-permute-start | bytes 663560 | tf_op jit(solution)/shard_map/ppermute | solution.py:413
  9.0 0.9 %copy-done.2 = bf16[48,2304]{1,0:T(8,128)(2,1)S(1)} copy-done((bf16[48,2304]{1,0:T(8,128)(2,1)S(1)}, bf16[48,2304]{1,0:T(8,128)(2,1)}, u32[]{:S(2)}) %copy-start.2) | copy-done | bytes 221208
  9.9 1.8 %fold_kernel.1.matrix_ref = bf16[96,1280]{1,0:T(8,128)(2,1)S(1)} custom-call(bf16[48,2304]{1,0:T(8,128)(2,1)S(1)} %copy-done.2), custom_call_target="tpu_custom_call" | custom-call | tf_op jit(solution)/shard_map/fold_kernel/pallas_call | solution.py:34
  11.7 2.7 %collective-permute-start.4 = (s32[24,576]{1,0:T(8,128)S(1)}, s32[24,576]{1,0:T(8,128)S(1)}, u32[]{:S(2)}, u32[]{:S(2)}) collective-permute-start(s32[24,576]{1,0:T(8,128)S(1)} %pad_add_fusion.refs_0_), channel_id=1, source_target_pairs={{0,32},{16,48},{32,0},{48,16},{1,33},{17,49},{33,1},{49,17},{2,34}... | collective-permute-start | bytes 165896 | tf_op jit(solution)/shard_map/ppermute | solution.py:413
  14.4 2.0 %split_planes.1 = (f32[48,1024]{1,0:T(8,128)S(1)}, f32[48,1024]{1,0:T(8,128)S(1)}, f32[48,1024]{1,0:T(8,128)S(1)}, f32[48,1024]{1,0:T(8,128)S(1)}, f32[48,1152]{1,0:T(8,128)}) custom-call(f32[48,4,1024]{2,1,0:T(4,128)} %bitcast.7, f32[48,1152]{1,0:T(8,128)} %bitcast.14), custom_call_target="tpu_custom_call" | custom-call | tf_op jit(solution)/shard_map/split_planes/pallas_call | solution.py:107
  16.5 2.2 %coagulate_fine.1 = (f32[48,1024]{1,0:T(8,128)S(1)}, f32[48,1024]{1,0:T(8,128)S(1)}, f32[48,1024]{1,0:T(8,128)S(1)}, f32[48,1024]{1,0:T(8,128)S(1)}) custom-call(bf16[96,1280]{1,0:T(8,128)(2,1)S(1)} %fold_kernel.1.matrix_ref, f32[48,1024]{1,0:T(8,128)S(1)} %get-tuple-element.79.refs_0_, f32[48,1024]{1,0:T(8,128)S(1)} %get-tuple-element.80.refs_1_, ...), custom_call_target="tpu_custom_call" | custom-call | tf_op jit(solution)/shard_map/coagulate_fine/pallas_call | solution.py:34
  18.7 1.1 %collective-permute-done.refs_4_ = f32[48,1152]{1,0:T(8,128)S(1)} collective-permute-done((f32[48,1152]{1,0:T(8,128)}, f32[48,1152]{1,0:T(8,128)S(1)}, u32[]{:S(2)}, u32[]{:S(2)}) %collective-permute-start) | collective-permute-done | bytes 221216 | tf_op jit(solution)/shard_map/ppermute | solution.py:413
  19.8 0.5 collective-permute-start.6
  20.3 0.5 collective-permute-start.8
  20.8 5.6 %collective-permute-start.14 = (f32[48,1024]{1,0:T(8,128)S(1)}, f32[48,1024]{1,0:T(8,128)S(1)}, u32[]{:S(2)}, u32[]{:S(2)}) collective-permute-start(f32[48,1024]{1,0:T(8,128)S(1)} %get-tuple-element.79.refs_0_), channel_id=1, source_target_pairs={{0,7},{1,0},{2,1},{3,2},{4,3},{5,4},{6,5},{7,6},{8,15},{9,8},{10,9... | collective-permute-start | bytes 589832 | tf_op jit(solution)/shard_map/ppermute | solution.py:413
  26.5 0.9 %copy-done = f32[48,1152]{1,0:T(8,128)S(1)} copy-done((f32[48,1152]{1,0:T(8,128)S(1)}, f32[48,1152]{1,0:T(8,128)}, u32[]{:S(2)}) %copy-start) | copy-done | bytes 221208
  27.4 1.8 %gather_first.1 = (f32[48,640]{1,0:T(8,128)S(1)}, bf16[768,1152]{1,0:T(8,128)(2,1)S(1)}, s32[4,576]{1,0:T(4,128)S(1)}) custom-call(s32[24,576]{1,0:T(8,128)S(1)} %pad_add_fusion.refs_0_, s32[24,576]{1,0:T(8,128)S(1)} %collective-permute-done.4.refs_1_, f32[48,1152]{1,0:T(8,128)S(1)} %copy-done, f32[48,1152]{1,0:T(8,128)S(1)} %collective-permute-done.5.refs_3_, ...), custom_call_target="tpu_custom_call" | custom-call | tf_op jit(solution)/shard_map/gather_first/pallas_call | solution.py:34
  29.2 2.7 %collective-permute-start.9 = (f32[48,640]{1,0:T(8,128)S(1)}, f32[48,640]{1,0:T(8,128)S(1)}, u32[]{:S(2)}, u32[]{:S(2)}) collective-permute-start(f32[48,640]{1,0:T(8,128)S(1)} %get-tuple-element.95), channel_id=1, source_target_pairs={{0,32},{16,48},{32,0},{48,16},{1,33},{17,49},{33,1},{49,17},{2,34}... | collective-permute-start | bytes 368648 | tf_op jit(solution)/shard_map/ppermute | solution.py:413
  31.9 1.7 %gather_one.1 = f32[48,640]{1,0:T(8,128)S(1)} custom-call(s32[4,576]{1,0:T(4,128)S(1)} %get-tuple-element.96.request_ref.request_a, bf16[768,1152]{1,0:T(8,128)(2,1)S(1)} %get-tuple-element.93.rows_ref), custom_call_target="tpu_custom_call" | custom-call | tf_op jit(solution)/shard_map/gather_one/pallas_call | solution.py:34
  33.6 1.1 %collective-permute-start.10 = (f32[48,640]{1,0:T(8,128)S(1)}, f32[48,640]{1,0:T(8,128)S(1)}, u32[]{:S(2)}, u32[]{:S(2)}) collective-permute-start(f32[48,640]{1,0:T(8,128)S(1)} %gather_one.1), channel_id=1, source_target_pairs={{0,48},{16,0},{32,16},{48,32},{1,49},{17,1},{33,17},{49,33},{2,50}... | collective-permute-start | bytes 368648 | tf_op jit(solution)/shard_map/ppermute | solution.py:413
  34.8 1.7 %gather_three.1 = f32[48,640]{1,0:T(8,128)S(1)} custom-call(s32[4,576]{1,0:T(4,128)S(1)} %get-tuple-element.96.request_ref.request_a, bf16[768,1152]{1,0:T(8,128)(2,1)S(1)} %get-tuple-element.93.rows_ref), custom_call_target="tpu_custom_call" | custom-call | tf_op jit(solution)/shard_map/gather_three/pallas_call | solution.py:34
  36.5 0.5 collective-permute-start.11
  37.0 1.1 %collective-permute-start.12 = (s32[4,576]{1,0:T(4,128)S(1)}, s32[4,576]{1,0:T(4,128)S(1)}, u32[]{:S(2)}, u32[]{:S(2)}) collective-permute-start(s32[4,576]{1,0:T(4,128)S(1)} %get-tuple-element.96.request_ref.request_a), channel_id=1, source_target_pairs={{0,8},{8,0},{1,9},{9,1},{2,10},{10,2},{3,11},{11,3},{4,12},{12,4},... | collective-permute-start | bytes 27656 | tf_op jit(solution)/shard_map/ppermute | solution.py:413
  38.1 1.7 %gather_own.1.refs_8_ = f32[48,640]{1,0:T(8,128)S(1)} custom-call(s32[4,576]{1,0:T(4,128)S(1)} %get-tuple-element.96.request_ref.request_a, bf16[768,1152]{1,0:T(8,128)(2,1)S(1)} %get-tuple-element.93.rows_ref), custom_call_target="tpu_custom_call" | custom-call | tf_op jit(solution)/shard_map/gather_own/pallas_call | solution.py:34
  39.9 0.7 coagulate_coarse.1.growth_ref
  40.6 0.9 %collective-permute-done.11.refs_11_ = f32[48,640]{1,0:T(8,128)S(1)} collective-permute-done((f32[48,640]{1,0:T(8,128)S(1)}, f32[48,640]{1,0:T(8,128)S(1)}, u32[]{:S(2)}, u32[]{:S(2)}) %collective-permute-start.11) | collective-permute-done | bytes 122912 | tf_op jit(solution)/shard_map/ppermute | solution.py:413
  41.6 1.8 %first_stage.1 = (f32[48,1024]{1,0:T(8,128)S(1)}, f32[48,1024]{1,0:T(8,128)S(1)}, f32[48,1024]{1,0:T(8,128)S(1)}, f32[48,1024]{1,0:T(8,128)S(1)}, f32[48,1024]{1...) custom-call(s32[1,8]{1,0:T(1,128)S(1)} %copy-done.3, ...), custom_call_target="tpu_custom_call" | custom-call | tf_op jit(solution)/shard_map/first_stage/pallas_call | solution.py:34
  43.4 1.5 %collective-permute-start.19 = (f32[48,640]{1,0:T(8,128)S(1)}, f32[48,640]{1,0:T(8,128)S(1)}, u32[]{:S(2)}, u32[]{:S(2)}) collective-permute-start(f32[48,640]{1,0:T(8,128)S(1)} %get-tuple-element.116.refs_0_), channel_id=1, source_target_pairs={{0,48},{16,0},{32,16},{48,32},{1,49},{17,1},{33,17},{49,33},{2,50}... | collective-permute-start | bytes 368648 | tf_op jit(solution)/shard_map/ppermute | solution.py:413
  44.9 0.7 collective-permute-start.17
  45.6 2.9 %collective-permute-start.16 = (f32[48,1024]{1,0:T(8,128)S(1)}, f32[48,1024]{1,0:T(8,128)S(1)}, u32[]{:S(2)}, u32[]{:S(2)}) collective-permute-start(f32[48,1024]{1,0:T(8,128)S(1)} %get-tuple-element.110.refs_0_), channel_id=1, source_target_pairs={{0,7},{1,0},{2,1},{3,2},{4,3},{5,4},{6,5},{7,6},{8,15},{9,8},{10,9... | collective-permute-start | bytes 589832 | tf_op jit(solution)/shard_map/ppermute | solution.py:413
  48.5 0.9 %cells_by_row.1.cell_ref = s32[5120,128]{1,0:T(8,128)S(1)} custom-call(s32[4,576]{1,0:T(4,128)S(1)} %get-tuple-element.96.request_ref.request_a, s32[4,576]{1,0:T(4,128)S(1)} %collective-permute-done.12.request_b), custom_call_target="tpu_custom_call" | custom-call | tf_op jit(solution)/shard_map/cells_by_row/pallas_call | solution.py:34
  49.4 2.3 %coagulate_middle.1 = (f32[48,1024]{1,0:T(8,128)S(1)}, f32[48,1024]{1,0:T(8,128)S(1)}, f32[48,1024]{1,0:T(8,128)S(1)}, f32[48,1024]{1,0:T(8,128)S(1)}) custom-call(bf16[96,1280]{1,0:T(8,128)(2,1)S(1)} %fold_kernel.1.matrix_ref, f32[48,1024]{1,0:T(8,128)S(1)} %get-tuple-element.110.refs_0_, f32[48,1024]{1,0:T(8,128)S(1)} %get-tuple-element.113.refs_1_, ...), custom_call_target="tpu_custom_call" | custom-call | tf_op jit(solution)/shard_map/coagulate_middle/pallas_call | solution.py:34
  51.7 2.3 %collective-permute-start.20 = (f32[48,640]{1,0:T(8,128)S(1)}, f32[48,640]{1,0:T(8,128)S(1)}, u32[]{:S(2)}, u32[]{:S(2)}) collective-permute-start(f32[48,640]{1,0:T(8,128)S(1)} %get-tuple-element.116.refs_0_), channel_id=1, source_target_pairs={{0,8},{8,0},{1,9},{9,1},{2,10},{10,2},{3,11},{11,3},{4,12},{12,4},... | collective-permute-start | bytes 368648 | tf_op jit(solution)/shard_map/ppermute | solution.py:413
  54.1 0.4 collective-permute-start.21
  54.6 0.4 collective-permute-start.23
  55.0 0.4 collective-permute-done.21.refs_5_
  55.5 0.4 collective-permute-done.22.refs_6_
  55.8 0.2 collective-permute-done.23.refs_7_
  56.0 2.9 %scatter_far.1 = f32[48,1152]{1,0:T(8,128)S(1)} custom-call(s32[4,576]{1,0:T(4,128)S(1)} %get-tuple-element.96.request_ref.request_a, s32[4,576]{1,0:T(4,128)S(1)} %collective-permute-done.12.request_b, s32[5120,128]{1,0:T(8,128)S(1)} %cells_by_row.1.cell_ref, f32[48,640]{1,0:T(8,128)S(1)} %get-tuple-element.116.refs_0_, ...), custom_call_target="tpu_custom_call" | custom-call | tf_op jit(solution)/shard_map/scatter_far/pallas_call | solution.py:34
  58.9 0.6 collective-permute-start.25
  59.5 5.3 %scatter_near.1 = (f32[48,1152]{1,0:T(8,128)S(1)}, f32[48,1152]{1,0:T(8,128)S(1)}, f32[48,1152]{1,0:T(8,128)S(1)}) custom-call(s32[4,576]{1,0:T(4,128)S(1)} %get-tuple-element.96.request_ref.request_a, s32[4,576]{1,0:T(4,128)S(1)} %collective-permute-done.12.request_b, s32[5120,128]{1,0:T(8,128)S(1)} %cells_by_row.1.cell_ref, ...), custom_call_target="tpu_custom_call" | custom-call | tf_op jit(solution)/shard_map/scatter_near/pallas_call | solution.py:34
  64.8 1.1 %collective-permute-start.26 = (f32[48,1152]{1,0:T(8,128)S(1)}, f32[48,1152]{1,0:T(8,128)S(1)}, u32[]{:S(2)}, u32[]{:S(2)}) collective-permute-start(f32[48,1152]{1,0:T(8,128)S(1)} %get-tuple-element.123), channel_id=1, source_target_pairs={{0,192},{64,0},{128,64},{192,128},{1,193},{65,1},{129,65},{193,129... | collective-permute-start | bytes 663560 | tf_op jit(solution)/shard_map/ppermute | solution.py:413
  65.9 0.5 collective-permute-start.24
  66.3 0.9 %collective-permute-done.25.c = f32[48,1152]{1,0:T(8,128)S(1)} collective-permute-done((f32[48,1152]{1,0:T(8,128)S(1)}, f32[48,1152]{1,0:T(8,128)S(1)}, u32[]{:S(2)}, u32[]{:S(2)}) %collective-permute-start.25) | collective-permute-done | bytes 221216 | tf_op jit(solution)/shard_map/ppermute | solution.py:413
  67.2 2.2 %second_stage.1 = f32[48,4,1024]{2,1,0:T(4,128)} custom-call(s32[1,8]{1,0:T(1,128)S(1)} %copy-done.3, f32[1,48]{1,0:T(1,128)S(1)} %bitcast.6, f32[48,1024]{1,0:T(8,128)S(1)} %get-tuple-element.110.refs_0_, f32[48,1024]{1,0:T(8,128)S(1)} %get-tuple-element.113.refs_1_, f32[48,1024]{1,0:T(8,128)S(1)} %get-tuple-element.114.refs_2_, ...), custom_call_target="tpu_custom_call" | custom-call | tf_op jit(solution)/shard_map/second_stage/pallas_call | solution.py:391
  69.4 1.8 %collective-permute-done.26.d = f32[48,1152]{1,0:T(8,128)S(1)} collective-permute-done((f32[48,1152]{1,0:T(8,128)S(1)}, f32[48,1152]{1,0:T(8,128)S(1)}, u32[]{:S(2)}, u32[]{:S(2)}) %collective-permute-start.26) | collective-permute-done | bytes 221216 | tf_op jit(solution)/shard_map/ppermute | solution.py:413
  71.2 1.9 %collective-permute-done.24.b = f32[48,1152]{1,0:T(8,128)S(1)} collective-permute-done((f32[48,1152]{1,0:T(8,128)S(1)}, f32[48,1152]{1,0:T(8,128)S(1)}, u32[]{:S(2)}, u32[]{:S(2)}) %collective-permute-start.24) | collective-permute-done | bytes 221216 | tf_op jit(solution)/shard_map/ppermute | solution.py:413
  73.1 0.8 %finish_coarse.1 = f32[48,1152]{1,0:T(8,128)} custom-call(f32[48,1152]{1,0:T(8,128)S(1)} %copy-done.1, f32[48,1152]{1,0:T(8,128)S(1)} %coagulate_coarse.1.growth_ref, f32[48,1152]{1,0:T(8,128)S(1)} %get-tuple-element.142.a, f32[48,1152]{1,0:T(8,128)S(1)} %collective-permute-done.24.b, f32[48,1152]{1,0:T(8,128)S(1)} %collective-permute-done.25.c, ...), custom_call_target="tpu_custom_call" | custom-call | tf_op jit(solution)/shard_map/finish_coarse/pallas_call | solution.py:34
  (36 shorter events, 0.3 us)
Async XLA Ops:
  1.3 10.3 %collective-permute-start.3 = (s32[24,576]{1,0:T(8,128)S(1)}, s32[24,576]{1,0:T(8,128)S(1)}, u32[]{:S(2)}, u32[]{:S(2)}) collective-permute-start(s32[24,576]{1,0:T(8,128)S(1)} %add.8), channel_id=1, source_target_pairs={{0,16},{16,32},{32,48},{48,0},{1,17},{17,33},{33,49},{49,1},{2,18}... | collective-permute-start | bytes 165896 | tf_op jit(solution)/shard_map/ppermute | solution.py:413
  3.5 15.2 %collective-permute-start.2 = (f32[48,1152]{1,0:T(8,128)}, f32[48,1152]{1,0:T(8,128)S(1)}, u32[]{:S(2)}, u32[]{:S(2)}) collective-permute-start(f32[48,1152]{1,0:T(8,128)} %bitcast.10), channel_id=1, source_target_pairs={{0,192},{64,0},{128,64},{192,128},{1,193},{65,1},{129,65},{193,129... | collective-permute-start | bytes 663560 | tf_op jit(solution)/shard_map/ppermute | solution.py:413
  6.0 12.7 %collective-permute-start.1 = (f32[48,1152]{1,0:T(8,128)}, f32[48,1152]{1,0:T(8,128)S(1)}, u32[]{:S(2)}, u32[]{:S(2)}) collective-permute-start(f32[48,1152]{1,0:T(8,128)} %bitcast.11), channel_id=1, source_target_pairs={{0,128},{64,192},{128,0},{192,64},{1,129},{65,193},{129,1},{193,65... | collective-permute-start | bytes 663560 | tf_op jit(solution)/shard_map/ppermute | solution.py:413
  6.5 13.3 %collective-permute-start = (f32[48,1152]{1,0:T(8,128)}, f32[48,1152]{1,0:T(8,128)S(1)}, u32[]{:S(2)}, u32[]{:S(2)}) collective-permute-start(f32[48,1152]{1,0:T(8,128)} %bitcast.12), channel_id=1, source_target_pairs={{0,64},{64,128},{128,192},{192,0},{1,65},{65,129},{129,193},{193,1... | collective-permute-start | bytes 663560 | tf_op jit(solution)/shard_map/ppermute | solution.py:413
  7.2 19.3 %collective-permute-start.5 = (f32[48,1152]{1,0:T(8,128)}, f32[48,1152]{1,0:T(8,128)S(1)}, u32[]{:S(2)}, u32[]{:S(2)}) collective-permute-start(f32[48,1152]{1,0:T(8,128)} %bitcast.13), channel_id=1, source_target_pairs={{0,8},{8,0},{1,9},{9,1},{2,10},{10,2},{3,11},{11,3},{4,12},{12,4},... | collective-permute-start | bytes 663560 | tf_op jit(solution)/shard_map/ppermute | solution.py:413
  8.9 0.9 %copy-start.2 = (bf16[48,2304]{1,0:T(8,128)(2,1)S(1)}, bf16[48,2304]{1,0:T(8,128)(2,1)}, u32[]{:S(2)}) copy-start(bf16[48,2304]{1,0:T(8,128)(2,1)} %matrix_ref.1) | copy-start | bytes 663556
  11.7 7.0 %collective-permute-start.4 = (s32[24,576]{1,0:T(8,128)S(1)}, s32[24,576]{1,0:T(8,128)S(1)}, u32[]{:S(2)}, u32[]{:S(2)}) collective-permute-start(s32[24,576]{1,0:T(8,128)S(1)} %pad_add_fusion.refs_0_), channel_id=1, source_target_pairs={{0,32},{16,48},{32,0},{48,16},{1,33},{17,49},{33,1},{49,17},{2,34}... | collective-permute-start | bytes 165896 | tf_op jit(solution)/shard_map/ppermute | solution.py:413
  19.8 6.6 %collective-permute-start.6 = (f32[48,1152]{1,0:T(8,128)S(1)}, f32[48,1152]{1,0:T(8,128)S(1)}, u32[]{:S(2)}, u32[]{:S(2)}) collective-permute-start(f32[48,1152]{1,0:T(8,128)S(1)} %collective-permute-done.refs_4_), channel_id=1, source_target_pairs={{0,8},{8,0},{1,9},{9,1},{2,10},{10,2},{3,11},{11,3},{4,12},{12,4},... | collective-permute-start | bytes 663560 | tf_op jit(solution)/shard_map/ppermute | solution.py:413
  20.3 6.1 %collective-permute-start.7 = (f32[48,1152]{1,0:T(8,128)S(1)}, f32[48,1152]{1,0:T(8,128)S(1)}, u32[]{:S(2)}, u32[]{:S(2)}) collective-permute-start(f32[48,1152]{1,0:T(8,128)S(1)} %collective-permute-done.2.refs_6_), channel_id=1, source_target_pairs={{0,8},{8,0},{1,9},{9,1},{2,10},{10,2},{3,11},{11,3},{4,12},{12,4},... | collective-permute-start | bytes 663560 | tf_op jit(solution)/shard_map/ppermute | solution.py:413
  20.3 6.1 %collective-permute-start.8 = (f32[48,1152]{1,0:T(8,128)S(1)}, f32[48,1152]{1,0:T(8,128)S(1)}, u32[]{:S(2)}, u32[]{:S(2)}) collective-permute-start(f32[48,1152]{1,0:T(8,128)S(1)} %collective-permute-done.1.refs_8_), channel_id=1, source_target_pairs={{0,8},{8,0},{1,9},{9,1},{2,10},{10,2},{3,11},{11,3},{4,12},{12,4},... | collective-permute-start | bytes 663560 | tf_op jit(solution)/shard_map/ppermute | solution.py:413
  20.8 20.7 %collective-permute-start.14 = (f32[48,1024]{1,0:T(8,128)S(1)}, f32[48,1024]{1,0:T(8,128)S(1)}, u32[]{:S(2)}, u32[]{:S(2)}) collective-permute-start(f32[48,1024]{1,0:T(8,128)S(1)} %get-tuple-element.79.refs_0_), channel_id=1, source_target_pairs={{0,7},{1,0},{2,1},{3,2},{4,3},{5,4},{6,5},{7,6},{8,15},{9,8},{10,9... | collective-permute-start | bytes 589832 | tf_op jit(solution)/shard_map/ppermute | solution.py:413
  26.4 15.1 %collective-permute-start.13 = (f32[48,1024]{1,0:T(8,128)S(1)}, f32[48,1024]{1,0:T(8,128)S(1)}, u32[]{:S(2)}, u32[]{:S(2)}) collective-permute-start(f32[48,1024]{1,0:T(8,128)S(1)} %get-tuple-element.82.refs_3_), channel_id=1, source_target_pairs={{0,1},{1,2},{2,3},{3,4},{4,5},{5,6},{6,7},{7,0},{8,9},{9,10},{10,1... | collective-permute-start | bytes 589832 | tf_op jit(solution)/shard_map/ppermute | solution.py:413
  26.4 0.9 %copy-start = (f32[48,1152]{1,0:T(8,128)S(1)}, f32[48,1152]{1,0:T(8,128)}, u32[]{:S(2)}) copy-start(f32[48,1152]{1,0:T(8,128)} %get-tuple-element.77.refs_2_.refs_0_.coarse_ref) | copy-start | bytes 663556
  29.2 7.8 %collective-permute-start.9 = (f32[48,640]{1,0:T(8,128)S(1)}, f32[48,640]{1,0:T(8,128)S(1)}, u32[]{:S(2)}, u32[]{:S(2)}) collective-permute-start(f32[48,640]{1,0:T(8,128)S(1)} %get-tuple-element.95), channel_id=1, source_target_pairs={{0,32},{16,48},{32,0},{48,16},{1,33},{17,49},{33,1},{49,17},{2,34}... | collective-permute-start | bytes 368648 | tf_op jit(solution)/shard_map/ppermute | solution.py:413
  33.6 7.9 %copy-start.3 = (s32[1,8]{1,0:T(1,128)S(1)}, s32[1,8]{1,0:T(1,128)}, u32[]{:S(2)}) copy-start(s32[1,8]{1,0:T(1,128)} %levels_ref.3) | copy-start | bytes 100
  33.6 7.9 %copy-start.4 = (f32[48]{0:T(128)S(1)}, f32[48]{0:T(128)}, u32[]{:S(2)}) copy-start(f32[48]{0:T(128)} %param.9) | copy-start | bytes 580
  33.6 6.2 %collective-permute-start.10 = (f32[48,640]{1,0:T(8,128)S(1)}, f32[48,640]{1,0:T(8,128)S(1)}, u32[]{:S(2)}, u32[]{:S(2)}) collective-permute-start(f32[48,640]{1,0:T(8,128)S(1)} %gather_one.1), channel_id=1, source_target_pairs={{0,48},{16,0},{32,16},{48,32},{1,49},{17,1},{33,17},{49,33},{2,50}... | collective-permute-start | bytes 368648 | tf_op jit(solution)/shard_map/ppermute | solution.py:413
  36.5 5.0 %collective-permute-start.11 = (f32[48,640]{1,0:T(8,128)S(1)}, f32[48,640]{1,0:T(8,128)S(1)}, u32[]{:S(2)}, u32[]{:S(2)}) collective-permute-start(f32[48,640]{1,0:T(8,128)S(1)} %gather_three.1), channel_id=1, source_target_pairs={{0,16},{16,32},{32,48},{48,0},{1,17},{17,33},{33,49},{49,1},{2,18}... | collective-permute-start | bytes 368648 | tf_op jit(solution)/shard_map/ppermute | solution.py:413
  37.0 3.6 %collective-permute-start.12 = (s32[4,576]{1,0:T(4,128)S(1)}, s32[4,576]{1,0:T(4,128)S(1)}, u32[]{:S(2)}, u32[]{:S(2)}) collective-permute-start(s32[4,576]{1,0:T(4,128)S(1)} %get-tuple-element.96.request_ref.request_a), channel_id=1, source_target_pairs={{0,8},{8,0},{1,9},{9,1},{2,10},{10,2},{3,11},{11,3},{4,12},{12,4},... | collective-permute-start | bytes 27656 | tf_op jit(solution)/shard_map/ppermute | solution.py:413
  43.3 11.3 %collective-permute-start.15 = (f32[48,1024]{1,0:T(8,128)S(1)}, f32[48,1024]{1,0:T(8,128)S(1)}, u32[]{:S(2)}, u32[]{:S(2)}) collective-permute-start(f32[48,1024]{1,0:T(8,128)S(1)} %get-tuple-element.109.refs_3_), channel_id=1, source_target_pairs={{0,1},{1,2},{2,3},{3,4},{4,5},{5,6},{6,7},{7,0},{8,9},{9,10},{10,1... | collective-permute-start | bytes 589832 | tf_op jit(solution)/shard_map/ppermute | solution.py:413
  43.4 8.3 %collective-permute-start.19 = (f32[48,640]{1,0:T(8,128)S(1)}, f32[48,640]{1,0:T(8,128)S(1)}, u32[]{:S(2)}, u32[]{:S(2)}) collective-permute-start(f32[48,640]{1,0:T(8,128)S(1)} %get-tuple-element.116.refs_0_), channel_id=1, source_target_pairs={{0,48},{16,0},{32,16},{48,32},{1,49},{17,1},{33,17},{49,33},{2,50}... | collective-permute-start | bytes 368648 | tf_op jit(solution)/shard_map/ppermute | solution.py:413
  44.9 9.2 %collective-permute-start.18 = (f32[48,640]{1,0:T(8,128)S(1)}, f32[48,640]{1,0:T(8,128)S(1)}, u32[]{:S(2)}, u32[]{:S(2)}) collective-permute-start(f32[48,640]{1,0:T(8,128)S(1)} %get-tuple-element.116.refs_0_), channel_id=1, source_target_pairs={{0,32},{16,48},{32,0},{48,16},{1,33},{17,49},{33,1},{49,17},{2,34}... | collective-permute-start | bytes 368648 | tf_op jit(solution)/shard_map/ppermute | solution.py:413
  44.9 9.2 %collective-permute-start.17 = (f32[48,640]{1,0:T(8,128)S(1)}, f32[48,640]{1,0:T(8,128)S(1)}, u32[]{:S(2)}, u32[]{:S(2)}) collective-permute-start(f32[48,640]{1,0:T(8,128)S(1)} %get-tuple-element.116.refs_0_), channel_id=1, source_target_pairs={{0,16},{16,32},{32,48},{48,0},{1,17},{17,33},{33,49},{49,1},{2,18}... | collective-permute-start | bytes 368648 | tf_op jit(solution)/shard_map/ppermute | solution.py:413
  45.6 9.4 %collective-permute-start.16 = (f32[48,1024]{1,0:T(8,128)S(1)}, f32[48,1024]{1,0:T(8,128)S(1)}, u32[]{:S(2)}, u32[]{:S(2)}) collective-permute-start(f32[48,1024]{1,0:T(8,128)S(1)} %get-tuple-element.110.refs_0_), channel_id=1, source_target_pairs={{0,7},{1,0},{2,1},{3,2},{4,3},{5,4},{6,5},{7,6},{8,15},{9,8},{10,9... | collective-permute-start | bytes 589832 | tf_op jit(solution)/shard_map/ppermute | solution.py:413
  51.7 3.3 %collective-permute-start.20 = (f32[48,640]{1,0:T(8,128)S(1)}, f32[48,640]{1,0:T(8,128)S(1)}, u32[]{:S(2)}, u32[]{:S(2)}) collective-permute-start(f32[48,640]{1,0:T(8,128)S(1)} %get-tuple-element.116.refs_0_), channel_id=1, source_target_pairs={{0,8},{8,0},{1,9},{9,1},{2,10},{10,2},{3,11},{11,3},{4,12},{12,4},... | collective-permute-start | bytes 368648 | tf_op jit(solution)/shard_map/ppermute | solution.py:413
  54.1 1.4 %collective-permute-start.21 = (f32[48,640]{1,0:T(8,128)S(1)}, f32[48,640]{1,0:T(8,128)S(1)}, u32[]{:S(2)}, u32[]{:S(2)}) collective-permute-start(f32[48,640]{1,0:T(8,128)S(1)} %collective-permute-done.17.refs_1_), channel_id=1, source_target_pairs={{0,8},{8,0},{1,9},{9,1},{2,10},{10,2},{3,11},{11,3},{4,12},{12,4},... | collective-permute-start | bytes 368648 | tf_op jit(solution)/shard_map/ppermute | solution.py:413
  54.5 1.3 %collective-permute-start.22 = (f32[48,640]{1,0:T(8,128)S(1)}, f32[48,640]{1,0:T(8,128)S(1)}, u32[]{:S(2)}, u32[]{:S(2)}) collective-permute-start(f32[48,640]{1,0:T(8,128)S(1)} %collective-permute-done.18.refs_2_), channel_id=1, source_target_pairs={{0,8},{8,0},{1,9},{9,1},{2,10},{10,2},{3,11},{11,3},{4,12},{12,4},... | collective-permute-start | bytes 368648 | tf_op jit(solution)/shard_map/ppermute | solution.py:413
  54.6 1.4 %collective-permute-start.23 = (f32[48,640]{1,0:T(8,128)S(1)}, f32[48,640]{1,0:T(8,128)S(1)}, u32[]{:S(2)}, u32[]{:S(2)}) collective-permute-start(f32[48,640]{1,0:T(8,128)S(1)} %collective-permute-done.19.refs_3_), channel_id=1, source_target_pairs={{0,8},{8,0},{1,9},{9,1},{2,10},{10,2},{3,11},{11,3},{4,12},{12,4},... | collective-permute-start | bytes 368648 | tf_op jit(solution)/shard_map/ppermute | solution.py:413
  58.9 8.3 %collective-permute-start.25 = (f32[48,1152]{1,0:T(8,128)S(1)}, f32[48,1152]{1,0:T(8,128)S(1)}, u32[]{:S(2)}, u32[]{:S(2)}) collective-permute-start(f32[48,1152]{1,0:T(8,128)S(1)} %scatter_far.1), channel_id=1, source_target_pairs={{0,128},{64,192},{128,0},{192,64},{1,129},{65,193},{129,1},{193,65... | collective-permute-start | bytes 663560 | tf_op jit(solution)/shard_map/ppermute | solution.py:413
  64.8 8.3 %copy-start.1 = (f32[48,1152]{1,0:T(8,128)S(1)}, f32[48,1152]{1,0:T(8,128)}, u32[]{:S(2)}) copy-start(f32[48,1152]{1,0:T(8,128)} %get-tuple-element.77.refs_2_.refs_0_.coarse_ref) | copy-start | bytes 663556
  64.8 6.4 %collective-permute-start.26 = (f32[48,1152]{1,0:T(8,128)S(1)}, f32[48,1152]{1,0:T(8,128)S(1)}, u32[]{:S(2)}, u32[]{:S(2)}) collective-permute-start(f32[48,1152]{1,0:T(8,128)S(1)} %get-tuple-element.123), channel_id=1, source_target_pairs={{0,192},{64,0},{128,64},{192,128},{1,193},{65,1},{129,65},{193,129... | collective-permute-start | bytes 663560 | tf_op jit(solution)/shard_map/ppermute | solution.py:413
  65.9 7.2 %collective-permute-start.24 = (f32[48,1152]{1,0:T(8,128)S(1)}, f32[48,1152]{1,0:T(8,128)S(1)}, u32[]{:S(2)}, u32[]{:S(2)}) collective-permute-start(f32[48,1152]{1,0:T(8,128)S(1)} %get-tuple-element.122), channel_id=1, source_target_pairs={{0,64},{64,128},{128,192},{192,0},{1,65},{65,129},{129,193},{193,1... | collective-permute-start | bytes 663560 | tf_op jit(solution)/shard_map/ppermute | solution.py:413

commit v9 on v8

--- a/solution.py
+++ b/solution.py
@@ -110,7 +110,7 @@
         in_specs=[pl.BlockSpec(memory_space=pl.ANY)] * 2,
         out_specs=[VMEM] * (X + 1),
         scratch_shapes=[pltpu.VMEM((S, X, PLANE), f32), pltpu.SemaphoreType.DMA((1 + S // rows,))],
-        compiler_params=pltpu.CompilerParams(vmem_limit_bytes=LIMIT * MIB),
+        compiler_params=pltpu.CompilerParams(vmem_limit_bytes=LIMIT * MIB - MIB // 2),
         cost_estimate=COST,
         name="split_planes",
     )(fine, coarse)
@@ -206,34 +206,50 @@
     return call(kernel, sds(S, WIDE), [VMEM] * 2, requests, rows, name=name)
 
 
+def side_by_side(boxes):
+    columns = []
+    for first, second in zip(boxes[::2], boxes[1::2]):
+        both = jnp.concatenate([first[:, 512:GHOSTS], second[:, 512:GHOSTS]], axis=1)
+        columns += [first[:, :512], both, second[:, :512]]
+    return columns
+
+
 def cells_by_row(requests):
     def kernel(request_a, request_b, out_ref):
-        for i in range(8):
-            cell = owner_and_cell((request_a if i < 4 else request_b)[i % 4 : i % 4 + 1, :])[1].astype(f32)
-            for t in range(WIDE // 128):
-                block = jnp.broadcast_to(cell[:, t * 128 : (t + 1) * 128], (128, 128))
-                out_ref[i * WIDE + t * 128 : i * WIDE + (t + 1) * 128, :] = block.T.astype(i32)
-
-    out = jax.ShapeDtypeStruct((8 * WIDE, 128), i32)
+        cells = [
+            owner_and_cell((request_a if i < 4 else request_b)[i % 4 : i % 4 + 1, :])[1].astype(f32) for i in range(8)
+        ]
+        row = 0
+        for part in side_by_side(cells):
+            for t in range(part.shape[1] // 128):
+                block = jnp.broadcast_to(part[:, t * 128 : (t + 1) * 128], (128, 128))
+                out_ref[row : row + 128, :] = block.T.astype(i32)
+                row += 128
+
+    out = jax.ShapeDtypeStruct((8 * GHOSTS, 128), i32)
     return call(kernel, out, [VMEM] * 2, *requests, name="cells_by_row")
 
 
 def scatter_columns(requests, cells, registers, steps, name):
-    total = 8 * WIDE
+    total = 8 * GHOSTS
 
     def kernel(request_a, request_b, cell_ref, *refs):
         register_refs, outs, rows_ref = refs[:8], refs[8:-1], refs[-1]
         x, y, c = lax.axis_index("x"), lax.axis_index("y"), lax.axis_index("core")
         lane = lax.broadcasted_iota(i32, (1, 128), 1)
-        for i in range(8):
-            request = (request_a if i < 4 else request_b)[i % 4 : i % 4 + 1, :]
-            owner, _ = owner_and_cell(request)
-            high, low = halves(register_refs[i][...])
+        owners = side_by_side(
+            [owner_and_cell((request_a if i < 4 else request_b)[i % 4 : i % 4 + 1, :])[0].astype(f32) for i in range(8)]
+        )
+        at = 0
+        for owner, value in zip(owners, side_by_side([ref[...] for ref in register_refs])):
+            width = value.shape[1]
+            high, low = halves(value)
             for k, step in enumerate(steps):
-                to_x = jnp.bitwise_and(x + step, 3)
-                mine = jnp.broadcast_to(jnp.where(owner == (to_x * 4 + y) * 2 + c, 1.0, 0.0).astype(bf16), (S, WIDE))
-                rows_ref[2 * S * k : 2 * S * k + S, i * WIDE : (i + 1) * WIDE] = high * mine
-                rows_ref[2 * S * k + S : 2 * S * (k + 1), i * WIDE : (i + 1) * WIDE] = low * mine
+                to = ((jnp.bitwise_and(x + step, 3) * 4 + y) * 2 + c).astype(f32)
+                mine = jnp.broadcast_to(jnp.where(owner == to, 1.0, 0.0).astype(bf16), (S, width))
+                rows_ref[2 * S * k : 2 * S * k + S, at : at + width] = high * mine
+                rows_ref[2 * S * k + S : 2 * S * (k + 1), at : at + width] = low * mine
+            at += width
 
         def block(start, width):
             marks = [ones_where(cell_ref[...] == lane + (start + 128 * t)) for t in range(width // 128)]
@@ -468,9 +484,10 @@
     sent = {}
     (part,) = scatter_columns([request_rows, mate_rows], cells, held, (2,), "scatter_far")
     sent[2] = shifted(part, "x", 2)
-    parts = scatter_columns([request_rows, mate_rows], after(cells, part), held, (1, 3, 0), "scatter_near")
-    sent[1], sent[3], sent[0] = shifted(parts[0], "x", 1), shifted(parts[1], "x", 3), parts[2]
-    base = after(base, (parts[0], sent[2]))
+    parts = scatter_columns([request_rows, mate_rows], after(cells, part), held, (1, 3), "scatter_near")
+    sent[1], sent[3] = shifted(parts[0], "x", 1), shifted(parts[1], "x", 3)
+    (sent[0],) = scatter_columns([request_rows, mate_rows], after(cells, parts[0]), held, (0,), "scatter_own")
+    base = after(base, (sent[0], sent[2]))
     fine_out = second_stage(levels, row, middle, base, growth, x_ghosts, y_ghosts, below_plane, above_plane)
     sent = [sent[k] for k in range(4)]
     sent, fine_out, coarse_growth = lax.optimization_barrier((sent, fine_out, coarse_growth))

time: 75.2 us -> 72.3 us (0.961)
  waiting for transfers between devices: 7.59 us -> 4.77 us
    ppermute x27, waiting for transfers between devices: 7.59 us -> 4.77 us  [shifted(): lax.ppermute(value, axis, [(i, (i + shift) % size) for i in range(size)])]
    pallas_call x13 -> x14, Pallas kernels: 25.6 us -> 26.5 us  [call(): pl.pallas_call(kernel, out_shape=out_shape, in_specs=in_specs, out_specs=...]
    unnamed x10 -> x8, local copies, waits for them, and re-layouts: 1.89 us -> 1.88 us
  transfers between devices with their start and end apart: 27 -> 27, of which waited for: 8 -> 6; matrix products, arithmetic and copies ran while one was open for 0% -> 0% of each run, Pallas kernels for 33% -> 35%
where the time goes in v9:
time: 72.3 us; the launch traced here: 71.4 us
  starting transfers between devices  33.1 us (46%)
  Pallas kernels  30 us (41%)
  waiting for transfers between devices  4.77 us (7%)
  local copies, waits for them, and re-layouts  1.9 us (3%)
  between operations  0.91 us (1%)
    ppermute x27, starting transfers between devices, shifted(): lax.ppermute(value, axis, [(i, (i + shift) % size) for i in range(size)])  33.1 us
    pallas_call x14, Pallas kernels, call(): pl.pallas_call(kernel, out_shape=out_shape, in_specs=in_specs, out_specs=...  26.5 us
    ppermute x27, waiting for transfers between devices, shifted(): lax.ppermute(value, axis, [(i, (i + shift) % size) for i in range(size)])  4.77 us
    pallas_call x1, Pallas kernels, second_stage(): pl.pallas_call(kernel, out_shape=sds(S, X, PLANE), in_specs=[SMEM] + [VME...  2.24 us
    unnamed x8, local copies, waits for them, and re-layouts  1.88 us
  transfers between devices with their start and end apart: 27, of which 6 were waited for; matrix products, arithmetic and copies ran while one was open for 0% of the time, Pallas kernels for 35%

profile of v9, /device:TPU:1, one launch (start us, length us, event | category | flops | bytes accessed | tf_op | source)
XLA Modules:
  0.0 71.4 jit_solution(2554723149115684457)
XLA Ops:
  0.6 0.7 reduce
  1.3 2.2 %collective-permute-start.3 = (s32[24,576]{1,0:T(8,128)S(1)}, s32[24,576]{1,0:T(8,128)S(1)}, u32[]{:S(2)}, u32[]{:S(2)}) collective-permute-start(s32[24,576]{1,0:T(8,128)S(1)} %add.8), channel_id=1, source_target_pairs={{0,16},{16,32},{32,48},{48,0},{1,17},{17,33},{33,49},{49,1},{2,18}... | collective-permute-start | bytes 165896 | tf_op jit(solution)/shard_map/ppermute | solution.py:429
  3.5 2.5 %collective-permute-start.2 = (f32[48,1152]{1,0:T(8,128)}, f32[48,1152]{1,0:T(8,128)S(1)}, u32[]{:S(2)}, u32[]{:S(2)}) collective-permute-start(f32[48,1152]{1,0:T(8,128)} %bitcast.5), channel_id=1, source_target_pairs={{0,192},{64,0},{128,64},{192,128},{1,193},{65,1},{129,65},{193,129... | collective-permute-start | bytes 663560 | tf_op jit(solution)/shard_map/ppermute | solution.py:429
  6.0 0.5 collective-permute-start.1
  6.5 0.6 collective-permute-start
  7.2 1.8 %collective-permute-start.5 = (f32[48,1152]{1,0:T(8,128)}, f32[48,1152]{1,0:T(8,128)S(1)}, u32[]{:S(2)}, u32[]{:S(2)}) collective-permute-start(f32[48,1152]{1,0:T(8,128)} %bitcast.8), channel_id=1, source_target_pairs={{0,8},{8,0},{1,9},{9,1},{2,10},{10,2},{3,11},{11,3},{4,12},{12,4},... | collective-permute-start | bytes 663560 | tf_op jit(solution)/shard_map/ppermute | solution.py:429
  9.0 0.9 %copy-done = bf16[48,2304]{1,0:T(8,128)(2,1)S(1)} copy-done((bf16[48,2304]{1,0:T(8,128)(2,1)S(1)}, bf16[48,2304]{1,0:T(8,128)(2,1)}, u32[]{:S(2)}) %copy-start) | copy-done | bytes 221208
  9.9 1.8 %fold_kernel.1.matrix_ref = bf16[96,1280]{1,0:T(8,128)(2,1)S(1)} custom-call(bf16[48,2304]{1,0:T(8,128)(2,1)S(1)} %copy-done), custom_call_target="tpu_custom_call" | custom-call | tf_op jit(solution)/shard_map/fold_kernel/pallas_call | solution.py:34
  11.7 2.7 %collective-permute-start.4 = (s32[24,576]{1,0:T(8,128)S(1)}, s32[24,576]{1,0:T(8,128)S(1)}, u32[]{:S(2)}, u32[]{:S(2)}) collective-permute-start(s32[24,576]{1,0:T(8,128)S(1)} %pad_add_fusion.refs_0_), channel_id=1, source_target_pairs={{0,32},{16,48},{32,0},{48,16},{1,33},{17,49},{33,1},{49,17},{2,34}... | collective-permute-start | bytes 165896 | tf_op jit(solution)/shard_map/ppermute | solution.py:429
  14.4 0.9 %copy-done.1 = f32[1,1,48,1152]{3,2,1,0:T(8,128)S(1)} copy-done((f32[1,1,48,1152]{3,2,1,0:T(8,128)S(1)}, f32[1,1,48,1152]{3,2,1,0:T(8,128)}, u32[]{:S(2)}) %copy-start.1) | copy-done | bytes 221208
  15.4 1.3 %split_planes.1 = (f32[48,1024]{1,0:T(8,128)S(1)}, f32[48,1024]{1,0:T(8,128)S(1)}, f32[48,1024]{1,0:T(8,128)S(1)}, f32[48,1024]{1,0:T(8,128)S(1)}, f32[48,1152]{1,0:T(8,128)S(1)}) custom-call(f32[48,4,1024]{2,1,0:T(4,128)} %bitcast.12, f32[48,1152]{1,0:T(8,128)S(1)} %bitcast.9), custom_call_target="tpu_custom_call" | custom-call | tf_op jit(solution)/shard_map/split_planes/pallas_call | solution.py:107
  16.7 2.3 %coagulate_fine.1 = (f32[48,1024]{1,0:T(8,128)S(1)}, f32[48,1024]{1,0:T(8,128)S(1)}, f32[48,1024]{1,0:T(8,128)S(1)}, f32[48,1024]{1,0:T(8,128)S(1)}) custom-call(bf16[96,1280]{1,0:T(8,128)(2,1)S(1)} %fold_kernel.1.matrix_ref, f32[48,1024]{1,0:T(8,128)S(1)} %get-tuple-element.79.refs_0_, f32[48,1024]{1,0:T(8,128)S(1)} %get-tuple-element.80.refs_1_, ...), custom_call_target="tpu_custom_call" | custom-call | tf_op jit(solution)/shard_map/coagulate_fine/pallas_call | solution.py:34
  19.1 0.8 %collective-permute-done.refs_4_ = f32[48,1152]{1,0:T(8,128)S(1)} collective-permute-done((f32[48,1152]{1,0:T(8,128)}, f32[48,1152]{1,0:T(8,128)S(1)}, u32[]{:S(2)}, u32[]{:S(2)}) %collective-permute-start) | collective-permute-done | bytes 221216 | tf_op jit(solution)/shard_map/ppermute | solution.py:429
  19.8 0.5 collective-permute-start.6
  20.3 0.5 collective-permute-start.8
  20.8 5.6 %collective-permute-start.14 = (f32[48,1024]{1,0:T(8,128)S(1)}, f32[48,1024]{1,0:T(8,128)S(1)}, u32[]{:S(2)}, u32[]{:S(2)}) collective-permute-start(f32[48,1024]{1,0:T(8,128)S(1)} %get-tuple-element.79.refs_0_), channel_id=1, source_target_pairs={{0,7},{1,0},{2,1},{3,2},{4,3},{5,4},{6,5},{7,6},{8,15},{9,8},{10,9... | collective-permute-start | bytes 589832 | tf_op jit(solution)/shard_map/ppermute | solution.py:429
  26.4 1.8 %gather_first.1 = (f32[48,640]{1,0:T(8,128)S(1)}, bf16[768,1152]{1,0:T(8,128)(2,1)S(1)}, s32[4,576]{1,0:T(4,128)S(1)}) custom-call(s32[24,576]{1,0:T(8,128)S(1)} %pad_add_fusion.refs_0_, s32[24,576]{1,0:T(8,128)S(1)} %collective-permute-done.4.refs_1_, f32[48,1152]{1,0:T(8,128)S(1)} %get-tuple-element.77.refs_2_.refs_0_.coarse_ref, ...), custom_call_target="tpu_custom_call" | custom-call | tf_op jit(solution)/shard_map/gather_first/pallas_call | solution.py:34
  28.2 2.7 %collective-permute-start.9 = (f32[48,640]{1,0:T(8,128)S(1)}, f32[48,640]{1,0:T(8,128)S(1)}, u32[]{:S(2)}, u32[]{:S(2)}) collective-permute-start(f32[48,640]{1,0:T(8,128)S(1)} %get-tuple-element.95), channel_id=1, source_target_pairs={{0,32},{16,48},{32,0},{48,16},{1,33},{17,49},{33,1},{49,17},{2,34}... | collective-permute-start | bytes 368648 | tf_op jit(solution)/shard_map/ppermute | solution.py:429
  30.9 1.7 %gather_one.1 = f32[48,640]{1,0:T(8,128)S(1)} custom-call(s32[4,576]{1,0:T(4,128)S(1)} %get-tuple-element.96.request_ref.request_a, bf16[768,1152]{1,0:T(8,128)(2,1)S(1)} %get-tuple-element.93.rows_ref), custom_call_target="tpu_custom_call" | custom-call | tf_op jit(solution)/shard_map/gather_one/pallas_call | solution.py:34
  32.7 1.1 %collective-permute-start.10 = (f32[48,640]{1,0:T(8,128)S(1)}, f32[48,640]{1,0:T(8,128)S(1)}, u32[]{:S(2)}, u32[]{:S(2)}) collective-permute-start(f32[48,640]{1,0:T(8,128)S(1)} %gather_one.1), channel_id=1, source_target_pairs={{0,48},{16,0},{32,16},{48,32},{1,49},{17,1},{33,17},{49,33},{2,50}... | collective-permute-start | bytes 368648 | tf_op jit(solution)/shard_map/ppermute | solution.py:429
  33.8 1.7 %gather_three.1 = f32[48,640]{1,0:T(8,128)S(1)} custom-call(s32[4,576]{1,0:T(4,128)S(1)} %get-tuple-element.96.request_ref.request_a, bf16[768,1152]{1,0:T(8,128)(2,1)S(1)} %get-tuple-element.93.rows_ref), custom_call_target="tpu_custom_call" | custom-call | tf_op jit(solution)/shard_map/gather_three/pallas_call | solution.py:34
  35.6 0.5 collective-permute-start.11
  36.1 1.1 %collective-permute-start.12 = (s32[4,576]{1,0:T(4,128)S(1)}, s32[4,576]{1,0:T(4,128)S(1)}, u32[]{:S(2)}, u32[]{:S(2)}) collective-permute-start(s32[4,576]{1,0:T(4,128)S(1)} %get-tuple-element.96.request_ref.request_a), channel_id=1, source_target_pairs={{0,8},{8,0},{1,9},{9,1},{2,10},{10,2},{3,11},{11,3},{4,12},{12,4},... | collective-permute-start | bytes 27656 | tf_op jit(solution)/shard_map/ppermute | solution.py:429
  37.2 1.7 %gather_own.1.refs_8_ = f32[48,640]{1,0:T(8,128)S(1)} custom-call(s32[4,576]{1,0:T(4,128)S(1)} %get-tuple-element.96.request_ref.request_a, bf16[768,1152]{1,0:T(8,128)(2,1)S(1)} %get-tuple-element.93.rows_ref), custom_call_target="tpu_custom_call" | custom-call | tf_op jit(solution)/shard_map/gather_own/pallas_call | solution.py:34
  39.0 0.8 %coagulate_coarse.1.growth_ref = f32[48,1152]{1,0:T(8,128)S(1)} custom-call(bf16[96,1280]{1,0:T(8,128)(2,1)S(1)} %fold_kernel.1.matrix_ref, f32[48,1152]{1,0:T(8,128)S(1)} %get-tuple-element.77.refs_2_.refs_0_.coarse_ref), custom_call_target="tpu_custom_call" | custom-call | tf_op jit(solution)/shard_map/coagulate_coarse/pallas_call | solution.py:34
  39.7 0.9 %collective-permute-done.11.refs_11_ = f32[48,640]{1,0:T(8,128)S(1)} collective-permute-done((f32[48,640]{1,0:T(8,128)S(1)}, f32[48,640]{1,0:T(8,128)S(1)}, u32[]{:S(2)}, u32[]{:S(2)}) %collective-permute-start.11) | collective-permute-done | bytes 122912 | tf_op jit(solution)/shard_map/ppermute | solution.py:429
  40.6 1.8 %first_stage.1 = (f32[48,1024]{1,0:T(8,128)S(1)}, f32[48,1024]{1,0:T(8,128)S(1)}, f32[48,1024]{1,0:T(8,128)S(1)}, f32[48,1024]{1,0:T(8,128)S(1)}, f32[48,1024]{1...) custom-call(s32[1,8]{1,0:T(1,128)S(1)} %copy-done.2, ...), custom_call_target="tpu_custom_call" | custom-call | tf_op jit(solution)/shard_map/first_stage/pallas_call | solution.py:34
  42.5 0.1 collective-permute-start.15
  42.6 1.5 %collective-permute-start.19 = (f32[48,640]{1,0:T(8,128)S(1)}, f32[48,640]{1,0:T(8,128)S(1)}, u32[]{:S(2)}, u32[]{:S(2)}) collective-permute-start(f32[48,640]{1,0:T(8,128)S(1)} %get-tuple-element.116.refs_0_), channel_id=1, source_target_pairs={{0,48},{16,0},{32,16},{48,32},{1,49},{17,1},{33,17},{49,33},{2,50}... | collective-permute-start | bytes 368648 | tf_op jit(solution)/shard_map/ppermute | solution.py:429
  44.1 0.7 collective-permute-start.17
  44.8 2.9 %collective-permute-start.16 = (f32[48,1024]{1,0:T(8,128)S(1)}, f32[48,1024]{1,0:T(8,128)S(1)}, u32[]{:S(2)}, u32[]{:S(2)}) collective-permute-start(f32[48,1024]{1,0:T(8,128)S(1)} %get-tuple-element.110.refs_0_), channel_id=1, source_target_pairs={{0,7},{1,0},{2,1},{3,2},{4,3},{5,4},{6,5},{7,6},{8,15},{9,8},{10,9... | collective-permute-start | bytes 589832 | tf_op jit(solution)/shard_map/ppermute | solution.py:429
  47.7 0.8 %cells_by_row.1.cell_ref = s32[4608,128]{1,0:T(8,128)S(1)} custom-call(s32[4,576]{1,0:T(4,128)S(1)} %get-tuple-element.96.request_ref.request_a, s32[4,576]{1,0:T(4,128)S(1)} %collective-permute-done.12.request_b), custom_call_target="tpu_custom_call" | custom-call | tf_op jit(solution)/shard_map/cells_by_row/pallas_call | solution.py:34
  48.4 2.3 %coagulate_middle.1 = (f32[48,1024]{1,0:T(8,128)S(1)}, f32[48,1024]{1,0:T(8,128)S(1)}, f32[48,1024]{1,0:T(8,128)S(1)}, f32[48,1024]{1,0:T(8,128)S(1)}) custom-call(bf16[96,1280]{1,0:T(8,128)(2,1)S(1)} %fold_kernel.1.matrix_ref, f32[48,1024]{1,0:T(8,128)S(1)} %get-tuple-element.110.refs_0_, f32[48,1024]{1,0:T(8,128)S(1)} %get-tuple-element.113.refs_1_, ...), custom_call_target="tpu_custom_call" | custom-call | tf_op jit(solution)/shard_map/coagulate_middle/pallas_call | solution.py:34
  50.8 2.3 %collective-permute-start.20 = (f32[48,640]{1,0:T(8,128)S(1)}, f32[48,640]{1,0:T(8,128)S(1)}, u32[]{:S(2)}, u32[]{:S(2)}) collective-permute-start(f32[48,640]{1,0:T(8,128)S(1)} %get-tuple-element.116.refs_0_), channel_id=1, source_target_pairs={{0,8},{8,0},{1,9},{9,1},{2,10},{10,2},{3,11},{11,3},{4,12},{12,4},... | collective-permute-start | bytes 368648 | tf_op jit(solution)/shard_map/ppermute | solution.py:429
  53.1 0.5 collective-permute-start.21
  53.7 0.5 collective-permute-start.23
  54.2 0.5 collective-permute-done.21.refs_5_
  54.6 0.4 collective-permute-done.22.refs_6_
  55.0 0.2 collective-permute-done.23.refs_7_
  55.2 2.7 %scatter_far.1 = f32[48,1152]{1,0:T(8,128)S(1)} custom-call(s32[4,576]{1,0:T(4,128)S(1)} %get-tuple-element.96.request_ref.request_a, s32[4,576]{1,0:T(4,128)S(1)} %collective-permute-done.12.request_b, s32[4608,128]{1,0:T(8,128)S(1)} %cells_by_row.1.cell_ref, f32[48,640]{1,0:T(8,128)S(1)} %get-tuple-element.116.refs_0_, ...), custom_call_target="tpu_custom_call" | custom-call | tf_op jit(solution)/shard_map/scatter_far/pallas_call | solution.py:34
  57.9 0.6 collective-permute-start.25
  58.5 3.5 %scatter_near.1 = (f32[48,1152]{1,0:T(8,128)S(1)}, f32[48,1152]{1,0:T(8,128)S(1)}) custom-call(s32[4,576]{1,0:T(4,128)S(1)} %get-tuple-element.96.request_ref.request_a, s32[4,576]{1,0:T(4,128)S(1)} %collective-permute-done.12.request_b, s32[4608,128]{1,0:T(8,128)S(1)} %cells_by_row.1.cell_ref, f32[48,640]{1,0:T(8,128)S(1)} %get-tuple-element.116.refs_0_, ...), custom_call_target="tpu_custom_call" | custom-call | tf_op jit(solution)/shard_map/scatter_near/pallas_call | solution.py:34
  62.0 1.3 %collective-permute-start.26 = (f32[48,1152]{1,0:T(8,128)S(1)}, f32[48,1152]{1,0:T(8,128)S(1)}, u32[]{:S(2)}, u32[]{:S(2)}) collective-permute-start(f32[48,1152]{1,0:T(8,128)S(1)} %get-tuple-element.123), channel_id=1, source_target_pairs={{0,192},{64,0},{128,64},{192,128},{1,193},{65,1},{129,65},{193,129... | collective-permute-start | bytes 663560 | tf_op jit(solution)/shard_map/ppermute | solution.py:429
  63.3 0.2 collective-permute-start.24
  63.5 2.7 %scatter_own.1.a = f32[48,1152]{1,0:T(8,128)S(1)} custom-call(s32[4,576]{1,0:T(4,128)S(1)} %get-tuple-element.96.request_ref.request_a, s32[4,576]{1,0:T(4,128)S(1)} %collective-permute-done.12.request_b, s32[4608,128]{1,0:T(8,128)S(1)} %cells_by_row.1.cell_ref, f32[48,640]{1,0:T(8,128)S(1)} %get-tuple-element.116.refs_0_, ...), custom_call_target="tpu_custom_call" | custom-call | tf_op jit(solution)/shard_map/scatter_own/pallas_call | solution.py:34
  66.3 2.2 %second_stage.1 = f32[48,4,1024]{2,1,0:T(4,128)} custom-call(s32[1,8]{1,0:T(1,128)S(1)} %copy-done.2, f32[1,48]{1,0:T(1,128)S(1)} %bitcast.11, f32[48,1024]{1,0:T(8,128)S(1)} %get-tuple-element.110.refs_0_, f32[48,1024]{1,0:T(8,128)S(1)} %get-tuple-element.113.refs_1_, f32[48,1024]{1,0:T(8,128)S(1)} %get-tuple-element.114.refs_2_, ...), custom_call_target="tpu_custom_call" | custom-call | tf_op jit(solution)/shard_map/second_stage/pallas_call | solution.py:407
  68.5 2.1 %collective-permute-done.24.b = f32[48,1152]{1,0:T(8,128)S(1)} collective-permute-done((f32[48,1152]{1,0:T(8,128)S(1)}, f32[48,1152]{1,0:T(8,128)S(1)}, u32[]{:S(2)}, u32[]{:S(2)}) %collective-permute-start.24) | collective-permute-done | bytes 221216 | tf_op jit(solution)/shard_map/ppermute | solution.py:429
  70.6 0.8 %finish_coarse.1 = f32[48,1152]{1,0:T(8,128)} custom-call(f32[48,1152]{1,0:T(8,128)S(1)} %get-tuple-element.77.refs_2_.refs_0_.coarse_ref, f32[48,1152]{1,0:T(8,128)S(1)} %coagulate_coarse.1.growth_ref, f32[48,1152]{1,0:T(8,128)S(1)} %scatter_own.1.a, f32[48,1152]{1,0:T(8,128)S(1)} %collective-permute-done.24.b, f32[48,1152]{1,0:T(8,128)S(1)} %collective-permute-done.25.c, ...), custom_call_target="tpu_custom_call" | custom-call | tf_op jit(solution)/shard_map/finish_coarse/pallas_call | solution.py:34
  (35 shorter events, 0.1 us)
Async XLA Ops:
  1.3 10.3 %collective-permute-start.3 = (s32[24,576]{1,0:T(8,128)S(1)}, s32[24,576]{1,0:T(8,128)S(1)}, u32[]{:S(2)}, u32[]{:S(2)}) collective-permute-start(s32[24,576]{1,0:T(8,128)S(1)} %add.8), channel_id=1, source_target_pairs={{0,16},{16,32},{32,48},{48,0},{1,17},{17,33},{33,49},{49,1},{2,18}... | collective-permute-start | bytes 165896 | tf_op jit(solution)/shard_map/ppermute | solution.py:429
  3.5 15.5 %collective-permute-start.2 = (f32[48,1152]{1,0:T(8,128)}, f32[48,1152]{1,0:T(8,128)S(1)}, u32[]{:S(2)}, u32[]{:S(2)}) collective-permute-start(f32[48,1152]{1,0:T(8,128)} %bitcast.5), channel_id=1, source_target_pairs={{0,192},{64,0},{128,64},{192,128},{1,193},{65,1},{129,65},{193,129... | collective-permute-start | bytes 663560 | tf_op jit(solution)/shard_map/ppermute | solution.py:429
  6.0 13.0 %collective-permute-start.1 = (f32[48,1152]{1,0:T(8,128)}, f32[48,1152]{1,0:T(8,128)S(1)}, u32[]{:S(2)}, u32[]{:S(2)}) collective-permute-start(f32[48,1152]{1,0:T(8,128)} %bitcast.6), channel_id=1, source_target_pairs={{0,128},{64,192},{128,0},{192,64},{1,129},{65,193},{129,1},{193,65... | collective-permute-start | bytes 663560 | tf_op jit(solution)/shard_map/ppermute | solution.py:429
  6.5 13.3 %collective-permute-start = (f32[48,1152]{1,0:T(8,128)}, f32[48,1152]{1,0:T(8,128)S(1)}, u32[]{:S(2)}, u32[]{:S(2)}) collective-permute-start(f32[48,1152]{1,0:T(8,128)} %bitcast.7), channel_id=1, source_target_pairs={{0,64},{64,128},{128,192},{192,0},{1,65},{65,129},{129,193},{193,1... | collective-permute-start | bytes 663560 | tf_op jit(solution)/shard_map/ppermute | solution.py:429
  7.2 19.3 %collective-permute-start.5 = (f32[48,1152]{1,0:T(8,128)}, f32[48,1152]{1,0:T(8,128)S(1)}, u32[]{:S(2)}, u32[]{:S(2)}) collective-permute-start(f32[48,1152]{1,0:T(8,128)} %bitcast.8), channel_id=1, source_target_pairs={{0,8},{8,0},{1,9},{9,1},{2,10},{10,2},{3,11},{11,3},{4,12},{12,4},... | collective-permute-start | bytes 663560 | tf_op jit(solution)/shard_map/ppermute | solution.py:429
  8.9 0.9 %copy-start = (bf16[48,2304]{1,0:T(8,128)(2,1)S(1)}, bf16[48,2304]{1,0:T(8,128)(2,1)}, u32[]{:S(2)}) copy-start(bf16[48,2304]{1,0:T(8,128)(2,1)} %matrix_ref.1) | copy-start | bytes 663556
  11.7 7.3 %collective-permute-start.4 = (s32[24,576]{1,0:T(8,128)S(1)}, s32[24,576]{1,0:T(8,128)S(1)}, u32[]{:S(2)}, u32[]{:S(2)}) collective-permute-start(s32[24,576]{1,0:T(8,128)S(1)} %pad_add_fusion.refs_0_), channel_id=1, source_target_pairs={{0,32},{16,48},{32,0},{48,16},{1,33},{17,49},{33,1},{49,17},{2,34}... | collective-permute-start | bytes 165896 | tf_op jit(solution)/shard_map/ppermute | solution.py:429
  14.4 0.9 %copy-start.1 = (f32[1,1,48,1152]{3,2,1,0:T(8,128)S(1)}, f32[1,1,48,1152]{3,2,1,0:T(8,128)}, u32[]{:S(2)}) copy-start(f32[1,1,48,1152]{3,2,1,0:T(8,128)} %param.7) | copy-start | bytes 663556
  19.8 6.6 %collective-permute-start.6 = (f32[48,1152]{1,0:T(8,128)S(1)}, f32[48,1152]{1,0:T(8,128)S(1)}, u32[]{:S(2)}, u32[]{:S(2)}) collective-permute-start(f32[48,1152]{1,0:T(8,128)S(1)} %collective-permute-done.refs_4_), channel_id=1, source_target_pairs={{0,8},{8,0},{1,9},{9,1},{2,10},{10,2},{3,11},{11,3},{4,12},{12,4},... | collective-permute-start | bytes 663560 | tf_op jit(solution)/shard_map/ppermute | solution.py:429
  20.3 6.1 %collective-permute-start.7 = (f32[48,1152]{1,0:T(8,128)S(1)}, f32[48,1152]{1,0:T(8,128)S(1)}, u32[]{:S(2)}, u32[]{:S(2)}) collective-permute-start(f32[48,1152]{1,0:T(8,128)S(1)} %collective-permute-done.2.refs_6_), channel_id=1, source_target_pairs={{0,8},{8,0},{1,9},{9,1},{2,10},{10,2},{3,11},{11,3},{4,12},{12,4},... | collective-permute-start | bytes 663560 | tf_op jit(solution)/shard_map/ppermute | solution.py:429
  20.3 6.1 %collective-permute-start.8 = (f32[48,1152]{1,0:T(8,128)S(1)}, f32[48,1152]{1,0:T(8,128)S(1)}, u32[]{:S(2)}, u32[]{:S(2)}) collective-permute-start(f32[48,1152]{1,0:T(8,128)S(1)} %collective-permute-done.1.refs_8_), channel_id=1, source_target_pairs={{0,8},{8,0},{1,9},{9,1},{2,10},{10,2},{3,11},{11,3},{4,12},{12,4},... | collective-permute-start | bytes 663560 | tf_op jit(solution)/shard_map/ppermute | solution.py:429
  20.8 19.8 %collective-permute-start.14 = (f32[48,1024]{1,0:T(8,128)S(1)}, f32[48,1024]{1,0:T(8,128)S(1)}, u32[]{:S(2)}, u32[]{:S(2)}) collective-permute-start(f32[48,1024]{1,0:T(8,128)S(1)} %get-tuple-element.79.refs_0_), channel_id=1, source_target_pairs={{0,7},{1,0},{2,1},{3,2},{4,3},{5,4},{6,5},{7,6},{8,15},{9,8},{10,9... | collective-permute-start | bytes 589832 | tf_op jit(solution)/shard_map/ppermute | solution.py:429
  26.4 14.2 %collective-permute-start.13 = (f32[48,1024]{1,0:T(8,128)S(1)}, f32[48,1024]{1,0:T(8,128)S(1)}, u32[]{:S(2)}, u32[]{:S(2)}) collective-permute-start(f32[48,1024]{1,0:T(8,128)S(1)} %get-tuple-element.82.refs_3_), channel_id=1, source_target_pairs={{0,1},{1,2},{2,3},{3,4},{4,5},{5,6},{6,7},{7,0},{8,9},{9,10},{10,1... | collective-permute-start | bytes 589832 | tf_op jit(solution)/shard_map/ppermute | solution.py:429
  28.2 7.8 %collective-permute-start.9 = (f32[48,640]{1,0:T(8,128)S(1)}, f32[48,640]{1,0:T(8,128)S(1)}, u32[]{:S(2)}, u32[]{:S(2)}) collective-permute-start(f32[48,640]{1,0:T(8,128)S(1)} %get-tuple-element.95), channel_id=1, source_target_pairs={{0,32},{16,48},{32,0},{48,16},{1,33},{17,49},{33,1},{49,17},{2,34}... | collective-permute-start | bytes 368648 | tf_op jit(solution)/shard_map/ppermute | solution.py:429
  32.7 7.9 %copy-start.2 = (s32[1,8]{1,0:T(1,128)S(1)}, s32[1,8]{1,0:T(1,128)}, u32[]{:S(2)}) copy-start(s32[1,8]{1,0:T(1,128)} %levels_ref.3) | copy-start | bytes 100
  32.7 7.9 %copy-start.3 = (f32[48]{0:T(128)S(1)}, f32[48]{0:T(128)}, u32[]{:S(2)}) copy-start(f32[48]{0:T(128)} %param.9) | copy-start | bytes 580
  32.7 6.3 %collective-permute-start.10 = (f32[48,640]{1,0:T(8,128)S(1)}, f32[48,640]{1,0:T(8,128)S(1)}, u32[]{:S(2)}, u32[]{:S(2)}) collective-permute-start(f32[48,640]{1,0:T(8,128)S(1)} %gather_one.1), channel_id=1, source_target_pairs={{0,48},{16,0},{32,16},{48,32},{1,49},{17,1},{33,17},{49,33},{2,50}... | collective-permute-start | bytes 368648 | tf_op jit(solution)/shard_map/ppermute | solution.py:429
  35.6 5.0 %collective-permute-start.11 = (f32[48,640]{1,0:T(8,128)S(1)}, f32[48,640]{1,0:T(8,128)S(1)}, u32[]{:S(2)}, u32[]{:S(2)}) collective-permute-start(f32[48,640]{1,0:T(8,128)S(1)} %gather_three.1), channel_id=1, source_target_pairs={{0,16},{16,32},{32,48},{48,0},{1,17},{17,33},{33,49},{49,1},{2,18}... | collective-permute-start | bytes 368648 | tf_op jit(solution)/shard_map/ppermute | solution.py:429
  36.1 3.7 %collective-permute-start.12 = (s32[4,576]{1,0:T(4,128)S(1)}, s32[4,576]{1,0:T(4,128)S(1)}, u32[]{:S(2)}, u32[]{:S(2)}) collective-permute-start(s32[4,576]{1,0:T(4,128)S(1)} %get-tuple-element.96.request_ref.request_a), channel_id=1, source_target_pairs={{0,8},{8,0},{1,9},{9,1},{2,10},{10,2},{3,11},{11,3},{4,12},{12,4},... | collective-permute-start | bytes 27656 | tf_op jit(solution)/shard_map/ppermute | solution.py:429
  42.5 11.2 %collective-permute-start.15 = (f32[48,1024]{1,0:T(8,128)S(1)}, f32[48,1024]{1,0:T(8,128)S(1)}, u32[]{:S(2)}, u32[]{:S(2)}) collective-permute-start(f32[48,1024]{1,0:T(8,128)S(1)} %get-tuple-element.109.refs_3_), channel_id=1, source_target_pairs={{0,1},{1,2},{2,3},{3,4},{4,5},{5,6},{6,7},{7,0},{8,9},{9,10},{10,1... | collective-permute-start | bytes 589832 | tf_op jit(solution)/shard_map/ppermute | solution.py:429
  42.6 8.2 %collective-permute-start.19 = (f32[48,640]{1,0:T(8,128)S(1)}, f32[48,640]{1,0:T(8,128)S(1)}, u32[]{:S(2)}, u32[]{:S(2)}) collective-permute-start(f32[48,640]{1,0:T(8,128)S(1)} %get-tuple-element.116.refs_0_), channel_id=1, source_target_pairs={{0,48},{16,0},{32,16},{48,32},{1,49},{17,1},{33,17},{49,33},{2,50}... | collective-permute-start | bytes 368648 | tf_op jit(solution)/shard_map/ppermute | solution.py:429
  44.1 9.1 %collective-permute-start.18 = (f32[48,640]{1,0:T(8,128)S(1)}, f32[48,640]{1,0:T(8,128)S(1)}, u32[]{:S(2)}, u32[]{:S(2)}) collective-permute-start(f32[48,640]{1,0:T(8,128)S(1)} %get-tuple-element.116.refs_0_), channel_id=1, source_target_pairs={{0,32},{16,48},{32,0},{48,16},{1,33},{17,49},{33,1},{49,17},{2,34}... | collective-permute-start | bytes 368648 | tf_op jit(solution)/shard_map/ppermute | solution.py:429
  44.1 9.1 %collective-permute-start.17 = (f32[48,640]{1,0:T(8,128)S(1)}, f32[48,640]{1,0:T(8,128)S(1)}, u32[]{:S(2)}, u32[]{:S(2)}) collective-permute-start(f32[48,640]{1,0:T(8,128)S(1)} %get-tuple-element.116.refs_0_), channel_id=1, source_target_pairs={{0,16},{16,32},{32,48},{48,0},{1,17},{17,33},{33,49},{49,1},{2,18}... | collective-permute-start | bytes 368648 | tf_op jit(solution)/shard_map/ppermute | solution.py:429
  44.8 9.4 %collective-permute-start.16 = (f32[48,1024]{1,0:T(8,128)S(1)}, f32[48,1024]{1,0:T(8,128)S(1)}, u32[]{:S(2)}, u32[]{:S(2)}) collective-permute-start(f32[48,1024]{1,0:T(8,128)S(1)} %get-tuple-element.110.refs_0_), channel_id=1, source_target_pairs={{0,7},{1,0},{2,1},{3,2},{4,3},{5,4},{6,5},{7,6},{8,15},{9,8},{10,9... | collective-permute-start | bytes 589832 | tf_op jit(solution)/shard_map/ppermute | solution.py:429
  50.8 3.4 %collective-permute-start.20 = (f32[48,640]{1,0:T(8,128)S(1)}, f32[48,640]{1,0:T(8,128)S(1)}, u32[]{:S(2)}, u32[]{:S(2)}) collective-permute-start(f32[48,640]{1,0:T(8,128)S(1)} %get-tuple-element.116.refs_0_), channel_id=1, source_target_pairs={{0,8},{8,0},{1,9},{9,1},{2,10},{10,2},{3,11},{11,3},{4,12},{12,4},... | collective-permute-start | bytes 368648 | tf_op jit(solution)/shard_map/ppermute | solution.py:429
  53.1 1.5 %collective-permute-start.21 = (f32[48,640]{1,0:T(8,128)S(1)}, f32[48,640]{1,0:T(8,128)S(1)}, u32[]{:S(2)}, u32[]{:S(2)}) collective-permute-start(f32[48,640]{1,0:T(8,128)S(1)} %collective-permute-done.17.refs_1_), channel_id=1, source_target_pairs={{0,8},{8,0},{1,9},{9,1},{2,10},{10,2},{3,11},{11,3},{4,12},{12,4},... | collective-permute-start | bytes 368648 | tf_op jit(solution)/shard_map/ppermute | solution.py:429
  53.7 1.3 %collective-permute-start.22 = (f32[48,640]{1,0:T(8,128)S(1)}, f32[48,640]{1,0:T(8,128)S(1)}, u32[]{:S(2)}, u32[]{:S(2)}) collective-permute-start(f32[48,640]{1,0:T(8,128)S(1)} %collective-permute-done.18.refs_2_), channel_id=1, source_target_pairs={{0,8},{8,0},{1,9},{9,1},{2,10},{10,2},{3,11},{11,3},{4,12},{12,4},... | collective-permute-start | bytes 368648 | tf_op jit(solution)/shard_map/ppermute | solution.py:429
  53.7 1.5 %collective-permute-start.23 = (f32[48,640]{1,0:T(8,128)S(1)}, f32[48,640]{1,0:T(8,128)S(1)}, u32[]{:S(2)}, u32[]{:S(2)}) collective-permute-start(f32[48,640]{1,0:T(8,128)S(1)} %collective-permute-done.19.refs_3_), channel_id=1, source_target_pairs={{0,8},{8,0},{1,9},{9,1},{2,10},{10,2},{3,11},{11,3},{4,12},{12,4},... | collective-permute-start | bytes 368648 | tf_op jit(solution)/shard_map/ppermute | solution.py:429
  57.9 8.4 %collective-permute-start.25 = (f32[48,1152]{1,0:T(8,128)S(1)}, f32[48,1152]{1,0:T(8,128)S(1)}, u32[]{:S(2)}, u32[]{:S(2)}) collective-permute-start(f32[48,1152]{1,0:T(8,128)S(1)} %scatter_far.1), channel_id=1, source_target_pairs={{0,128},{64,192},{128,0},{192,64},{1,129},{65,193},{129,1},{193,65... | collective-permute-start | bytes 663560 | tf_op jit(solution)/shard_map/ppermute | solution.py:429
  62.0 6.5 %collective-permute-start.26 = (f32[48,1152]{1,0:T(8,128)S(1)}, f32[48,1152]{1,0:T(8,128)S(1)}, u32[]{:S(2)}, u32[]{:S(2)}) collective-permute-start(f32[48,1152]{1,0:T(8,128)S(1)} %get-tuple-element.123), channel_id=1, source_target_pairs={{0,192},{64,0},{128,64},{192,128},{1,193},{65,1},{129,65},{193,129... | collective-permute-start | bytes 663560 | tf_op jit(solution)/shard_map/ppermute | solution.py:429
  63.3 7.3 %collective-permute-start.24 = (f32[48,1152]{1,0:T(8,128)S(1)}, f32[48,1152]{1,0:T(8,128)S(1)}, u32[]{:S(2)}, u32[]{:S(2)}) collective-permute-start(f32[48,1152]{1,0:T(8,128)S(1)} %get-tuple-element.121), channel_id=1, source_target_pairs={{0,64},{64,128},{128,192},{192,0},{1,65},{65,129},{129,193},{193,1... | collective-permute-start | bytes 663560 | tf_op jit(solution)/shard_map/ppermute | solution.py:429

commit v10 on v9

--- a/solution.py
+++ b/solution.py
@@ -158,12 +158,12 @@
     return jnp.sum(jnp.where(same, jnp.broadcast_to(row, (S, S)), 0.0), axis=1, keepdims=True)
 
 
-def pick(rows, request, shifts):
+def pick(rows, requests, shifts):
     x, y, c = lax.axis_index("x"), lax.axis_index("y"), lax.axis_index("core")
-    owner, cell = owner_and_cell(request)
-    cell_id = lax.broadcasted_iota(i32, (CELLS, WIDE), 0)
-    product = mm(rows, ones_where(jnp.broadcast_to(cell, (CELLS, WIDE)) == cell_id))
-    total = jnp.zeros((S, WIDE), f32)
+    owner, cell = [jnp.concatenate(both, axis=1) for both in zip(*map(owner_and_cell, requests))]
+    cell_id = lax.broadcasted_iota(i32, (CELLS, cell.shape[1]), 0)
+    product = mm(rows, ones_where(jnp.broadcast_to(cell, cell_id.shape) == cell_id))
+    total = jnp.zeros((S, cell.shape[1]), f32)
     for part, (shift, mate) in zip(sums_of(product, len(shifts)), shifts):
         from_x = jnp.bitwise_and(x - shift, 3)
         source_owner = (from_x * 4 + y) * 2 + (1 - c if mate else c)
@@ -183,7 +183,7 @@
             high, low = halves(ref[...])
             rows_ref[2 * S * i : 2 * S * i + S] = high
             rows_ref[2 * S * i + S : 2 * S * (i + 1)] = low
-        out_ref[...] = pick(rows_ref[...], request_out[row : row + 1, :], shifts)
+        out_ref[...] = pick(rows_ref[...], [request_out[row : row + 1, :]], shifts)
 
     return call(
         kernel,
@@ -199,11 +199,13 @@
     )
 
 
-def gather_next(requests, rows, shifts, row, name):
-    def kernel(request_ref, rows_ref, out_ref):
-        out_ref[...] = pick(rows_ref[...], request_ref[row : row + 1, :], shifts)
-
-    return call(kernel, sds(S, WIDE), [VMEM] * 2, requests, rows, name=name)
+def gather_next(requests, rows, shifts, boxes, name):
+    def kernel(request_ref, rows_ref, *outs):
+        total = pick(rows_ref[...], [request_ref[i : i + 1, :] for i in boxes], shifts)
+        for i, out in enumerate(outs):
+            out[...] = total[:, i * WIDE : (i + 1) * WIDE]
+
+    return call(kernel, [sds(S, WIDE)] * len(boxes), [VMEM] * 2, requests, rows, name=name)
 
 
 def side_by_side(boxes):
@@ -459,14 +461,13 @@
     part, strips = {}, {}
     part[2], rows, request_rows = gather_first(requests, sources, shifts, 2)
     strips[2] = shifted(part[2], "y", 2)
-    part[1] = gather_next(request_rows, rows, shifts, 1, "gather_one")
-    strips[1] = shifted(part[1], "y", 3)
-    part[3] = gather_next(after(request_rows, part[1]), rows, shifts, 3, "gather_three")
-    strips[3] = shifted(part[3], "y", 1)
-    strips[0] = gather_next(after(request_rows, (part[3], strips[2])), rows, shifts, 0, "gather_own")
+    part[1], part[3] = gather_next(request_rows, rows, shifts, (1, 3), "gather_near")
+    strips[1], strips[3] = shifted(part[1], "y", 3), shifted(part[3], "y", 1)
+    (strips[0],) = gather_next(after(request_rows, (part[3], strips[2])), rows, shifts, (0,), "gather_own")
     coarse_growth = coagulate(after(folded, (strips[0], strips[1])), [held_coarse], "coagulate_coarse")[0]
     mate_rows = shifted(request_rows, "core", 1)
-    strips, coarse_growth, mate_rows = lax.optimization_barrier((strips, coarse_growth, mate_rows))
+    cells = cells_by_row([request_rows, after(mate_rows, coarse_growth)])
+    strips, cells = lax.optimization_barrier((strips, cells))
     strips = [strips[k] for k in range(4)]
 
     middle, base, registers, x_ghosts, y_ghosts = first_stage(
@@ -475,9 +476,9 @@
 
     held = {k: shifted(registers, "y", k) for k in (2, 1, 3)}
     held[0] = registers
-    cells = cells_by_row([request_rows, after(mate_rows, registers)])
-    below_plane, above_plane = shifted(middle[3], "box", 1), shifted(middle[0], "box", 7)
-    growth = coagulate(after(folded, cells), middle, "coagulate_middle")
+    growth = coagulate(folded, middle, "coagulate_middle")
+    ends = (middle[3], middle[0])
+    below_plane, above_plane = shifted(ends[0], "box", 1), shifted(ends[1], "box", 7)
     held = [after(held[k], growth[0]) for k in range(4)]
     held += [shifted(value, "core", 1) for value in held]
     cells = after(cells, (below_plane, above_plane))

time: 72.3 us -> 71.6 us (level); the launches traced: 71.4 us -> 71.4 us
  starting transfers between devices: 33.1 us -> 34.3 us
    ppermute x27, starting transfers between devices: 33.1 us -> 34.3 us  [shifted(): lax.ppermute(value, axis, [(i, (i + shift) % size) for i in range(size)])]
    pallas_call x14 -> x13, Pallas kernels: 26.5 us -> 25.9 us  [call(): pl.pallas_call(kernel, out_shape=out_shape, in_specs=in_specs, out_specs=...]
  transfers between devices with their start and end apart: 27 -> 27, of which waited for: 6 -> 7; matrix products, arithmetic and copies ran while one was open for 0% -> 0% of each run, Pallas kernels for 35% -> 34%
where the time goes in v10:
time: 71.6 us; the launch traced here: 71.4 us
  starting transfers between devices  34.3 us (48%)
  Pallas kernels  29.4 us (41%)
  waiting for transfers between devices  4.21 us (6%)
  local copies, waits for them, and re-layouts  1.89 us (3%)
  between operations  0.9 us (1%)
    ppermute x27, starting transfers between devices, shifted(): lax.ppermute(value, axis, [(i, (i + shift) % size) for i in range(size)])  34.3 us
    pallas_call x13, Pallas kernels, call(): pl.pallas_call(kernel, out_shape=out_shape, in_specs=in_specs, out_specs=...  25.9 us
    ppermute x27, waiting for transfers between devices, shifted(): lax.ppermute(value, axis, [(i, (i + shift) % size) for i in range(size)])  4.21 us
    pallas_call x1, Pallas kernels, second_stage(): pl.pallas_call(kernel, out_shape=sds(S, X, PLANE), in_specs=[SMEM] + [VME...  2.24 us
    unnamed x8, local copies, waits for them, and re-layouts  1.88 us
  transfers between devices with their start and end apart: 27, of which 7 were waited for; matrix products, arithmetic and copies ran while one was open for 0% of the time, Pallas kernels for 34%

profile of v10, /device:TPU:1, one launch (start us, length us, event | category | flops | bytes accessed | tf_op | source)
XLA Modules:
  0.0 71.4 jit_solution(11050496794955266678)
XLA Ops:
  0.6 0.7 reduce
  1.3 2.2 %collective-permute-start.3 = (s32[24,576]{1,0:T(8,128)S(1)}, s32[24,576]{1,0:T(8,128)S(1)}, u32[]{:S(2)}, u32[]{:S(2)}) collective-permute-start(s32[24,576]{1,0:T(8,128)S(1)} %add.8), channel_id=1, source_target_pairs={{0,16},{16,32},{32,48},{48,0},{1,17},{17,33},{33,49},{49,1},{2,18}... | collective-permute-start | bytes 165896 | tf_op jit(solution)/shard_map/ppermute | solution.py:431
  3.5 2.5 %collective-permute-start.2 = (f32[48,1152]{1,0:T(8,128)}, f32[48,1152]{1,0:T(8,128)S(1)}, u32[]{:S(2)}, u32[]{:S(2)}) collective-permute-start(f32[48,1152]{1,0:T(8,128)} %bitcast.5), channel_id=1, source_target_pairs={{0,192},{64,0},{128,64},{192,128},{1,193},{65,1},{129,65},{193,129... | collective-permute-start | bytes 663560 | tf_op jit(solution)/shard_map/ppermute | solution.py:431
  6.0 0.5 collective-permute-start.1
  6.5 0.6 collective-permute-start
  7.2 1.8 %collective-permute-start.5 = (f32[48,1152]{1,0:T(8,128)}, f32[48,1152]{1,0:T(8,128)S(1)}, u32[]{:S(2)}, u32[]{:S(2)}) collective-permute-start(f32[48,1152]{1,0:T(8,128)} %bitcast.8), channel_id=1, source_target_pairs={{0,8},{8,0},{1,9},{9,1},{2,10},{10,2},{3,11},{11,3},{4,12},{12,4},... | collective-permute-start | bytes 663560 | tf_op jit(solution)/shard_map/ppermute | solution.py:431
  9.0 0.9 %copy-done = bf16[48,2304]{1,0:T(8,128)(2,1)S(1)} copy-done((bf16[48,2304]{1,0:T(8,128)(2,1)S(1)}, bf16[48,2304]{1,0:T(8,128)(2,1)}, u32[]{:S(2)}) %copy-start) | copy-done | bytes 221208
  9.9 1.8 %fold_kernel.1.matrix_ref = bf16[96,1280]{1,0:T(8,128)(2,1)S(1)} custom-call(bf16[48,2304]{1,0:T(8,128)(2,1)S(1)} %copy-done), custom_call_target="tpu_custom_call" | custom-call | tf_op jit(solution)/shard_map/fold_kernel/pallas_call | solution.py:34
  11.7 2.7 %collective-permute-start.4 = (s32[24,576]{1,0:T(8,128)S(1)}, s32[24,576]{1,0:T(8,128)S(1)}, u32[]{:S(2)}, u32[]{:S(2)}) collective-permute-start(s32[24,576]{1,0:T(8,128)S(1)} %pad_add_fusion.refs_0_), channel_id=1, source_target_pairs={{0,32},{16,48},{32,0},{48,16},{1,33},{17,49},{33,1},{49,17},{2,34}... | collective-permute-start | bytes 165896 | tf_op jit(solution)/shard_map/ppermute | solution.py:431
  14.4 0.9 %copy-done.1 = f32[1,1,48,1152]{3,2,1,0:T(8,128)S(1)} copy-done((f32[1,1,48,1152]{3,2,1,0:T(8,128)S(1)}, f32[1,1,48,1152]{3,2,1,0:T(8,128)}, u32[]{:S(2)}) %copy-start.1) | copy-done | bytes 221208
  15.4 1.3 %split_planes.1 = (f32[48,1024]{1,0:T(8,128)S(1)}, f32[48,1024]{1,0:T(8,128)S(1)}, f32[48,1024]{1,0:T(8,128)S(1)}, f32[48,1024]{1,0:T(8,128)S(1)}, f32[48,1152]{1,0:T(8,128)S(1)}) custom-call(f32[48,4,1024]{2,1,0:T(4,128)} %bitcast.12, f32[48,1152]{1,0:T(8,128)S(1)} %bitcast.9), custom_call_target="tpu_custom_call" | custom-call | tf_op jit(solution)/shard_map/split_planes/pallas_call | solution.py:107
  16.7 2.3 %coagulate_fine.1 = (f32[48,1024]{1,0:T(8,128)S(1)}, f32[48,1024]{1,0:T(8,128)S(1)}, f32[48,1024]{1,0:T(8,128)S(1)}, f32[48,1024]{1,0:T(8,128)S(1)}) custom-call(bf16[96,1280]{1,0:T(8,128)(2,1)S(1)} %fold_kernel.1.matrix_ref, f32[48,1024]{1,0:T(8,128)S(1)} %get-tuple-element.78.refs_0_, f32[48,1024]{1,0:T(8,128)S(1)} %get-tuple-element.79.refs_1_, ...), custom_call_target="tpu_custom_call" | custom-call | tf_op jit(solution)/shard_map/coagulate_fine/pallas_call | solution.py:34
  19.1 0.8 %collective-permute-done.refs_4_ = f32[48,1152]{1,0:T(8,128)S(1)} collective-permute-done((f32[48,1152]{1,0:T(8,128)}, f32[48,1152]{1,0:T(8,128)S(1)}, u32[]{:S(2)}, u32[]{:S(2)}) %collective-permute-start) | collective-permute-done | bytes 221216 | tf_op jit(solution)/shard_map/ppermute | solution.py:431
  19.8 0.5 collective-permute-start.6
  20.3 0.5 collective-permute-start.8
  20.8 5.6 %collective-permute-start.14 = (f32[48,1024]{1,0:T(8,128)S(1)}, f32[48,1024]{1,0:T(8,128)S(1)}, u32[]{:S(2)}, u32[]{:S(2)}) collective-permute-start(f32[48,1024]{1,0:T(8,128)S(1)} %get-tuple-element.78.refs_0_), channel_id=1, source_target_pairs={{0,7},{1,0},{2,1},{3,2},{4,3},{5,4},{6,5},{7,6},{8,15},{9,8},{10,9... | collective-permute-start | bytes 589832 | tf_op jit(solution)/shard_map/ppermute | solution.py:431
  26.4 1.8 %gather_first.1 = (f32[48,640]{1,0:T(8,128)S(1)}, bf16[768,1152]{1,0:T(8,128)(2,1)S(1)}, s32[4,576]{1,0:T(4,128)S(1)}) custom-call(s32[24,576]{1,0:T(8,128)S(1)} %pad_add_fusion.refs_0_, s32[24,576]{1,0:T(8,128)S(1)} %collective-permute-done.4.refs_1_, f32[48,1152]{1,0:T(8,128)S(1)} %get-tuple-element.76.refs_2_.refs_0_.coarse_ref, ...), custom_call_target="tpu_custom_call" | custom-call | tf_op jit(solution)/shard_map/gather_first/pallas_call | solution.py:34
  28.2 2.7 %collective-permute-start.10 = (f32[48,640]{1,0:T(8,128)S(1)}, f32[48,640]{1,0:T(8,128)S(1)}, u32[]{:S(2)}, u32[]{:S(2)}) collective-permute-start(f32[48,640]{1,0:T(8,128)S(1)} %get-tuple-element.94), channel_id=1, source_target_pairs={{0,32},{16,48},{32,0},{48,16},{1,33},{17,49},{33,1},{49,17},{2,34}... | collective-permute-start | bytes 368648 | tf_op jit(solution)/shard_map/ppermute | solution.py:431
  30.9 2.8 %gather_near.1 = (f32[48,640]{1,0:T(8,128)S(1)}, f32[48,640]{1,0:T(8,128)S(1)}) custom-call(s32[4,576]{1,0:T(4,128)S(1)} %get-tuple-element.95.request_ref.request_a, bf16[768,1152]{1,0:T(8,128)(2,1)S(1)} %get-tuple-element.92.rows_ref), custom_call_target="tpu_custom_call" | custom-call | tf_op jit(solution)/shard_map/gather_near/pallas_call | solution.py:34
  33.8 1.2 %collective-permute-start.11 = (f32[48,640]{1,0:T(8,128)S(1)}, f32[48,640]{1,0:T(8,128)S(1)}, u32[]{:S(2)}, u32[]{:S(2)}) collective-permute-start(f32[48,640]{1,0:T(8,128)S(1)} %get-tuple-element.96), channel_id=1, source_target_pairs={{0,48},{16,0},{32,16},{48,32},{1,49},{17,1},{33,17},{49,33},{2,50}... | collective-permute-start | bytes 368648 | tf_op jit(solution)/shard_map/ppermute | solution.py:431
  34.9 0.4 collective-permute-start.12
  35.3 1.1 %collective-permute-start.9 = (s32[4,576]{1,0:T(4,128)S(1)}, s32[4,576]{1,0:T(4,128)S(1)}, u32[]{:S(2)}, u32[]{:S(2)}) collective-permute-start(s32[4,576]{1,0:T(4,128)S(1)} %get-tuple-element.95.request_ref.request_a), channel_id=1, source_target_pairs={{0,8},{8,0},{1,9},{9,1},{2,10},{10,2},{3,11},{11,3},{4,12},{12,4},... | collective-permute-start | bytes 27656 | tf_op jit(solution)/shard_map/ppermute | solution.py:431
  36.5 1.7 %gather_own.1.refs_8_ = f32[48,640]{1,0:T(8,128)S(1)} custom-call(s32[4,576]{1,0:T(4,128)S(1)} %get-tuple-element.95.request_ref.request_a, bf16[768,1152]{1,0:T(8,128)(2,1)S(1)} %get-tuple-element.92.rows_ref), custom_call_target="tpu_custom_call" | custom-call | tf_op jit(solution)/shard_map/gather_own/pallas_call | solution.py:34
  38.2 0.7 %coagulate_coarse.1.growth_ref = f32[48,1152]{1,0:T(8,128)S(1)} custom-call(bf16[96,1280]{1,0:T(8,128)(2,1)S(1)} %fold_kernel.1.matrix_ref, f32[48,1152]{1,0:T(8,128)S(1)} %get-tuple-element.76.refs_2_.refs_0_.coarse_ref), custom_call_target="tpu_custom_call" | custom-call | tf_op jit(solution)/shard_map/coagulate_coarse/pallas_call | solution.py:34
  39.0 0.8 %cells_by_row.1.cell_ref = s32[4608,128]{1,0:T(8,128)S(1)} custom-call(s32[4,576]{1,0:T(4,128)S(1)} %get-tuple-element.95.request_ref.request_a, s32[4,576]{1,0:T(4,128)S(1)} %collective-permute-done.9.request_b), custom_call_target="tpu_custom_call" | custom-call | tf_op jit(solution)/shard_map/cells_by_row/pallas_call | solution.py:34
  39.8 0.1 collective-permute-done.12.refs_11_
  39.9 1.9 %first_stage.1 = (f32[48,1024]{1,0:T(8,128)S(1)}, f32[48,1024]{1,0:T(8,128)S(1)}, f32[48,1024]{1,0:T(8,128)S(1)}, f32[48,1024]{1,0:T(8,128)S(1)}, f32[48,1024]{1...) custom-call(s32[1,8]{1,0:T(1,128)S(1)} %copy-done.2, ...), custom_call_target="tpu_custom_call" | custom-call | tf_op jit(solution)/shard_map/first_stage/pallas_call | solution.py:34
  41.8 0.1 collective-permute-start.15
  41.9 2.3 %collective-permute-start.19 = (f32[48,640]{1,0:T(8,128)S(1)}, f32[48,640]{1,0:T(8,128)S(1)}, u32[]{:S(2)}, u32[]{:S(2)}) collective-permute-start(f32[48,640]{1,0:T(8,128)S(1)} %get-tuple-element.115.refs_0_), channel_id=1, source_target_pairs={{0,48},{16,0},{32,16},{48,32},{1,49},{17,1},{33,17},{49,33},{2,50}... | collective-permute-start | bytes 368648 | tf_op jit(solution)/shard_map/ppermute | solution.py:431
  44.1 0.7 collective-permute-start.17
  44.8 2.9 %collective-permute-start.16 = (f32[48,1024]{1,0:T(8,128)S(1)}, f32[48,1024]{1,0:T(8,128)S(1)}, u32[]{:S(2)}, u32[]{:S(2)}) collective-permute-start(f32[48,1024]{1,0:T(8,128)S(1)} %get-tuple-element.109.refs_0_), channel_id=1, source_target_pairs={{0,7},{1,0},{2,1},{3,2},{4,3},{5,4},{6,5},{7,6},{8,15},{9,8},{10,9... | collective-permute-start | bytes 589832 | tf_op jit(solution)/shard_map/ppermute | solution.py:431
  47.7 2.3 %coagulate_middle.1 = (f32[48,1024]{1,0:T(8,128)S(1)}, f32[48,1024]{1,0:T(8,128)S(1)}, f32[48,1024]{1,0:T(8,128)S(1)}, f32[48,1024]{1,0:T(8,128)S(1)}) custom-call(bf16[96,1280]{1,0:T(8,128)(2,1)S(1)} %fold_kernel.1.matrix_ref, f32[48,1024]{1,0:T(8,128)S(1)} %get-tuple-element.109.refs_0_, f32[48,1024]{1,0:T(8,128)S(1)} %get-tuple-element.112.refs_1_, ...), custom_call_target="tpu_custom_call" | custom-call | tf_op jit(solution)/shard_map/coagulate_middle/pallas_call | solution.py:34
  50.1 2.1 %collective-permute-start.20 = (f32[48,640]{1,0:T(8,128)S(1)}, f32[48,640]{1,0:T(8,128)S(1)}, u32[]{:S(2)}, u32[]{:S(2)}) collective-permute-start(f32[48,640]{1,0:T(8,128)S(1)} %get-tuple-element.115.refs_0_), channel_id=1, source_target_pairs={{0,8},{8,0},{1,9},{9,1},{2,10},{10,2},{3,11},{11,3},{4,12},{12,4},... | collective-permute-start | bytes 368648 | tf_op jit(solution)/shard_map/ppermute | solution.py:431
  52.2 0.2 collective-permute-done.17.refs_1_
  52.5 1.3 %collective-permute-start.21 = (f32[48,640]{1,0:T(8,128)S(1)}, f32[48,640]{1,0:T(8,128)S(1)}, u32[]{:S(2)}, u32[]{:S(2)}) collective-permute-start(f32[48,640]{1,0:T(8,128)S(1)} %collective-permute-done.17.refs_1_), channel_id=1, source_target_pairs={{0,8},{8,0},{1,9},{9,1},{2,10},{10,2},{3,11},{11,3},{4,12},{12,4},... | collective-permute-start | bytes 368648 | tf_op jit(solution)/shard_map/ppermute | solution.py:431
  53.7 0.5 collective-permute-start.23
  54.2 0.5 collective-permute-done.21.refs_5_
  54.7 0.4 collective-permute-done.22.refs_6_
  55.1 0.2 collective-permute-done.23.refs_7_
  55.2 2.7 %scatter_far.1 = f32[48,1152]{1,0:T(8,128)S(1)} custom-call(s32[4,576]{1,0:T(4,128)S(1)} %get-tuple-element.95.request_ref.request_a, s32[4,576]{1,0:T(4,128)S(1)} %collective-permute-done.9.request_b, s32[4608,128]{1,0:T(8,128)S(1)} %cells_by_row.1.cell_ref, f32[48,640]{1,0:T(8,128)S(1)} %get-tuple-element.115.refs_0_, ...), custom_call_target="tpu_custom_call" | custom-call | tf_op jit(solution)/shard_map/scatter_far/pallas_call | solution.py:34
  57.9 0.6 collective-permute-start.25
  58.5 3.5 %scatter_near.1 = (f32[48,1152]{1,0:T(8,128)S(1)}, f32[48,1152]{1,0:T(8,128)S(1)}) custom-call(s32[4,576]{1,0:T(4,128)S(1)} %get-tuple-element.95.request_ref.request_a, s32[4,576]{1,0:T(4,128)S(1)} %collective-permute-done.9.request_b, s32[4608,128]{1,0:T(8,128)S(1)} %cells_by_row.1.cell_ref, f32[48,640]{1,0:T(8,128)S(1)} %get-tuple-element.115.refs_0_, ...), custom_call_target="tpu_custom_call" | custom-call | tf_op jit(solution)/shard_map/scatter_near/pallas_call | solution.py:34
  62.1 1.3 %collective-permute-start.26 = (f32[48,1152]{1,0:T(8,128)S(1)}, f32[48,1152]{1,0:T(8,128)S(1)}, u32[]{:S(2)}, u32[]{:S(2)}) collective-permute-start(f32[48,1152]{1,0:T(8,128)S(1)} %get-tuple-element.122), channel_id=1, source_target_pairs={{0,192},{64,0},{128,64},{192,128},{1,193},{65,1},{129,65},{193,129... | collective-permute-start | bytes 663560 | tf_op jit(solution)/shard_map/ppermute | solution.py:431
  63.4 0.2 collective-permute-start.24
  63.6 2.7 %scatter_own.1.a = f32[48,1152]{1,0:T(8,128)S(1)} custom-call(s32[4,576]{1,0:T(4,128)S(1)} %get-tuple-element.95.request_ref.request_a, s32[4,576]{1,0:T(4,128)S(1)} %collective-permute-done.9.request_b, s32[4608,128]{1,0:T(8,128)S(1)} %cells_by_row.1.cell_ref, f32[48,640]{1,0:T(8,128)S(1)} %get-tuple-element.115.refs_0_, ...), custom_call_target="tpu_custom_call" | custom-call | tf_op jit(solution)/shard_map/scatter_own/pallas_call | solution.py:34
  66.3 2.2 %second_stage.1 = f32[48,4,1024]{2,1,0:T(4,128)} custom-call(s32[1,8]{1,0:T(1,128)S(1)} %copy-done.2, f32[1,48]{1,0:T(1,128)S(1)} %bitcast.11, f32[48,1024]{1,0:T(8,128)S(1)} %get-tuple-element.109.refs_0_, f32[48,1024]{1,0:T(8,128)S(1)} %get-tuple-element.112.refs_1_, f32[48,1024]{1,0:T(8,128)S(1)} %get-tuple-element.113.refs_2_, ...), custom_call_target="tpu_custom_call" | custom-call | tf_op jit(solution)/shard_map/second_stage/pallas_call | solution.py:409
  68.6 2.0 %collective-permute-done.24.b = f32[48,1152]{1,0:T(8,128)S(1)} collective-permute-done((f32[48,1152]{1,0:T(8,128)S(1)}, f32[48,1152]{1,0:T(8,128)S(1)}, u32[]{:S(2)}, u32[]{:S(2)}) %collective-permute-start.24) | collective-permute-done | bytes 221216 | tf_op jit(solution)/shard_map/ppermute | solution.py:431
  70.6 0.8 %finish_coarse.1 = f32[48,1152]{1,0:T(8,128)} custom-call(f32[48,1152]{1,0:T(8,128)S(1)} %get-tuple-element.76.refs_2_.refs_0_.coarse_ref, f32[48,1152]{1,0:T(8,128)S(1)} %coagulate_coarse.1.growth_ref, f32[48,1152]{1,0:T(8,128)S(1)} %scatter_own.1.a, f32[48,1152]{1,0:T(8,128)S(1)} %collective-permute-done.24.b, f32[48,1152]{1,0:T(8,128)S(1)} %collective-permute-done.25.c, ...), custom_call_target="tpu_custom_call" | custom-call | tf_op jit(solution)/shard_map/finish_coarse/pallas_call | solution.py:34
  (34 shorter events, 0.1 us)
Async XLA Ops:
  1.3 10.3 %collective-permute-start.3 = (s32[24,576]{1,0:T(8,128)S(1)}, s32[24,576]{1,0:T(8,128)S(1)}, u32[]{:S(2)}, u32[]{:S(2)}) collective-permute-start(s32[24,576]{1,0:T(8,128)S(1)} %add.8), channel_id=1, source_target_pairs={{0,16},{16,32},{32,48},{48,0},{1,17},{17,33},{33,49},{49,1},{2,18}... | collective-permute-start | bytes 165896 | tf_op jit(solution)/shard_map/ppermute | solution.py:431
  3.5 15.5 %collective-permute-start.2 = (f32[48,1152]{1,0:T(8,128)}, f32[48,1152]{1,0:T(8,128)S(1)}, u32[]{:S(2)}, u32[]{:S(2)}) collective-permute-start(f32[48,1152]{1,0:T(8,128)} %bitcast.5), channel_id=1, source_target_pairs={{0,192},{64,0},{128,64},{192,128},{1,193},{65,1},{129,65},{193,129... | collective-permute-start | bytes 663560 | tf_op jit(solution)/shard_map/ppermute | solution.py:431
  6.0 13.0 %collective-permute-start.1 = (f32[48,1152]{1,0:T(8,128)}, f32[48,1152]{1,0:T(8,128)S(1)}, u32[]{:S(2)}, u32[]{:S(2)}) collective-permute-start(f32[48,1152]{1,0:T(8,128)} %bitcast.6), channel_id=1, source_target_pairs={{0,128},{64,192},{128,0},{192,64},{1,129},{65,193},{129,1},{193,65... | collective-permute-start | bytes 663560 | tf_op jit(solution)/shard_map/ppermute | solution.py:431
  6.5 13.3 %collective-permute-start = (f32[48,1152]{1,0:T(8,128)}, f32[48,1152]{1,0:T(8,128)S(1)}, u32[]{:S(2)}, u32[]{:S(2)}) collective-permute-start(f32[48,1152]{1,0:T(8,128)} %bitcast.7), channel_id=1, source_target_pairs={{0,64},{64,128},{128,192},{192,0},{1,65},{65,129},{129,193},{193,1... | collective-permute-start | bytes 663560 | tf_op jit(solution)/shard_map/ppermute | solution.py:431
  7.2 19.3 %collective-permute-start.5 = (f32[48,1152]{1,0:T(8,128)}, f32[48,1152]{1,0:T(8,128)S(1)}, u32[]{:S(2)}, u32[]{:S(2)}) collective-permute-start(f32[48,1152]{1,0:T(8,128)} %bitcast.8), channel_id=1, source_target_pairs={{0,8},{8,0},{1,9},{9,1},{2,10},{10,2},{3,11},{11,3},{4,12},{12,4},... | collective-permute-start | bytes 663560 | tf_op jit(solution)/shard_map/ppermute | solution.py:431
  8.9 0.9 %copy-start = (bf16[48,2304]{1,0:T(8,128)(2,1)S(1)}, bf16[48,2304]{1,0:T(8,128)(2,1)}, u32[]{:S(2)}) copy-start(bf16[48,2304]{1,0:T(8,128)(2,1)} %matrix_ref.1) | copy-start | bytes 663556
  11.7 7.3 %collective-permute-start.4 = (s32[24,576]{1,0:T(8,128)S(1)}, s32[24,576]{1,0:T(8,128)S(1)}, u32[]{:S(2)}, u32[]{:S(2)}) collective-permute-start(s32[24,576]{1,0:T(8,128)S(1)} %pad_add_fusion.refs_0_), channel_id=1, source_target_pairs={{0,32},{16,48},{32,0},{48,16},{1,33},{17,49},{33,1},{49,17},{2,34}... | collective-permute-start | bytes 165896 | tf_op jit(solution)/shard_map/ppermute | solution.py:431
  14.4 0.9 %copy-start.1 = (f32[1,1,48,1152]{3,2,1,0:T(8,128)S(1)}, f32[1,1,48,1152]{3,2,1,0:T(8,128)}, u32[]{:S(2)}) copy-start(f32[1,1,48,1152]{3,2,1,0:T(8,128)} %param.7) | copy-start | bytes 663556
  19.8 6.6 %collective-permute-start.6 = (f32[48,1152]{1,0:T(8,128)S(1)}, f32[48,1152]{1,0:T(8,128)S(1)}, u32[]{:S(2)}, u32[]{:S(2)}) collective-permute-start(f32[48,1152]{1,0:T(8,128)S(1)} %collective-permute-done.refs_4_), channel_id=1, source_target_pairs={{0,8},{8,0},{1,9},{9,1},{2,10},{10,2},{3,11},{11,3},{4,12},{12,4},... | collective-permute-start | bytes 663560 | tf_op jit(solution)/shard_map/ppermute | solution.py:431
  20.3 6.1 %collective-permute-start.7 = (f32[48,1152]{1,0:T(8,128)S(1)}, f32[48,1152]{1,0:T(8,128)S(1)}, u32[]{:S(2)}, u32[]{:S(2)}) collective-permute-start(f32[48,1152]{1,0:T(8,128)S(1)} %collective-permute-done.2.refs_6_), channel_id=1, source_target_pairs={{0,8},{8,0},{1,9},{9,1},{2,10},{10,2},{3,11},{11,3},{4,12},{12,4},... | collective-permute-start | bytes 663560 | tf_op jit(solution)/shard_map/ppermute | solution.py:431
  20.3 6.1 %collective-permute-start.8 = (f32[48,1152]{1,0:T(8,128)S(1)}, f32[48,1152]{1,0:T(8,128)S(1)}, u32[]{:S(2)}, u32[]{:S(2)}) collective-permute-start(f32[48,1152]{1,0:T(8,128)S(1)} %collective-permute-done.1.refs_8_), channel_id=1, source_target_pairs={{0,8},{8,0},{1,9},{9,1},{2,10},{10,2},{3,11},{11,3},{4,12},{12,4},... | collective-permute-start | bytes 663560 | tf_op jit(solution)/shard_map/ppermute | solution.py:431
  20.8 19.1 %collective-permute-start.14 = (f32[48,1024]{1,0:T(8,128)S(1)}, f32[48,1024]{1,0:T(8,128)S(1)}, u32[]{:S(2)}, u32[]{:S(2)}) collective-permute-start(f32[48,1024]{1,0:T(8,128)S(1)} %get-tuple-element.78.refs_0_), channel_id=1, source_target_pairs={{0,7},{1,0},{2,1},{3,2},{4,3},{5,4},{6,5},{7,6},{8,15},{9,8},{10,9... | collective-permute-start | bytes 589832 | tf_op jit(solution)/shard_map/ppermute | solution.py:431
  26.4 13.5 %collective-permute-start.13 = (f32[48,1024]{1,0:T(8,128)S(1)}, f32[48,1024]{1,0:T(8,128)S(1)}, u32[]{:S(2)}, u32[]{:S(2)}) collective-permute-start(f32[48,1024]{1,0:T(8,128)S(1)} %get-tuple-element.81.refs_3_), channel_id=1, source_target_pairs={{0,1},{1,2},{2,3},{3,4},{4,5},{5,6},{6,7},{7,0},{8,9},{9,10},{10,1... | collective-permute-start | bytes 589832 | tf_op jit(solution)/shard_map/ppermute | solution.py:431
  28.2 7.1 %collective-permute-start.10 = (f32[48,640]{1,0:T(8,128)S(1)}, f32[48,640]{1,0:T(8,128)S(1)}, u32[]{:S(2)}, u32[]{:S(2)}) collective-permute-start(f32[48,640]{1,0:T(8,128)S(1)} %get-tuple-element.94), channel_id=1, source_target_pairs={{0,32},{16,48},{32,0},{48,16},{1,33},{17,49},{33,1},{49,17},{2,34}... | collective-permute-start | bytes 368648 | tf_op jit(solution)/shard_map/ppermute | solution.py:431
  33.8 4.4 %collective-permute-start.11 = (f32[48,640]{1,0:T(8,128)S(1)}, f32[48,640]{1,0:T(8,128)S(1)}, u32[]{:S(2)}, u32[]{:S(2)}) collective-permute-start(f32[48,640]{1,0:T(8,128)S(1)} %get-tuple-element.96), channel_id=1, source_target_pairs={{0,48},{16,0},{32,16},{48,32},{1,49},{17,1},{33,17},{49,33},{2,50}... | collective-permute-start | bytes 368648 | tf_op jit(solution)/shard_map/ppermute | solution.py:431
  34.9 5.0 %copy-start.2 = (s32[1,8]{1,0:T(1,128)S(1)}, s32[1,8]{1,0:T(1,128)}, u32[]{:S(2)}) copy-start(s32[1,8]{1,0:T(1,128)} %levels_ref.3) | copy-start | bytes 100
  34.9 5.0 %copy-start.3 = (f32[48]{0:T(128)S(1)}, f32[48]{0:T(128)}, u32[]{:S(2)}) copy-start(f32[48]{0:T(128)} %param.9) | copy-start | bytes 580
  34.9 4.9 %collective-permute-start.12 = (f32[48,640]{1,0:T(8,128)S(1)}, f32[48,640]{1,0:T(8,128)S(1)}, u32[]{:S(2)}, u32[]{:S(2)}) collective-permute-start(f32[48,640]{1,0:T(8,128)S(1)} %get-tuple-element.93), channel_id=1, source_target_pairs={{0,16},{16,32},{32,48},{48,0},{1,17},{17,33},{33,49},{49,1},{2,18}... | collective-permute-start | bytes 368648 | tf_op jit(solution)/shard_map/ppermute | solution.py:431
  35.3 3.7 %collective-permute-start.9 = (s32[4,576]{1,0:T(4,128)S(1)}, s32[4,576]{1,0:T(4,128)S(1)}, u32[]{:S(2)}, u32[]{:S(2)}) collective-permute-start(s32[4,576]{1,0:T(4,128)S(1)} %get-tuple-element.95.request_ref.request_a), channel_id=1, source_target_pairs={{0,8},{8,0},{1,9},{9,1},{2,10},{10,2},{3,11},{11,3},{4,12},{12,4},... | collective-permute-start | bytes 27656 | tf_op jit(solution)/shard_map/ppermute | solution.py:431
  41.8 12.0 %collective-permute-start.15 = (f32[48,1024]{1,0:T(8,128)S(1)}, f32[48,1024]{1,0:T(8,128)S(1)}, u32[]{:S(2)}, u32[]{:S(2)}) collective-permute-start(f32[48,1024]{1,0:T(8,128)S(1)} %get-tuple-element.108.refs_3_), channel_id=1, source_target_pairs={{0,1},{1,2},{2,3},{3,4},{4,5},{5,6},{6,7},{7,0},{8,9},{9,10},{10,1... | collective-permute-start | bytes 589832 | tf_op jit(solution)/shard_map/ppermute | solution.py:431
  41.9 8.2 %collective-permute-start.19 = (f32[48,640]{1,0:T(8,128)S(1)}, f32[48,640]{1,0:T(8,128)S(1)}, u32[]{:S(2)}, u32[]{:S(2)}) collective-permute-start(f32[48,640]{1,0:T(8,128)S(1)} %get-tuple-element.115.refs_0_), channel_id=1, source_target_pairs={{0,48},{16,0},{32,16},{48,32},{1,49},{17,1},{33,17},{49,33},{2,50}... | collective-permute-start | bytes 368648 | tf_op jit(solution)/shard_map/ppermute | solution.py:431
  44.1 8.1 %collective-permute-start.18 = (f32[48,640]{1,0:T(8,128)S(1)}, f32[48,640]{1,0:T(8,128)S(1)}, u32[]{:S(2)}, u32[]{:S(2)}) collective-permute-start(f32[48,640]{1,0:T(8,128)S(1)} %get-tuple-element.115.refs_0_), channel_id=1, source_target_pairs={{0,32},{16,48},{32,0},{48,16},{1,33},{17,49},{33,1},{49,17},{2,34}... | collective-permute-start | bytes 368648 | tf_op jit(solution)/shard_map/ppermute | solution.py:431
  44.1 8.3 %collective-permute-start.17 = (f32[48,640]{1,0:T(8,128)S(1)}, f32[48,640]{1,0:T(8,128)S(1)}, u32[]{:S(2)}, u32[]{:S(2)}) collective-permute-start(f32[48,640]{1,0:T(8,128)S(1)} %get-tuple-element.115.refs_0_), channel_id=1, source_target_pairs={{0,16},{16,32},{32,48},{48,0},{1,17},{17,33},{33,49},{49,1},{2,18}... | collective-permute-start | bytes 368648 | tf_op jit(solution)/shard_map/ppermute | solution.py:431
  44.8 9.4 %collective-permute-start.16 = (f32[48,1024]{1,0:T(8,128)S(1)}, f32[48,1024]{1,0:T(8,128)S(1)}, u32[]{:S(2)}, u32[]{:S(2)}) collective-permute-start(f32[48,1024]{1,0:T(8,128)S(1)} %get-tuple-element.109.refs_0_), channel_id=1, source_target_pairs={{0,7},{1,0},{2,1},{3,2},{4,3},{5,4},{6,5},{7,6},{8,15},{9,8},{10,9... | collective-permute-start | bytes 589832 | tf_op jit(solution)/shard_map/ppermute | solution.py:431
  50.1 4.1 %collective-permute-start.20 = (f32[48,640]{1,0:T(8,128)S(1)}, f32[48,640]{1,0:T(8,128)S(1)}, u32[]{:S(2)}, u32[]{:S(2)}) collective-permute-start(f32[48,640]{1,0:T(8,128)S(1)} %get-tuple-element.115.refs_0_), channel_id=1, source_target_pairs={{0,8},{8,0},{1,9},{9,1},{2,10},{10,2},{3,11},{11,3},{4,12},{12,4},... | collective-permute-start | bytes 368648 | tf_op jit(solution)/shard_map/ppermute | solution.py:431
  52.5 2.2 %collective-permute-start.21 = (f32[48,640]{1,0:T(8,128)S(1)}, f32[48,640]{1,0:T(8,128)S(1)}, u32[]{:S(2)}, u32[]{:S(2)}) collective-permute-start(f32[48,640]{1,0:T(8,128)S(1)} %collective-permute-done.17.refs_1_), channel_id=1, source_target_pairs={{0,8},{8,0},{1,9},{9,1},{2,10},{10,2},{3,11},{11,3},{4,12},{12,4},... | collective-permute-start | bytes 368648 | tf_op jit(solution)/shard_map/ppermute | solution.py:431
  53.7 1.3 %collective-permute-start.22 = (f32[48,640]{1,0:T(8,128)S(1)}, f32[48,640]{1,0:T(8,128)S(1)}, u32[]{:S(2)}, u32[]{:S(2)}) collective-permute-start(f32[48,640]{1,0:T(8,128)S(1)} %collective-permute-done.18.refs_2_), channel_id=1, source_target_pairs={{0,8},{8,0},{1,9},{9,1},{2,10},{10,2},{3,11},{11,3},{4,12},{12,4},... | collective-permute-start | bytes 368648 | tf_op jit(solution)/shard_map/ppermute | solution.py:431
  53.7 1.5 %collective-permute-start.23 = (f32[48,640]{1,0:T(8,128)S(1)}, f32[48,640]{1,0:T(8,128)S(1)}, u32[]{:S(2)}, u32[]{:S(2)}) collective-permute-start(f32[48,640]{1,0:T(8,128)S(1)} %collective-permute-done.19.refs_3_), channel_id=1, source_target_pairs={{0,8},{8,0},{1,9},{9,1},{2,10},{10,2},{3,11},{11,3},{4,12},{12,4},... | collective-permute-start | bytes 368648 | tf_op jit(solution)/shard_map/ppermute | solution.py:431
  57.9 8.4 %collective-permute-start.25 = (f32[48,1152]{1,0:T(8,128)S(1)}, f32[48,1152]{1,0:T(8,128)S(1)}, u32[]{:S(2)}, u32[]{:S(2)}) collective-permute-start(f32[48,1152]{1,0:T(8,128)S(1)} %scatter_far.1), channel_id=1, source_target_pairs={{0,128},{64,192},{128,0},{192,64},{1,129},{65,193},{129,1},{193,65... | collective-permute-start | bytes 663560 | tf_op jit(solution)/shard_map/ppermute | solution.py:431
  62.1 6.5 %collective-permute-start.26 = (f32[48,1152]{1,0:T(8,128)S(1)}, f32[48,1152]{1,0:T(8,128)S(1)}, u32[]{:S(2)}, u32[]{:S(2)}) collective-permute-start(f32[48,1152]{1,0:T(8,128)S(1)} %get-tuple-element.122), channel_id=1, source_target_pairs={{0,192},{64,0},{128,64},{192,128},{1,193},{65,1},{129,65},{193,129... | collective-permute-start | bytes 663560 | tf_op jit(solution)/shard_map/ppermute | solution.py:431
  63.4 7.2 %collective-permute-start.24 = (f32[48,1152]{1,0:T(8,128)S(1)}, f32[48,1152]{1,0:T(8,128)S(1)}, u32[]{:S(2)}, u32[]{:S(2)}) collective-permute-start(f32[48,1152]{1,0:T(8,128)S(1)} %get-tuple-element.120), channel_id=1, source_target_pairs={{0,64},{64,128},{128,192},{192,0},{1,65},{65,129},{129,193},{193,1... | collective-permute-start | bytes 663560 | tf_op jit(solution)/shard_map/ppermute | solution.py:431

commit v11 on v10

--- a/solution.py
+++ b/solution.py
@@ -477,10 +477,11 @@
     held = {k: shifted(registers, "y", k) for k in (2, 1, 3)}
     held[0] = registers
     growth = coagulate(folded, middle, "coagulate_middle")
-    ends = (middle[3], middle[0])
+    own_mate = shifted(registers, "core", 1)
+    ends = after((middle[3], middle[0]), own_mate)
     below_plane, above_plane = shifted(ends[0], "box", 1), shifted(ends[1], "box", 7)
     held = [after(held[k], growth[0]) for k in range(4)]
-    held += [shifted(value, "core", 1) for value in held]
+    held += [own_mate] + [shifted(value, "core", 1) for value in held[1:]]
     cells = after(cells, (below_plane, above_plane))
     sent = {}
     (part,) = scatter_columns([request_rows, mate_rows], cells, held, (2,), "scatter_far")

time: 71.6 us -> 72.7 us (1.015)
  waiting for transfers between devices: 4.21 us -> 6.99 us
  starting transfers between devices: 34.3 us -> 32.6 us
    ppermute x27, waiting for transfers between devices: 4.21 us -> 6.99 us  [shifted(): lax.ppermute(value, axis, [(i, (i + shift) % size) for i in range(size)])]
    ppermute x27, starting transfers between devices: 34.3 us -> 32.6 us  [shifted(): lax.ppermute(value, axis, [(i, (i + shift) % size) for i in range(size)])]
  transfers between devices with their start and end apart: 27 -> 27, of which waited for: 7 -> 8; matrix products, arithmetic and copies ran while one was open for 0% -> 0% of each run, Pallas kernels for 34% -> 33%
where the time goes in v11:
time: 72.7 us; the launch traced here: 72.5 us
  starting transfers between devices  32.6 us (45%)
  Pallas kernels  29.4 us (40%)
  waiting for transfers between devices  6.99 us (10%)
  local copies, waits for them, and re-layouts  1.89 us (3%)
  between operations  0.88 us (1%)
    ppermute x27, starting transfers between devices, shifted(): lax.ppermute(value, axis, [(i, (i + shift) % size) for i in range(size)])  32.6 us
    pallas_call x13, Pallas kernels, call(): pl.pallas_call(kernel, out_shape=out_shape, in_specs=in_specs, out_specs=...  25.9 us
    ppermute x27, waiting for transfers between devices, shifted(): lax.ppermute(value, axis, [(i, (i + shift) % size) for i in range(size)])  6.99 us
    pallas_call x1, Pallas kernels, second_stage(): pl.pallas_call(kernel, out_shape=sds(S, X, PLANE), in_specs=[SMEM] + [VME...  2.24 us
    unnamed x8, local copies, waits for them, and re-layouts  1.88 us
  transfers between devices with their start and end apart: 27, of which 8 were waited for; matrix products, arithmetic and copies ran while one was open for 0% of the time, Pallas kernels for 33%

profile of v11, /device:TPU:1, one launch (start us, length us, event | category | flops | bytes accessed | tf_op | source)
XLA Modules:
  0.0 72.5 jit_solution(5298152133393673918)
XLA Ops:
  0.6 0.7 reduce
  1.3 2.2 %collective-permute-start.3 = (s32[24,576]{1,0:T(8,128)S(1)}, s32[24,576]{1,0:T(8,128)S(1)}, u32[]{:S(2)}, u32[]{:S(2)}) collective-permute-start(s32[24,576]{1,0:T(8,128)S(1)} %add.8), channel_id=1, source_target_pairs={{0,16},{16,32},{32,48},{48,0},{1,17},{17,33},{33,49},{49,1},{2,18}... | collective-permute-start | bytes 165896 | tf_op jit(solution)/shard_map/ppermute | solution.py:431
  3.5 2.5 %collective-permute-start.2 = (f32[48,1152]{1,0:T(8,128)}, f32[48,1152]{1,0:T(8,128)S(1)}, u32[]{:S(2)}, u32[]{:S(2)}) collective-permute-start(f32[48,1152]{1,0:T(8,128)} %bitcast.5), channel_id=1, source_target_pairs={{0,192},{64,0},{128,64},{192,128},{1,193},{65,1},{129,65},{193,129... | collective-permute-start | bytes 663560 | tf_op jit(solution)/shard_map/ppermute | solution.py:431
  6.0 0.5 collective-permute-start.1
  6.5 0.6 collective-permute-start
  7.2 1.8 %collective-permute-start.5 = (f32[48,1152]{1,0:T(8,128)}, f32[48,1152]{1,0:T(8,128)S(1)}, u32[]{:S(2)}, u32[]{:S(2)}) collective-permute-start(f32[48,1152]{1,0:T(8,128)} %bitcast.8), channel_id=1, source_target_pairs={{0,8},{8,0},{1,9},{9,1},{2,10},{10,2},{3,11},{11,3},{4,12},{12,4},... | collective-permute-start | bytes 663560 | tf_op jit(solution)/shard_map/ppermute | solution.py:431
  9.0 0.9 %copy-done = bf16[48,2304]{1,0:T(8,128)(2,1)S(1)} copy-done((bf16[48,2304]{1,0:T(8,128)(2,1)S(1)}, bf16[48,2304]{1,0:T(8,128)(2,1)}, u32[]{:S(2)}) %copy-start) | copy-done | bytes 221208
  9.9 1.8 %fold_kernel.1.matrix_ref = bf16[96,1280]{1,0:T(8,128)(2,1)S(1)} custom-call(bf16[48,2304]{1,0:T(8,128)(2,1)S(1)} %copy-done), custom_call_target="tpu_custom_call" | custom-call | tf_op jit(solution)/shard_map/fold_kernel/pallas_call | solution.py:34
  11.7 2.7 %collective-permute-start.4 = (s32[24,576]{1,0:T(8,128)S(1)}, s32[24,576]{1,0:T(8,128)S(1)}, u32[]{:S(2)}, u32[]{:S(2)}) collective-permute-start(s32[24,576]{1,0:T(8,128)S(1)} %pad_add_fusion.refs_0_), channel_id=1, source_target_pairs={{0,32},{16,48},{32,0},{48,16},{1,33},{17,49},{33,1},{49,17},{2,34}... | collective-permute-start | bytes 165896 | tf_op jit(solution)/shard_map/ppermute | solution.py:431
  14.4 0.9 %copy-done.1 = f32[1,1,48,1152]{3,2,1,0:T(8,128)S(1)} copy-done((f32[1,1,48,1152]{3,2,1,0:T(8,128)S(1)}, f32[1,1,48,1152]{3,2,1,0:T(8,128)}, u32[]{:S(2)}) %copy-start.1) | copy-done | bytes 221208
  15.4 1.3 %split_planes.1 = (f32[48,1024]{1,0:T(8,128)S(1)}, f32[48,1024]{1,0:T(8,128)S(1)}, f32[48,1024]{1,0:T(8,128)S(1)}, f32[48,1024]{1,0:T(8,128)S(1)}, f32[48,1152]{1,0:T(8,128)S(1)}) custom-call(f32[48,4,1024]{2,1,0:T(4,128)} %bitcast.12, f32[48,1152]{1,0:T(8,128)S(1)} %bitcast.9), custom_call_target="tpu_custom_call" | custom-call | tf_op jit(solution)/shard_map/split_planes/pallas_call | solution.py:107
  16.7 2.3 %coagulate_fine.1 = (f32[48,1024]{1,0:T(8,128)S(1)}, f32[48,1024]{1,0:T(8,128)S(1)}, f32[48,1024]{1,0:T(8,128)S(1)}, f32[48,1024]{1,0:T(8,128)S(1)}) custom-call(bf16[96,1280]{1,0:T(8,128)(2,1)S(1)} %fold_kernel.1.matrix_ref, f32[48,1024]{1,0:T(8,128)S(1)} %get-tuple-element.80.refs_0_, f32[48,1024]{1,0:T(8,128)S(1)} %get-tuple-element.81.refs_1_, ...), custom_call_target="tpu_custom_call" | custom-call | tf_op jit(solution)/shard_map/coagulate_fine/pallas_call | solution.py:34
  19.1 0.8 %collective-permute-done.refs_4_ = f32[48,1152]{1,0:T(8,128)S(1)} collective-permute-done((f32[48,1152]{1,0:T(8,128)}, f32[48,1152]{1,0:T(8,128)S(1)}, u32[]{:S(2)}, u32[]{:S(2)}) %collective-permute-start) | collective-permute-done | bytes 221216 | tf_op jit(solution)/shard_map/ppermute | solution.py:431
  19.8 0.5 collective-permute-start.6
  20.3 0.5 collective-permute-start.8
  20.8 5.6 %collective-permute-start.14 = (f32[48,1024]{1,0:T(8,128)S(1)}, f32[48,1024]{1,0:T(8,128)S(1)}, u32[]{:S(2)}, u32[]{:S(2)}) collective-permute-start(f32[48,1024]{1,0:T(8,128)S(1)} %get-tuple-element.80.refs_0_), channel_id=1, source_target_pairs={{0,7},{1,0},{2,1},{3,2},{4,3},{5,4},{6,5},{7,6},{8,15},{9,8},{10,9... | collective-permute-start | bytes 589832 | tf_op jit(solution)/shard_map/ppermute | solution.py:431
  26.4 1.8 %gather_first.1 = (f32[48,640]{1,0:T(8,128)S(1)}, bf16[768,1152]{1,0:T(8,128)(2,1)S(1)}, s32[4,576]{1,0:T(4,128)S(1)}) custom-call(s32[24,576]{1,0:T(8,128)S(1)} %pad_add_fusion.refs_0_, s32[24,576]{1,0:T(8,128)S(1)} %collective-permute-done.4.refs_1_, f32[48,1152]{1,0:T(8,128)S(1)} %get-tuple-element.78.refs_2_.refs_0_.coarse_ref, ...), custom_call_target="tpu_custom_call" | custom-call | tf_op jit(solution)/shard_map/gather_first/pallas_call | solution.py:34
  28.2 2.7 %collective-permute-start.10 = (f32[48,640]{1,0:T(8,128)S(1)}, f32[48,640]{1,0:T(8,128)S(1)}, u32[]{:S(2)}, u32[]{:S(2)}) collective-permute-start(f32[48,640]{1,0:T(8,128)S(1)} %get-tuple-element.96), channel_id=1, source_target_pairs={{0,32},{16,48},{32,0},{48,16},{1,33},{17,49},{33,1},{49,17},{2,34}... | collective-permute-start | bytes 368648 | tf_op jit(solution)/shard_map/ppermute | solution.py:431
  30.9 2.8 %gather_near.1 = (f32[48,640]{1,0:T(8,128)S(1)}, f32[48,640]{1,0:T(8,128)S(1)}) custom-call(s32[4,576]{1,0:T(4,128)S(1)} %get-tuple-element.97.request_ref.request_a, bf16[768,1152]{1,0:T(8,128)(2,1)S(1)} %get-tuple-element.94.rows_ref), custom_call_target="tpu_custom_call" | custom-call | tf_op jit(solution)/shard_map/gather_near/pallas_call | solution.py:34
  33.8 1.2 %collective-permute-start.11 = (f32[48,640]{1,0:T(8,128)S(1)}, f32[48,640]{1,0:T(8,128)S(1)}, u32[]{:S(2)}, u32[]{:S(2)}) collective-permute-start(f32[48,640]{1,0:T(8,128)S(1)} %get-tuple-element.98), channel_id=1, source_target_pairs={{0,48},{16,0},{32,16},{48,32},{1,49},{17,1},{33,17},{49,33},{2,50}... | collective-permute-start | bytes 368648 | tf_op jit(solution)/shard_map/ppermute | solution.py:431
  34.9 0.4 collective-permute-start.12
  35.3 1.1 %collective-permute-start.9 = (s32[4,576]{1,0:T(4,128)S(1)}, s32[4,576]{1,0:T(4,128)S(1)}, u32[]{:S(2)}, u32[]{:S(2)}) collective-permute-start(s32[4,576]{1,0:T(4,128)S(1)} %get-tuple-element.97.request_ref.request_a), channel_id=1, source_target_pairs={{0,8},{8,0},{1,9},{9,1},{2,10},{10,2},{3,11},{11,3},{4,12},{12,4},... | collective-permute-start | bytes 27656 | tf_op jit(solution)/shard_map/ppermute | solution.py:431
  36.5 1.7 %gather_own.1.refs_8_ = f32[48,640]{1,0:T(8,128)S(1)} custom-call(s32[4,576]{1,0:T(4,128)S(1)} %get-tuple-element.97.request_ref.request_a, bf16[768,1152]{1,0:T(8,128)(2,1)S(1)} %get-tuple-element.94.rows_ref), custom_call_target="tpu_custom_call" | custom-call | tf_op jit(solution)/shard_map/gather_own/pallas_call | solution.py:34
  38.2 0.7 %coagulate_coarse.1.growth_ref = f32[48,1152]{1,0:T(8,128)S(1)} custom-call(bf16[96,1280]{1,0:T(8,128)(2,1)S(1)} %fold_kernel.1.matrix_ref, f32[48,1152]{1,0:T(8,128)S(1)} %get-tuple-element.78.refs_2_.refs_0_.coarse_ref), custom_call_target="tpu_custom_call" | custom-call | tf_op jit(solution)/shard_map/coagulate_coarse/pallas_call | solution.py:34
  39.0 0.8 %cells_by_row.1.cell_ref = s32[4608,128]{1,0:T(8,128)S(1)} custom-call(s32[4,576]{1,0:T(4,128)S(1)} %get-tuple-element.97.request_ref.request_a, s32[4,576]{1,0:T(4,128)S(1)} %collective-permute-done.9.request_b), custom_call_target="tpu_custom_call" | custom-call | tf_op jit(solution)/shard_map/cells_by_row/pallas_call | solution.py:34
  39.8 0.1 collective-permute-done.12.refs_11_
  39.9 1.9 %first_stage.1 = (f32[48,1024]{1,0:T(8,128)S(1)}, f32[48,1024]{1,0:T(8,128)S(1)}, f32[48,1024]{1,0:T(8,128)S(1)}, f32[48,1024]{1,0:T(8,128)S(1)}, f32[48,1024]{1...) custom-call(s32[1,8]{1,0:T(1,128)S(1)} %copy-done.2, ...), custom_call_target="tpu_custom_call" | custom-call | tf_op jit(solution)/shard_map/first_stage/pallas_call | solution.py:34
  41.8 2.1 %collective-permute-start.15 = (f32[48,640]{1,0:T(8,128)S(1)}, f32[48,640]{1,0:T(8,128)S(1)}, u32[]{:S(2)}, u32[]{:S(2)}) collective-permute-start(f32[48,640]{1,0:T(8,128)S(1)} %get-tuple-element.119.refs_0_), channel_id=1, source_target_pairs={{0,8},{8,0},{1,9},{9,1},{2,10},{10,2},{3,11},{11,3},{4,12},{12,4},... | collective-permute-start | bytes 368648 | tf_op jit(solution)/shard_map/ppermute | solution.py:431
  43.9 1.6 %collective-permute-start.20 = (f32[48,640]{1,0:T(8,128)S(1)}, f32[48,640]{1,0:T(8,128)S(1)}, u32[]{:S(2)}, u32[]{:S(2)}) collective-permute-start(f32[48,640]{1,0:T(8,128)S(1)} %get-tuple-element.119.refs_0_), channel_id=1, source_target_pairs={{0,48},{16,0},{32,16},{48,32},{1,49},{17,1},{33,17},{49,33},{2,50}... | collective-permute-start | bytes 368648 | tf_op jit(solution)/shard_map/ppermute | solution.py:431
  45.4 0.6 collective-permute-start.18
  46.0 2.7 %collective-permute-start.17 = (f32[48,1024]{1,0:T(8,128)S(1)}, f32[48,1024]{1,0:T(8,128)S(1)}, u32[]{:S(2)}, u32[]{:S(2)}) collective-permute-start(f32[48,1024]{1,0:T(8,128)S(1)} %get-tuple-element.114.refs_0_), channel_id=1, source_target_pairs={{0,7},{1,0},{2,1},{3,2},{4,3},{5,4},{6,5},{7,6},{8,15},{9,8},{10,9... | collective-permute-start | bytes 589832 | tf_op jit(solution)/shard_map/ppermute | solution.py:431
  48.7 2.3 %coagulate_middle.1 = (f32[48,1024]{1,0:T(8,128)S(1)}, f32[48,1024]{1,0:T(8,128)S(1)}, f32[48,1024]{1,0:T(8,128)S(1)}, f32[48,1024]{1,0:T(8,128)S(1)}) custom-call(bf16[96,1280]{1,0:T(8,128)(2,1)S(1)} %fold_kernel.1.matrix_ref, f32[48,1024]{1,0:T(8,128)S(1)} %get-tuple-element.114.refs_0_, f32[48,1024]{1,0:T(8,128)S(1)} %get-tuple-element.116.refs_1_, ...), custom_call_target="tpu_custom_call" | custom-call | tf_op jit(solution)/shard_map/coagulate_middle/pallas_call | solution.py:34
  51.0 0.5 collective-permute-done.19.refs_2_
  51.5 2.7 %collective-permute-done.18.refs_1_ = f32[48,640]{1,0:T(8,128)S(1)} collective-permute-done((f32[48,640]{1,0:T(8,128)S(1)}, f32[48,640]{1,0:T(8,128)S(1)}, u32[]{:S(2)}, u32[]{:S(2)}) %collective-permute-start.18) | collective-permute-done | bytes 122912 | tf_op jit(solution)/shard_map/ppermute | solution.py:431
  54.3 0.8 %collective-permute-start.21 = (f32[48,640]{1,0:T(8,128)S(1)}, f32[48,640]{1,0:T(8,128)S(1)}, u32[]{:S(2)}, u32[]{:S(2)}) collective-permute-start(f32[48,640]{1,0:T(8,128)S(1)} %collective-permute-done.18.refs_1_), channel_id=1, source_target_pairs={{0,8},{8,0},{1,9},{9,1},{2,10},{10,2},{3,11},{11,3},{4,12},{12,4},... | collective-permute-start | bytes 368648 | tf_op jit(solution)/shard_map/ppermute | solution.py:431
  55.0 0.5 collective-permute-start.23
  55.5 0.5 collective-permute-done.21.refs_5_
  56.0 0.4 collective-permute-done.22.refs_6_
  56.4 0.2 collective-permute-done.23.refs_7_
  56.5 2.7 %scatter_far.1 = f32[48,1152]{1,0:T(8,128)S(1)} custom-call(s32[4,576]{1,0:T(4,128)S(1)} %get-tuple-element.97.request_ref.request_a, s32[4,576]{1,0:T(4,128)S(1)} %collective-permute-done.9.request_b, s32[4608,128]{1,0:T(8,128)S(1)} %cells_by_row.1.cell_ref, f32[48,640]{1,0:T(8,128)S(1)} %get-tuple-element.119.refs_0_, ...), custom_call_target="tpu_custom_call" | custom-call | tf_op jit(solution)/shard_map/scatter_far/pallas_call | solution.py:34
  59.2 0.6 collective-permute-start.25
  59.9 3.5 %scatter_near.1 = (f32[48,1152]{1,0:T(8,128)S(1)}, f32[48,1152]{1,0:T(8,128)S(1)}) custom-call(s32[4,576]{1,0:T(4,128)S(1)} %get-tuple-element.97.request_ref.request_a, s32[4,576]{1,0:T(4,128)S(1)} %collective-permute-done.9.request_b, s32[4608,128]{1,0:T(8,128)S(1)} %cells_by_row.1.cell_ref, f32[48,640]{1,0:T(8,128)S(1)} %get-tuple-element.119.refs_0_, ...), custom_call_target="tpu_custom_call" | custom-call | tf_op jit(solution)/shard_map/scatter_near/pallas_call | solution.py:34
  63.4 1.1 %collective-permute-start.26 = (f32[48,1152]{1,0:T(8,128)S(1)}, f32[48,1152]{1,0:T(8,128)S(1)}, u32[]{:S(2)}, u32[]{:S(2)}) collective-permute-start(f32[48,1152]{1,0:T(8,128)S(1)} %get-tuple-element.126), channel_id=1, source_target_pairs={{0,192},{64,0},{128,64},{192,128},{1,193},{65,1},{129,65},{193,129... | collective-permute-start | bytes 663560 | tf_op jit(solution)/shard_map/ppermute | solution.py:431
  64.5 0.4 collective-permute-start.24
  64.9 2.7 %scatter_own.1.a = f32[48,1152]{1,0:T(8,128)S(1)} custom-call(s32[4,576]{1,0:T(4,128)S(1)} %get-tuple-element.97.request_ref.request_a, s32[4,576]{1,0:T(4,128)S(1)} %collective-permute-done.9.request_b, s32[4608,128]{1,0:T(8,128)S(1)} %cells_by_row.1.cell_ref, f32[48,640]{1,0:T(8,128)S(1)} %get-tuple-element.119.refs_0_, ...), custom_call_target="tpu_custom_call" | custom-call | tf_op jit(solution)/shard_map/scatter_own/pallas_call | solution.py:34
  67.6 2.2 %second_stage.1 = f32[48,4,1024]{2,1,0:T(4,128)} custom-call(s32[1,8]{1,0:T(1,128)S(1)} %copy-done.2, f32[1,48]{1,0:T(1,128)S(1)} %bitcast.11, f32[48,1024]{1,0:T(8,128)S(1)} %get-tuple-element.114.refs_0_, f32[48,1024]{1,0:T(8,128)S(1)} %get-tuple-element.116.refs_1_, f32[48,1024]{1,0:T(8,128)S(1)} %get-tuple-element.117.refs_2_, ...), custom_call_target="tpu_custom_call" | custom-call | tf_op jit(solution)/shard_map/second_stage/pallas_call | solution.py:409
  69.9 1.8 %collective-permute-done.24.b = f32[48,1152]{1,0:T(8,128)S(1)} collective-permute-done((f32[48,1152]{1,0:T(8,128)S(1)}, f32[48,1152]{1,0:T(8,128)S(1)}, u32[]{:S(2)}, u32[]{:S(2)}) %collective-permute-start.24) | collective-permute-done | bytes 221216 | tf_op jit(solution)/shard_map/ppermute | solution.py:431
  71.7 0.8 %finish_coarse.1 = f32[48,1152]{1,0:T(8,128)} custom-call(f32[48,1152]{1,0:T(8,128)S(1)} %get-tuple-element.78.refs_2_.refs_0_.coarse_ref, f32[48,1152]{1,0:T(8,128)S(1)} %coagulate_coarse.1.growth_ref, f32[48,1152]{1,0:T(8,128)S(1)} %scatter_own.1.a, f32[48,1152]{1,0:T(8,128)S(1)} %collective-permute-done.24.b, f32[48,1152]{1,0:T(8,128)S(1)} %collective-permute-done.25.c, ...), custom_call_target="tpu_custom_call" | custom-call | tf_op jit(solution)/shard_map/finish_coarse/pallas_call | solution.py:34
  (34 shorter events, 0.1 us)
Async XLA Ops:
  1.3 10.3 %collective-permute-start.3 = (s32[24,576]{1,0:T(8,128)S(1)}, s32[24,576]{1,0:T(8,128)S(1)}, u32[]{:S(2)}, u32[]{:S(2)}) collective-permute-start(s32[24,576]{1,0:T(8,128)S(1)} %add.8), channel_id=1, source_target_pairs={{0,16},{16,32},{32,48},{48,0},{1,17},{17,33},{33,49},{49,1},{2,18}... | collective-permute-start | bytes 165896 | tf_op jit(solution)/shard_map/ppermute | solution.py:431
  3.5 15.5 %collective-permute-start.2 = (f32[48,1152]{1,0:T(8,128)}, f32[48,1152]{1,0:T(8,128)S(1)}, u32[]{:S(2)}, u32[]{:S(2)}) collective-permute-start(f32[48,1152]{1,0:T(8,128)} %bitcast.5), channel_id=1, source_target_pairs={{0,192},{64,0},{128,64},{192,128},{1,193},{65,1},{129,65},{193,129... | collective-permute-start | bytes 663560 | tf_op jit(solution)/shard_map/ppermute | solution.py:431
  6.0 13.0 %collective-permute-start.1 = (f32[48,1152]{1,0:T(8,128)}, f32[48,1152]{1,0:T(8,128)S(1)}, u32[]{:S(2)}, u32[]{:S(2)}) collective-permute-start(f32[48,1152]{1,0:T(8,128)} %bitcast.6), channel_id=1, source_target_pairs={{0,128},{64,192},{128,0},{192,64},{1,129},{65,193},{129,1},{193,65... | collective-permute-start | bytes 663560 | tf_op jit(solution)/shard_map/ppermute | solution.py:431
  6.5 13.3 %collective-permute-start = (f32[48,1152]{1,0:T(8,128)}, f32[48,1152]{1,0:T(8,128)S(1)}, u32[]{:S(2)}, u32[]{:S(2)}) collective-permute-start(f32[48,1152]{1,0:T(8,128)} %bitcast.7), channel_id=1, source_target_pairs={{0,64},{64,128},{128,192},{192,0},{1,65},{65,129},{129,193},{193,1... | collective-permute-start | bytes 663560 | tf_op jit(solution)/shard_map/ppermute | solution.py:431
  7.2 19.3 %collective-permute-start.5 = (f32[48,1152]{1,0:T(8,128)}, f32[48,1152]{1,0:T(8,128)S(1)}, u32[]{:S(2)}, u32[]{:S(2)}) collective-permute-start(f32[48,1152]{1,0:T(8,128)} %bitcast.8), channel_id=1, source_target_pairs={{0,8},{8,0},{1,9},{9,1},{2,10},{10,2},{3,11},{11,3},{4,12},{12,4},... | collective-permute-start | bytes 663560 | tf_op jit(solution)/shard_map/ppermute | solution.py:431
  8.9 0.9 %copy-start = (bf16[48,2304]{1,0:T(8,128)(2,1)S(1)}, bf16[48,2304]{1,0:T(8,128)(2,1)}, u32[]{:S(2)}) copy-start(bf16[48,2304]{1,0:T(8,128)(2,1)} %matrix_ref.1) | copy-start | bytes 663556
  11.7 7.3 %collective-permute-start.4 = (s32[24,576]{1,0:T(8,128)S(1)}, s32[24,576]{1,0:T(8,128)S(1)}, u32[]{:S(2)}, u32[]{:S(2)}) collective-permute-start(s32[24,576]{1,0:T(8,128)S(1)} %pad_add_fusion.refs_0_), channel_id=1, source_target_pairs={{0,32},{16,48},{32,0},{48,16},{1,33},{17,49},{33,1},{49,17},{2,34}... | collective-permute-start | bytes 165896 | tf_op jit(solution)/shard_map/ppermute | solution.py:431
  14.4 0.9 %copy-start.1 = (f32[1,1,48,1152]{3,2,1,0:T(8,128)S(1)}, f32[1,1,48,1152]{3,2,1,0:T(8,128)}, u32[]{:S(2)}) copy-start(f32[1,1,48,1152]{3,2,1,0:T(8,128)} %param.7) | copy-start | bytes 663556
  19.8 6.6 %collective-permute-start.6 = (f32[48,1152]{1,0:T(8,128)S(1)}, f32[48,1152]{1,0:T(8,128)S(1)}, u32[]{:S(2)}, u32[]{:S(2)}) collective-permute-start(f32[48,1152]{1,0:T(8,128)S(1)} %collective-permute-done.refs_4_), channel_id=1, source_target_pairs={{0,8},{8,0},{1,9},{9,1},{2,10},{10,2},{3,11},{11,3},{4,12},{12,4},... | collective-permute-start | bytes 663560 | tf_op jit(solution)/shard_map/ppermute | solution.py:431
  20.3 6.1 %collective-permute-start.7 = (f32[48,1152]{1,0:T(8,128)S(1)}, f32[48,1152]{1,0:T(8,128)S(1)}, u32[]{:S(2)}, u32[]{:S(2)}) collective-permute-start(f32[48,1152]{1,0:T(8,128)S(1)} %collective-permute-done.2.refs_6_), channel_id=1, source_target_pairs={{0,8},{8,0},{1,9},{9,1},{2,10},{10,2},{3,11},{11,3},{4,12},{12,4},... | collective-permute-start | bytes 663560 | tf_op jit(solution)/shard_map/ppermute | solution.py:431
  20.3 6.1 %collective-permute-start.8 = (f32[48,1152]{1,0:T(8,128)S(1)}, f32[48,1152]{1,0:T(8,128)S(1)}, u32[]{:S(2)}, u32[]{:S(2)}) collective-permute-start(f32[48,1152]{1,0:T(8,128)S(1)} %collective-permute-done.1.refs_8_), channel_id=1, source_target_pairs={{0,8},{8,0},{1,9},{9,1},{2,10},{10,2},{3,11},{11,3},{4,12},{12,4},... | collective-permute-start | bytes 663560 | tf_op jit(solution)/shard_map/ppermute | solution.py:431
  20.8 19.1 %collective-permute-start.14 = (f32[48,1024]{1,0:T(8,128)S(1)}, f32[48,1024]{1,0:T(8,128)S(1)}, u32[]{:S(2)}, u32[]{:S(2)}) collective-permute-start(f32[48,1024]{1,0:T(8,128)S(1)} %get-tuple-element.80.refs_0_), channel_id=1, source_target_pairs={{0,7},{1,0},{2,1},{3,2},{4,3},{5,4},{6,5},{7,6},{8,15},{9,8},{10,9... | collective-permute-start | bytes 589832 | tf_op jit(solution)/shard_map/ppermute | solution.py:431
  26.4 13.5 %collective-permute-start.13 = (f32[48,1024]{1,0:T(8,128)S(1)}, f32[48,1024]{1,0:T(8,128)S(1)}, u32[]{:S(2)}, u32[]{:S(2)}) collective-permute-start(f32[48,1024]{1,0:T(8,128)S(1)} %get-tuple-element.83.refs_3_), channel_id=1, source_target_pairs={{0,1},{1,2},{2,3},{3,4},{4,5},{5,6},{6,7},{7,0},{8,9},{9,10},{10,1... | collective-permute-start | bytes 589832 | tf_op jit(solution)/shard_map/ppermute | solution.py:431
  28.2 7.1 %collective-permute-start.10 = (f32[48,640]{1,0:T(8,128)S(1)}, f32[48,640]{1,0:T(8,128)S(1)}, u32[]{:S(2)}, u32[]{:S(2)}) collective-permute-start(f32[48,640]{1,0:T(8,128)S(1)} %get-tuple-element.96), channel_id=1, source_target_pairs={{0,32},{16,48},{32,0},{48,16},{1,33},{17,49},{33,1},{49,17},{2,34}... | collective-permute-start | bytes 368648 | tf_op jit(solution)/shard_map/ppermute | solution.py:431
  33.8 4.4 %collective-permute-start.11 = (f32[48,640]{1,0:T(8,128)S(1)}, f32[48,640]{1,0:T(8,128)S(1)}, u32[]{:S(2)}, u32[]{:S(2)}) collective-permute-start(f32[48,640]{1,0:T(8,128)S(1)} %get-tuple-element.98), channel_id=1, source_target_pairs={{0,48},{16,0},{32,16},{48,32},{1,49},{17,1},{33,17},{49,33},{2,50}... | collective-permute-start | bytes 368648 | tf_op jit(solution)/shard_map/ppermute | solution.py:431
  34.9 5.0 %copy-start.2 = (s32[1,8]{1,0:T(1,128)S(1)}, s32[1,8]{1,0:T(1,128)}, u32[]{:S(2)}) copy-start(s32[1,8]{1,0:T(1,128)} %levels_ref.3) | copy-start | bytes 100
  34.9 5.0 %copy-start.3 = (f32[48]{0:T(128)S(1)}, f32[48]{0:T(128)}, u32[]{:S(2)}) copy-start(f32[48]{0:T(128)} %param.9) | copy-start | bytes 580
  34.9 4.9 %collective-permute-start.12 = (f32[48,640]{1,0:T(8,128)S(1)}, f32[48,640]{1,0:T(8,128)S(1)}, u32[]{:S(2)}, u32[]{:S(2)}) collective-permute-start(f32[48,640]{1,0:T(8,128)S(1)} %get-tuple-element.95), channel_id=1, source_target_pairs={{0,16},{16,32},{32,48},{48,0},{1,17},{17,33},{33,49},{49,1},{2,18}... | collective-permute-start | bytes 368648 | tf_op jit(solution)/shard_map/ppermute | solution.py:431
  35.3 3.7 %collective-permute-start.9 = (s32[4,576]{1,0:T(4,128)S(1)}, s32[4,576]{1,0:T(4,128)S(1)}, u32[]{:S(2)}, u32[]{:S(2)}) collective-permute-start(s32[4,576]{1,0:T(4,128)S(1)} %get-tuple-element.97.request_ref.request_a), channel_id=1, source_target_pairs={{0,8},{8,0},{1,9},{9,1},{2,10},{10,2},{3,11},{11,3},{4,12},{12,4},... | collective-permute-start | bytes 27656 | tf_op jit(solution)/shard_map/ppermute | solution.py:431
  41.8 4.2 %collective-permute-start.15 = (f32[48,640]{1,0:T(8,128)S(1)}, f32[48,640]{1,0:T(8,128)S(1)}, u32[]{:S(2)}, u32[]{:S(2)}) collective-permute-start(f32[48,640]{1,0:T(8,128)S(1)} %get-tuple-element.119.refs_0_), channel_id=1, source_target_pairs={{0,8},{8,0},{1,9},{9,1},{2,10},{10,2},{3,11},{11,3},{4,12},{12,4},... | collective-permute-start | bytes 368648 | tf_op jit(solution)/shard_map/ppermute | solution.py:431
  43.9 7.2 %collective-permute-start.20 = (f32[48,640]{1,0:T(8,128)S(1)}, f32[48,640]{1,0:T(8,128)S(1)}, u32[]{:S(2)}, u32[]{:S(2)}) collective-permute-start(f32[48,640]{1,0:T(8,128)S(1)} %get-tuple-element.119.refs_0_), channel_id=1, source_target_pairs={{0,48},{16,0},{32,16},{48,32},{1,49},{17,1},{33,17},{49,33},{2,50}... | collective-permute-start | bytes 368648 | tf_op jit(solution)/shard_map/ppermute | solution.py:431
  45.4 6.1 %collective-permute-start.19 = (f32[48,640]{1,0:T(8,128)S(1)}, f32[48,640]{1,0:T(8,128)S(1)}, u32[]{:S(2)}, u32[]{:S(2)}) collective-permute-start(f32[48,640]{1,0:T(8,128)S(1)} %get-tuple-element.119.refs_0_), channel_id=1, source_target_pairs={{0,32},{16,48},{32,0},{48,16},{1,33},{17,49},{33,1},{49,17},{2,34}... | collective-permute-start | bytes 368648 | tf_op jit(solution)/shard_map/ppermute | solution.py:431
  45.4 8.8 %collective-permute-start.18 = (f32[48,640]{1,0:T(8,128)S(1)}, f32[48,640]{1,0:T(8,128)S(1)}, u32[]{:S(2)}, u32[]{:S(2)}) collective-permute-start(f32[48,640]{1,0:T(8,128)S(1)} %get-tuple-element.119.refs_0_), channel_id=1, source_target_pairs={{0,16},{16,32},{32,48},{48,0},{1,17},{17,33},{33,49},{49,1},{2,18}... | collective-permute-start | bytes 368648 | tf_op jit(solution)/shard_map/ppermute | solution.py:431
  46.0 9.5 %collective-permute-start.16 = (f32[48,1024]{1,0:T(8,128)S(1)}, f32[48,1024]{1,0:T(8,128)S(1)}, u32[]{:S(2)}, u32[]{:S(2)}) collective-permute-start(f32[48,1024]{1,0:T(8,128)S(1)} %get-tuple-element.113.refs_3_), channel_id=1, source_target_pairs={{0,1},{1,2},{2,3},{3,4},{4,5},{5,6},{6,7},{7,0},{8,9},{9,10},{10,1... | collective-permute-start | bytes 589832 | tf_op jit(solution)/shard_map/ppermute | solution.py:431
  46.0 9.5 %collective-permute-start.17 = (f32[48,1024]{1,0:T(8,128)S(1)}, f32[48,1024]{1,0:T(8,128)S(1)}, u32[]{:S(2)}, u32[]{:S(2)}) collective-permute-start(f32[48,1024]{1,0:T(8,128)S(1)} %get-tuple-element.114.refs_0_), channel_id=1, source_target_pairs={{0,7},{1,0},{2,1},{3,2},{4,3},{5,4},{6,5},{7,6},{8,15},{9,8},{10,9... | collective-permute-start | bytes 589832 | tf_op jit(solution)/shard_map/ppermute | solution.py:431
  54.3 1.7 %collective-permute-start.21 = (f32[48,640]{1,0:T(8,128)S(1)}, f32[48,640]{1,0:T(8,128)S(1)}, u32[]{:S(2)}, u32[]{:S(2)}) collective-permute-start(f32[48,640]{1,0:T(8,128)S(1)} %collective-permute-done.18.refs_1_), channel_id=1, source_target_pairs={{0,8},{8,0},{1,9},{9,1},{2,10},{10,2},{3,11},{11,3},{4,12},{12,4},... | collective-permute-start | bytes 368648 | tf_op jit(solution)/shard_map/ppermute | solution.py:431
  55.0 1.3 %collective-permute-start.22 = (f32[48,640]{1,0:T(8,128)S(1)}, f32[48,640]{1,0:T(8,128)S(1)}, u32[]{:S(2)}, u32[]{:S(2)}) collective-permute-start(f32[48,640]{1,0:T(8,128)S(1)} %collective-permute-done.19.refs_2_), channel_id=1, source_target_pairs={{0,8},{8,0},{1,9},{9,1},{2,10},{10,2},{3,11},{11,3},{4,12},{12,4},... | collective-permute-start | bytes 368648 | tf_op jit(solution)/shard_map/ppermute | solution.py:431
  55.0 1.5 %collective-permute-start.23 = (f32[48,640]{1,0:T(8,128)S(1)}, f32[48,640]{1,0:T(8,128)S(1)}, u32[]{:S(2)}, u32[]{:S(2)}) collective-permute-start(f32[48,640]{1,0:T(8,128)S(1)} %collective-permute-done.20.refs_3_), channel_id=1, source_target_pairs={{0,8},{8,0},{1,9},{9,1},{2,10},{10,2},{3,11},{11,3},{4,12},{12,4},... | collective-permute-start | bytes 368648 | tf_op jit(solution)/shard_map/ppermute | solution.py:431
  59.2 8.4 %collective-permute-start.25 = (f32[48,1152]{1,0:T(8,128)S(1)}, f32[48,1152]{1,0:T(8,128)S(1)}, u32[]{:S(2)}, u32[]{:S(2)}) collective-permute-start(f32[48,1152]{1,0:T(8,128)S(1)} %scatter_far.1), channel_id=1, source_target_pairs={{0,128},{64,192},{128,0},{192,64},{1,129},{65,193},{129,1},{193,65... | collective-permute-start | bytes 663560 | tf_op jit(solution)/shard_map/ppermute | solution.py:431
  63.4 6.5 %collective-permute-start.26 = (f32[48,1152]{1,0:T(8,128)S(1)}, f32[48,1152]{1,0:T(8,128)S(1)}, u32[]{:S(2)}, u32[]{:S(2)}) collective-permute-start(f32[48,1152]{1,0:T(8,128)S(1)} %get-tuple-element.126), channel_id=1, source_target_pairs={{0,192},{64,0},{128,64},{192,128},{1,193},{65,1},{129,65},{193,129... | collective-permute-start | bytes 663560 | tf_op jit(solution)/shard_map/ppermute | solution.py:431
  64.5 7.2 %collective-permute-start.24 = (f32[48,1152]{1,0:T(8,128)S(1)}, f32[48,1152]{1,0:T(8,128)S(1)}, u32[]{:S(2)}, u32[]{:S(2)}) collective-permute-start(f32[48,1152]{1,0:T(8,128)S(1)} %get-tuple-element.124), channel_id=1, source_target_pairs={{0,64},{64,128},{128,192},{192,0},{1,65},{65,129},{129,193},{193,1... | collective-permute-start | bytes 663560 | tf_op jit(solution)/shard_map/ppermute | solution.py:431
